TPU v7x, 32 devices: a whole 2x2x4 slice. The times are simulated.
32 devices in a mesh: row: 8 (over y, x, core), col: 4 (over z).
Axes of the slice: x: 2, y: 2, z: 4, core: 2. Of those that a mesh axis runs over, the one named last changes fastest.
Arguments:
- fine_input: bfloat16 [1, 256, 512, 256], P(None, 'row', 'col'), may hold values from -6 to 6
- coarse_feat: bfloat16 [1, 64, 128, 256], P(None, ('row', 'col')), may hold values from -6 to 6
- conv_weight: bfloat16 [3, 3, 256, 256], replicated, may hold values from -0.125 to 0.125
- step_scale: float32 [1000, 256], replicated, may hold values from 0.5 to 2
- timesteps: int32 [1], replicated, may hold values from 0 to 999
- cotangent: bfloat16 [1, 256, 512, 256], P(None, 'row', 'col'), may hold values from -6 to 6
Outputs:
- grad_fine: bfloat16 [1, 256, 512, 256], P(None, 'row', 'col')
- grad_coarse: bfloat16 [1, 64, 128, 256], P(None, ('row', 'col'))
- grad_weight: float32 [3, 3, 256, 256], replicated
All inputs are finite; a program needn't handle non-finite values.
Results may differ from a plain program's by a relative error of at most 0.013.
Values may be sent and summed in bfloat16 or wider, within the bound.
No kernel may reach another device: no remote copies, remote signals or barrier semaphores. Data moves between devices by JAX's collectives and lax.ppermute only.
A program may use at most 128 MiB of HBM per device.

v0:
```python
import jax
import jax.numpy as jnp
from jax import lax
from jax.sharding import PartitionSpec as P


def with_halo(block, sides, width):
    for axis, dim in sides:
        count = lax.axis_size(axis)
        forward = [(i, i + 1) for i in range(count - 1)]
        backward = [(target, source) for source, target in forward]
        low = lax.ppermute(
            lax.slice_in_dim(block, block.shape[dim] - width, None, axis=dim), axis, forward
        )
        high = lax.ppermute(lax.slice_in_dim(block, 0, width, axis=dim), axis, backward)
        block = jnp.concatenate([low, block, high], axis=dim)
    return block


def per_device(fine_input, coarse_feat, conv_weight, step_scale, timesteps, cotangent):
    frames, tile_rows, tile_cols, chans = fine_input.shape
    strip = lax.all_gather(coarse_feat, "col", axis=1, tiled=True)
    block = lax.dynamic_slice_in_dim(
        strip, lax.axis_index("col") * (tile_cols // 4), tile_cols // 4, 2
    )
    upper = jnp.repeat(jnp.repeat(block.astype(jnp.float32), 4, axis=1), 4, axis=2)
    hidden = fine_input.astype(jnp.float32) + upper
    sig = jax.nn.sigmoid(hidden)
    act = (hidden * sig).astype(jnp.bfloat16)
    onehot = (
        timesteps[:, None] == jnp.arange(step_scale.shape[0], dtype=jnp.int32)[None, :]
    ).astype(jnp.float32)
    picked = jnp.dot(onehot, step_scale, precision=lax.Precision.HIGHEST)
    dpre = (cotangent.astype(jnp.float32) * picked[:, None, None, :]).astype(jnp.bfloat16)
    pad_act = with_halo(act, (("row", 1), ("col", 2)), 1)
    pad_grad = with_halo(dpre, (("row", 1), ("col", 2)), 1)
    flat_grad = dpre.reshape(-1, chans)
    rows_w = []
    dact = jnp.zeros((frames * tile_rows * tile_cols, chans), jnp.float32)
    for i in range(3):
        taps = []
        for j in range(3):
            window = pad_act[:, i : i + tile_rows, j : j + tile_cols, :].reshape(-1, chans)
            taps.append(
                lax.dot_general(
                    window, flat_grad, (((0,), (0,)), ((), ())), preferred_element_type=jnp.float32
                )
            )
            moved = pad_grad[:, 2 - i : 2 - i + tile_rows, 2 - j : 2 - j + tile_cols, :].reshape(
                -1, chans
            )
            dact = dact + lax.dot_general(
                moved,
                conv_weight[i, j],
                (((1,), (1,)), ((), ())),
                preferred_element_type=jnp.float32,
            )
        rows_w.append(jnp.stack(taps))
    local_weight = jnp.stack(rows_w)
    summed = lax.psum(local_weight, ("row", "col"))
    pixels = frames * tile_rows * lax.axis_size("row") * tile_cols * lax.axis_size("col")
    grad_weight = summed / jnp.sqrt(jnp.float32(pixels))
    dhidden = dact.reshape(frames, tile_rows, tile_cols, chans) * sig * (1.0 + hidden * (1.0 - sig))
    grad_fine = dhidden.astype(jnp.bfloat16)
    pooled = (
        dhidden.reshape(frames, tile_rows // 4, 4, tile_cols // 4, 4, chans)
        .sum(axis=(2, 4))
        .astype(jnp.bfloat16)
    )
    grad_coarse = lax.all_to_all(pooled, "col", split_axis=1, concat_axis=2, tiled=True)
    return (grad_fine, grad_coarse, grad_weight)


def solution(mesh):
    return jax.shard_map(
        per_device,
        mesh=mesh,
        in_specs=(
            P(None, "row", "col", None),
            P(None, ("row", "col"), None, None),
            P(),
            P(),
            P(),
            P(None, "row", "col", None),
        ),
        out_specs=(P(None, "row", "col", None), P(None, ("row", "col"), None, None), P()),
        check_vma=False,
    )
```

profile of v0, /device:TPU:0, one launch (start us, length us, event | category | flops | bytes accessed | tf_op | source)
XLA Modules:
  0.0 279.2 jit_solution(6089069000665934525)
XLA Ops:
  8.9 2.1 multiply_convert_fusion.1
  11.0 2.4 collective-permute-start
  13.3 1.3 collective-permute-start.1
  14.6 18.1 %all_gather.3 = bf16[1,8,128,256]{3,2,0,1:T(8,128)(2,1)} all-gather(bf16[1,2,128,256]{3,2,0,1:T(8,128)(2,1)S(1)} %bitcast.194), channel_id=1, replica_groups=mesh['row'=8,'col'=4] {'col'}, dimensions={1}, use_global_device_ids=true | all-gather | bytes 655360 | tf_op jit(solution)/shard_map/all_gather | solution.py:22
  32.8 0.9 bitcast_convert_fusion
  33.8 1.3 broadcast_in_dim.13
  35.1 2.6 broadcast_in_dim.14
  37.7 3.7 %broadcast_in_dim.15 = f32[32,32,4,256]{3,0,2,1:T(8,128)} broadcast(f32[32,32,256]{2,0,1:T(8,128)} %broadcast_in_dim.14), dimensions={0,1,3} | broadcast | bytes 5242880 | tf_op jit(solution)/shard_map/broadcast_in_dim | solution.py:26
  41.4 5.4 %copy.29 = f32[1,32,128,256]{2,3,1,0:T(8,128)} copy(f32[1,32,128,256]{3,1,2,0:T(8,128)} %bitcast.184) | data formatting | bytes 8388608 | tf_op jit(solution)/shard_map/broadcast_in_dim | solution.py:26
  46.8 4.1 %copy.26 = bf16[1,32,128,256]{2,3,1,0:T(8,128)(2,1)} copy(bf16[1,32,128,256]{3,2,1,0:T(8,128)(2,1)} %param.6) | data formatting | bytes 4194304 | tf_op args[0]
  50.9 1.3 collective-permute-start.2
  52.2 4.9 %collective-permute-start.3 = (bf16[1,34,1,256]{3,2,1,0:T(2,128)(2,1)S(1)}, bf16[1,34,1,256]{3,2,1,0:T(2,128)(2,1)S(1)}, u32[]{:S(2)}, u32[]{:S(2)}) collective-permute-start(bf16[1,34,1,256]{3,2,1,0:T(2,128)(2,1)S(1)} %get-tuple-element.31), channel_id=1, source_target_pairs={{0,1},{1,2},{2,3},{4,5},{5,6},{6,7},{8,9},{9,10},{10,11},{12,13},{... | collective-permute-start | bytes 52232 | tf_op jit(solution)/shard_map/ppermute | solution.py:12
  58.5 1.2 pad_maximum_fusion.1
  59.7 4.0 %fusion.82 = (bf16[1,32,128,256]{3,2,1,0:T(8,128)(2,1)S(1)}, bf16[1,32,128,256]{3,2,1,0:T(8,128)(2,1)S(1)}, bf16[1,32,128,256]{3,2,1,0:T(8,128)(2,1)S(1)}, bf16[...) fusion(bf16[1,34,129,256]{3,2,1,0:T(8,128)(2,1)S(1)} %get-tuple-ele, ...), kind=kLoop, calls=%fused_computation.94 | loop fusion | bytes 25165824 | tf_op jit(solution)/shard_map/slice | solution.py:49
  63.7 0.7 fusion.59
  64.5 0.7 convolution_add_fusion.6
  65.2 0.7 convolution_add_fusion.5
  66.0 0.7 convolution_add_fusion.4
  66.7 0.8 convolution_add_fusion.3
  69.0 2.7 fusion
  71.7 5.6 %copy.30 = f32[1,32,128,256]{2,3,1,0:T(8,128)} copy(f32[1,32,128,256]{3,2,1,0:T(8,128)} %bitcast.183) | data formatting | bytes 8388608 | tf_op jit(solution)/shard_map/reshape | solution.py:63
  77.3 6.7 %fusion.81 = (bf16[1,32,128,256]{2,3,1,0:T(8,128)(2,1)}, f32[1,32,128,256]{2,3,1,0:T(8,128)}, bf16[1,32,128,256]{2,3,1,0:T(8,128)(2,1)S(1)}) fusion(f32[1,32,128,256]{2,3,1,0:T(8,128)} %copy.30, f32[1,32,128,256]{2,3,1,0:T(8,128)} %copy.29, bf16[1,32,128,256]{2,3,1,0:T(8,128)(2,1)} %copy.26), kind=kLoop, calls=%fused_computation.93 | loop fusion | flops 13631488 | bytes 18874368 | tf_op jit(solution)/shard_map/convert_element_type | solution.py:64
  84.1 1.3 collective-permute-start.4
  85.4 1.3 collective-permute-start.5
  87.4 4.9 %collective-permute-done.5 = bf16[1,1,128,256]{2,3,1,0:T(8,128)(2,1)S(1)} collective-permute-done((bf16[1,1,128,256]{2,3,1,0:T(8,128)(2,1)S(1)}, bf16[1,1,128,256]{2,3,1,0:T(8,128)(2,1)S(1)}, u32[]{:S(2)}, u32[]{:S(2)}) %collective-permute-start.5) | collective-permute-done | bytes 65568 | tf_op jit(solution)/shard_map/ppermute | solution.py:15
  92.6 3.1 %fusion.84 = (bf16[1,34,1,256]{2,3,1,0:T(8,128)(2,1)}, bf16[1,34,1,256]{2,3,1,0:T(8,128)(2,1)}) fusion(bf16[1,34,128,256]{2,3,1,0:T(8,128)(2,1)S(1)} %pad_maximum_fusion.3), kind=kLoop, calls=%fused_computation.96 | loop fusion | bytes 69632 | tf_op jit(solution)/shard_map/slice | solution.py:13
  95.6 2.2 copy.33
  97.8 4.2 %collective-permute-start.6 = (bf16[1,34,1,256]{3,1,2,0:T(8,128)(2,1)S(1)}, bf16[1,34,1,256]{3,1,2,0:T(8,128)(2,1)S(1)}, u32[]{:S(2)}, u32[]{:S(2)}) collective-permute-start(bf16[1,34,1,256]{3,1,2,0:T(8,128)(2,1)S(1)} %copy.33), channel_id=1, source_target_pairs={{0,1},{1,2},{2,3},{4,5},{5,6},{6,7},{8,9},{9,10},{10,11},{12,13},{... | collective-permute-start | bytes 52232 | tf_op jit(solution)/shard_map/ppermute | solution.py:12
  102.0 2.2 copy.35
  104.2 1.6 collective-permute-start.7
  105.8 3.0 %fusion.34 = f32[1,256,256]{2,1,0:T(8,128)} fusion(bf16[1,32,128,256]{3,2,1,0:T(8,128)(2,1)S(1)} %multiply_convert_fusion.1, bf16[1,32,128,256]{2,3,1,0:T(8,128)(2,1)} %copy-done.2, bf16[1,1,128,256]{2,3,1,0:T(8,128)(2,1)S(1)} %collective-permute-done.4), kind=kOutput, calls=%fused_computation.55 | convolution fusion | flops 537919488 | bytes 4521984 | tf_op jit(solution)/shard_map/dot_general | solution.py:45
  108.9 1.4 fusion.51
  110.3 1.9 copy.34
  112.2 1.9 copy.36
  114.1 6.5 %maximum_maximum_fusion = (bf16[1,34,129,256]{2,3,1,0:T(8,128)(2,1)S(1)}, bf16[1,34,129,256]{2,3,1,0:T(8,128)(2,1)S(1)}) fusion(bf16[1,1,128,256]{2,3,1,0:T(8,128)(2,1)S(1)} %collective-permute-done.5, bf16[1,32,128,256]{2,3,1,0:T(8,128)(2,1)} %copy-done.2, bf16[1,1,128,256]{2,3,1,0:T(8,128)(2,1)S(1)} %collective-permute-done.4, ...), kind=kLoop, calls=%fused_computation.8 | loop fusion | flops 17965056 | bytes 6754304 | tf_op jit(solution)/shard_map/concatenate | solution.py:16
  122.1 1.0 fusion.39
  123.1 1.0 fusion.45
  124.9 1.0 fusion.56
  126.1 0.8 copy-done.6
  127.0 1.6 pad_maximum_fusion.2
  128.6 5.6 %copy.31 = f32[1,32,128,256]{3,2,1,0:T(8,128)} copy(f32[1,32,128,256]{2,3,1,0:T(8,128)} %get-tuple-element.16) | data formatting | bytes 8388608 | tf_op jit(solution)/shard_map/mul | solution.py:63
  134.2 5.2 %reshape.129 = f32[8,4,32,4,256]{4,3,2,1,0:T(4,128)} reshape(f32[1,32,128,256]{3,2,1,0:T(8,128)} %copy.31) | data formatting | bytes 8388608 | tf_op jit(solution)/shard_map/reshape | solution.py:66
  139.3 4.3 %reduce_sum.9 = bf16[8,32,256]{2,1,0:T(8,128)(2,1)} reduce(f32[8,4,32,4,256]{4,3,2,1,0:T(4,128)} %reshape.129, f32[]{:T(128)} %constant.6.clone.1), dimensions={1,3}, to_apply=%region_0.0 | reduce | flops 983040 | bytes 4325380 | tf_op jit(solution)/shard_map/reduce_sum | solution.py:67
  143.6 5.5 %all-to-all-start = ((bf16[1,8,32,256]{3,2,0,1:T(8,128)(2,1)}), bf16[1,8,32,256]{3,2,0,1:T(8,128)(2,1)S(1)}, u32[]{:S(2)}, u32[]{:S(2)}) async-start(bf16[1,8,32,256]{3,2,0,1:T(8,128)(2,1)} %bitcast.169), calls=%async_computation | async-start | bytes 262144 | tf_op jit(solution)/shard_map/all_to_all | solution.py:70
  149.1 2.9 %copy.37 = bf16[1,32,128,256]{3,2,1,0:T(8,128)(2,1)} copy(bf16[1,32,128,256]{2,3,1,0:T(8,128)(2,1)S(1)} %copy-done.4) | data formatting | bytes 4194304
  152.0 3.6 %all-to-all-done = bf16[1,8,32,256]{3,2,0,1:T(8,128)(2,1)S(1)} async-done(((bf16[1,8,32,256]{3,2,0,1:T(8,128)(2,1)}), bf16[1,8,32,256]{3,2,0,1:T(8,128)(2,1)S(1)}, u32[]{:S(2)}, u32[]{:S(2)}) %all-to-all-start) | async-done | bytes 131104 | tf_op jit(solution)/shard_map/all_to_all | solution.py:70
  156.3 112.8 %all-reduce.2.cloned.1.call-done = f32[3,3,256,256]{3,2,1,0:T(8,128)} async-done(((f32[3,3,256,256]{3,2,1,0:T(8,128)}), f32[3,3,256,256]{3,2,1,0:T(8,128)}) %all-reduce.2.cloned.1.call-update) | async-done | bytes 2359312 | tf_op jit(solution)/shard_map/psum | solution.py:60
  269.1 3.3 %broadcast_multiply_fusion = f32[3,3,256,256]{3,2,1,0:T(8,128)} fusion(f32[3,3,256,256]{3,2,1,0:T(8,128)} %all-reduce.2.cloned.1.call-done), kind=kLoop, calls=%fused_computation.52 | loop fusion | flops 589824 | bytes 4718592 | tf_op jit(solution)/shard_map/div | solution.py:62
  (46 shorter events, 8.1 us)
Async XLA Ops:
  7.2 1.2 copy-start
  7.2 261.9 %all-reduce.2.cloned.1.call-start = ((), (), s32[]{:S(2)}) async-start(), calls=%async_computation.1 | async-start | bytes 4718592 | tf_op jit(solution)/shard_map/psum | solution.py:60
  8.9 5.8 %copy-start.8 = (bf16[1,2,128,256]{3,2,1,0:T(8,128)(2,1)S(1)}, bf16[1,2,128,256]{3,2,1,0:T(8,128)(2,1)}, u32[]{:S(2)}) copy-start(bf16[1,2,128,256]{3,2,1,0:T(8,128)(2,1)} %param.7) | copy-start | bytes 393220
  11.0 39.9 %collective-permute-start = (bf16[1,1,128,256]{3,2,1,0:T(8,128)(2,1)S(1)}, bf16[1,1,128,256]{3,2,1,0:T(8,128)(2,1)S(1)}, u32[]{:S(2)}, u32[]{:S(2)}) collective-permute-start(bf16[1,1,128,256]{3,2,1,0:T(8,128)(2,1)S(1)} %get-tuple-element.36), channel_id=1, source_target_pairs={{0,4},{4,8},{8,12},{12,16},{16,20},{20,24},{24,28},{1,5},{5,9},{9,... | collective-permute-start | bytes 196616 | tf_op jit(solution)/shard_map/ppermute | solution.py:12
  13.3 37.5 %collective-permute-start.1 = (bf16[1,1,128,256]{3,2,1,0:T(8,128)(2,1)S(1)}, bf16[1,1,128,256]{3,2,1,0:T(8,128)(2,1)S(1)}, u32[]{:S(2)}, u32[]{:S(2)}) collective-permute-start(bf16[1,1,128,256]{3,2,1,0:T(8,128)(2,1)S(1)} %get-tuple-element.37), channel_id=1, source_target_pairs={{4,0},{8,4},{12,8},{16,12},{20,16},{24,20},{28,24},{5,1},{9,5},{13... | collective-permute-start | bytes 196616 | tf_op jit(solution)/shard_map/ppermute | solution.py:15
  50.9 7.2 %collective-permute-start.2 = (bf16[1,34,1,256]{3,2,1,0:T(2,128)(2,1)S(1)}, bf16[1,34,1,256]{3,2,1,0:T(2,128)(2,1)S(1)}, u32[]{:S(2)}, u32[]{:S(2)}) collective-permute-start(bf16[1,34,1,256]{3,2,1,0:T(2,128)(2,1)S(1)} %get-tuple-element.30), channel_id=1, source_target_pairs={{1,0},{2,1},{3,2},{5,4},{6,5},{7,6},{9,8},{10,9},{11,10},{13,12},{... | collective-permute-start | bytes 52232 | tf_op jit(solution)/shard_map/ppermute | solution.py:15
  52.2 5.2 %copy-start.5 = (bf16[3,3,256,256]{3,2,1,0:T(8,128)(2,1)S(1)}, bf16[3,3,256,256]{3,2,1,0:T(8,128)(2,1)}, u32[]{:S(2)}) copy-start(bf16[3,3,256,256]{3,2,1,0:T(8,128)(2,1)} %param.8) | copy-start | bytes 3538948
  52.2 6.3 %collective-permute-start.3 = (bf16[1,34,1,256]{3,2,1,0:T(2,128)(2,1)S(1)}, bf16[1,34,1,256]{3,2,1,0:T(2,128)(2,1)S(1)}, u32[]{:S(2)}, u32[]{:S(2)}) collective-permute-start(bf16[1,34,1,256]{3,2,1,0:T(2,128)(2,1)S(1)} %get-tuple-element.31), channel_id=1, source_target_pairs={{0,1},{1,2},{2,3},{4,5},{5,6},{6,7},{8,9},{9,10},{10,11},{12,13},{... | collective-permute-start | bytes 52232 | tf_op jit(solution)/shard_map/ppermute | solution.py:12
  84.0 8.2 %copy-start.2 = (bf16[1,32,128,256]{2,3,1,0:T(8,128)(2,1)}, bf16[1,32,128,256]{2,3,1,0:T(8,128)(2,1)S(1)}, u32[]{:S(2)}) copy-start(bf16[1,32,128,256]{2,3,1,0:T(8,128)(2,1)S(1)} %get-tuple-element.17) | copy-start | bytes 6291460
  84.1 3.3 %collective-permute-start.4 = (bf16[1,1,128,256]{2,3,1,0:T(8,128)(2,1)S(1)}, bf16[1,1,128,256]{2,3,1,0:T(8,128)(2,1)S(1)}, u32[]{:S(2)}, u32[]{:S(2)}) collective-permute-start(bf16[1,1,128,256]{2,3,1,0:T(8,128)(2,1)S(1)} %get-tuple-element.32), channel_id=1, source_target_pairs={{0,4},{4,8},{8,12},{12,16},{16,20},{20,24},{24,28},{1,5},{5,9},{9,... | collective-permute-start | bytes 196616 | tf_op jit(solution)/shard_map/ppermute | solution.py:12
  85.4 6.9 %collective-permute-start.5 = (bf16[1,1,128,256]{2,3,1,0:T(8,128)(2,1)S(1)}, bf16[1,1,128,256]{2,3,1,0:T(8,128)(2,1)S(1)}, u32[]{:S(2)}, u32[]{:S(2)}) collective-permute-start(bf16[1,1,128,256]{2,3,1,0:T(8,128)(2,1)S(1)} %get-tuple-element.33), channel_id=1, source_target_pairs={{4,0},{8,4},{12,8},{16,12},{20,16},{24,20},{28,24},{5,1},{9,5},{13... | collective-permute-start | bytes 196616 | tf_op jit(solution)/shard_map/ppermute | solution.py:15
  97.8 12.5 %collective-permute-start.6 = (bf16[1,34,1,256]{3,1,2,0:T(8,128)(2,1)S(1)}, bf16[1,34,1,256]{3,1,2,0:T(8,128)(2,1)S(1)}, u32[]{:S(2)}, u32[]{:S(2)}) collective-permute-start(bf16[1,34,1,256]{3,1,2,0:T(8,128)(2,1)S(1)} %copy.33), channel_id=1, source_target_pairs={{0,1},{1,2},{2,3},{4,5},{5,6},{6,7},{8,9},{9,10},{10,11},{12,13},{... | collective-permute-start | bytes 52232 | tf_op jit(solution)/shard_map/ppermute | solution.py:12
  104.2 4.7 %copy-start.3 = (bf16[1,32,128,256]{2,3,1,0:T(8,128)(2,1)S(1)}, bf16[1,32,128,256]{2,3,1,0:T(8,128)(2,1)}, u32[]{:S(2)}) copy-start(bf16[1,32,128,256]{2,3,1,0:T(8,128)(2,1)} %copy-done.2) | copy-start | bytes 6291460
  104.2 8.0 %collective-permute-start.7 = (bf16[1,34,1,256]{3,1,2,0:T(8,128)(2,1)S(1)}, bf16[1,34,1,256]{3,1,2,0:T(8,128)(2,1)S(1)}, u32[]{:S(2)}, u32[]{:S(2)}) collective-permute-start(bf16[1,34,1,256]{3,1,2,0:T(8,128)(2,1)S(1)} %copy.35), channel_id=1, source_target_pairs={{1,0},{2,1},{3,2},{5,4},{6,5},{7,6},{9,8},{10,9},{11,10},{13,12},{... | collective-permute-start | bytes 52232 | tf_op jit(solution)/shard_map/ppermute | solution.py:15
  124.9 1.1 copy-start.7
  125.9 1.0 copy-start.6
  139.3 9.8 %copy-start.4 = (bf16[1,32,128,256]{2,3,1,0:T(8,128)(2,1)S(1)}, bf16[1,32,128,256]{2,3,1,0:T(8,128)(2,1)}, u32[]{:S(2)}) copy-start(bf16[1,32,128,256]{2,3,1,0:T(8,128)(2,1)} %get-tuple-element.15) | copy-start | bytes 6291460
  143.6 12.0 %all-to-all-start = ((bf16[1,8,32,256]{3,2,0,1:T(8,128)(2,1)}), bf16[1,8,32,256]{3,2,0,1:T(8,128)(2,1)S(1)}, u32[]{:S(2)}, u32[]{:S(2)}) async-start(bf16[1,8,32,256]{3,2,0,1:T(8,128)(2,1)} %bitcast.169), calls=%async_computation | async-start | bytes 262144 | tf_op jit(solution)/shard_map/all_to_all | solution.py:70
  155.6 116.7 %copy-start.1 = (f32[1000,256]{1,0:T(8,128)S(1)}, f32[1000,256]{1,0:T(8,128)}, u32[]{:S(2)}) copy-start(f32[1000,256]{1,0:T(8,128)} %param.9) | copy-start | bytes 3072004
Sparse Core Ops, SparseCore 0:
  128.7 140.3 all-reduce.1
where the time goes:
time: 280 us; the launch traced here: 279 us
  waiting for transfers between devices  122 us (44%)
  local copies, waits for them, and re-layouts  53.5 us (19%)
  other arithmetic  27.4 us (10%)
  starting transfers between devices  23.8 us (8%)
  matrix products  19.6 us (7%)
  blocking collectives  18.1 us (6%)
  between operations  15.1 us (5%)
    psum x1, waiting for transfers between devices, per_device(): summed = lax.psum(local_weight, ('row', 'col'))  113 us
    all_gather x1, blocking collectives, per_device(): strip = lax.all_gather(coarse_feat, 'col', axis=1, tiled=True)  18.1 us
    ppermute x4, starting transfers between devices, with_halo(): lax.ppermute(lax.slice_in_dim(block, block.shape[dim] - width, None, axis...  12.7 us
    dot_general x9, matrix products, per_device(): lax.dot_general(window, flat_grad, (((0,), (0,)), ((), ())), preferred_el...  10.4 us
    broadcast_in_dim x2, local copies, waits for them, and re-layouts, per_device(): jnp.repeat(jnp.repeat(block.astype(jnp.float32), 4, axis=1), 4, axis=2)  9.09 us
    dot_general x9, matrix products, per_device(): lax.dot_general(moved, conv_weight[i, j], (((1,), (1,)), ((), ())), prefe...  8.69 us
    concatenate x4, other arithmetic, with_halo(): block = jnp.concatenate([low, block, high], axis=dim)  8.31 us
    unnamed x20, local copies, waits for them, and re-layouts  8.22 us
  transfers between devices with their start and end apart: 10, of which 4 were waited for; matrix products, arithmetic and copies ran while one was open for 17% of the time, Pallas kernels for 0%

commit v1 on v0

v1 whole, which is shorter than its diff:
```python
import functools
import jax
import jax.numpy as jnp
from jax import lax
from jax.experimental import pallas as pl
from jax.experimental.pallas import tpu as pltpu
from jax.sharding import PartitionSpec as P

BF = jnp.bfloat16
F32 = jnp.float32
MB = 1024 * 1024
START_MIB = 53.7
LOAD_MIB = 50


def smem():
    return pl.BlockSpec(memory_space=pltpu.SMEM)


def vmem():
    return pl.BlockSpec(memory_space=pltpu.VMEM)


def params(mib):
    return pltpu.CompilerParams(vmem_limit_bytes=int(mib * MB))


def cost(flops, nbytes):
    return pl.CostEstimate(flops=flops, bytes_accessed=nbytes, transcendentals=0)


def hbm():
    return pl.BlockSpec(memory_space=pltpu.HBM)


def place():
    row = lax.axis_index("row")
    return lax.rem(row, 2), row // 2, lax.axis_index("col")


def start_kernel(n, cot, coarse, ahead, behind, *refs):
    blocks, (rough, high, low, sems) = refs[: n - 2], refs[n - 2 :]
    _, _, me = place()
    cr, _, ch = rough.shape
    rows, width, _ = cot.shape
    cols = rough.shape[1] // n
    pairs = (coarse, rough), (cot.at[:, width - 16 :, :], high), (cot.at[:, :16, :], low)
    copies = [pltpu.make_async_copy(*pair, sems.at[k]) for k, pair in enumerate(pairs)]
    for c in copies:
        c.start()
    copies[0].wait()
    outs = [blocks[0], ahead, *blocks[1:], behind]
    for s, out in enumerate(outs):
        start = pl.multiple_of(lax.rem(me + s, n) * cols, cols)
        for j in range(cr):
            out[j * cols : (j + 1) * cols, :] = rough[j, pl.ds(start, cols), :]
    r = lax.broadcasted_iota(jnp.int32, (rows, rows * 16), 0)
    p = lax.broadcasted_iota(jnp.int32, (rows, rows * 16), 1)
    for out, edge, pick, c in ((ahead, high, 15, copies[1]), (behind, low, 0, copies[2])):
        c.wait()
        sel = jnp.where(p == r * 16 + pick, 1.0, 0.0).astype(BF)
        col = jnp.dot(sel, edge[...].reshape(rows * 16, ch), preferred_element_type=F32)
        out[cr * cols :, :] = col.astype(BF)


def load_kernel(steps, cot, scales, near, scale, table, sems):
    rows = cot.shape[0]
    parts = sems.shape[0] - 1
    tall = rows // parts
    at = pl.multiple_of(steps[0] // 8 * 8, 8)
    pairs = [(scales.at[pl.ds(at, 8)], table)]
    pairs += [(cot.at[pl.ds(k * tall, tall)], near.at[pl.ds(k * tall, tall)]) for k in range(parts)]
    copies = [pltpu.make_async_copy(*pair, sems.at[k]) for k, pair in enumerate(pairs)]
    for c in copies:
        c.start()
    for c in copies:
        c.wait()
    scale[...] = table[pl.ds(lax.rem(steps[0], 8), 1), :]


def edge_kernel(n, offset, scale, cot, from_left, from_right, t_out, b_out, left, right):
    _, _, me = place()
    rows, width, _ = cot.shape
    sides = ((left, from_left, me > 0), (right, from_right, me < n - 1))
    for side, block, inside in sides:
        col = (block[offset:, :].astype(F32) * scale[...]).astype(BF).astype(F32)
        side[...] = jnp.where(inside, col, 0.0)
    idx = lax.broadcasted_iota(jnp.int32, (16, left.shape[1]), 0)
    for out, k in ((t_out, 0), (b_out, rows - 1)):
        out[:width, :] = (cot[k].astype(F32) * scale[...]).astype(BF)
        two = jnp.where(idx == 1, right[k : k + 1, :], 0.0)
        out[width:, :] = jnp.where(idx == 0, left[k : k + 1, :], two).astype(BF)


def gate(fine, coarse_row):
    width = fine.shape[1]
    cols = coarse_row.shape[0]
    a = lax.broadcasted_iota(jnp.int32, (width, cols), 0)
    b = lax.broadcasted_iota(jnp.int32, (width, cols), 1)
    up = jnp.where(a // (width // cols) == b, 1.0, 0.0).astype(BF)
    upper = jnp.dot(up, coarse_row, preferred_element_type=F32)
    hidden = fine.astype(F32) + upper[None]
    sig = 0.5 * jnp.tanh(0.5 * hidden) + 0.5
    return hidden, sig


def spread(moved, slot, rounded, left, right):
    width = rounded.shape[0]
    row = rounded.astype(F32)
    idx = lax.broadcasted_iota(jnp.int32, row.shape, 0)
    moved[0, slot] = jnp.where(idx == 0, left, pltpu.roll(row, 1, 0)).astype(BF)
    moved[1, slot] = rounded
    moved[2, slot] = jnp.where(idx == width - 1, right, pltpu.roll(row, width - 1, 0)).astype(BF)


def prepare_kernel(n, cr, scale, fine, cot, left, right, *refs):
    blocks, (act_t, moved, strip) = refs[:n], refs[n:]
    _, _, me = place()
    rows, width, ch = cot.shape
    cols = strip.shape[1]
    for s in range(n):
        src = lax.rem(me + n - s, n)
        for j in range(cr):
            strip[src * cr + j] = blocks[s][j * cols : (j + 1) * cols, :]

    def group(g, _):
        for q in range(4):
            r = g * 4 + q
            rounded = (cot[r].astype(F32) * scale[...]).astype(BF)
            spread(moved, r + 1, rounded, left[pl.ds(r, 1), :], right[pl.ds(r, 1), :])
        hidden, sig = gate(fine[pl.ds(g * 4, 4)], strip[g])
        act = (hidden * sig).astype(BF).reshape(4 * width, ch)
        act_t[:, pl.ds(pl.multiple_of(g * 4 * width, 4 * width), 4 * width)] = act.T
        return 0

    lax.fori_loop(0, rows // 4, group, 0)


def weight_kernel(act_t, above, below, moved_in, keep, send, moved):
    core, plane, z = place()
    _, rows, width, ch = moved.shape
    rows -= 2
    planes, zs, depth, half = keep.shape
    for slot, halo in ((0, above), (rows + 1, below)):
        ends = halo[width:, :].astype(F32)
        spread(moved, slot, halo[:width, :], ends[0:1], ends[1:2])
    step = ch // (planes * zs)
    z = lax.rem(z, zs)

    def tap(t, _):
        i, j = t // 3, lax.rem(t, 3)
        window = moved[2 - j, pl.ds(2 - i, rows)].reshape(rows * width, ch)
        acc = jnp.dot(act_t[...], window, preferred_element_type=F32)
        low, high = acc[:, :half], acc[:, half:]
        mine = jnp.where(core == 0, low, high).astype(BF)
        other = jnp.where(core == 0, high, low).astype(BF)
        at = pl.multiple_of(t * step, step)
        for p in range(planes):
            for c in range(zs):
                b = (p * zs + c) * step
                keep[p ^ plane, c ^ z, pl.ds(at, step), :] = mine[b : b + step]
                send[p ^ plane, c ^ z, pl.ds(at, step), :] = other[b : b + step]
        return 0

    lax.fori_loop(0, 9, tap, 0)


def input_kernel(first, size, n, after, moved, fine, strip, weight, *refs):
    gf, gc, fines, pooled, sems = refs[-5:]
    _, _, me = place()
    cr = strip.shape[0] // n
    _, width, ch = fine.shape
    cols = strip.shape[1]
    wide = jnp.concatenate([weight[t] for t in range(9)], axis=1)
    copies = []
    for g in range(size):
        k = ((n - 1 - (first + g) // cr) ^ me) * cr + (first + g) % cr
        r = 4 * k
        taps = [
            moved[2 - t % 3, pl.ds(2 - t // 3 + r, 4)].reshape(4 * width, ch) for t in range(9)
        ]
        dact = lax.dot_general(
            jnp.concatenate(taps, axis=1),
            wide,
            (((1,), (1,)), ((), ())),
            preferred_element_type=F32,
        ).reshape(4, width, ch)
        hidden, sig = gate(fine[pl.ds(r, 4)], strip[k])
        dhidden = dact * sig * (1.0 + hidden * (1.0 - sig))
        fines[g] = dhidden.astype(BF)
        tall = dhidden[0] + dhidden[1] + dhidden[2] + dhidden[3]
        for h in range(ch // 128):
            pooled[...] = tall[:, 128 * h : 128 * h + 128]
            every = [pooled[pl.ds(k, cols, stride=width // cols), :] for k in range(width // cols)]
            gc[g, :, 128 * h : 128 * h + 128] = functools.reduce(jnp.add, every).astype(BF)
        copies.append(pltpu.make_async_copy(fines.at[g], gf.at[pl.ds(r, 4)], sems.at[g]))
        copies[-1].start()
    for c in copies:
        c.wait()


def finish_kernel(norm, zs, spots, n, *refs):
    pieces, parts = refs[: len(spots)], refs[len(spots) : len(spots) + n]
    scratch, sems = refs[-2:]
    out = refs[-3] if not n else refs[-4]
    core, plane, me = place()
    planes = lax.axis_size("row") // 2
    ch = out.shape[1]
    half = ch // 2
    tall = ch // planes
    step = tall // zs
    z = lax.rem(me, zs)
    copies = []
    for k, (flip, s, first) in enumerate(spots):
        lanes = pl.ds(pl.multiple_of((core ^ flip) * half, half), half)
        for c in range(pieces[k].shape[0]):
            x = pieces[k][c].astype(F32) * norm
            for t in range(9):
                scratch[k, c, t] = x[t * step : (t + 1) * step]
            b = pl.multiple_of((plane ^ s) * tall + ((first + c) ^ z) * step, step)
            copies.append(
                pltpu.make_async_copy(
                    scratch.at[k, c], out.at[:, pl.ds(b, step), lanes], sems.at[k, c]
                )
            )
            copies[-1].start()
    if n:
        coarse = refs[-3]
        cols = parts[0].shape[1]
        for s in range(n):
            start = pl.multiple_of((me ^ s) * cols, cols)
            coarse[:, pl.ds(start, cols), :] = parts[s][...]
    for c in copies:
        c.wait()


def xor_pairs(count, bit):
    return [(i, i ^ bit) for i in range(count)]


def per_device(fine_input, coarse_feat, conv_weight, step_scale, timesteps, cotangent):
    _, rows, width, ch = fine_input.shape
    n = lax.axis_size("col")
    nrow = lax.axis_size("row")
    planes = nrow // 2
    cr = coarse_feat.shape[1]
    cols = width // 4
    fine, cot, coarse = fine_input[0], cotangent[0], coarse_feat[0]
    weight = conv_weight.reshape(9, ch, ch)

    def shape(*dims, dtype=BF):
        return jax.ShapeDtypeStruct(dims, dtype)

    block, packed = shape(cr * cols, ch), shape(cr * cols + rows, ch)
    ahead, behind, *blocks = pl.pallas_call(
        functools.partial(start_kernel, n),
        out_shape=[packed, packed] + [block] * (n - 2),
        in_specs=[hbm(), hbm()],
        out_specs=[vmem()] * n,
        scratch_shapes=[
            pltpu.VMEM(coarse.shape, BF),
            pltpu.VMEM((rows, 16, ch), BF),
            pltpu.VMEM((rows, 16, ch), BF),
            pltpu.SemaphoreType.DMA((3,)),
        ],
        compiler_params=params(START_MIB),
        cost_estimate=cost(1 << 20, 1 << 20),
        name="start",
    )(cot, coarse)
    cot, scale = pl.pallas_call(
        load_kernel,
        out_shape=[shape(*cot.shape), shape(1, ch, dtype=F32)],
        in_specs=[smem(), hbm(), hbm()],
        out_specs=[vmem()] * 2,
        scratch_shapes=[pltpu.VMEM((8, ch), F32), pltpu.SemaphoreType.DMA((9,))],
        compiler_params=params(LOAD_MIB),
        cost_estimate=cost(1 << 20, 4 << 20),
        name="load",
    )(timesteps, cot, step_scale)

    def turn(x, s):
        return lax.ppermute(x, "col", [(i, (i + s) % n) for i in range(n)])

    from_left, from_right = turn(ahead, 1), turn(behind, n - 1)
    blocks = [blocks[0], from_left]+[turn(blocks[s - 1], s) for s in range(2, n - 1)] + [from_right]

    halo, side = shape(width + 16, ch), shape(rows, ch, dtype=F32)
    top, bottom, left, right = pl.pallas_call(
        functools.partial(edge_kernel, n, cr * cols),
        out_shape=[halo, halo, side, side],
        in_specs=[vmem()] * 4,
        out_specs=[vmem()] * 4,
        compiler_params=params(4),
        cost_estimate=cost(1 << 18, 1 << 19),
        name="edges",
    )(scale, cot, from_left, from_right)
    row_up = [(i, i + 1) for i in range(nrow - 1)]
    above = lax.ppermute(bottom, "row", row_up)
    below = lax.ppermute(top, "row", [(j, i) for i, j in row_up])

    groups = rows // 4
    act_t, moved, strip = pl.pallas_call(
        functools.partial(prepare_kernel, n, cr),
        out_shape=[
            shape(ch, rows * width),
            shape(3, rows + 2, width, ch),
            shape(groups, cols, ch),
        ],
        in_specs=[vmem()] * (5 + n),
        out_specs=[vmem()] * 3,
        compiler_params=params(8),
        cost_estimate=cost(1 << 32, 4 << 20),
        name="prepare",
    )(scale, fine, cot, left, right, *blocks)

    halves = n // 2
    aligned = ch // (planes * halves) % 16 == 0
    zs = halves if aligned else 1
    depth = 9 * ch // (planes * zs)
    half = ch // 2
    part = shape(planes, zs, depth, half)
    keep, send, moved = pl.pallas_call(
        weight_kernel,
        out_shape=[part, part, shape(*moved.shape)],
        in_specs=[vmem()] * 4,
        out_specs=[vmem()] * 3,
        input_output_aliases={3: 2},
        compiler_params=params(8),
        cost_estimate=cost(2 * 9 * rows * width * ch * ch, 8 << 20),
        name="weight_grad",
    )(act_t, above, below, moved)

    done, pooled, made = [], [], 0

    def input_piece(size, after):
        nonlocal done, made
        *done, gc = pl.pallas_call(
            functools.partial(input_kernel, made, size, n),
            out_shape=[shape(rows, width, ch), shape(size, cols, ch)],
            in_specs=[pl.BlockSpec(memory_space=pl.ANY)]
            + [vmem()] * 4
            + [pl.BlockSpec(memory_space=pl.ANY) for _ in done],
            out_specs=[pl.BlockSpec(memory_space=pl.ANY), vmem()],
            input_output_aliases={5: 0} if done else {},
            scratch_shapes=[
                pltpu.VMEM((size, 4, width, ch), BF),
                pltpu.VMEM((width, 128), F32),
                pltpu.SemaphoreType.DMA((size,)),
            ],
            compiler_params=params(12),
            cost_estimate=cost(2 * 9 * 4 * size * width * ch * ch, 4 << 20),
            name="input_grad",
        )(after, moved, fine, strip, weight, *done)
        pooled.append(gc)
        made += size

    def beside(got, size, after):
        nonlocal done, pooled
        if size:
            input_piece(size, after)
            got, done, pooled = lax.optimization_barrier((got, done, pooled))
        return got

    parts = {}

    def pooled_strip(s):
        rows_done = [x[g : g + 1] for x in pooled for g in range(x.shape[0])]
        return jnp.concatenate(rows_done[(n - 1 - s) * cr : (n - s) * cr])

    def send_pooled(got, limit):
        nonlocal parts
        ready = [s for s in range(n - 1, 0, -1) if s not in parts and (n - s) * cr <= made]
        for s in ready[:limit]:
            parts[s] = col_swap(pooled_strip(s), s)
        if ready:
            got, parts = lax.optimization_barrier((got, parts))
        return got

    def add(*terms):
        return functools.reduce(jnp.add, [t.astype(F32) for t in terms]).astype(BF)

    def core_swap(x):
        return lax.ppermute(x, "row", xor_pairs(nrow, 1))

    def plane_swap(x, s):
        return lax.ppermute(x, "row", xor_pairs(nrow, 2 * s))

    def col_swap(x, s):
        return lax.ppermute(x, "col", xor_pairs(n, s))

    sizes = piece_sizes(rows // 4)
    total = add(keep, *beside([core_swap(send)], sizes[0], send))
    got = [plane_swap(total[s], s) for s in range(1, planes)]
    total = add(total[0], *beside(got, sizes[1], total))
    if not aligned:
        order = jnp.arange(halves) ^ (lax.axis_index("col") % halves)
        total = total.reshape(halves, depth // halves, half)[order]
    bit = halves // 2
    while bit:
        got = [col_swap(total[bit:], bit)]
        if bit == 1:
            got = send_pooled(got, n // 2)
        total = add(total[:bit], *got)
        bit //= 2
    got = [col_swap(total, halves)]
    got = send_pooled(got, n)
    total = add(total, *beside(got, sizes[2], total))
    bit = 1
    while bit < (halves // 2 if aligned else halves):
        total = jnp.concatenate([total, col_swap(total, bit)])
        bit *= 2
    if not aligned:
        total = total[order].reshape(1, depth, half)
    ways = list(range(planes - 1, 0, -1))
    near = [total] + [plane_swap(total, s) for s in ways]
    waves = [near] + ([[col_swap(x, bit) for x in near]] if aligned else [])
    missing = [s for s in range(1, n) if s not in parts]
    parts.update({s: col_swap(pooled_strip(s), s) for s in missing})
    parts[0] = pooled_strip(0)
    pixels = rows * nrow * width * n

    def finish(out, pieces, spots, parts=()):
        coarse = [shape(cr, n * cols, ch)] if parts else []
        count, tall = len(pieces), pieces[0].shape[0]
        return pl.pallas_call(
            functools.partial(finish_kernel, float(pixels) ** -0.5, zs, spots, len(parts)),
            out_shape=[shape(9, ch, ch, dtype=F32)] + coarse,
            in_specs=[vmem()] * (count + len(parts)) + [hbm() for _ in out],
            out_specs=[hbm()] + [vmem() for _ in coarse],
            input_output_aliases={count + len(parts): 0} if out else {},
            scratch_shapes=[
                pltpu.VMEM((count, tall, 9, depth // 9, half), F32),
                pltpu.SemaphoreType.DMA((count, tall)),
            ],
            compiler_params=params(8),
            cost_estimate=cost(1 << 20, 4 << 20),
            name="finish",
        )(*pieces, *parts, *out)

    *out, grad_coarse = finish([], near[:1], ((0, 0, 0),), [parts[s] for s in range(n)])
    for k, wave in enumerate(waves):
        final = k + 1 == len(waves)
        spots = [(s, k * total.shape[0]) for s in [0] + ways]
        heads = wave[:-1] if final else wave
        swapped = core_swap(jnp.stack(heads))
        others = [swapped[i] for i in range(len(heads))]
        here = list(zip(wave, spots))[1 if k == 0 else 0 :]
        there = list(zip(others, spots))
        pieces = [x for x, _ in here + there]
        places = [(0, *spot) for _, spot in here] + [(1, *spot) for _, spot in there]
        out = finish(out, pieces, tuple(places))
        if final:
            out = finish(out, [core_swap(wave[-1])], ((1, *spots[-1]),))
    return (done[0][None], grad_coarse[None], out[0].reshape(3, 3, ch, ch))


def piece_sizes(groups):
    sizes = [groups // 8, groups * 5 // 8]
    return sizes + [groups - sum(sizes)]


def solution(mesh):
    return jax.shard_map(
        per_device,
        mesh=mesh,
        in_specs=(
            P(None, "row", "col", None),
            P(None, ("row", "col"), None, None),
            P(),
            P(),
            P(),
            P(None, "row", "col", None),
        ),
        out_specs=(P(None, "row", "col", None), P(None, ("row", "col"), None, None), P()),
        check_vma=False,
    )
```

time: 280 us -> 74.6 us (0.27)
  waiting for transfers between devices: 122 us -> 15.6 us
  local copies, waits for them, and re-layouts: 53.5 us -> 0.09 us
  other arithmetic: 27.4 us -> 0.36 us
  Pallas kernels: 0 us -> 26.3 us
  matrix products: 19.6 us -> 0 us
  blocking collectives: 18.1 us -> 0 us
  between operations: 15.1 us -> 1.58 us
  starting transfers between devices: 23.8 us -> 30.5 us
    psum x1 -> x0, waiting for transfers between devices: 113 us -> none  [per_device(): summed = lax.psum(local_weight, ('row', 'col'))]
    pallas_call x0 -> x12, Pallas kernels: none -> 26.3 us  [the longest x3 8.93 us: input_piece(): pl.pallas_call(functools.partial(input_kernel, made, size, n), out_shape=...]
    dot_general x19 -> x0, matrix products: 19.6 us -> none  [the longest x9 10.4 us: per_device(): lax.dot_general(window, flat_grad, (((0,), (0,)), ((), ())), preferred_el...]
    all_gather x1 -> x0, blocking collectives: 18.1 us -> none  [per_device(): strip = lax.all_gather(coarse_feat, 'col', axis=1, tiled=True)]
    broadcast_in_dim x4 -> x0, local copies, waits for them, and re-layouts: 12.9 us -> none  [the longest x2 9.09 us: per_device(): jnp.repeat(jnp.repeat(block.astype(jnp.float32), 4, axis=1), 4, axis=2)]
    ppermute x8 -> x24, starting transfers between devices: 18.2 us -> 30.5 us  [the longest x9 11 us: col_swap(): return lax.ppermute(x, 'col', xor_pairs(n, s))]
    slice x6 -> x2, local copies, waits for them, and re-layouts: 11.4 us -> 0.01 us  [the longest x1 0.01 us: per_device(): got = [col_swap(total[bit:], bit)]]
    reshape x2 -> x0, local copies, waits for them, and re-layouts: 10.7 us -> none  [the longest x1 5.57 us: per_device(): dact.reshape(frames, tile_rows, tile_cols, chans) * sig]
  transfers between devices with their start and end apart: 10 -> 24, of which waited for: 4 -> 13; matrix products, arithmetic and copies ran while one was open for 17% -> 0% of each run, Pallas kernels for 0% -> 24%
where the time goes in v1:
time: 74.6 us; the launch traced here: 74.4 us
  starting transfers between devices  30.5 us (41%)
  Pallas kernels  26.3 us (35%)
  waiting for transfers between devices  15.6 us (21%)
  between operations  1.58 us (2%)
    ppermute x9, starting transfers between devices, col_swap(): return lax.ppermute(x, 'col', xor_pairs(n, s))  11 us
    pallas_call x3, Pallas kernels, input_piece(): pl.pallas_call(functools.partial(input_kernel, made, size, n), out_shape=...  8.93 us
    ppermute x9, waiting for transfers between devices, col_swap(): return lax.ppermute(x, 'col', xor_pairs(n, s))  8.76 us
    ppermute x6, starting transfers between devices, plane_swap(): return lax.ppermute(x, 'row', xor_pairs(nrow, 2 * s))  7.63 us
    pallas_call x1, Pallas kernels, per_device(): pl.pallas_call(weight_kernel, out_shape=[part, part, shape(*moved.shape)]...  6.52 us
    ppermute x6, waiting for transfers between devices, plane_swap(): return lax.ppermute(x, 'row', xor_pairs(nrow, 2 * s))  6.25 us
    ppermute x3, starting transfers between devices, turn(): return lax.ppermute(x, 'col', [(i, (i + s) % n) for i in range(n)])  6.11 us
    pallas_call x4, Pallas kernels, finish(): pl.pallas_call(functools.partial(finish_kernel, float(pixels) ** (-0.5),...  4.13 us
  transfers between devices with their start and end apart: 24, of which 13 were waited for; matrix products, arithmetic and copies ran while one was open for 0% of the time, Pallas kernels for 24%

profile of v1, /device:TPU:0, one launch (start us, length us, event | category | flops | bytes accessed | tf_op | source)
XLA Modules:
  0.0 74.4 jit_solution(12428644427525907153)
XLA Ops:
  0.6 1.5 %start.1 = (bf16[96,256]{1,0:T(8,128)(2,1)S(1)}, bf16[96,256]{1,0:T(8,128)(2,1)S(1)}, bf16[64,256]{1,0:T(8,128)(2,1)S(1)}, bf16[64,256]{1,0:T(8,128)(2,1)S(1)}) custom-call(bf16[32,128,256]{2,1,0:T(8,128)(2,1)} %bitcast.54, bf16[2,128,256]{2,1,0:T(8,128)(2,1)} %bitcast.57), custom_call_target="tpu_custom_call" | custom-call | flops 1048576 | bytes 1048576 | tf_op jit(solution)/shard_map/start/pallas_call | solution.py:255
  2.2 3.1 %collective-permute-start = (bf16[96,256]{1,0:T(8,128)(2,1)S(1)}, bf16[96,256]{1,0:T(8,128)(2,1)S(1)}, u32[]{:S(2)}, u32[]{:S(2)}) collective-permute-start(bf16[96,256]{1,0:T(8,128)(2,1)S(1)} %get-tuple-element.48), channel_id=1, source_target_pairs={{0,1},{1,2},{2,3},{3,0},{4,5},{5,6},{6,7},{7,4},{8,9},{9,10},{10,1... | collective-permute-start | bytes 147464 | tf_op jit(solution)/shard_map/ppermute | solution.py:282
  5.2 2.1 %collective-permute-start.1 = (bf16[96,256]{1,0:T(8,128)(2,1)S(1)}, bf16[96,256]{1,0:T(8,128)(2,1)S(1)}, u32[]{:S(2)}, u32[]{:S(2)}) collective-permute-start(bf16[96,256]{1,0:T(8,128)(2,1)S(1)} %get-tuple-element.49), channel_id=1, source_target_pairs={{0,3},{1,0},{2,1},{3,2},{4,7},{5,4},{6,5},{7,6},{8,11},{9,8},{10,9... | collective-permute-start | bytes 147464 | tf_op jit(solution)/shard_map/ppermute | solution.py:282
  7.3 0.9 %collective-permute-start.2 = (bf16[64,256]{1,0:T(8,128)(2,1)S(1)}, bf16[64,256]{1,0:T(8,128)(2,1)S(1)}, u32[]{:S(2)}, u32[]{:S(2)}) collective-permute-start(bf16[64,256]{1,0:T(8,128)(2,1)S(1)} %get-tuple-element.53), channel_id=1, source_target_pairs={{0,2},{1,3},{2,0},{3,1},{4,6},{5,7},{6,4},{7,5},{8,10},{9,11},{10,... | collective-permute-start | bytes 98312 | tf_op jit(solution)/shard_map/ppermute | solution.py:282
  8.9 1.7 %load.1 = (bf16[32,128,256]{2,1,0:T(8,128)(2,1)S(1)}, f32[1,256]{1,0:T(1,128)S(1)}) custom-call(s32[1]{0:T(128)S(6)} %copy.21.steps, bf16[32,128,256]{2,1,0:T(8,128)(2,1)} %bitcast.55, f32[1000,256]{1,0:T(8,128)S(1)} %copy-done.2), custom_call_target="tpu_custom_call" | custom-call | flops 1048576 | bytes 4194304 | tf_op jit(solution)/shard_map/load/pallas_call | solution.py:270
  10.8 1.3 %collective-permute-start.3 = (bf16[144,256]{1,0:T(8,128)(2,1)S(1)}, bf16[144,256]{1,0:T(8,128)(2,1)S(1)}, u32[]{:S(2)}, u32[]{:S(2)}) collective-permute-start(bf16[144,256]{1,0:T(8,128)(2,1)S(1)} %get-tuple-element.55), channel_id=1, source_target_pairs={{0,4},{4,8},{8,12},{12,16},{16,20},{20,24},{24,28},{1,5},{5,9},{9,... | collective-permute-start | bytes 221192 | tf_op jit(solution)/shard_map/ppermute | solution.py:298
  12.1 1.3 %collective-permute-start.4 = (bf16[144,256]{1,0:T(8,128)(2,1)S(1)}, bf16[144,256]{1,0:T(8,128)(2,1)S(1)}, u32[]{:S(2)}, u32[]{:S(2)}) collective-permute-start(bf16[144,256]{1,0:T(8,128)(2,1)S(1)} %get-tuple-element.56), channel_id=1, source_target_pairs={{4,0},{8,4},{12,8},{16,12},{20,16},{24,20},{28,24},{5,1},{9,5},{13... | collective-permute-start | bytes 221192 | tf_op jit(solution)/shard_map/ppermute | solution.py:299
  13.4 3.4 %prepare.1 = (bf16[256,4096]{1,0:T(8,128)(2,1)S(1)}, bf16[3,34,128,256]{3,2,1,0:T(8,128)(2,1)S(1)}, bf16[8,32,256]{2,1,0:T(8,128)(2,1)S(1)}) custom-call(f32[1,256]{1,0:T(1,128)S(1)} %get-tuple-element.46.scale, bf16[32,128,256]{2,1,0:T(8,128)(2,1)S(1)} %bitcast.39, bf16[32,128,256]{2,1,0:T(8,128)(2,1)S(1)} %get-tuple-element.47.cot, ...), custom_call_target="tpu_custom_call" | custom-call | flops 4294967296 | bytes 4194304 | tf_op jit(solution)/shard_map/prepare/pallas_call | solution.py:302
  16.8 0.1 collective-permute-done.4.below
  17.0 6.5 %weight_grad.1 = (bf16[4,2,288,128]{3,2,1,0:T(8,128)(2,1)S(1)}, bf16[4,2,288,128]{3,2,1,0:T(8,128)(2,1)S(1)}, bf16[3,34,128,256]{3,2,1,0:T(8,128)(2,1)S(1)}) custom-call(bf16[256,4096]{1,0:T(8,128)(2,1)S(1)} %get-tuple-element.54.act_t, bf16[144,256]{1,0:T(8,128)(2,1)S(1)} %collective-permute-done.3.above, ...), custom_call_target="tpu_custom_call", output_to_operand_aliasing={{2}: (3, {})} | custom-call | flops 4831838208 | bytes 8388608 | tf_op jit(solution)/shard_map/weight_grad/pallas_call | solution.py:322
  23.5 3.1 %collective-permute-start.5 = (bf16[4,2,288,128]{3,2,1,0:T(8,128)(2,1)S(1)}, bf16[4,2,288,128]{3,2,1,0:T(8,128)(2,1)S(1)}, u32[]{:S(2)}, u32[]{:S(2)}) collective-permute-start(bf16[4,2,288,128]{3,2,1,0:T(8,128)(2,1)S(1)} %get-tuple-element.59.after), channel_id=1, source_target_pairs={{0,4},{4,0},{8,12},{12,8},{16,20},{20,16},{24,28},{28,24},{1,5},{5... | collective-permute-start | bytes 1769480 | tf_op jit(solution)/shard_map/ppermute | solution.py:383
  26.6 1.7 %input_grad.3 = (bf16[32,128,256]{2,1,0:T(8,128)(2,1)}, bf16[1,32,256]{2,1,0:T(8,128)(2,1)S(1)}) custom-call(bf16[4,2,288,128]{3,2,1,0:T(8,128)(2,1)S(1)} %get-tuple-element.59.after, bf16[3,34,128,256]{3,2,1,0:T(8,128)(2,1)S(1)} %get-tuple-element.60.moved, bf16[32,128,256]{2,1,0:T(8,128)(2,1)S(1)} %bitcast.40, ...), custom_call_target="tpu_custom_call" | custom-call | flops 603979776 | bytes 4194304 | tf_op jit(solution)/shard_map/input_grad/pallas_call | solution.py:337
  28.3 0.2 add_convert_fusion.after
  28.5 2.6 %collective-permute-start.8 = (bf16[2,288,128]{2,1,0:T(8,128)(2,1)S(1)}, bf16[2,288,128]{2,1,0:T(8,128)(2,1)S(1)}, u32[]{:S(2)}, u32[]{:S(2)}) collective-permute-start(bf16[2,288,128]{2,1,0:T(8,128)(2,1)S(1)} %get-tuple-element.89), channel_id=1, source_target_pairs={{0,24},{4,28},{8,16},{12,20},{16,8},{20,12},{24,0},{28,4},{1,25},{... | collective-permute-start | bytes 442376 | tf_op jit(solution)/shard_map/ppermute | solution.py:386
  31.1 1.3 %collective-permute-start.7 = (bf16[2,288,128]{2,1,0:T(8,128)(2,1)S(1)}, bf16[2,288,128]{2,1,0:T(8,128)(2,1)S(1)}, u32[]{:S(2)}, u32[]{:S(2)}) collective-permute-start(bf16[2,288,128]{2,1,0:T(8,128)(2,1)S(1)} %get-tuple-element.90), channel_id=1, source_target_pairs={{0,16},{4,20},{8,24},{12,28},{16,0},{20,4},{24,8},{28,12},{1,17},{... | collective-permute-start | bytes 442376 | tf_op jit(solution)/shard_map/ppermute | solution.py:386
  32.4 0.2 collective-permute-start.6
  32.6 4.8 %input_grad.4 = (bf16[32,128,256]{2,1,0:T(8,128)(2,1)}, bf16[5,32,256]{2,1,0:T(8,128)(2,1)S(1)}) custom-call(bf16[4,2,288,128]{3,2,1,0:T(8,128)(2,1)S(1)} %add_convert_fusion.after, bf16[3,34,128,256]{3,2,1,0:T(8,128)(2,1)S(1)} %get-tuple-element.60.moved, bf16[32,128,256]{2,1,0:T(8,128)(2,1)S(1)} %bitcast.41, ...), custom_call_target="tpu_custom_call", output_to_operand_aliasing={{0}: (5, {})} | custom-call | flops 3019898880 | bytes 4194304 | tf_op jit(solution)/shard_map/input_grad/pallas_call | solution.py:337
  37.4 1.3 %collective-permute-done.7 = bf16[2,288,128]{2,1,0:T(8,128)(2,1)S(1)} collective-permute-done((bf16[2,288,128]{2,1,0:T(8,128)(2,1)S(1)}, bf16[2,288,128]{2,1,0:T(8,128)(2,1)S(1)}, u32[]{:S(2)}, u32[]{:S(2)}) %collective-permute-start.7) | collective-permute-done | bytes 147488 | tf_op jit(solution)/shard_map/ppermute | solution.py:386
  38.7 1.1 %collective-permute-done.6 = bf16[2,288,128]{2,1,0:T(8,128)(2,1)S(1)} collective-permute-done((bf16[2,288,128]{2,1,0:T(8,128)(2,1)S(1)}, bf16[2,288,128]{2,1,0:T(8,128)(2,1)S(1)}, u32[]{:S(2)}, u32[]{:S(2)}) %collective-permute-start.6) | collective-permute-done | bytes 147488 | tf_op jit(solution)/shard_map/ppermute | solution.py:386
  39.8 0.1 fusion.2
  39.9 1.6 %collective-permute-start.9 = (bf16[1,288,128]{2,1,0:T(8,128)(2,1)S(1)}, bf16[1,288,128]{2,1,0:T(8,128)(2,1)S(1)}, u32[]{:S(2)}, u32[]{:S(2)}) collective-permute-start(bf16[1,288,128]{2,1,0:T(8,128)(2,1)S(1)} %slice.70), channel_id=1, source_target_pairs={{0,1},{1,0},{2,3},{3,2},{4,5},{5,4},{6,7},{7,6},{8,9},{9,8},{10,11... | collective-permute-start | bytes 221192 | tf_op jit(solution)/shard_map/ppermute | solution.py:389
  41.5 2.0 %collective-permute-start.11 = (bf16[2,32,256]{2,1,0:T(8,128)(2,1)S(1)}, bf16[2,32,256]{2,1,0:T(8,128)(2,1)S(1)}, u32[]{:S(2)}, u32[]{:S(2)}) collective-permute-start(bf16[2,32,256]{2,1,0:T(8,128)(2,1)S(1)} %pad_maximum_fusion.2), channel_id=1, source_target_pairs={{0,3},{1,2},{2,1},{3,0},{4,7},{5,6},{6,5},{7,4},{8,11},{9,10},{10,... | collective-permute-start | bytes 98312 | tf_op jit(solution)/shard_map/ppermute | solution.py:389
  43.6 2.4 %collective-permute-start.13 = (bf16[2,32,256]{2,1,0:T(8,128)(2,1)S(1)}, bf16[2,32,256]{2,1,0:T(8,128)(2,1)S(1)}, u32[]{:S(2)}, u32[]{:S(2)}) collective-permute-start(bf16[2,32,256]{2,1,0:T(8,128)(2,1)S(1)} %get-tuple-element.99), channel_id=1, source_target_pairs={{0,1},{1,0},{2,3},{3,2},{4,5},{5,4},{6,7},{7,6},{8,9},{9,8},{10,11... | collective-permute-start | bytes 98312 | tf_op jit(solution)/shard_map/ppermute | solution.py:389
  45.9 1.4 %collective-permute-done.11.refs_4_ = bf16[2,32,256]{2,1,0:T(8,128)(2,1)S(1)} collective-permute-done((bf16[2,32,256]{2,1,0:T(8,128)(2,1)S(1)}, bf16[2,32,256]{2,1,0:T(8,128)(2,1)S(1)}, u32[]{:S(2)}, u32[]{:S(2)}) %collective-permute-start.11) | collective-permute-done | bytes 32800 | tf_op jit(solution)/shard_map/ppermute | solution.py:389
  47.4 1.0 %collective-permute-done.10.refs_3_ = bf16[2,32,256]{2,1,0:T(8,128)(2,1)S(1)} collective-permute-done((bf16[2,32,256]{2,1,0:T(8,128)(2,1)S(1)}, bf16[2,32,256]{2,1,0:T(8,128)(2,1)S(1)}, u32[]{:S(2)}, u32[]{:S(2)}) %collective-permute-start.10) | collective-permute-done | bytes 32800 | tf_op jit(solution)/shard_map/ppermute | solution.py:389
  48.4 0.8 %collective-permute-start.12 = (bf16[1,288,128]{2,1,0:T(8,128)(2,1)S(1)}, bf16[1,288,128]{2,1,0:T(8,128)(2,1)S(1)}, u32[]{:S(2)}, u32[]{:S(2)}) collective-permute-start(bf16[1,288,128]{2,1,0:T(8,128)(2,1)S(1)} %add_convert_fusion.2.after), channel_id=1, source_target_pairs={{0,2},{1,3},{2,0},{3,1},{4,6},{5,7},{6,4},{7,5},{8,10},{9,11},{10,... | collective-permute-start | bytes 221192 | tf_op jit(solution)/shard_map/ppermute | solution.py:389
  49.2 2.4 %input_grad.5 = (bf16[32,128,256]{2,1,0:T(8,128)(2,1)}, bf16[2,32,256]{2,1,0:T(8,128)(2,1)S(1)}) custom-call(bf16[1,288,128]{2,1,0:T(8,128)(2,1)S(1)} %add_convert_fusion.2.after, bf16[3,34,128,256]{3,2,1,0:T(8,128)(2,1)S(1)} %get-tuple-element.60.moved, bf16[32,128,256]{2,1,0:T(8,128)(2,1)S(1)} %bitcast.42, ...), custom_call_target="tpu_custom_call", output_to_operand_aliasing={{0}: (5, {})} | custom-call | flops 1207959552 | bytes 4194304 | tf_op jit(solution)/shard_map/input_grad/pallas_call | solution.py:337
  51.6 2.5 %collective-permute-done.12 = bf16[1,288,128]{2,1,0:T(8,128)(2,1)S(1)} collective-permute-done((bf16[1,288,128]{2,1,0:T(8,128)(2,1)S(1)}, bf16[1,288,128]{2,1,0:T(8,128)(2,1)S(1)}, u32[]{:S(2)}, u32[]{:S(2)}) %collective-permute-start.12) | collective-permute-done | bytes 73760 | tf_op jit(solution)/shard_map/ppermute | solution.py:389
  54.1 1.8 %collective-permute-start.20 = (bf16[1,288,128]{2,1,0:T(8,128)(2,1)S(1)}, bf16[1,288,128]{2,1,0:T(8,128)(2,1)S(1)}, u32[]{:S(2)}, u32[]{:S(2)}) collective-permute-start(bf16[1,288,128]{2,1,0:T(8,128)(2,1)S(1)} %add_convert_fusion.1.refs_0_), channel_id=1, source_target_pairs={{0,16},{4,20},{8,24},{12,28},{16,0},{20,4},{24,8},{28,12},{1,17},{... | collective-permute-start | bytes 221192 | tf_op jit(solution)/shard_map/ppermute | solution.py:386
  55.9 1.3 %collective-permute-start.18 = (bf16[1,288,128]{2,1,0:T(8,128)(2,1)S(1)}, bf16[1,288,128]{2,1,0:T(8,128)(2,1)S(1)}, u32[]{:S(2)}, u32[]{:S(2)}) collective-permute-start(bf16[1,288,128]{2,1,0:T(8,128)(2,1)S(1)} %add_convert_fusion.1.refs_0_), channel_id=1, source_target_pairs={{0,24},{4,28},{8,16},{12,20},{16,8},{20,12},{24,0},{28,4},{1,25},{... | collective-permute-start | bytes 221192 | tf_op jit(solution)/shard_map/ppermute | solution.py:386
  57.2 0.5 collective-permute-start.14
  57.7 0.9 %collective-permute-done.20.refs_1_ = bf16[1,288,128]{2,1,0:T(8,128)(2,1)S(1)} collective-permute-done((bf16[1,288,128]{2,1,0:T(8,128)(2,1)S(1)}, bf16[1,288,128]{2,1,0:T(8,128)(2,1)S(1)}, u32[]{:S(2)}, u32[]{:S(2)}) %collective-permute-start.20) | collective-permute-done | bytes 73760 | tf_op jit(solution)/shard_map/ppermute | solution.py:386
  58.6 2.6 %collective-permute-done.18.refs_0_ = bf16[1,288,128]{2,1,0:T(8,128)(2,1)S(1)} collective-permute-done((bf16[1,288,128]{2,1,0:T(8,128)(2,1)S(1)}, bf16[1,288,128]{2,1,0:T(8,128)(2,1)S(1)}, u32[]{:S(2)}, u32[]{:S(2)}) %collective-permute-start.18) | collective-permute-done | bytes 73760 | tf_op jit(solution)/shard_map/ppermute | solution.py:386
  61.2 0.4 collective-permute-done.14.refs_2_
  61.6 0.1 collective-permute-start.23
  61.7 0.1 collective-permute-start.17
  61.8 2.0 %collective-permute-start.21 = (bf16[1,288,128]{2,1,0:T(8,128)(2,1)S(1)}, bf16[1,288,128]{2,1,0:T(8,128)(2,1)S(1)}, u32[]{:S(2)}, u32[]{:S(2)}) collective-permute-start(bf16[1,288,128]{2,1,0:T(8,128)(2,1)S(1)} %collective-permute-done.20.refs_1_), channel_id=1, source_target_pairs={{0,1},{1,0},{2,3},{3,2},{4,5},{5,4},{6,7},{7,6},{8,9},{9,8},{10,11... | collective-permute-start | bytes 221192 | tf_op jit(solution)/shard_map/ppermute | solution.py:389
  63.8 0.1 collective-permute-start.19
  63.9 1.3 %finish.4 = (f32[9,256,256]{2,1,0:T(8,128)}, bf16[2,128,256]{2,1,0:T(8,128)(2,1)}) custom-call(bf16[1,288,128]{2,1,0:T(8,128)(2,1)S(1)} %add_convert_fusion.1.refs_0_, bf16[2,32,256]{2,1,0:T(8,128)(2,1)S(1)} %get-tuple-element.83.refs_1_, bf16[2,32,256]{2,1,0:T(8,128)(2,1)S(1)} %collective-permute-done.13.refs_2_, ...), custom_call_target="tpu_custom_call" | custom-call | flops 1048576 | bytes 4194304 | tf_op jit(solution)/shard_map/finish/pallas_call | solution.py:425
  65.2 2.0 %collective-permute-start.15 = (bf16[1,288,128]{2,1,0:T(8,128)(2,1)S(1)}, bf16[1,288,128]{2,1,0:T(8,128)(2,1)S(1)}, u32[]{:S(2)}, u32[]{:S(2)}) collective-permute-start(bf16[1,288,128]{2,1,0:T(8,128)(2,1)S(1)} %collective-permute-done.14.refs_2_), channel_id=1, source_target_pairs={{0,1},{1,0},{2,3},{3,2},{4,5},{5,4},{6,7},{7,6},{8,9},{9,8},{10,11... | collective-permute-start | bytes 221192 | tf_op jit(solution)/shard_map/ppermute | solution.py:389
  67.2 1.2 %collective-permute-done.21.refs_2_ = bf16[1,288,128]{2,1,0:T(8,128)(2,1)S(1)} collective-permute-done((bf16[1,288,128]{2,1,0:T(8,128)(2,1)S(1)}, bf16[1,288,128]{2,1,0:T(8,128)(2,1)S(1)}, u32[]{:S(2)}, u32[]{:S(2)}) %collective-permute-start.21) | collective-permute-done | bytes 73760 | tf_op jit(solution)/shard_map/ppermute | solution.py:389
  68.4 1.6 %collective-permute-done.19.refs_1_ = bf16[1,288,128]{2,1,0:T(8,128)(2,1)S(1)} collective-permute-done((bf16[1,288,128]{2,1,0:T(8,128)(2,1)S(1)}, bf16[1,288,128]{2,1,0:T(8,128)(2,1)S(1)}, u32[]{:S(2)}, u32[]{:S(2)}) %collective-permute-start.19) | collective-permute-done | bytes 73760 | tf_op jit(solution)/shard_map/ppermute | solution.py:389
  70.0 0.1 collective-permute-start.22
  70.1 1.0 %collective-permute-done.15.refs_3_ = bf16[1,288,128]{2,1,0:T(8,128)(2,1)S(1)} collective-permute-done((bf16[1,288,128]{2,1,0:T(8,128)(2,1)S(1)}, bf16[1,288,128]{2,1,0:T(8,128)(2,1)S(1)}, u32[]{:S(2)}, u32[]{:S(2)}) %collective-permute-start.15) | collective-permute-done | bytes 73760 | tf_op jit(solution)/shard_map/ppermute | solution.py:389
  71.2 0.4 collective-permute-done.22
  71.6 1.0 %finish.5.refs_7_ = f32[9,256,256]{2,1,0:T(8,128)} custom-call(bf16[1,288,128]{2,1,0:T(8,128)(2,1)S(1)} %collective-permute-done.18.refs_0_, bf16[1,288,128]{2,1,0:T(8,128)(2,1)S(1)} %collective-permute-done.20.refs_1_, bf16[1,288,128]{2,1,0:T(8,128)(2,1)S(1)} %collective-permute-done.14.refs_2_, ...), custom_call_target="tpu_custom_call", output_to_operand_aliasing={{}: (7, {})} | custom-call | flops 1048576 | bytes 4194304 | tf_op jit(solution)/shard_map/finish/pallas_call | solution.py:425
  72.6 1.0 %finish.6.refs_1_ = f32[9,256,256]{2,1,0:T(8,128)} custom-call(bf16[1,288,128]{2,1,0:T(8,128)(2,1)S(1)} %collective-permute-done.17.refs_0_, bf16[1,288,128]{2,1,0:T(8,128)(2,1)S(1)} %collective-permute-done.19.refs_1_, bf16[1,288,128]{2,1,0:T(8,128)(2,1)S(1)} %collective-permute-done.21.refs_2_, ...), custom_call_target="tpu_custom_call", output_to_operand_aliasing={{}: (7, {})} | custom-call | flops 1048576 | bytes 4194304 | tf_op jit(solution)/shard_map/finish/pallas_call | solution.py:425
  73.7 0.7 finish.7
  (31 shorter events, 0.3 us)
Async XLA Ops:
  0.6 8.3 %copy-start.2 = (f32[1000,256]{1,0:T(8,128)S(1)}, f32[1000,256]{1,0:T(8,128)}, u32[]{:S(2)}) copy-start(f32[1000,256]{1,0:T(8,128)} %scales.1) | copy-start | bytes 3072004
  2.2 8.5 %collective-permute-start = (bf16[96,256]{1,0:T(8,128)(2,1)S(1)}, bf16[96,256]{1,0:T(8,128)(2,1)S(1)}, u32[]{:S(2)}, u32[]{:S(2)}) collective-permute-start(bf16[96,256]{1,0:T(8,128)(2,1)S(1)} %get-tuple-element.48), channel_id=1, source_target_pairs={{0,1},{1,2},{2,3},{3,0},{4,5},{5,6},{6,7},{7,4},{8,9},{9,10},{10,1... | collective-permute-start | bytes 147464 | tf_op jit(solution)/shard_map/ppermute | solution.py:282
  5.2 5.5 %collective-permute-start.1 = (bf16[96,256]{1,0:T(8,128)(2,1)S(1)}, bf16[96,256]{1,0:T(8,128)(2,1)S(1)}, u32[]{:S(2)}, u32[]{:S(2)}) collective-permute-start(bf16[96,256]{1,0:T(8,128)(2,1)S(1)} %get-tuple-element.49), channel_id=1, source_target_pairs={{0,3},{1,0},{2,1},{3,2},{4,7},{5,4},{6,5},{7,6},{8,11},{9,8},{10,9... | collective-permute-start | bytes 147464 | tf_op jit(solution)/shard_map/ppermute | solution.py:282
  7.3 6.0 %collective-permute-start.2 = (bf16[64,256]{1,0:T(8,128)(2,1)S(1)}, bf16[64,256]{1,0:T(8,128)(2,1)S(1)}, u32[]{:S(2)}, u32[]{:S(2)}) collective-permute-start(bf16[64,256]{1,0:T(8,128)(2,1)S(1)} %get-tuple-element.53), channel_id=1, source_target_pairs={{0,2},{1,3},{2,0},{3,1},{4,6},{5,7},{6,4},{7,5},{8,10},{9,11},{10,... | collective-permute-start | bytes 98312 | tf_op jit(solution)/shard_map/ppermute | solution.py:282
  8.9 4.4 %copy-start = (bf16[1,32,128,256]{3,2,1,0:T(8,128)(2,1)S(1)}, bf16[1,32,128,256]{3,2,1,0:T(8,128)(2,1)}, u32[]{:S(2)}) copy-start(bf16[1,32,128,256]{3,2,1,0:T(8,128)(2,1)} %param.6) | copy-start | bytes 6291460
  10.8 6.1 %collective-permute-start.3 = (bf16[144,256]{1,0:T(8,128)(2,1)S(1)}, bf16[144,256]{1,0:T(8,128)(2,1)S(1)}, u32[]{:S(2)}, u32[]{:S(2)}) collective-permute-start(bf16[144,256]{1,0:T(8,128)(2,1)S(1)} %get-tuple-element.55), channel_id=1, source_target_pairs={{0,4},{4,8},{8,12},{12,16},{16,20},{20,24},{24,28},{1,5},{5,9},{9,... | collective-permute-start | bytes 221192 | tf_op jit(solution)/shard_map/ppermute | solution.py:298
  12.1 4.9 %collective-permute-start.4 = (bf16[144,256]{1,0:T(8,128)(2,1)S(1)}, bf16[144,256]{1,0:T(8,128)(2,1)S(1)}, u32[]{:S(2)}, u32[]{:S(2)}) collective-permute-start(bf16[144,256]{1,0:T(8,128)(2,1)S(1)} %get-tuple-element.56), channel_id=1, source_target_pairs={{4,0},{8,4},{12,8},{16,12},{20,16},{24,20},{28,24},{5,1},{9,5},{13... | collective-permute-start | bytes 221192 | tf_op jit(solution)/shard_map/ppermute | solution.py:299
  17.0 9.6 %copy-start.1 = (bf16[3,3,256,256]{3,2,1,0:T(8,128)(2,1)S(1)}, bf16[3,3,256,256]{3,2,1,0:T(8,128)(2,1)}, u32[]{:S(2)}) copy-start(bf16[3,3,256,256]{3,2,1,0:T(8,128)(2,1)} %param.8) | copy-start | bytes 3538948
  23.5 4.8 %collective-permute-start.5 = (bf16[4,2,288,128]{3,2,1,0:T(8,128)(2,1)S(1)}, bf16[4,2,288,128]{3,2,1,0:T(8,128)(2,1)S(1)}, u32[]{:S(2)}, u32[]{:S(2)}) collective-permute-start(bf16[4,2,288,128]{3,2,1,0:T(8,128)(2,1)S(1)} %get-tuple-element.59.after), channel_id=1, source_target_pairs={{0,4},{4,0},{8,12},{12,8},{16,20},{20,16},{24,28},{28,24},{1,5},{5... | collective-permute-start | bytes 1769480 | tf_op jit(solution)/shard_map/ppermute | solution.py:383
  28.5 8.9 %collective-permute-start.8 = (bf16[2,288,128]{2,1,0:T(8,128)(2,1)S(1)}, bf16[2,288,128]{2,1,0:T(8,128)(2,1)S(1)}, u32[]{:S(2)}, u32[]{:S(2)}) collective-permute-start(bf16[2,288,128]{2,1,0:T(8,128)(2,1)S(1)} %get-tuple-element.89), channel_id=1, source_target_pairs={{0,24},{4,28},{8,16},{12,20},{16,8},{20,12},{24,0},{28,4},{1,25},{... | collective-permute-start | bytes 442376 | tf_op jit(solution)/shard_map/ppermute | solution.py:386
  31.1 7.6 %collective-permute-start.7 = (bf16[2,288,128]{2,1,0:T(8,128)(2,1)S(1)}, bf16[2,288,128]{2,1,0:T(8,128)(2,1)S(1)}, u32[]{:S(2)}, u32[]{:S(2)}) collective-permute-start(bf16[2,288,128]{2,1,0:T(8,128)(2,1)S(1)} %get-tuple-element.90), channel_id=1, source_target_pairs={{0,16},{4,20},{8,24},{12,28},{16,0},{20,4},{24,8},{28,12},{1,17},{... | collective-permute-start | bytes 442376 | tf_op jit(solution)/shard_map/ppermute | solution.py:386
  32.4 7.3 %collective-permute-start.6 = (bf16[2,288,128]{2,1,0:T(8,128)(2,1)S(1)}, bf16[2,288,128]{2,1,0:T(8,128)(2,1)S(1)}, u32[]{:S(2)}, u32[]{:S(2)}) collective-permute-start(bf16[2,288,128]{2,1,0:T(8,128)(2,1)S(1)} %get-tuple-element.91), channel_id=1, source_target_pairs={{0,8},{4,12},{8,0},{12,4},{16,24},{20,28},{24,16},{28,20},{1,9},{5... | collective-permute-start | bytes 442376 | tf_op jit(solution)/shard_map/ppermute | solution.py:386
  39.9 8.5 %collective-permute-start.9 = (bf16[1,288,128]{2,1,0:T(8,128)(2,1)S(1)}, bf16[1,288,128]{2,1,0:T(8,128)(2,1)S(1)}, u32[]{:S(2)}, u32[]{:S(2)}) collective-permute-start(bf16[1,288,128]{2,1,0:T(8,128)(2,1)S(1)} %slice.70), channel_id=1, source_target_pairs={{0,1},{1,0},{2,3},{3,2},{4,5},{5,4},{6,7},{7,6},{8,9},{9,8},{10,11... | collective-permute-start | bytes 221192 | tf_op jit(solution)/shard_map/ppermute | solution.py:389
  41.5 5.8 %collective-permute-start.11 = (bf16[2,32,256]{2,1,0:T(8,128)(2,1)S(1)}, bf16[2,32,256]{2,1,0:T(8,128)(2,1)S(1)}, u32[]{:S(2)}, u32[]{:S(2)}) collective-permute-start(bf16[2,32,256]{2,1,0:T(8,128)(2,1)S(1)} %pad_maximum_fusion.2), channel_id=1, source_target_pairs={{0,3},{1,2},{2,1},{3,0},{4,7},{5,6},{6,5},{7,4},{8,11},{9,10},{10,... | collective-permute-start | bytes 98312 | tf_op jit(solution)/shard_map/ppermute | solution.py:389
  43.6 4.8 %collective-permute-start.10 = (bf16[2,32,256]{2,1,0:T(8,128)(2,1)S(1)}, bf16[2,32,256]{2,1,0:T(8,128)(2,1)S(1)}, u32[]{:S(2)}, u32[]{:S(2)}) collective-permute-start(bf16[2,32,256]{2,1,0:T(8,128)(2,1)S(1)} %get-tuple-element.100), channel_id=1, source_target_pairs={{0,2},{1,3},{2,0},{3,1},{4,6},{5,7},{6,4},{7,5},{8,10},{9,11},{10,... | collective-permute-start | bytes 98312 | tf_op jit(solution)/shard_map/ppermute | solution.py:389
  43.6 8.0 %collective-permute-start.13 = (bf16[2,32,256]{2,1,0:T(8,128)(2,1)S(1)}, bf16[2,32,256]{2,1,0:T(8,128)(2,1)S(1)}, u32[]{:S(2)}, u32[]{:S(2)}) collective-permute-start(bf16[2,32,256]{2,1,0:T(8,128)(2,1)S(1)} %get-tuple-element.99), channel_id=1, source_target_pairs={{0,1},{1,0},{2,3},{3,2},{4,5},{5,4},{6,7},{7,6},{8,9},{9,8},{10,11... | collective-permute-start | bytes 98312 | tf_op jit(solution)/shard_map/ppermute | solution.py:389
  48.4 5.7 %collective-permute-start.12 = (bf16[1,288,128]{2,1,0:T(8,128)(2,1)S(1)}, bf16[1,288,128]{2,1,0:T(8,128)(2,1)S(1)}, u32[]{:S(2)}, u32[]{:S(2)}) collective-permute-start(bf16[1,288,128]{2,1,0:T(8,128)(2,1)S(1)} %add_convert_fusion.2.after), channel_id=1, source_target_pairs={{0,2},{1,3},{2,0},{3,1},{4,6},{5,7},{6,4},{7,5},{8,10},{9,11},{10,... | collective-permute-start | bytes 221192 | tf_op jit(solution)/shard_map/ppermute | solution.py:389
  54.1 4.4 %collective-permute-start.20 = (bf16[1,288,128]{2,1,0:T(8,128)(2,1)S(1)}, bf16[1,288,128]{2,1,0:T(8,128)(2,1)S(1)}, u32[]{:S(2)}, u32[]{:S(2)}) collective-permute-start(bf16[1,288,128]{2,1,0:T(8,128)(2,1)S(1)} %add_convert_fusion.1.refs_0_), channel_id=1, source_target_pairs={{0,16},{4,20},{8,24},{12,28},{16,0},{20,4},{24,8},{28,12},{1,17},{... | collective-permute-start | bytes 221192 | tf_op jit(solution)/shard_map/ppermute | solution.py:386
  55.9 5.3 %collective-permute-start.18 = (bf16[1,288,128]{2,1,0:T(8,128)(2,1)S(1)}, bf16[1,288,128]{2,1,0:T(8,128)(2,1)S(1)}, u32[]{:S(2)}, u32[]{:S(2)}) collective-permute-start(bf16[1,288,128]{2,1,0:T(8,128)(2,1)S(1)} %add_convert_fusion.1.refs_0_), channel_id=1, source_target_pairs={{0,24},{4,28},{8,16},{12,20},{16,8},{20,12},{24,0},{28,4},{1,25},{... | collective-permute-start | bytes 221192 | tf_op jit(solution)/shard_map/ppermute | solution.py:386
  57.2 4.4 %collective-permute-start.14 = (bf16[1,288,128]{2,1,0:T(8,128)(2,1)S(1)}, bf16[1,288,128]{2,1,0:T(8,128)(2,1)S(1)}, u32[]{:S(2)}, u32[]{:S(2)}) collective-permute-start(bf16[1,288,128]{2,1,0:T(8,128)(2,1)S(1)} %add_convert_fusion.1.refs_0_), channel_id=1, source_target_pairs={{0,8},{4,12},{8,0},{12,4},{16,24},{20,28},{24,16},{28,20},{1,9},{5... | collective-permute-start | bytes 221192 | tf_op jit(solution)/shard_map/ppermute | solution.py:386
  61.6 9.5 %collective-permute-start.23 = (bf16[4,1,288,128]{3,2,1,0:T(8,128)(2,1)S(1)}, bf16[4,1,288,128]{3,2,1,0:T(8,128)(2,1)S(1)}, u32[]{:S(2)}, u32[]{:S(2)}) collective-permute-start(bf16[4,1,288,128]{3,2,1,0:T(8,128)(2,1)S(1)} %pad_maximum_fusion), channel_id=1, source_target_pairs={{0,4},{4,0},{8,12},{12,8},{16,20},{20,16},{24,28},{28,24},{1,5},{5... | collective-permute-start | bytes 884744 | tf_op jit(solution)/shard_map/ppermute | solution.py:383
  61.7 5.5 %collective-permute-start.17 = (bf16[1,288,128]{2,1,0:T(8,128)(2,1)S(1)}, bf16[1,288,128]{2,1,0:T(8,128)(2,1)S(1)}, u32[]{:S(2)}, u32[]{:S(2)}) collective-permute-start(bf16[1,288,128]{2,1,0:T(8,128)(2,1)S(1)} %add_convert_fusion.1.refs_0_), channel_id=1, source_target_pairs={{0,1},{1,0},{2,3},{3,2},{4,5},{5,4},{6,7},{7,6},{8,9},{9,8},{10,11... | collective-permute-start | bytes 221192 | tf_op jit(solution)/shard_map/ppermute | solution.py:389
  61.8 6.6 %collective-permute-start.21 = (bf16[1,288,128]{2,1,0:T(8,128)(2,1)S(1)}, bf16[1,288,128]{2,1,0:T(8,128)(2,1)S(1)}, u32[]{:S(2)}, u32[]{:S(2)}) collective-permute-start(bf16[1,288,128]{2,1,0:T(8,128)(2,1)S(1)} %collective-permute-done.20.refs_1_), channel_id=1, source_target_pairs={{0,1},{1,0},{2,3},{3,2},{4,5},{5,4},{6,7},{7,6},{8,9},{9,8},{10,11... | collective-permute-start | bytes 221192 | tf_op jit(solution)/shard_map/ppermute | solution.py:389
  63.8 6.2 %collective-permute-start.19 = (bf16[1,288,128]{2,1,0:T(8,128)(2,1)S(1)}, bf16[1,288,128]{2,1,0:T(8,128)(2,1)S(1)}, u32[]{:S(2)}, u32[]{:S(2)}) collective-permute-start(bf16[1,288,128]{2,1,0:T(8,128)(2,1)S(1)} %collective-permute-done.18.refs_0_), channel_id=1, source_target_pairs={{0,1},{1,0},{2,3},{3,2},{4,5},{5,4},{6,7},{7,6},{8,9},{9,8},{10,11... | collective-permute-start | bytes 221192 | tf_op jit(solution)/shard_map/ppermute | solution.py:389
  65.2 5.9 %collective-permute-start.15 = (bf16[1,288,128]{2,1,0:T(8,128)(2,1)S(1)}, bf16[1,288,128]{2,1,0:T(8,128)(2,1)S(1)}, u32[]{:S(2)}, u32[]{:S(2)}) collective-permute-start(bf16[1,288,128]{2,1,0:T(8,128)(2,1)S(1)} %collective-permute-done.14.refs_2_), channel_id=1, source_target_pairs={{0,1},{1,0},{2,3},{3,2},{4,5},{5,4},{6,7},{7,6},{8,9},{9,8},{10,11... | collective-permute-start | bytes 221192 | tf_op jit(solution)/shard_map/ppermute | solution.py:389
  70.0 1.5 %collective-permute-start.22 = (bf16[3,1,288,128]{3,2,1,0:T(8,128)(2,1)S(1)}, bf16[3,1,288,128]{3,2,1,0:T(8,128)(2,1)S(1)}, u32[]{:S(2)}, u32[]{:S(2)}) collective-permute-start(bf16[3,1,288,128]{3,2,1,0:T(8,128)(2,1)S(1)} %pad_maximum_fusion.1), channel_id=1, source_target_pairs={{0,4},{4,0},{8,12},{12,8},{16,20},{20,16},{24,28},{28,24},{1,5},{5... | collective-permute-start | bytes 663560 | tf_op jit(solution)/shard_map/ppermute | solution.py:383
  71.1 2.6 %collective-permute-start.16 = (bf16[1,288,128]{2,1,0:T(8,128)(2,1)S(1)}, bf16[1,288,128]{2,1,0:T(8,128)(2,1)S(1)}, u32[]{:S(2)}, u32[]{:S(2)}) collective-permute-start(bf16[1,288,128]{2,1,0:T(8,128)(2,1)S(1)} %collective-permute-done.15.refs_3_), channel_id=1, source_target_pairs={{0,4},{4,0},{8,12},{12,8},{16,20},{20,16},{24,28},{28,24},{1,5},{5... | collective-permute-start | bytes 221192 | tf_op jit(solution)/shard_map/ppermute | solution.py:383

commit v2 on v1

v2 whole, which is shorter than its diff:
```python
import functools
import jax
import jax.numpy as jnp
from jax import lax
from jax.experimental import pallas as pl
from jax.experimental.pallas import tpu as pltpu
from jax.sharding import PartitionSpec as P

BF = jnp.bfloat16
F32 = jnp.float32
MB = 1024 * 1024
START_MIB = 53.7


def smem():
    return pl.BlockSpec(memory_space=pltpu.SMEM)


def vmem():
    return pl.BlockSpec(memory_space=pltpu.VMEM)


def params(mib):
    return pltpu.CompilerParams(vmem_limit_bytes=int(mib * MB))


def cost(flops, nbytes):
    return pl.CostEstimate(flops=flops, bytes_accessed=nbytes, transcendentals=0)


def hbm():
    return pl.BlockSpec(memory_space=pltpu.HBM)


def place():
    row = lax.axis_index("row")
    return lax.rem(row, 2), row // 2, lax.axis_index("col")


def is_edge(s):
    return s & (s + 1) == 0


def start_kernel(n, cot, coarse, *refs):
    outs, (rough, low, high, sems) = refs[:n], refs[n:]
    _, _, me = place()
    cr, _, ch = rough.shape
    rows, width, _ = cot.shape
    cols = rough.shape[1] // n
    pairs = (coarse, rough), (cot.at[:, :16, :], low), (cot.at[:, width - 16 :, :], high)
    copies = [pltpu.make_async_copy(*pair, sems.at[k]) for k, pair in enumerate(pairs)]
    for c in copies:
        c.start()
    copies[0].wait()
    for s, out in enumerate(outs):
        start = pl.multiple_of((me ^ s) * cols, cols)
        for j in range(cr):
            out[j * cols : (j + 1) * cols, :] = rough[j, pl.ds(start, cols), :]
    r = lax.broadcasted_iota(jnp.int32, (rows, rows * 16), 0)
    p = lax.broadcasted_iota(jnp.int32, (rows, rows * 16), 1)
    sides = []
    for c, edge, pick in ((copies[1], low, 0), (copies[2], high, 15)):
        c.wait()
        sel = jnp.where(p == r * 16 + pick, 1.0, 0.0).astype(BF)
        flat = edge[...].reshape(rows * 16, ch)
        sides.append(jnp.dot(sel, flat, preferred_element_type=F32))
    for s in range(1, n):
        if is_edge(s):
            col = jnp.where((me ^ s) > me, sides[1], sides[0])
            outs[s][cr * cols :, :] = col.astype(BF)


def load_kernel(steps, cot, scales, moved, scale):
    rows, width, ch = cot.shape
    by = scales[pl.ds(steps[0], 1), :]
    scale[...] = by
    zero = jnp.zeros((1, ch), F32)

    def group(g, _):
        for q in range(4):
            r = g * 4 + q
            spread(moved, r + 1, (cot[r].astype(F32) * by).astype(BF), zero, zero)
        return 0

    lax.fori_loop(0, rows // 4, group, 0)


def edge_kernel(offset, shifts, scale, moved, *refs):
    blocks, (one, two, left, right) = refs[: len(shifts)], refs[len(shifts) :]
    core, _, me = place()
    _, rows, width, ch = moved.shape
    rows -= 2
    by = scale[...]
    for side, place_of in ((left, me - 1), (right, me + 1)):
        col = jnp.zeros((rows, ch), F32)
        for s, block in zip(shifts, blocks):
            edge = (block[offset:, :].astype(F32) * by).astype(BF).astype(F32)
            col = jnp.where((me ^ s) == place_of, edge, col)
        side[...] = col
    idx = lax.broadcasted_iota(jnp.int32, (16, ch), 0)
    ends = []
    for k in (0, rows - 1):
        tip = jnp.where(idx == 1, right[k : k + 1, :], 0.0)
        tip = jnp.where(idx == 0, left[k : k + 1, :], tip)
        ends.append((moved[1, k + 1].astype(F32), tip))
    (top, top_tip), (bottom, bottom_tip) = ends
    for out, first in ((one, core == 1), (two, core == 0)):
        out[:width, :] = jnp.where(first, top, bottom).astype(BF)
        out[width:, :] = jnp.where(first, top_tip, bottom_tip).astype(BF)


def spread_up(coarse_row, width):
    cols = coarse_row.shape[0]
    a = lax.broadcasted_iota(jnp.int32, (width, cols), 0)
    b = lax.broadcasted_iota(jnp.int32, (width, cols), 1)
    up = jnp.where(a // (width // cols) == b, 1.0, 0.0).astype(BF)
    return jnp.dot(up, coarse_row, preferred_element_type=F32)


def sigmoid(x):
    return 0.5 * jnp.tanh(0.5 * x) + 0.5


def gate(fine, coarse_row):
    hidden = fine.astype(F32) + spread_up(coarse_row, fine.shape[1])[None]
    return hidden, sigmoid(hidden)


def spread(moved, slot, rounded, left, right):
    width = rounded.shape[0]
    row = rounded.astype(F32)
    idx = lax.broadcasted_iota(jnp.int32, row.shape, 0)
    moved[0, slot] = jnp.where(idx == 0, left, pltpu.roll(row, 1, 0)).astype(BF)
    moved[1, slot] = rounded
    moved[2, slot] = jnp.where(idx == width - 1, right, pltpu.roll(row, width - 1, 0)).astype(BF)


def prepare_kernel(n, cr, fine, left, right, moved_in, *refs):
    blocks, (moved, act_t, strip, up) = refs[:n], refs[n:]
    _, _, me = place()
    rows, width, ch = fine.shape
    cols = strip.shape[1]
    for s in range(n):
        for j in range(cr):
            strip[(me ^ s) * cr + j] = blocks[s][j * cols : (j + 1) * cols, :]
    idx = lax.broadcasted_iota(jnp.int32, (16, ch), 0)

    def group(g, _):
        up[...] = spread_up(strip[g], width)
        for q in range(4):
            r = g * 4 + q
            for k, low, pick, side in ((0, 0, 0, left), (2, width - 16, 15, right)):
                tile = moved[k, r + 1, low : low + 16, :].astype(F32)
                tile = jnp.where(idx == pick, side[pl.ds(r, 1), :], tile)
                moved[k, r + 1, low : low + 16, :] = tile.astype(BF)
            hidden = fine[r].astype(F32) + up[...]
            act = (hidden * sigmoid(hidden)).astype(BF)
            act_t[:, pl.ds(pl.multiple_of(r * width, width), width)] = act.T
        return 0

    lax.fori_loop(0, rows // 4, group, 0)


def weight_kernel(act_t, one, two, moved_in, keep, send, moved):
    core, plane, z = place()
    _, rows, width, ch = moved.shape
    rows -= 2
    planes, zs, depth, half = keep.shape
    for slot, first in ((0, core == 1), (rows + 1, core == 0)):
        halo = jnp.where(first, one[...].astype(F32), two[...].astype(F32))
        spread(moved, slot, halo[:width].astype(BF), halo[width : width + 1], halo[width + 1 : width + 2])
    step = ch // (planes * zs)
    z = lax.rem(z, zs)

    def tap(t, _):
        i, j = t // 3, lax.rem(t, 3)
        window = moved[2 - j, pl.ds(2 - i, rows)].reshape(rows * width, ch)
        acc = jnp.dot(act_t[...], window, preferred_element_type=F32)
        low, high = acc[:, :half], acc[:, half:]
        mine = jnp.where(core == 0, low, high).astype(BF)
        other = jnp.where(core == 0, high, low).astype(BF)
        at = pl.multiple_of(t * step, step)
        for p in range(planes):
            for c in range(zs):
                b = (p * zs + c) * step
                keep[p ^ plane, c ^ z, pl.ds(at, step), :] = mine[b : b + step]
                send[p ^ plane, c ^ z, pl.ds(at, step), :] = other[b : b + step]
        return 0

    lax.fori_loop(0, 9, tap, 0)


def strip_order(n):
    return list(range(n - 1, 0, -2)) + list(range(n - 2, -1, -2))


def input_kernel(first, size, n, after, moved, fine, strip, weight, *refs):
    gf, gc, fines, pooled, sems = refs[-5:]
    _, _, me = place()
    cr = strip.shape[0] // n
    _, width, ch = fine.shape
    cols = strip.shape[1]
    wide = jnp.concatenate([weight[t] for t in range(9)], axis=1)
    copies = []
    for g in range(size):
        k = (strip_order(n)[(first + g) // cr] ^ me) * cr + (first + g) % cr
        r = 4 * k
        taps = [
            moved[2 - t % 3, pl.ds(2 - t // 3 + r, 4)].reshape(4 * width, ch) for t in range(9)
        ]
        dact = lax.dot_general(
            jnp.concatenate(taps, axis=1),
            wide,
            (((1,), (1,)), ((), ())),
            preferred_element_type=F32,
        ).reshape(4, width, ch)
        hidden, sig = gate(fine[pl.ds(r, 4)], strip[k])
        dhidden = dact * sig * (1.0 + hidden * (1.0 - sig))
        fines[g] = dhidden.astype(BF)
        tall = dhidden[0] + dhidden[1] + dhidden[2] + dhidden[3]
        for h in range(ch // 128):
            pooled[...] = tall[:, 128 * h : 128 * h + 128]
            every = [pooled[pl.ds(k, cols, stride=width // cols), :] for k in range(width // cols)]
            gc[g, h] = functools.reduce(jnp.add, every).astype(BF)
        copies.append(pltpu.make_async_copy(fines.at[g], gf.at[pl.ds(r, 4)], sems.at[g]))
        copies[-1].start()
    for c in copies:
        c.wait()


def finish_kernel(norm, zs, spots, n, *refs):
    pieces, parts = refs[: len(spots)], refs[len(spots) : len(spots) + n]
    if n:
        out, coarse_out, scratch, sems, coarse, coarse_sem = refs[-6:]
    else:
        out, scratch, sems = refs[-3:]
    core, plane, me = place()
    planes = lax.axis_size("row") // 2
    ch = out.shape[1]
    half = ch // 2
    tall = ch // planes
    step = tall // zs
    z = lax.rem(me, zs)
    copies = []
    for k, (flip, s, first) in enumerate(spots):
        lanes = pl.ds(pl.multiple_of((core ^ flip) * half, half), half)
        for c in range(pieces[k].shape[0]):
            x = pieces[k][c].astype(F32) * norm
            for t in range(9):
                scratch[k, c, t] = x[t * step : (t + 1) * step]
            b = pl.multiple_of((plane ^ s) * tall + ((first + c) ^ z) * step, step)
            copies.append(
                pltpu.make_async_copy(
                    scratch.at[k, c], out.at[:, pl.ds(b, step), lanes], sems.at[k, c]
                )
            )
            copies[-1].start()
    if n:
        cr = coarse.shape[0]
        cols = coarse.shape[1] // n
        for s in range(n):
            start = pl.multiple_of((me ^ s) * cols, cols)
            for j in range(cr):
                for h in range(2):
                    b = (j * 2 + h) * cols
                    coarse[j, pl.ds(start, cols), pl.ds(h * half, half)] = parts[s][b : b + cols]
        copies.append(pltpu.make_async_copy(coarse, coarse_out, coarse_sem.at[0]))
        copies[-1].start()
    for c in copies:
        c.wait()


def xor_pairs(count, bit):
    return [(i, i ^ bit) for i in range(count)]


def per_device(fine_input, coarse_feat, conv_weight, step_scale, timesteps, cotangent):
    _, rows, width, ch = fine_input.shape
    n = lax.axis_size("col")
    nrow = lax.axis_size("row")
    planes = nrow // 2
    cr = coarse_feat.shape[1]
    cols = width // 4
    fine, cot, coarse = fine_input[0], cotangent[0], coarse_feat[0]
    weight = conv_weight.reshape(9, ch, ch)

    def shape(*dims, dtype=BF):
        return jax.ShapeDtypeStruct(dims, dtype)

    def col_swap(x, s):
        return lax.ppermute(x, "col", xor_pairs(n, s))

    blocks = pl.pallas_call(
        functools.partial(start_kernel, n),
        out_shape=[shape(cr * cols + (rows if s and is_edge(s) else 0), ch) for s in range(n)],
        in_specs=[hbm(), hbm()],
        out_specs=[vmem()] * n,
        scratch_shapes=[
            pltpu.VMEM(coarse.shape, BF),
            pltpu.VMEM((rows, 16, ch), BF),
            pltpu.VMEM((rows, 16, ch), BF),
            pltpu.SemaphoreType.DMA((3,)),
        ],
        compiler_params=params(START_MIB),
        cost_estimate=cost(1 << 20, 4 << 20),
        name="start",
    )(cot, coarse)
    blocks = list(blocks)
    moved, scale = pl.pallas_call(
        load_kernel,
        out_shape=[shape(3, rows + 2, width, ch), shape(1, ch, dtype=F32)],
        in_specs=[smem(), vmem(), vmem()],
        out_specs=[vmem()] * 2,
        compiler_params=params(4),
        cost_estimate=cost(1 << 20, 4 << 20),
        name="load",
    )(timesteps, cot, step_scale)

    shifts = [s for s in range(1, n) if is_edge(s)]
    for s in shifts + [s for s in range(1, n) if not is_edge(s)]:
        blocks[s] = col_swap(blocks[s], s)

    halo, side = shape(width + 16, ch), shape(rows, ch, dtype=F32)
    one, two, left, right = pl.pallas_call(
        functools.partial(edge_kernel, cr * cols, shifts),
        out_shape=[halo, halo, side, side],
        in_specs=[vmem()] * (2 + len(shifts)),
        out_specs=[vmem()] * 4,
        compiler_params=params(4),
        cost_estimate=cost(1 << 18, 1 << 19),
        name="edges",
    )(scale, moved, *[blocks[s] for s in shifts])
    one = lax.ppermute(one, "row", xor_pairs(nrow, 1))
    odd = range(1, nrow - 1, 2)
    two = lax.ppermute(two, "row", [(i, i + 1) for i in odd] + [(i + 1, i) for i in odd])

    groups = rows // 4
    moved, act_t, strip = pl.pallas_call(
        functools.partial(prepare_kernel, n, cr),
        out_shape=[shape(*moved.shape), shape(ch, rows * width), shape(groups, cols, ch)],
        in_specs=[vmem()] * (4 + n),
        out_specs=[vmem()] * 3,
        input_output_aliases={3: 0},
        scratch_shapes=[pltpu.VMEM((width, ch), F32)],
        compiler_params=params(8),
        cost_estimate=cost(1 << 32, 4 << 20),
        name="prepare",
    )(fine, left, right, moved, *blocks)

    halves = n // 2
    aligned = ch // (planes * halves) % 16 == 0
    zs = halves if aligned else 1
    depth = 9 * ch // (planes * zs)
    half = ch // 2
    part = shape(planes, zs, depth, half)
    keep, send, moved = pl.pallas_call(
        weight_kernel,
        out_shape=[part, part, shape(*moved.shape)],
        in_specs=[vmem()] * 4,
        out_specs=[vmem()] * 3,
        input_output_aliases={3: 2},
        compiler_params=params(8),
        cost_estimate=cost(2 * 9 * rows * width * ch * ch, 8 << 20),
        name="weight_grad",
    )(act_t, one, two, moved)

    done, pooled, made = [], [], 0

    def input_piece(size, after):
        nonlocal done, made
        *done, gc = pl.pallas_call(
            functools.partial(input_kernel, made, size, n),
            out_shape=[shape(rows, width, ch), shape(size, 2, cols, ch // 2)],
            in_specs=[pl.BlockSpec(memory_space=pl.ANY)]
            + [vmem()] * 4
            + [pl.BlockSpec(memory_space=pl.ANY) for _ in done],
            out_specs=[pl.BlockSpec(memory_space=pl.ANY), vmem()],
            input_output_aliases={5: 0} if done else {},
            scratch_shapes=[
                pltpu.VMEM((size, 4, width, ch), BF),
                pltpu.VMEM((width, 128), F32),
                pltpu.SemaphoreType.DMA((size,)),
            ],
            compiler_params=params(12),
            cost_estimate=cost(2 * 9 * 4 * size * width * ch * ch, 4 << 20),
            name="input_grad",
        )(after, moved, fine, strip, weight, *done)
        pooled.append(gc)
        made += size

    def beside(got, size, after):
        nonlocal done, pooled
        if size:
            input_piece(size, after)
            got, done, pooled = lax.optimization_barrier((got, done, pooled))
        return got

    def pooled_strip(s):
        at = strip_order(n).index(s) * cr
        groups_done = [x[g] for x in pooled for g in range(x.shape[0])]
        return jnp.concatenate([x.reshape(-1, ch // 2) for x in groups_done[at : at + cr]])

    def add(*terms):
        return functools.reduce(jnp.add, [t.astype(F32) for t in terms]).astype(BF)

    def core_swap(x):
        return lax.ppermute(x, "row", xor_pairs(nrow, 1))

    def plane_swap(x, s):
        return lax.ppermute(x, "row", xor_pairs(nrow, 2 * s))

    sizes = piece_sizes(rows // 4)
    total = add(keep, *beside([core_swap(send)], sizes[0], send))
    got = [plane_swap(total[s], s) for s in range(1, planes)]
    total = add(total[0], *beside(got, sizes[1], total))
    if not aligned:
        order = jnp.arange(halves) ^ (lax.axis_index("col") % halves)
        total = total.reshape(halves, depth // halves, half)[order]
    bit = halves // 2
    while bit:
        got = [col_swap(total[bit:], bit)]
        total = add(total[:bit], *beside(got, sizes[2] if bit == 1 else 0, total))
        bit //= 2
    total = add(total, *beside([col_swap(total, halves)], sizes[3], total))

    strips = {s: [(0, pooled_strip(s))] for s in range(n)}

    def hop(bit, extra):
        sent = [(s, src, x) for s in strips if s & bit for src, x in strips[s]]
        got = col_swap(jnp.concatenate(extra + [x for _, _, x in sent]), bit)
        at = sum(x.shape[0] for x in extra)
        head = got[:at]
        for s, src, x in sent:
            strips.pop(s, None)
            strips[s ^ bit].append((src ^ bit, got[at : at + x.shape[0]]))
            at += x.shape[0]
        return head

    bit = 1
    while bit < halves // 2:
        head = hop(bit, [total.reshape(-1, half)])
        total = jnp.concatenate([total, head.reshape(total.shape)])
        bit *= 2
    head = hop(bit, [total.reshape(-1, half)])
    if aligned:
        waves = [total, head.reshape(total.shape)]
    else:
        total = jnp.concatenate([total, head.reshape(total.shape)])
        waves = [total[order].reshape(1, depth, half)]
    ways = list(range(planes - 1, 0, -1))
    waves = [[x] + [plane_swap(x, s) for s in ways] for x in waves]
    if aligned:
        waves[0][1:], waves[1][0] = lax.optimization_barrier((waves[0][1:], waves[1][0]))

    hop(bit * 2, [])
    parts = [x for _, x in sorted(strips[0], key=lambda pair: pair[0])]
    pixels = rows * nrow * width * n

    def finish(out, pieces, spots, parts=()):
        coarse = [shape(cr, n * cols, ch)] if parts else []
        count, tall = len(pieces), pieces[0].shape[0]
        return pl.pallas_call(
            functools.partial(finish_kernel, float(pixels) ** -0.5, zs, spots, len(parts)),
            out_shape=[shape(9, ch, ch, dtype=F32)] + coarse,
            in_specs=[vmem()] * (count + len(parts)) + [hbm() for _ in out],
            out_specs=[hbm()] + [hbm() for _ in coarse],
            input_output_aliases={count + len(parts): 0} if out else {},
            scratch_shapes=[
                pltpu.VMEM((count, tall, 9, depth // 9, half), F32),
                pltpu.SemaphoreType.DMA((count, tall)),
            ]
            + [x for c in coarse for x in (pltpu.VMEM(c.shape, BF), pltpu.SemaphoreType.DMA((1,)))],
            compiler_params=params(8),
            cost_estimate=cost(1 << 20, 4 << 20),
            name="finish",
        )(*pieces, *parts, *out)

    spots = [(s, k * wave[0].shape[0]) for k, wave in enumerate(waves) for s in [0] + ways]
    mine = [x for wave in waves for x in wave]
    other = []
    for wave in waves:
        swapped = core_swap(jnp.stack(wave))
        other += [swapped[i] for i in range(len(wave))]
    out = finish([], mine, tuple((0, *spot) for spot in spots))
    grad_weight, grad_coarse = finish(out, other, tuple((1, *spot) for spot in spots), parts)
    return (done[0][None], grad_coarse[None], grad_weight.reshape(3, 3, ch, ch))


def piece_sizes(groups):
    sizes = [groups // 8, groups * 5 // 8, groups // 8]
    return sizes + [groups - sum(sizes)]


def solution(mesh):
    return jax.shard_map(
        per_device,
        mesh=mesh,
        in_specs=(
            P(None, "row", "col", None),
            P(None, ("row", "col"), None, None),
            P(),
            P(),
            P(),
            P(None, "row", "col", None),
        ),
        out_specs=(P(None, "row", "col", None), P(None, ("row", "col"), None, None), P()),
        check_vma=False,
    )
```

time: 74.6 us -> 65.8 us (0.88)
  starting transfers between devices: 30.5 us -> 25 us
  waiting for transfers between devices: 15.6 us -> 12.8 us
  Pallas kernels: 26.3 us -> 24.1 us
  local copies, waits for them, and re-layouts: 0.09 us -> 1.65 us
    ppermute x5 -> x2, starting transfers between devices: 8.7 us -> 0.87 us  [the longest x1 0.8 us: per_device(): lax.ppermute(two, 'row', [(i, i + 1) for i in odd] + [(i + 1, i) for i in...]
    ppermute x6 -> x9, starting transfers between devices: 7.63 us -> 10.8 us  [plane_swap(): return lax.ppermute(x, 'row', xor_pairs(nrow, 2 * s))]
    pallas_call x4 -> x2, Pallas kernels: 4.13 us -> 2.25 us  [finish(): pl.pallas_call(functools.partial(finish_kernel, float(pixels) ** (-0.5),...]
    ppermute x6 -> x9, waiting for transfers between devices: 6.25 us -> 4.54 us  [plane_swap(): return lax.ppermute(x, 'row', xor_pairs(nrow, 2 * s))]
    unnamed x6 -> x11, local copies, waits for them, and re-layouts: 0.01 us -> 1.54 us
    pallas_call x3 -> x4, Pallas kernels: 8.93 us -> 9.95 us  [input_piece(): pl.pallas_call(functools.partial(input_kernel, made, size, n), out_shape=...]
    ppermute x4 -> x3, starting transfers between devices: 3.22 us -> 2.63 us  [core_swap(): return lax.ppermute(x, 'row', xor_pairs(nrow, 1))]
    ppermute x9 -> x7, waiting for transfers between devices: 8.76 us -> 8.27 us  [col_swap(): return lax.ppermute(x, 'col', xor_pairs(n, s))]
  transfers between devices with their start and end apart: 24 -> 21, of which waited for: 13 -> 10; matrix products, arithmetic and copies ran while one was open for 0% -> 0% of each run, Pallas kernels for 24% -> 23%
where the time goes in v2:
time: 65.8 us; the launch traced here: 65.6 us
  starting transfers between devices  25 us (38%)
  Pallas kernels  24.1 us (37%)
  waiting for transfers between devices  12.8 us (19%)
  local copies, waits for them, and re-layouts  1.65 us (3%)
  between operations  1.58 us (2%)
    ppermute x7, starting transfers between devices, col_swap(): return lax.ppermute(x, 'col', xor_pairs(n, s))  10.8 us
    ppermute x9, starting transfers between devices, plane_swap(): return lax.ppermute(x, 'row', xor_pairs(nrow, 2 * s))  10.8 us
    pallas_call x4, Pallas kernels, input_piece(): pl.pallas_call(functools.partial(input_kernel, made, size, n), out_shape=...  9.95 us
    ppermute x7, waiting for transfers between devices, col_swap(): return lax.ppermute(x, 'col', xor_pairs(n, s))  8.27 us
    pallas_call x1, Pallas kernels, per_device(): pl.pallas_call(weight_kernel, out_shape=[part, part, shape(*moved.shape)]...  6.56 us
    ppermute x9, waiting for transfers between devices, plane_swap(): return lax.ppermute(x, 'row', xor_pairs(nrow, 2 * s))  4.54 us
    pallas_call x1, Pallas kernels, per_device(): pl.pallas_call(functools.partial(prepare_kernel, n, cr), out_shape=[shape...  2.68 us
    ppermute x3, starting transfers between devices, core_swap(): return lax.ppermute(x, 'row', xor_pairs(nrow, 1))  2.63 us
  transfers between devices with their start and end apart: 21, of which 10 were waited for; matrix products, arithmetic and copies ran while one was open for 0% of the time, Pallas kernels for 23%

profile of v2, /device:TPU:0, one launch (start us, length us, event | category | flops | bytes accessed | tf_op | source)
XLA Modules:
  0.0 65.6 jit_solution(13455365833644998459)
XLA Ops:
  0.6 1.6 %start.1 = (bf16[64,256]{1,0:T(8,128)(2,1)S(1)}, bf16[96,256]{1,0:T(8,128)(2,1)S(1)}, bf16[64,256]{1,0:T(8,128)(2,1)S(1)}, bf16[96,256]{1,0:T(8,128)(2,1)S(1)}) custom-call(bf16[32,128,256]{2,1,0:T(8,128)(2,1)} %bitcast.63, bf16[2,128,256]{2,1,0:T(8,128)(2,1)} %bitcast.78), custom_call_target="tpu_custom_call" | custom-call | flops 1048576 | bytes 4194304 | tf_op jit(solution)/shard_map/start/pallas_call | solution.py:293
  2.2 3.1 %collective-permute-start = (bf16[96,256]{1,0:T(8,128)(2,1)S(1)}, bf16[96,256]{1,0:T(8,128)(2,1)S(1)}, u32[]{:S(2)}, u32[]{:S(2)}) collective-permute-start(bf16[96,256]{1,0:T(8,128)(2,1)S(1)} %get-tuple-element.55), channel_id=1, source_target_pairs={{0,1},{1,0},{2,3},{3,2},{4,5},{5,4},{6,7},{7,6},{8,9},{9,8},{10,11... | collective-permute-start | bytes 147464 | tf_op jit(solution)/shard_map/ppermute | solution.py:291
  5.3 2.5 %collective-permute-start.1 = (bf16[96,256]{1,0:T(8,128)(2,1)S(1)}, bf16[96,256]{1,0:T(8,128)(2,1)S(1)}, u32[]{:S(2)}, u32[]{:S(2)}) collective-permute-start(bf16[96,256]{1,0:T(8,128)(2,1)S(1)} %get-tuple-element.56), channel_id=1, source_target_pairs={{0,3},{1,2},{2,1},{3,0},{4,7},{5,6},{6,5},{7,4},{8,11},{9,10},{10,... | collective-permute-start | bytes 147464 | tf_op jit(solution)/shard_map/ppermute | solution.py:291
  7.8 0.1 collective-permute-start.2
  8.6 0.0 copy-start.3
  8.6 1.2 %copy-done.3 = f32[1000,256]{1,0:T(8,128)S(1)} copy-done((f32[1000,256]{1,0:T(8,128)S(1)}, f32[1000,256]{1,0:T(8,128)}, u32[]{:S(2)}) %copy-start.3) | copy-done | bytes 1024024
  9.8 1.1 %load.1 = (bf16[3,34,128,256]{3,2,1,0:T(8,128)(2,1)S(1)}, f32[1,256]{1,0:T(1,128)S(1)}) custom-call(s32[1]{0:T(128)S(6)} %copy.25.steps, bf16[32,128,256]{2,1,0:T(8,128)(2,1)S(1)} %bitcast.64, f32[1000,256]{1,0:T(8,128)S(1)} %copy-done.3), custom_call_target="tpu_custom_call" | custom-call | flops 1048576 | bytes 4194304 | tf_op jit(solution)/shard_map/load/pallas_call | solution.py:309
  10.9 0.8 %collective-permute-done.1.refs_1_.refs_3_ = bf16[96,256]{1,0:T(8,128)(2,1)S(1)} collective-permute-done((bf16[96,256]{1,0:T(8,128)(2,1)S(1)}, bf16[96,256]{1,0:T(8,128)(2,1)S(1)}, u32[]{:S(2)}, u32[]{:S(2)}) %collective-permute-start.1) | collective-permute-done | bytes 49184 | tf_op jit(solution)/shard_map/ppermute | solution.py:291
  11.6 0.1 edges.1
  11.7 0.1 collective-permute-start.3
  11.8 0.8 %collective-permute-start.4 = (bf16[144,256]{1,0:T(8,128)(2,1)S(1)}, bf16[144,256]{1,0:T(8,128)(2,1)S(1)}, u32[]{:S(2)}, u32[]{:S(2)}) collective-permute-start(bf16[144,256]{1,0:T(8,128)(2,1)S(1)} %get-tuple-element.63), channel_id=1, source_target_pairs={{4,8},{12,16},{20,24},{8,4},{16,12},{24,20},{5,9},{13,17},{21,25},... | collective-permute-start | bytes 221192 | tf_op jit(solution)/shard_map/ppermute | solution.py:335
  12.6 0.4 collective-permute-done.2.refs_2_
  12.9 0.3 copy-done
  13.2 2.7 %prepare.1 = (bf16[3,34,128,256]{3,2,1,0:T(8,128)(2,1)S(1)}, bf16[256,4096]{1,0:T(8,128)(2,1)S(1)}, bf16[8,32,256]{2,1,0:T(8,128)(2,1)S(1)}) custom-call(bf16[32,128,256]{2,1,0:T(8,128)(2,1)S(1)} %bitcast.54, f32[32,256]{1,0:T(8,128)S(1)} %get-tuple-element.57.left, f32[32,256]{1,0:T(8,128)S(1)} %get-tuple-element.58.right, ...), custom_call_target="tpu_custom_call", output_to_operand_aliasing={{0}: (3, {})} | custom-call | flops 4294967296 | bytes 4194304 | tf_op jit(solution)/shard_map/prepare/pallas_call | solution.py:338
  15.9 0.0 collective-permute-done.3.one
  15.9 0.0 copy-start.1
  16.0 6.6 %weight_grad.1 = (bf16[4,2,288,128]{3,2,1,0:T(8,128)(2,1)S(1)}, bf16[4,2,288,128]{3,2,1,0:T(8,128)(2,1)S(1)}, bf16[3,34,128,256]{3,2,1,0:T(8,128)(2,1)S(1)}) custom-call(bf16[256,4096]{1,0:T(8,128)(2,1)S(1)} %get-tuple-element.61.act_t, bf16[144,256]{1,0:T(8,128)(2,1)S(1)} %collective-permute-done.3.one, ...), custom_call_target="tpu_custom_call", output_to_operand_aliasing={{2}: (3, {})} | custom-call | flops 4831838208 | bytes 8388608 | tf_op jit(solution)/shard_map/weight_grad/pallas_call | solution.py:356
  22.5 2.5 %collective-permute-start.5 = (bf16[4,2,288,128]{3,2,1,0:T(8,128)(2,1)S(1)}, bf16[4,2,288,128]{3,2,1,0:T(8,128)(2,1)S(1)}, u32[]{:S(2)}, u32[]{:S(2)}) collective-permute-start(bf16[4,2,288,128]{3,2,1,0:T(8,128)(2,1)S(1)} %get-tuple-element.66.after), channel_id=1, source_target_pairs={{0,4},{4,0},{8,12},{12,8},{16,20},{20,16},{24,28},{28,24},{1,5},{5... | collective-permute-start | bytes 1769480 | tf_op jit(solution)/shard_map/ppermute | solution.py:407
  25.0 1.7 %input_grad.4 = (bf16[32,128,256]{2,1,0:T(8,128)(2,1)}, bf16[1,2,32,128]{3,2,1,0:T(8,128)(2,1)S(1)}) custom-call(bf16[4,2,288,128]{3,2,1,0:T(8,128)(2,1)S(1)} %get-tuple-element.66.after, bf16[3,34,128,256]{3,2,1,0:T(8,128)(2,1)S(1)} %get-tuple-element.67.moved, bf16[32,128,256]{2,1,0:T(8,128)(2,1)S(1)} %bitcast.55, ...), custom_call_target="tpu_custom_call" | custom-call | flops 603979776 | bytes 4194304 | tf_op jit(solution)/shard_map/input_grad/pallas_call | solution.py:371
  26.8 0.2 add_convert_fusion.after
  27.0 2.4 %collective-permute-start.8 = (bf16[2,288,128]{2,1,0:T(8,128)(2,1)S(1)}, bf16[2,288,128]{2,1,0:T(8,128)(2,1)S(1)}, u32[]{:S(2)}, u32[]{:S(2)}) collective-permute-start(bf16[2,288,128]{2,1,0:T(8,128)(2,1)S(1)} %get-tuple-element.105), channel_id=1, source_target_pairs={{0,24},{4,28},{8,16},{12,20},{16,8},{20,12},{24,0},{28,4},{1,25},{... | collective-permute-start | bytes 442376 | tf_op jit(solution)/shard_map/ppermute | solution.py:410
  29.3 1.4 %collective-permute-start.7 = (bf16[2,288,128]{2,1,0:T(8,128)(2,1)S(1)}, bf16[2,288,128]{2,1,0:T(8,128)(2,1)S(1)}, u32[]{:S(2)}, u32[]{:S(2)}) collective-permute-start(bf16[2,288,128]{2,1,0:T(8,128)(2,1)S(1)} %get-tuple-element.106), channel_id=1, source_target_pairs={{0,16},{4,20},{8,24},{12,28},{16,0},{20,4},{24,8},{28,12},{1,17},{... | collective-permute-start | bytes 442376 | tf_op jit(solution)/shard_map/ppermute | solution.py:410
  30.7 4.8 %input_grad.5 = (bf16[32,128,256]{2,1,0:T(8,128)(2,1)}, bf16[5,2,32,128]{3,2,1,0:T(8,128)(2,1)S(1)}) custom-call(bf16[4,2,288,128]{3,2,1,0:T(8,128)(2,1)S(1)} %add_convert_fusion.after, bf16[3,34,128,256]{3,2,1,0:T(8,128)(2,1)S(1)} %get-tuple-element.67.moved, bf16[32,128,256]{2,1,0:T(8,128)(2,1)S(1)} %bitcast.56, ...), custom_call_target="tpu_custom_call", output_to_operand_aliasing={{0}: (5, {})} | custom-call | flops 3019898880 | bytes 4194304 | tf_op jit(solution)/shard_map/input_grad/pallas_call | solution.py:371
  35.5 1.5 %collective-permute-done.7 = bf16[2,288,128]{2,1,0:T(8,128)(2,1)S(1)} collective-permute-done((bf16[2,288,128]{2,1,0:T(8,128)(2,1)S(1)}, bf16[2,288,128]{2,1,0:T(8,128)(2,1)S(1)}, u32[]{:S(2)}, u32[]{:S(2)}) %collective-permute-start.7) | collective-permute-done | bytes 147488 | tf_op jit(solution)/shard_map/ppermute | solution.py:410
  37.1 0.8 %collective-permute-done.6 = bf16[2,288,128]{2,1,0:T(8,128)(2,1)S(1)} collective-permute-done((bf16[2,288,128]{2,1,0:T(8,128)(2,1)S(1)}, bf16[2,288,128]{2,1,0:T(8,128)(2,1)S(1)}, u32[]{:S(2)}, u32[]{:S(2)}) %collective-permute-start.6) | collective-permute-done | bytes 147488 | tf_op jit(solution)/shard_map/ppermute | solution.py:410
  37.9 0.1 fusion.2.after
  38.0 1.1 %collective-permute-start.9 = (bf16[1,288,128]{2,1,0:T(8,128)(2,1)S(1)}, bf16[1,288,128]{2,1,0:T(8,128)(2,1)S(1)}, u32[]{:S(2)}, u32[]{:S(2)}) collective-permute-start(bf16[1,288,128]{2,1,0:T(8,128)(2,1)S(1)} %slice.101), channel_id=1, source_target_pairs={{0,1},{1,0},{2,3},{3,2},{4,5},{5,4},{6,7},{7,6},{8,9},{9,8},{10,11... | collective-permute-start | bytes 221192 | tf_op jit(solution)/shard_map/ppermute | solution.py:291
  39.1 1.7 %input_grad.6 = (bf16[32,128,256]{2,1,0:T(8,128)(2,1)}, bf16[1,2,32,128]{3,2,1,0:T(8,128)(2,1)S(1)}) custom-call(bf16[2,288,128]{2,1,0:T(8,128)(2,1)S(1)} %fusion.2.after, bf16[3,34,128,256]{3,2,1,0:T(8,128)(2,1)S(1)} %get-tuple-element.67.moved, bf16[32,128,256]{2,1,0:T(8,128)(2,1)S(1)} %bitcast.57, ...), custom_call_target="tpu_custom_call", output_to_operand_aliasing={{0}: (5, {})} | custom-call | flops 603979776 | bytes 4194304 | tf_op jit(solution)/shard_map/input_grad/pallas_call | solution.py:371
  40.8 1.6 %collective-permute-done.9 = bf16[1,288,128]{2,1,0:T(8,128)(2,1)S(1)} collective-permute-done((bf16[1,288,128]{2,1,0:T(8,128)(2,1)S(1)}, bf16[1,288,128]{2,1,0:T(8,128)(2,1)S(1)}, u32[]{:S(2)}, u32[]{:S(2)}) %collective-permute-start.9) | collective-permute-done | bytes 73760 | tf_op jit(solution)/shard_map/ppermute | solution.py:291
  42.5 2.1 %collective-permute-start.10 = (bf16[1,288,128]{2,1,0:T(8,128)(2,1)S(1)}, bf16[1,288,128]{2,1,0:T(8,128)(2,1)S(1)}, u32[]{:S(2)}, u32[]{:S(2)}) collective-permute-start(bf16[1,288,128]{2,1,0:T(8,128)(2,1)S(1)} %add_convert_fusion.2.after), channel_id=1, source_target_pairs={{0,2},{1,3},{2,0},{3,1},{4,6},{5,7},{6,4},{7,5},{8,10},{9,11},{10,... | collective-permute-start | bytes 221192 | tf_op jit(solution)/shard_map/ppermute | solution.py:291
  44.6 1.7 %input_grad.7 = (bf16[32,128,256]{2,1,0:T(8,128)(2,1)}, bf16[1,2,32,128]{3,2,1,0:T(8,128)(2,1)S(1)}) custom-call(bf16[1,288,128]{2,1,0:T(8,128)(2,1)S(1)} %add_convert_fusion.2.after, bf16[3,34,128,256]{3,2,1,0:T(8,128)(2,1)S(1)} %get-tuple-element.67.moved, bf16[32,128,256]{2,1,0:T(8,128)(2,1)S(1)} %bitcast.58, ...), custom_call_target="tpu_custom_call", output_to_operand_aliasing={{0}: (5, {})} | custom-call | flops 603979776 | bytes 4194304 | tf_op jit(solution)/shard_map/input_grad/pallas_call | solution.py:371
  46.3 2.3 %collective-permute-done.10 = bf16[1,288,128]{2,1,0:T(8,128)(2,1)S(1)} collective-permute-done((bf16[1,288,128]{2,1,0:T(8,128)(2,1)S(1)}, bf16[1,288,128]{2,1,0:T(8,128)(2,1)S(1)}, u32[]{:S(2)}, u32[]{:S(2)}) %collective-permute-start.10) | collective-permute-done | bytes 73760 | tf_op jit(solution)/shard_map/ppermute | solution.py:291
  48.7 0.4 collective-permute-start.14
  49.1 1.4 %collective-permute-start.13 = (bf16[1,288,128]{2,1,0:T(8,128)(2,1)S(1)}, bf16[1,288,128]{2,1,0:T(8,128)(2,1)S(1)}, u32[]{:S(2)}, u32[]{:S(2)}) collective-permute-start(bf16[1,288,128]{2,1,0:T(8,128)(2,1)S(1)} %get-tuple-element.104.refs_0_), channel_id=1, source_target_pairs={{0,8},{4,12},{8,0},{12,4},{16,24},{20,28},{24,16},{28,20},{1,9},{5... | collective-permute-start | bytes 221192 | tf_op jit(solution)/shard_map/ppermute | solution.py:410
  50.5 0.6 collective-permute-start.12
  51.1 1.4 %collective-permute-start.11 = (bf16[1,288,128]{2,1,0:T(8,128)(2,1)S(1)}, bf16[1,288,128]{2,1,0:T(8,128)(2,1)S(1)}, u32[]{:S(2)}, u32[]{:S(2)}) collective-permute-start(bf16[1,288,128]{2,1,0:T(8,128)(2,1)S(1)} %get-tuple-element.104.refs_0_), channel_id=1, source_target_pairs={{0,24},{4,28},{8,16},{12,20},{16,8},{20,12},{24,0},{28,4},{1,25},{... | collective-permute-start | bytes 221192 | tf_op jit(solution)/shard_map/ppermute | solution.py:410
  52.6 1.2 %collective-permute-done.14 = bf16[544,128]{1,0:T(8,128)(2,1)S(1)} collective-permute-done((bf16[544,128]{1,0:T(8,128)(2,1)S(1)}, bf16[544,128]{1,0:T(8,128)(2,1)S(1)}, u32[]{:S(2)}, u32[]{:S(2)}) %collective-permute-start.14) | collective-permute-done | bytes 139296 | tf_op jit(solution)/shard_map/ppermute | solution.py:291
  53.8 1.4 %collective-permute-start.18 = (bf16[1,288,128]{2,1,0:T(8,128)(2,1)S(1)}, bf16[1,288,128]{2,1,0:T(8,128)(2,1)S(1)}, u32[]{:S(2)}, u32[]{:S(2)}) collective-permute-start(bf16[1,288,128]{2,1,0:T(8,128)(2,1)S(1)} %slice_bitcast_fusion.12.refs_4_), channel_id=1, source_target_pairs={{0,8},{4,12},{8,0},{12,4},{16,24},{20,28},{24,16},{28,20},{1,9},{5... | collective-permute-start | bytes 221192 | tf_op jit(solution)/shard_map/ppermute | solution.py:410
  55.2 0.6 collective-permute-start.17
  55.8 1.5 %collective-permute-start.16 = (bf16[1,288,128]{2,1,0:T(8,128)(2,1)S(1)}, bf16[1,288,128]{2,1,0:T(8,128)(2,1)S(1)}, u32[]{:S(2)}, u32[]{:S(2)}) collective-permute-start(bf16[1,288,128]{2,1,0:T(8,128)(2,1)S(1)} %slice_bitcast_fusion.12.refs_4_), channel_id=1, source_target_pairs={{0,24},{4,28},{8,16},{12,20},{16,8},{20,12},{24,0},{28,4},{1,25},{... | collective-permute-start | bytes 221192 | tf_op jit(solution)/shard_map/ppermute | solution.py:410
  57.3 1.5 %collective-permute-start.20 = (bf16[256,128]{1,0:T(8,128)(2,1)S(1)}, bf16[256,128]{1,0:T(8,128)(2,1)S(1)}, u32[]{:S(2)}, u32[]{:S(2)}) collective-permute-start(bf16[256,128]{1,0:T(8,128)(2,1)S(1)} %pad_maximum_fusion.2), channel_id=1, source_target_pairs={{0,2},{1,3},{2,0},{3,1},{4,6},{5,7},{6,4},{7,5},{8,10},{9,11},{10,... | collective-permute-start | bytes 196616 | tf_op jit(solution)/shard_map/ppermute | solution.py:291
  58.8 0.1 collective-permute-start.15
  58.9 0.6 collective-permute-done.17.refs_6_
  59.6 1.5 %collective-permute-done.16.refs_5_ = bf16[1,288,128]{2,1,0:T(8,128)(2,1)S(1)} collective-permute-done((bf16[1,288,128]{2,1,0:T(8,128)(2,1)S(1)}, bf16[1,288,128]{2,1,0:T(8,128)(2,1)S(1)}, u32[]{:S(2)}, u32[]{:S(2)}) %collective-permute-start.16) | collective-permute-done | bytes 73760 | tf_op jit(solution)/shard_map/ppermute | solution.py:410
  61.1 0.1 collective-permute-start.19
  61.2 2.0 %collective-permute-done.20 = bf16[256,128]{1,0:T(8,128)(2,1)S(1)} collective-permute-done((bf16[256,128]{1,0:T(8,128)(2,1)S(1)}, bf16[256,128]{1,0:T(8,128)(2,1)S(1)}, u32[]{:S(2)}, u32[]{:S(2)}) %collective-permute-start.20) | collective-permute-done | bytes 65568 | tf_op jit(solution)/shard_map/ppermute | solution.py:291
  63.2 1.1 %finish.2.refs_12_ = f32[9,256,256]{2,1,0:T(8,128)} custom-call(bf16[1,288,128]{2,1,0:T(8,128)(2,1)S(1)} %get-tuple-element.104.refs_0_, bf16[1,288,128]{2,1,0:T(8,128)(2,1)S(1)} %collective-permute-done.11.refs_1_, bf16[1,288,128]{2,1,0:T(8,128)(2,1)S(1)} %collective-permute-done.12.refs_2_, bf16[1,288,128]{2,1,0:T(8,128)(2,1)S(1)} %collective-permute-done.13.refs_3_, ...), custom_call_target="tpu_custom_call" | custom-call | flops 1048576 | bytes 4194304 | tf_op jit(solution)/shard_map/finish/pallas_call | solution.py:462
  64.4 1.2 %finish.3 = (f32[9,256,256]{2,1,0:T(8,128)}, bf16[2,128,256]{2,1,0:T(8,128)(2,1)}) custom-call(bf16[1,288,128]{2,1,0:T(8,128)(2,1)S(1)} %get-tuple-element.115.refs_0_, bf16[1,288,128]{2,1,0:T(8,128)(2,1)S(1)} %get-tuple-element.114.refs_1_, bf16[1,288,128]{2,1,0:T(8,128)(2,1)S(1)} %get-tuple-element.113.refs_2_, ...), custom_call_target="tpu_custom_call", output_to_operand_aliasing={{0}: (12, {})} | custom-call | flops 1048576 | bytes 4194304 | tf_op jit(solution)/shard_map/finish/pallas_call | solution.py:462
  (33 shorter events, 0.3 us)
Async XLA Ops:
  0.6 7.9 %copy-start.2 = (bf16[1,32,128,256]{3,2,1,0:T(8,128)(2,1)S(1)}, bf16[1,32,128,256]{3,2,1,0:T(8,128)(2,1)}, u32[]{:S(2)}) copy-start(bf16[1,32,128,256]{3,2,1,0:T(8,128)(2,1)} %param.11) | copy-start | bytes 6291460
  2.2 8.6 %collective-permute-start = (bf16[96,256]{1,0:T(8,128)(2,1)S(1)}, bf16[96,256]{1,0:T(8,128)(2,1)S(1)}, u32[]{:S(2)}, u32[]{:S(2)}) collective-permute-start(bf16[96,256]{1,0:T(8,128)(2,1)S(1)} %get-tuple-element.55), channel_id=1, source_target_pairs={{0,1},{1,0},{2,3},{3,2},{4,5},{5,4},{6,7},{7,6},{8,9},{9,8},{10,11... | collective-permute-start | bytes 147464 | tf_op jit(solution)/shard_map/ppermute | solution.py:291
  5.3 6.3 %collective-permute-start.1 = (bf16[96,256]{1,0:T(8,128)(2,1)S(1)}, bf16[96,256]{1,0:T(8,128)(2,1)S(1)}, u32[]{:S(2)}, u32[]{:S(2)}) collective-permute-start(bf16[96,256]{1,0:T(8,128)(2,1)S(1)} %get-tuple-element.56), channel_id=1, source_target_pairs={{0,3},{1,2},{2,1},{3,0},{4,7},{5,6},{6,5},{7,4},{8,11},{9,10},{10,... | collective-permute-start | bytes 147464 | tf_op jit(solution)/shard_map/ppermute | solution.py:291
  7.8 5.2 %collective-permute-start.2 = (bf16[64,256]{1,0:T(8,128)(2,1)S(1)}, bf16[64,256]{1,0:T(8,128)(2,1)S(1)}, u32[]{:S(2)}, u32[]{:S(2)}) collective-permute-start(bf16[64,256]{1,0:T(8,128)(2,1)S(1)} %get-tuple-element.60), channel_id=1, source_target_pairs={{0,2},{1,3},{2,0},{3,1},{4,6},{5,7},{6,4},{7,5},{8,10},{9,11},{10,... | collective-permute-start | bytes 98312 | tf_op jit(solution)/shard_map/ppermute | solution.py:291
  8.6 1.2 %copy-start.3 = (f32[1000,256]{1,0:T(8,128)S(1)}, f32[1000,256]{1,0:T(8,128)}, u32[]{:S(2)}) copy-start(f32[1000,256]{1,0:T(8,128)} %scales.1) | copy-start | bytes 3072004
  11.6 1.6 %copy-start = (bf16[1,32,128,256]{3,2,1,0:T(8,128)(2,1)S(1)}, bf16[1,32,128,256]{3,2,1,0:T(8,128)(2,1)}, u32[]{:S(2)}) copy-start(bf16[1,32,128,256]{3,2,1,0:T(8,128)(2,1)} %param.6) | copy-start | bytes 6291460
  11.7 4.2 %collective-permute-start.3 = (bf16[144,256]{1,0:T(8,128)(2,1)S(1)}, bf16[144,256]{1,0:T(8,128)(2,1)S(1)}, u32[]{:S(2)}, u32[]{:S(2)}) collective-permute-start(bf16[144,256]{1,0:T(8,128)(2,1)S(1)} %get-tuple-element.62), channel_id=1, source_target_pairs={{0,4},{4,0},{8,12},{12,8},{16,20},{20,16},{24,28},{28,24},{1,5},{5... | collective-permute-start | bytes 221192 | tf_op jit(solution)/shard_map/ppermute | solution.py:333
  11.8 4.2 %collective-permute-start.4 = (bf16[144,256]{1,0:T(8,128)(2,1)S(1)}, bf16[144,256]{1,0:T(8,128)(2,1)S(1)}, u32[]{:S(2)}, u32[]{:S(2)}) collective-permute-start(bf16[144,256]{1,0:T(8,128)(2,1)S(1)} %get-tuple-element.63), channel_id=1, source_target_pairs={{4,8},{12,16},{20,24},{8,4},{16,12},{24,20},{5,9},{13,17},{21,25},... | collective-permute-start | bytes 221192 | tf_op jit(solution)/shard_map/ppermute | solution.py:335
  15.9 9.1 %copy-start.1 = (bf16[3,3,256,256]{3,2,1,0:T(8,128)(2,1)S(1)}, bf16[3,3,256,256]{3,2,1,0:T(8,128)(2,1)}, u32[]{:S(2)}) copy-start(bf16[3,3,256,256]{3,2,1,0:T(8,128)(2,1)} %param.8) | copy-start | bytes 3538948
  22.5 4.2 %collective-permute-start.5 = (bf16[4,2,288,128]{3,2,1,0:T(8,128)(2,1)S(1)}, bf16[4,2,288,128]{3,2,1,0:T(8,128)(2,1)S(1)}, u32[]{:S(2)}, u32[]{:S(2)}) collective-permute-start(bf16[4,2,288,128]{3,2,1,0:T(8,128)(2,1)S(1)} %get-tuple-element.66.after), channel_id=1, source_target_pairs={{0,4},{4,0},{8,12},{12,8},{16,20},{20,16},{24,28},{28,24},{1,5},{5... | collective-permute-start | bytes 1769480 | tf_op jit(solution)/shard_map/ppermute | solution.py:407
  27.0 8.6 %collective-permute-start.8 = (bf16[2,288,128]{2,1,0:T(8,128)(2,1)S(1)}, bf16[2,288,128]{2,1,0:T(8,128)(2,1)S(1)}, u32[]{:S(2)}, u32[]{:S(2)}) collective-permute-start(bf16[2,288,128]{2,1,0:T(8,128)(2,1)S(1)} %get-tuple-element.105), channel_id=1, source_target_pairs={{0,24},{4,28},{8,16},{12,20},{16,8},{20,12},{24,0},{28,4},{1,25},{... | collective-permute-start | bytes 442376 | tf_op jit(solution)/shard_map/ppermute | solution.py:410
  29.3 7.8 %collective-permute-start.7 = (bf16[2,288,128]{2,1,0:T(8,128)(2,1)S(1)}, bf16[2,288,128]{2,1,0:T(8,128)(2,1)S(1)}, u32[]{:S(2)}, u32[]{:S(2)}) collective-permute-start(bf16[2,288,128]{2,1,0:T(8,128)(2,1)S(1)} %get-tuple-element.106), channel_id=1, source_target_pairs={{0,16},{4,20},{8,24},{12,28},{16,0},{20,4},{24,8},{28,12},{1,17},{... | collective-permute-start | bytes 442376 | tf_op jit(solution)/shard_map/ppermute | solution.py:410
  30.7 7.2 %collective-permute-start.6 = (bf16[2,288,128]{2,1,0:T(8,128)(2,1)S(1)}, bf16[2,288,128]{2,1,0:T(8,128)(2,1)S(1)}, u32[]{:S(2)}, u32[]{:S(2)}) collective-permute-start(bf16[2,288,128]{2,1,0:T(8,128)(2,1)S(1)} %get-tuple-element.107), channel_id=1, source_target_pairs={{0,8},{4,12},{8,0},{12,4},{16,24},{20,28},{24,16},{28,20},{1,9},{5... | collective-permute-start | bytes 442376 | tf_op jit(solution)/shard_map/ppermute | solution.py:410
  38.0 4.4 %collective-permute-start.9 = (bf16[1,288,128]{2,1,0:T(8,128)(2,1)S(1)}, bf16[1,288,128]{2,1,0:T(8,128)(2,1)S(1)}, u32[]{:S(2)}, u32[]{:S(2)}) collective-permute-start(bf16[1,288,128]{2,1,0:T(8,128)(2,1)S(1)} %slice.101), channel_id=1, source_target_pairs={{0,1},{1,0},{2,3},{3,2},{4,5},{5,4},{6,7},{7,6},{8,9},{9,8},{10,11... | collective-permute-start | bytes 221192 | tf_op jit(solution)/shard_map/ppermute | solution.py:291
  42.5 6.1 %collective-permute-start.10 = (bf16[1,288,128]{2,1,0:T(8,128)(2,1)S(1)}, bf16[1,288,128]{2,1,0:T(8,128)(2,1)S(1)}, u32[]{:S(2)}, u32[]{:S(2)}) collective-permute-start(bf16[1,288,128]{2,1,0:T(8,128)(2,1)S(1)} %add_convert_fusion.2.after), channel_id=1, source_target_pairs={{0,2},{1,3},{2,0},{3,1},{4,6},{5,7},{6,4},{7,5},{8,10},{9,11},{10,... | collective-permute-start | bytes 221192 | tf_op jit(solution)/shard_map/ppermute | solution.py:291
  48.7 5.1 %collective-permute-start.14 = (bf16[544,128]{1,0:T(8,128)(2,1)S(1)}, bf16[544,128]{1,0:T(8,128)(2,1)S(1)}, u32[]{:S(2)}, u32[]{:S(2)}) collective-permute-start(bf16[544,128]{1,0:T(8,128)(2,1)S(1)} %constant_dynamic-update-slice_fusion), channel_id=1, source_target_pairs={{0,1},{1,0},{2,3},{3,2},{4,5},{5,4},{6,7},{7,6},{8,9},{9,8},{10,11... | collective-permute-start | bytes 417800 | tf_op jit(solution)/shard_map/ppermute | solution.py:291
  49.1 6.8 %collective-permute-start.13 = (bf16[1,288,128]{2,1,0:T(8,128)(2,1)S(1)}, bf16[1,288,128]{2,1,0:T(8,128)(2,1)S(1)}, u32[]{:S(2)}, u32[]{:S(2)}) collective-permute-start(bf16[1,288,128]{2,1,0:T(8,128)(2,1)S(1)} %get-tuple-element.104.refs_0_), channel_id=1, source_target_pairs={{0,8},{4,12},{8,0},{12,4},{16,24},{20,28},{24,16},{28,20},{1,9},{5... | collective-permute-start | bytes 221192 | tf_op jit(solution)/shard_map/ppermute | solution.py:410
  50.5 6.8 %collective-permute-start.12 = (bf16[1,288,128]{2,1,0:T(8,128)(2,1)S(1)}, bf16[1,288,128]{2,1,0:T(8,128)(2,1)S(1)}, u32[]{:S(2)}, u32[]{:S(2)}) collective-permute-start(bf16[1,288,128]{2,1,0:T(8,128)(2,1)S(1)} %get-tuple-element.104.refs_0_), channel_id=1, source_target_pairs={{0,16},{4,20},{8,24},{12,28},{16,0},{20,4},{24,8},{28,12},{1,17},{... | collective-permute-start | bytes 221192 | tf_op jit(solution)/shard_map/ppermute | solution.py:410
  51.1 6.2 %collective-permute-start.11 = (bf16[1,288,128]{2,1,0:T(8,128)(2,1)S(1)}, bf16[1,288,128]{2,1,0:T(8,128)(2,1)S(1)}, u32[]{:S(2)}, u32[]{:S(2)}) collective-permute-start(bf16[1,288,128]{2,1,0:T(8,128)(2,1)S(1)} %get-tuple-element.104.refs_0_), channel_id=1, source_target_pairs={{0,24},{4,28},{8,16},{12,20},{16,8},{20,12},{24,0},{28,4},{1,25},{... | collective-permute-start | bytes 221192 | tf_op jit(solution)/shard_map/ppermute | solution.py:410
  53.8 5.1 %collective-permute-start.18 = (bf16[1,288,128]{2,1,0:T(8,128)(2,1)S(1)}, bf16[1,288,128]{2,1,0:T(8,128)(2,1)S(1)}, u32[]{:S(2)}, u32[]{:S(2)}) collective-permute-start(bf16[1,288,128]{2,1,0:T(8,128)(2,1)S(1)} %slice_bitcast_fusion.12.refs_4_), channel_id=1, source_target_pairs={{0,8},{4,12},{8,0},{12,4},{16,24},{20,28},{24,16},{28,20},{1,9},{5... | collective-permute-start | bytes 221192 | tf_op jit(solution)/shard_map/ppermute | solution.py:410
  55.2 4.4 %collective-permute-start.17 = (bf16[1,288,128]{2,1,0:T(8,128)(2,1)S(1)}, bf16[1,288,128]{2,1,0:T(8,128)(2,1)S(1)}, u32[]{:S(2)}, u32[]{:S(2)}) collective-permute-start(bf16[1,288,128]{2,1,0:T(8,128)(2,1)S(1)} %slice_bitcast_fusion.12.refs_4_), channel_id=1, source_target_pairs={{0,16},{4,20},{8,24},{12,28},{16,0},{20,4},{24,8},{28,12},{1,17},{... | collective-permute-start | bytes 221192 | tf_op jit(solution)/shard_map/ppermute | solution.py:410
  55.8 5.3 %collective-permute-start.16 = (bf16[1,288,128]{2,1,0:T(8,128)(2,1)S(1)}, bf16[1,288,128]{2,1,0:T(8,128)(2,1)S(1)}, u32[]{:S(2)}, u32[]{:S(2)}) collective-permute-start(bf16[1,288,128]{2,1,0:T(8,128)(2,1)S(1)} %slice_bitcast_fusion.12.refs_4_), channel_id=1, source_target_pairs={{0,24},{4,28},{8,16},{12,20},{16,8},{20,12},{24,0},{28,4},{1,25},{... | collective-permute-start | bytes 221192 | tf_op jit(solution)/shard_map/ppermute | solution.py:410
  57.3 5.9 %collective-permute-start.20 = (bf16[256,128]{1,0:T(8,128)(2,1)S(1)}, bf16[256,128]{1,0:T(8,128)(2,1)S(1)}, u32[]{:S(2)}, u32[]{:S(2)}) collective-permute-start(bf16[256,128]{1,0:T(8,128)(2,1)S(1)} %pad_maximum_fusion.2), channel_id=1, source_target_pairs={{0,2},{1,3},{2,0},{3,1},{4,6},{5,7},{6,4},{7,5},{8,10},{9,11},{10,... | collective-permute-start | bytes 196616 | tf_op jit(solution)/shard_map/ppermute | solution.py:291
  58.8 5.5 %collective-permute-start.15 = (bf16[4,1,288,128]{3,2,1,0:T(8,128)(2,1)S(1)}, bf16[4,1,288,128]{3,2,1,0:T(8,128)(2,1)S(1)}, u32[]{:S(2)}, u32[]{:S(2)}) collective-permute-start(bf16[4,1,288,128]{3,2,1,0:T(8,128)(2,1)S(1)} %pad_maximum_fusion), channel_id=1, source_target_pairs={{0,4},{4,0},{8,12},{12,8},{16,20},{20,16},{24,28},{28,24},{1,5},{5... | collective-permute-start | bytes 884744 | tf_op jit(solution)/shard_map/ppermute | solution.py:407
  61.1 3.3 %collective-permute-start.19 = (bf16[4,1,288,128]{3,2,1,0:T(8,128)(2,1)S(1)}, bf16[4,1,288,128]{3,2,1,0:T(8,128)(2,1)S(1)}, u32[]{:S(2)}, u32[]{:S(2)}) collective-permute-start(bf16[4,1,288,128]{3,2,1,0:T(8,128)(2,1)S(1)} %pad_maximum_fusion.1), channel_id=1, source_target_pairs={{0,4},{4,0},{8,12},{12,8},{16,20},{20,16},{24,28},{28,24},{1,5},{5... | collective-permute-start | bytes 884744 | tf_op jit(solution)/shard_map/ppermute | solution.py:407

commit v3 on v2

--- a/solution.py
+++ b/solution.py
@@ -136,8 +136,8 @@
 
 
 def prepare_kernel(n, cr, fine, left, right, moved_in, *refs):
-    blocks, (moved, act_t, strip, up) = refs[:n], refs[n:]
-    _, _, me = place()
+    blocks, (moved, act_t, strip, sums, mid, up) = refs[:n], refs[n:]
+    core, _, me = place()
     rows, width, ch = fine.shape
     cols = strip.shape[1]
     for s in range(n):
@@ -145,49 +145,93 @@
             strip[(me ^ s) * cr + j] = blocks[s][j * cols : (j + 1) * cols, :]
     idx = lax.broadcasted_iota(jnp.int32, (16, ch), 0)
 
-    def group(g, _):
-        up[...] = spread_up(strip[g], width)
-        for q in range(4):
-            r = g * 4 + q
-            for k, low, pick, side in ((0, 0, 0, left), (2, width - 16, 15, right)):
-                tile = moved[k, r + 1, low : low + 16, :].astype(F32)
-                tile = jnp.where(idx == pick, side[pl.ds(r, 1), :], tile)
-                moved[k, r + 1, low : low + 16, :] = tile.astype(BF)
-            hidden = fine[r].astype(F32) + up[...]
-            act = (hidden * sigmoid(hidden)).astype(BF)
-            act_t[:, pl.ds(pl.multiple_of(r * width, width), width)] = act.T
+    def patch(r, _):
+        for k, low, pick, side in ((0, 0, 0, left), (2, width - 16, 15, right)):
+            tile = moved[k, r + 1, low : low + 16, :].astype(F32)
+            tile = jnp.where(idx == pick, side[pl.ds(r, 1), :], tile)
+            moved[k, r + 1, low : low + 16, :] = tile.astype(BF)
         return 0
 
-    lax.fori_loop(0, rows // 4, group, 0)
-
-
-def weight_kernel(act_t, one, two, moved_in, keep, send, moved):
-    core, plane, z = place()
-    _, rows, width, ch = moved.shape
-    rows -= 2
-    planes, zs, depth, half = keep.shape
-    for slot, first in ((0, core == 1), (rows + 1, core == 0)):
-        halo = jnp.where(first, one[...].astype(F32), two[...].astype(F32))
-        spread(moved, slot, halo[:width].astype(BF), halo[width : width + 1], halo[width + 1 : width + 2])
+    lax.fori_loop(0, rows, patch, 0)
+    tall = rows // 4
+
+    def build(c):
+        for g in range(c * tall // 4, (c + 1) * tall // 4):
+            up[g] = spread_up(strip[g], width)
+            for r in range(4 * g, 4 * g + 4):
+                hidden = fine[r].astype(F32) + up[g]
+                act = (hidden * sigmoid(hidden)).astype(BF)
+                act_t[:, r * width : (r + 1) * width] = act.T
+
+    def share(c, first):
+        for k in range(5):
+            out = mid if k == 4 else sums.at[k]
+            got = partial_tap(1 - core, k, c * tall, tall, act_t, moved)
+            out[...] = got if first else out[...] + got
+
+    build(1)
+    build(2)
+    share(1, True)
+    build(0)
+    share(2, False)
+    build(3)
+
+
+def partial_tap(part, k, row, tall, act_t, moved):
+    _, _, width, ch = moved.shape
+    half = ch // 2
+    lhs = act_t[:, row * width : (row + tall) * width]
+    if isinstance(k, int) and k == 4:
+        lanes = pl.ds(pl.multiple_of(part * half, half), half)
+        window = moved[1, 1 + row : 1 + row + tall, :, lanes]
+    else:
+        t = part * 5 + k
+        window = moved[2 - lax.rem(t, 3), pl.ds(2 - t // 3 + row, tall)]
+    return jnp.dot(lhs, window.reshape(tall * width, -1), preferred_element_type=F32)
+
+
+def weight_taps(part, pieces, act_t, moved, out, sums=None, mid=None):
+    _, plane, z = place()
+    planes, zs, depth, half = out.shape
+    ch = 2 * half
     step = ch // (planes * zs)
     z = lax.rem(z, zs)
 
-    def tap(t, _):
-        i, j = t // 3, lax.rem(t, 3)
-        window = moved[2 - j, pl.ds(2 - i, rows)].reshape(rows * width, ch)
-        acc = jnp.dot(act_t[...], window, preferred_element_type=F32)
-        low, high = acc[:, :half], acc[:, half:]
-        mine = jnp.where(core == 0, low, high).astype(BF)
-        other = jnp.where(core == 0, high, low).astype(BF)
-        at = pl.multiple_of(t * step, step)
+    def put(unit, acc):
+        at = pl.multiple_of(unit * step, step)
         for p in range(planes):
             for c in range(zs):
                 b = (p * zs + c) * step
-                keep[p ^ plane, c ^ z, pl.ds(at, step), :] = mine[b : b + step]
-                send[p ^ plane, c ^ z, pl.ds(at, step), :] = other[b : b + step]
+                out[p ^ plane, c ^ z, pl.ds(at, step), :] = acc[b : b + step].astype(BF)
+
+    def total(k, start):
+        got = [partial_tap(part, k, row, tall, act_t, moved) for row, tall in pieces]
+        return functools.reduce(jnp.add, got if start is None else [start] + got)
+
+    def tap(k, _):
+        acc = total(k, None if sums is None else sums[k])
+        put(k, acc[:, :half])
+        put(k + 4, acc[:, half:])
         return 0
 
-    lax.fori_loop(0, 9, tap, 0)
+    lax.fori_loop(0, 4, tap, 0)
+    put(8, total(4, None if mid is None else mid[...]))
+
+
+def other_kernel(act_t, one, two, sums, mid, moved_in, out, moved):
+    core, _, _ = place()
+    _, rows, width, ch = moved.shape
+    for slot, first in ((0, core == 1), (rows - 1, core == 0)):
+        halo = jnp.where(first, one[...].astype(F32), two[...].astype(F32))
+        left, right = halo[width : width + 1], halo[width + 1 : width + 2]
+        spread(moved, slot, halo[:width].astype(BF), left, right)
+    tall = (rows - 2) // 4
+    weight_taps(1 - core, ((0, tall), (3 * tall, tall)), act_t, moved, out, sums, mid)
+
+
+def mine_kernel(act_t, moved, out):
+    core, _, _ = place()
+    weight_taps(core, ((0, moved.shape[1] - 2),), act_t, moved, out)
 
 
 def strip_order(n):
@@ -243,18 +287,23 @@
     z = lax.rem(me, zs)
     copies = []
     for k, (flip, s, first) in enumerate(spots):
-        lanes = pl.ds(pl.multiple_of((core ^ flip) * half, half), half)
+        part = core ^ flip
+        lanes = pl.ds(pl.multiple_of(part * half, half), half)
         for c in range(pieces[k].shape[0]):
             x = pieces[k][c].astype(F32) * norm
             for t in range(9):
                 scratch[k, c, t] = x[t * step : (t + 1) * step]
             b = pl.multiple_of((plane ^ s) * tall + ((first + c) ^ z) * step, step)
-            copies.append(
-                pltpu.make_async_copy(
-                    scratch.at[k, c], out.at[:, pl.ds(b, step), lanes], sems.at[k, c]
-                )
+            span = pl.ds(b, step)
+            taps = pl.ds(part * 5, 4)
+            pairs = (
+                (scratch.at[k, c, :4], out.at[taps, span, :half]),
+                (scratch.at[k, c, 4:8], out.at[taps, span, half:]),
+                (scratch.at[k, c, 8], out.at[4, span, lanes]),
             )
-            copies[-1].start()
+            for i, pair in enumerate(pairs):
+                copies.append(pltpu.make_async_copy(*pair, sems.at[k, c, i]))
+                copies[-1].start()
     if n:
         cr = coarse.shape[0]
         cols = coarse.shape[1] // n
@@ -302,7 +351,7 @@
             pltpu.SemaphoreType.DMA((3,)),
         ],
         compiler_params=params(START_MIB),
-        cost_estimate=cost(1 << 20, 4 << 20),
+        cost_estimate=cost(1 << 31, 4 << 20),
         name="start",
     )(cot, coarse)
     blocks = list(blocks)
@@ -330,19 +379,25 @@
         cost_estimate=cost(1 << 18, 1 << 19),
         name="edges",
     )(scale, moved, *[blocks[s] for s in shifts])
-    one = lax.ppermute(one, "row", xor_pairs(nrow, 1))
     odd = range(1, nrow - 1, 2)
     two = lax.ppermute(two, "row", [(i, i + 1) for i in odd] + [(i + 1, i) for i in odd])
+    one = lax.ppermute(one, "row", xor_pairs(nrow, 1))
 
     groups = rows // 4
-    moved, act_t, strip = pl.pallas_call(
+    moved, act_t, strip, sums, mid = pl.pallas_call(
         functools.partial(prepare_kernel, n, cr),
-        out_shape=[shape(*moved.shape), shape(ch, rows * width), shape(groups, cols, ch)],
+        out_shape=[
+            shape(*moved.shape),
+            shape(ch, rows * width),
+            shape(groups, cols, ch),
+            shape(4, ch, ch, dtype=F32),
+            shape(ch, ch // 2, dtype=F32),
+        ],
         in_specs=[vmem()] * (4 + n),
-        out_specs=[vmem()] * 3,
+        out_specs=[vmem()] * 5,
         input_output_aliases={3: 0},
-        scratch_shapes=[pltpu.VMEM((width, ch), F32)],
-        compiler_params=params(8),
+        scratch_shapes=[pltpu.VMEM((groups, width, ch), F32)],
+        compiler_params=params(12),
         cost_estimate=cost(1 << 32, 4 << 20),
         name="prepare",
     )(fine, left, right, moved, *blocks)
@@ -353,16 +408,25 @@
     depth = 9 * ch // (planes * zs)
     half = ch // 2
     part = shape(planes, zs, depth, half)
-    keep, send, moved = pl.pallas_call(
-        weight_kernel,
-        out_shape=[part, part, shape(*moved.shape)],
-        in_specs=[vmem()] * 4,
-        out_specs=[vmem()] * 3,
-        input_output_aliases={3: 2},
+    send, moved = pl.pallas_call(
+        other_kernel,
+        out_shape=[part, shape(*moved.shape)],
+        in_specs=[vmem()] * 6,
+        out_specs=[vmem()] * 2,
+        input_output_aliases={5: 1},
         compiler_params=params(8),
-        cost_estimate=cost(2 * 9 * rows * width * ch * ch, 8 << 20),
-        name="weight_grad",
-    )(act_t, one, two, moved)
+        cost_estimate=cost(9 * rows * width * ch * ch // 2, 8 << 20),
+        name="weight_other",
+    )(act_t, one, two, sums, mid, moved)
+    keep = pl.pallas_call(
+        mine_kernel,
+        out_shape=part,
+        in_specs=[vmem()] * 2,
+        out_specs=vmem(),
+        compiler_params=params(8),
+        cost_estimate=cost(9 * rows * width * ch * ch, 8 << 20),
+        name="weight_mine",
+    )(act_t, moved)
 
     done, pooled, made = [], [], 0
 
@@ -410,50 +474,53 @@
         return lax.ppermute(x, "row", xor_pairs(nrow, 2 * s))
 
     sizes = piece_sizes(rows // 4)
-    total = add(keep, *beside([core_swap(send)], sizes[0], send))
+    total = add(keep, core_swap(send))
     got = [plane_swap(total[s], s) for s in range(1, planes)]
-    total = add(total[0], *beside(got, sizes[1], total))
+    total = add(total[0], *beside(got, sizes[0], total))
     if not aligned:
         order = jnp.arange(halves) ^ (lax.axis_index("col") % halves)
         total = total.reshape(halves, depth // halves, half)[order]
     bit = halves // 2
     while bit:
         got = [col_swap(total[bit:], bit)]
-        total = add(total[:bit], *beside(got, sizes[2] if bit == 1 else 0, total))
+        total = add(total[:bit], *beside(got, sizes[1] if bit == 1 else 0, total))
         bit //= 2
-    total = add(total, *beside([col_swap(total, halves)], sizes[3], total))
+    total = add(total, *beside([col_swap(total, halves)], sizes[2], total))
 
     strips = {s: [(0, pooled_strip(s))] for s in range(n)}
 
     def hop(bit, extra):
         sent = [(s, src, x) for s in strips if s & bit for src, x in strips[s]]
-        got = col_swap(jnp.concatenate(extra + [x for _, _, x in sent]), bit)
-        at = sum(x.shape[0] for x in extra)
-        head = got[:at]
+        return sent, col_swap(jnp.concatenate(extra + [x for _, _, x in sent]), bit)
+
+    def land(bit, sent, got, at):
         for s, src, x in sent:
             strips.pop(s, None)
             strips[s ^ bit].append((src ^ bit, got[at : at + x.shape[0]]))
             at += x.shape[0]
-        return head
+
+    def ride(bit, total):
+        sent, got = hop(bit, [total.reshape(-1, half)])
+        at = total.size // half
+        land(bit, sent, got, at)
+        return got[:at].reshape(total.shape)
 
     bit = 1
     while bit < halves // 2:
-        head = hop(bit, [total.reshape(-1, half)])
-        total = jnp.concatenate([total, head.reshape(total.shape)])
+        total = jnp.concatenate([total, ride(bit, total)])
         bit *= 2
-    head = hop(bit, [total.reshape(-1, half)])
+    came = ride(bit, total)
     if aligned:
-        waves = [total, head.reshape(total.shape)]
+        waves = [total, came]
     else:
-        total = jnp.concatenate([total, head.reshape(total.shape)])
+        total = jnp.concatenate([total, came])
         waves = [total[order].reshape(1, depth, half)]
-    ways = list(range(planes - 1, 0, -1))
+    ways = list(range(1, planes))
     waves = [[x] + [plane_swap(x, s) for s in ways] for x in waves]
     if aligned:
         waves[0][1:], waves[1][0] = lax.optimization_barrier((waves[0][1:], waves[1][0]))
 
-    hop(bit * 2, [])
-    parts = [x for _, x in sorted(strips[0], key=lambda pair: pair[0])]
+    sent, hopped = hop(bit * 2, [])
     pixels = rows * nrow * width * n
 
     def finish(out, pieces, spots, parts=()):
@@ -467,7 +534,7 @@
             input_output_aliases={count + len(parts): 0} if out else {},
             scratch_shapes=[
                 pltpu.VMEM((count, tall, 9, depth // 9, half), F32),
-                pltpu.SemaphoreType.DMA((count, tall)),
+                pltpu.SemaphoreType.DMA((count, tall, 3)),
             ]
             + [x for c in coarse for x in (pltpu.VMEM(c.shape, BF), pltpu.SemaphoreType.DMA((1,)))],
             compiler_params=params(8),
@@ -482,12 +549,15 @@
         swapped = core_swap(jnp.stack(wave))
         other += [swapped[i] for i in range(len(wave))]
     out = finish([], mine, tuple((0, *spot) for spot in spots))
+    last, out = lax.optimization_barrier((hopped, out))
+    land(bit * 2, sent, last, 0)
+    parts = [x for _, x in sorted(strips[0], key=lambda pair: pair[0])]
     grad_weight, grad_coarse = finish(out, other, tuple((1, *spot) for spot in spots), parts)
     return (done[0][None], grad_coarse[None], grad_weight.reshape(3, 3, ch, ch))
 
 
 def piece_sizes(groups):
-    sizes = [groups // 8, groups * 5 // 8, groups // 8]
+    sizes = [groups * 3 // 4, groups // 8]
     return sizes + [groups - sum(sizes)]
 
 

time: 65.8 us -> 61.9 us (0.941)
  Pallas kernels: 24.1 us -> 22.8 us
  local copies, waits for them, and re-layouts: 1.65 us -> 0.45 us
  starting transfers between devices: 25 us -> 23.9 us
    ppermute x7, starting transfers between devices: 10.8 us -> 9.53 us  [col_swap(): return lax.ppermute(x, 'col', xor_pairs(n, s))]
    unnamed x11, local copies, waits for them, and re-layouts: 1.54 us -> 0.33 us
    ppermute x9, waiting for transfers between devices: 4.54 us -> 3.39 us  [plane_swap(): return lax.ppermute(x, 'row', xor_pairs(nrow, 2 * s))]
    pallas_call x4 -> x3, Pallas kernels: 9.95 us -> 8.93 us  [input_piece(): pl.pallas_call(functools.partial(input_kernel, made, size, n), out_shape=...]
    ppermute x7, waiting for transfers between devices: 8.27 us -> 9.28 us  [col_swap(): return lax.ppermute(x, 'col', xor_pairs(n, s))]
    pallas_call x1 -> x2, Pallas kernels: 6.56 us -> 5.92 us  [the longest x1 3.58 us: per_device(): pl.pallas_call(mine_kernel, out_shape=part, in_specs=[vmem()] * 2, out_sp...]
  transfers between devices with their start and end apart: 21 -> 21, of which waited for: 10 -> 10; matrix products, arithmetic and copies ran while one was open for 0% -> 0% of each run, Pallas kernels for 23% -> 28%
where the time goes in v3:
time: 61.9 us; the launch traced here: 61.7 us
  starting transfers between devices  23.9 us (39%)
  Pallas kernels  22.8 us (37%)
  waiting for transfers between devices  12.7 us (21%)
  between operations  1.6 us (3%)
    ppermute x9, starting transfers between devices, plane_swap(): return lax.ppermute(x, 'row', xor_pairs(nrow, 2 * s))  10.8 us
    ppermute x7, starting transfers between devices, col_swap(): return lax.ppermute(x, 'col', xor_pairs(n, s))  9.53 us
    ppermute x7, waiting for transfers between devices, col_swap(): return lax.ppermute(x, 'col', xor_pairs(n, s))  9.28 us
    pallas_call x3, Pallas kernels, input_piece(): pl.pallas_call(functools.partial(input_kernel, made, size, n), out_shape=...  8.93 us
    pallas_call x1, Pallas kernels, per_device(): pl.pallas_call(mine_kernel, out_shape=part, in_specs=[vmem()] * 2, out_sp...  3.58 us
    ppermute x9, waiting for transfers between devices, plane_swap(): return lax.ppermute(x, 'row', xor_pairs(nrow, 2 * s))  3.39 us
    pallas_call x1, Pallas kernels, per_device(): pl.pallas_call(functools.partial(prepare_kernel, n, cr), out_shape=[shape...  2.7 us
    ppermute x3, starting transfers between devices, core_swap(): return lax.ppermute(x, 'row', xor_pairs(nrow, 1))  2.62 us
  transfers between devices with their start and end apart: 21, of which 10 were waited for; matrix products, arithmetic and copies ran while one was open for 0% of the time, Pallas kernels for 28%

profile of v3, /device:TPU:0, one launch (start us, length us, event | category | flops | bytes accessed | tf_op | source)
XLA Modules:
  0.0 61.7 jit_solution(17204542649093714371)
XLA Ops:
  0.7 1.6 %start.1 = (bf16[64,256]{1,0:T(8,128)(2,1)S(1)}, bf16[96,256]{1,0:T(8,128)(2,1)S(1)}, bf16[64,256]{1,0:T(8,128)(2,1)S(1)}, bf16[96,256]{1,0:T(8,128)(2,1)S(1)}) custom-call(bf16[32,128,256]{2,1,0:T(8,128)(2,1)} %bitcast.61, bf16[2,128,256]{2,1,0:T(8,128)(2,1)} %bitcast.81), custom_call_target="tpu_custom_call" | custom-call | flops 2147483648 | bytes 4194304 | tf_op jit(solution)/shard_map/start/pallas_call | solution.py:342
  2.2 3.1 %collective-permute-start = (bf16[96,256]{1,0:T(8,128)(2,1)S(1)}, bf16[96,256]{1,0:T(8,128)(2,1)S(1)}, u32[]{:S(2)}, u32[]{:S(2)}) collective-permute-start(bf16[96,256]{1,0:T(8,128)(2,1)S(1)} %get-tuple-element.50), channel_id=1, source_target_pairs={{0,1},{1,0},{2,3},{3,2},{4,5},{5,4},{6,7},{7,6},{8,9},{9,8},{10,11... | collective-permute-start | bytes 147464 | tf_op jit(solution)/shard_map/ppermute | solution.py:340
  5.3 2.5 %collective-permute-start.1 = (bf16[96,256]{1,0:T(8,128)(2,1)S(1)}, bf16[96,256]{1,0:T(8,128)(2,1)S(1)}, u32[]{:S(2)}, u32[]{:S(2)}) collective-permute-start(bf16[96,256]{1,0:T(8,128)(2,1)S(1)} %get-tuple-element.51), channel_id=1, source_target_pairs={{0,3},{1,2},{2,1},{3,0},{4,7},{5,6},{6,5},{7,4},{8,11},{9,10},{10,... | collective-permute-start | bytes 147464 | tf_op jit(solution)/shard_map/ppermute | solution.py:340
  7.8 0.1 collective-permute-start.2
  8.6 1.1 %load.1 = (bf16[3,34,128,256]{3,2,1,0:T(8,128)(2,1)S(1)}, f32[1,256]{1,0:T(1,128)S(1)}) custom-call(s32[1]{0:T(128)S(6)} %copy.23.steps, bf16[32,128,256]{2,1,0:T(8,128)(2,1)S(1)} %bitcast.62, f32[1000,256]{1,0:T(8,128)S(1)} %copy-done.3), custom_call_target="tpu_custom_call" | custom-call | flops 1048576 | bytes 4194304 | tf_op jit(solution)/shard_map/load/pallas_call | solution.py:358
  9.7 0.0 collective-permute-done.refs_0_.refs_1_
  9.7 2.0 %collective-permute-done.1.refs_1_.refs_3_ = bf16[96,256]{1,0:T(8,128)(2,1)S(1)} collective-permute-done((bf16[96,256]{1,0:T(8,128)(2,1)S(1)}, bf16[96,256]{1,0:T(8,128)(2,1)S(1)}, u32[]{:S(2)}, u32[]{:S(2)}) %collective-permute-start.1) | collective-permute-done | bytes 49184 | tf_op jit(solution)/shard_map/ppermute | solution.py:340
  11.7 0.1 edges.1
  11.7 0.1 collective-permute-start.3
  11.8 0.8 %collective-permute-start.4 = (bf16[144,256]{1,0:T(8,128)(2,1)S(1)}, bf16[144,256]{1,0:T(8,128)(2,1)S(1)}, u32[]{:S(2)}, u32[]{:S(2)}) collective-permute-start(bf16[144,256]{1,0:T(8,128)(2,1)S(1)} %get-tuple-element.58), channel_id=1, source_target_pairs={{4,8},{12,16},{20,24},{8,4},{16,12},{24,20},{5,9},{13,17},{21,25},... | collective-permute-start | bytes 221192 | tf_op jit(solution)/shard_map/ppermute | solution.py:383
  12.6 0.4 collective-permute-done.2.refs_2_
  13.0 0.3 copy-done
  13.2 2.7 %prepare.1 = (bf16[3,34,128,256]{3,2,1,0:T(8,128)(2,1)S(1)}, bf16[256,4096]{1,0:T(8,128)(2,1)S(1)}, bf16[8,32,256]{2,1,0:T(8,128)(2,1)S(1)}, f32[4,256,256]{2,1,0:T(8,128)S(1)}, f32[256,128]{1,0:T(8,128)S(1)}) custom-call(bf16[32,128,256]{2,1,0:T(8,128)(2,1)S(1)} %bitcast.54, f32[32,256]{1,0:T(8,128)S(1)} %get-tuple-element.52.left, ...), custom_call_target="tpu_custom_call", output_to_operand_aliasing={{0}: (3, {})} | custom-call | flops 4294967296 | bytes 4194304 | tf_op jit(solution)/shard_map/prepare/pallas_call | solution.py:387
  15.9 0.0 collective-permute-done.3.one
  16.0 2.3 %weight_other.1 = (bf16[4,2,288,128]{3,2,1,0:T(8,128)(2,1)S(1)}, bf16[3,34,128,256]{3,2,1,0:T(8,128)(2,1)S(1)}) custom-call(bf16[256,4096]{1,0:T(8,128)(2,1)S(1)} %get-tuple-element.56.act_t, bf16[144,256]{1,0:T(8,128)(2,1)S(1)} %collective-permute-done.3.one, bf16[144,256]{1,0:T(8,128)(2,1)S(1)} %collective-permute-done.4.two, ...), custom_call_target="tpu_custom_call", output_to_operand_aliasing={{1}: (5, {})} | custom-call | flops 1207959552 | bytes 8388608 | tf_op jit(solution)/shard_map/weight_other/pallas_call | solution.py:411
  18.3 2.5 %collective-permute-start.5 = (bf16[4,2,288,128]{3,2,1,0:T(8,128)(2,1)S(1)}, bf16[4,2,288,128]{3,2,1,0:T(8,128)(2,1)S(1)}, u32[]{:S(2)}, u32[]{:S(2)}) collective-permute-start(bf16[4,2,288,128]{3,2,1,0:T(8,128)(2,1)S(1)} %get-tuple-element.63), channel_id=1, source_target_pairs={{0,4},{4,0},{8,12},{12,8},{16,20},{20,16},{24,28},{28,24},{1,5},{5... | collective-permute-start | bytes 1769480 | tf_op jit(solution)/shard_map/ppermute | solution.py:471
  20.8 3.6 %weight_mine.1 = bf16[4,2,288,128]{3,2,1,0:T(8,128)(2,1)S(1)} custom-call(bf16[256,4096]{1,0:T(8,128)(2,1)S(1)} %get-tuple-element.56.act_t, bf16[3,34,128,256]{3,2,1,0:T(8,128)(2,1)S(1)} %get-tuple-element.62.moved), custom_call_target="tpu_custom_call" | custom-call | flops 2415919104 | bytes 8388608 | tf_op jit(solution)/shard_map/weight_mine/pallas_call | solution.py:421
  24.4 0.0 copy-start.1
  24.4 0.0 collective-permute-done.5
  24.4 0.2 add_convert_fusion.after
  24.6 2.2 %collective-permute-start.8 = (bf16[2,288,128]{2,1,0:T(8,128)(2,1)S(1)}, bf16[2,288,128]{2,1,0:T(8,128)(2,1)S(1)}, u32[]{:S(2)}, u32[]{:S(2)}) collective-permute-start(bf16[2,288,128]{2,1,0:T(8,128)(2,1)S(1)} %get-tuple-element.95), channel_id=1, source_target_pairs={{0,24},{4,28},{8,16},{12,20},{16,8},{20,12},{24,0},{28,4},{1,25},{... | collective-permute-start | bytes 442376 | tf_op jit(solution)/shard_map/ppermute | solution.py:474
  26.8 1.6 %collective-permute-start.7 = (bf16[2,288,128]{2,1,0:T(8,128)(2,1)S(1)}, bf16[2,288,128]{2,1,0:T(8,128)(2,1)S(1)}, u32[]{:S(2)}, u32[]{:S(2)}) collective-permute-start(bf16[2,288,128]{2,1,0:T(8,128)(2,1)S(1)} %get-tuple-element.96), channel_id=1, source_target_pairs={{0,16},{4,20},{8,24},{12,28},{16,0},{20,4},{24,8},{28,12},{1,17},{... | collective-permute-start | bytes 442376 | tf_op jit(solution)/shard_map/ppermute | solution.py:474
  28.4 5.5 %input_grad.3 = (bf16[32,128,256]{2,1,0:T(8,128)(2,1)}, bf16[6,2,32,128]{3,2,1,0:T(8,128)(2,1)S(1)}) custom-call(bf16[4,2,288,128]{3,2,1,0:T(8,128)(2,1)S(1)} %add_convert_fusion.after, bf16[3,34,128,256]{3,2,1,0:T(8,128)(2,1)S(1)} %get-tuple-element.62.moved, bf16[32,128,256]{2,1,0:T(8,128)(2,1)S(1)} %bitcast.55, ...), custom_call_target="tpu_custom_call" | custom-call | flops 3623878656 | bytes 4194304 | tf_op jit(solution)/shard_map/input_grad/pallas_call | solution.py:435
  33.9 0.6 %collective-permute-done.7 = bf16[2,288,128]{2,1,0:T(8,128)(2,1)S(1)} collective-permute-done((bf16[2,288,128]{2,1,0:T(8,128)(2,1)S(1)}, bf16[2,288,128]{2,1,0:T(8,128)(2,1)S(1)}, u32[]{:S(2)}, u32[]{:S(2)}) %collective-permute-start.7) | collective-permute-done | bytes 147488 | tf_op jit(solution)/shard_map/ppermute | solution.py:474
  34.5 1.0 %collective-permute-done.6 = bf16[2,288,128]{2,1,0:T(8,128)(2,1)S(1)} collective-permute-done((bf16[2,288,128]{2,1,0:T(8,128)(2,1)S(1)}, bf16[2,288,128]{2,1,0:T(8,128)(2,1)S(1)}, u32[]{:S(2)}, u32[]{:S(2)}) %collective-permute-start.6) | collective-permute-done | bytes 147488 | tf_op jit(solution)/shard_map/ppermute | solution.py:474
  35.6 0.1 fusion.2.after
  35.7 0.1 collective-permute-start.9
  35.7 1.7 %input_grad.4 = (bf16[32,128,256]{2,1,0:T(8,128)(2,1)}, bf16[1,2,32,128]{3,2,1,0:T(8,128)(2,1)S(1)}) custom-call(bf16[2,288,128]{2,1,0:T(8,128)(2,1)S(1)} %fusion.2.after, bf16[3,34,128,256]{3,2,1,0:T(8,128)(2,1)S(1)} %get-tuple-element.62.moved, bf16[32,128,256]{2,1,0:T(8,128)(2,1)S(1)} %bitcast.56, ...), custom_call_target="tpu_custom_call", output_to_operand_aliasing={{0}: (5, {})} | custom-call | flops 603979776 | bytes 4194304 | tf_op jit(solution)/shard_map/input_grad/pallas_call | solution.py:435
  37.5 2.6 %collective-permute-done.9 = bf16[1,288,128]{2,1,0:T(8,128)(2,1)S(1)} collective-permute-done((bf16[1,288,128]{2,1,0:T(8,128)(2,1)S(1)}, bf16[1,288,128]{2,1,0:T(8,128)(2,1)S(1)}, u32[]{:S(2)}, u32[]{:S(2)}) %collective-permute-start.9) | collective-permute-done | bytes 73760 | tf_op jit(solution)/shard_map/ppermute | solution.py:340
  40.1 1.9 %collective-permute-start.10 = (bf16[1,288,128]{2,1,0:T(8,128)(2,1)S(1)}, bf16[1,288,128]{2,1,0:T(8,128)(2,1)S(1)}, u32[]{:S(2)}, u32[]{:S(2)}) collective-permute-start(bf16[1,288,128]{2,1,0:T(8,128)(2,1)S(1)} %add_convert_fusion.2.after), channel_id=1, source_target_pairs={{0,2},{1,3},{2,0},{3,1},{4,6},{5,7},{6,4},{7,5},{8,10},{9,11},{10,... | collective-permute-start | bytes 221192 | tf_op jit(solution)/shard_map/ppermute | solution.py:340
  42.0 1.7 %input_grad.5 = (bf16[32,128,256]{2,1,0:T(8,128)(2,1)}, bf16[1,2,32,128]{3,2,1,0:T(8,128)(2,1)S(1)}) custom-call(bf16[1,288,128]{2,1,0:T(8,128)(2,1)S(1)} %add_convert_fusion.2.after, bf16[3,34,128,256]{3,2,1,0:T(8,128)(2,1)S(1)} %get-tuple-element.62.moved, bf16[32,128,256]{2,1,0:T(8,128)(2,1)S(1)} %bitcast.57, ...), custom_call_target="tpu_custom_call", output_to_operand_aliasing={{0}: (5, {})} | custom-call | flops 603979776 | bytes 4194304 | tf_op jit(solution)/shard_map/input_grad/pallas_call | solution.py:435
  43.7 1.9 %collective-permute-done.10 = bf16[1,288,128]{2,1,0:T(8,128)(2,1)S(1)} collective-permute-done((bf16[1,288,128]{2,1,0:T(8,128)(2,1)S(1)}, bf16[1,288,128]{2,1,0:T(8,128)(2,1)S(1)}, u32[]{:S(2)}, u32[]{:S(2)}) %collective-permute-start.10) | collective-permute-done | bytes 73760 | tf_op jit(solution)/shard_map/ppermute | solution.py:340
  45.8 0.1 collective-permute-start.14
  45.8 1.6 %collective-permute-start.13 = (bf16[1,288,128]{2,1,0:T(8,128)(2,1)S(1)}, bf16[1,288,128]{2,1,0:T(8,128)(2,1)S(1)}, u32[]{:S(2)}, u32[]{:S(2)}) collective-permute-start(bf16[1,288,128]{2,1,0:T(8,128)(2,1)S(1)} %get-tuple-element.94.refs_0_), channel_id=1, source_target_pairs={{0,24},{4,28},{8,16},{12,20},{16,8},{20,12},{24,0},{28,4},{1,25},{... | collective-permute-start | bytes 221192 | tf_op jit(solution)/shard_map/ppermute | solution.py:474
  47.4 1.3 %collective-permute-start.12 = (bf16[1,288,128]{2,1,0:T(8,128)(2,1)S(1)}, bf16[1,288,128]{2,1,0:T(8,128)(2,1)S(1)}, u32[]{:S(2)}, u32[]{:S(2)}) collective-permute-start(bf16[1,288,128]{2,1,0:T(8,128)(2,1)S(1)} %get-tuple-element.94.refs_0_), channel_id=1, source_target_pairs={{0,16},{4,20},{8,24},{12,28},{16,0},{20,4},{24,8},{28,12},{1,17},{... | collective-permute-start | bytes 221192 | tf_op jit(solution)/shard_map/ppermute | solution.py:474
  48.7 0.7 %collective-permute-start.11 = (bf16[1,288,128]{2,1,0:T(8,128)(2,1)S(1)}, bf16[1,288,128]{2,1,0:T(8,128)(2,1)S(1)}, u32[]{:S(2)}, u32[]{:S(2)}) collective-permute-start(bf16[1,288,128]{2,1,0:T(8,128)(2,1)S(1)} %get-tuple-element.94.refs_0_), channel_id=1, source_target_pairs={{0,8},{4,12},{8,0},{12,4},{16,24},{20,28},{24,16},{28,20},{1,9},{5... | collective-permute-start | bytes 221192 | tf_op jit(solution)/shard_map/ppermute | solution.py:474
  49.4 1.5 %collective-permute-done.14 = bf16[544,128]{1,0:T(8,128)(2,1)S(1)} collective-permute-done((bf16[544,128]{1,0:T(8,128)(2,1)S(1)}, bf16[544,128]{1,0:T(8,128)(2,1)S(1)}, u32[]{:S(2)}, u32[]{:S(2)}) %collective-permute-start.14) | collective-permute-done | bytes 139296 | tf_op jit(solution)/shard_map/ppermute | solution.py:340
  50.9 1.5 %collective-permute-start.18 = (bf16[1,288,128]{2,1,0:T(8,128)(2,1)S(1)}, bf16[1,288,128]{2,1,0:T(8,128)(2,1)S(1)}, u32[]{:S(2)}, u32[]{:S(2)}) collective-permute-start(bf16[1,288,128]{2,1,0:T(8,128)(2,1)S(1)} %slice_bitcast_fusion.12.refs_4_), channel_id=1, source_target_pairs={{0,24},{4,28},{8,16},{12,20},{16,8},{20,12},{24,0},{28,4},{1,25},{... | collective-permute-start | bytes 221192 | tf_op jit(solution)/shard_map/ppermute | solution.py:474
  52.4 1.3 %collective-permute-start.17 = (bf16[1,288,128]{2,1,0:T(8,128)(2,1)S(1)}, bf16[1,288,128]{2,1,0:T(8,128)(2,1)S(1)}, u32[]{:S(2)}, u32[]{:S(2)}) collective-permute-start(bf16[1,288,128]{2,1,0:T(8,128)(2,1)S(1)} %slice_bitcast_fusion.12.refs_4_), channel_id=1, source_target_pairs={{0,16},{4,20},{8,24},{12,28},{16,0},{20,4},{24,8},{28,12},{1,17},{... | collective-permute-start | bytes 221192 | tf_op jit(solution)/shard_map/ppermute | solution.py:474
  53.7 0.7 %collective-permute-start.16 = (bf16[1,288,128]{2,1,0:T(8,128)(2,1)S(1)}, bf16[1,288,128]{2,1,0:T(8,128)(2,1)S(1)}, u32[]{:S(2)}, u32[]{:S(2)}) collective-permute-start(bf16[1,288,128]{2,1,0:T(8,128)(2,1)S(1)} %slice_bitcast_fusion.12.refs_4_), channel_id=1, source_target_pairs={{0,8},{4,12},{8,0},{12,4},{16,24},{20,28},{24,16},{28,20},{1,9},{5... | collective-permute-start | bytes 221192 | tf_op jit(solution)/shard_map/ppermute | solution.py:474
  54.4 1.8 %collective-permute-start.20 = (bf16[256,128]{1,0:T(8,128)(2,1)S(1)}, bf16[256,128]{1,0:T(8,128)(2,1)S(1)}, u32[]{:S(2)}, u32[]{:S(2)}) collective-permute-start(bf16[256,128]{1,0:T(8,128)(2,1)S(1)} %pad_maximum_fusion.2), channel_id=1, source_target_pairs={{0,2},{1,3},{2,0},{3,1},{4,6},{5,7},{6,4},{7,5},{8,10},{9,11},{10,... | collective-permute-start | bytes 196616 | tf_op jit(solution)/shard_map/ppermute | solution.py:340
  56.3 0.1 collective-permute-start.15
  56.4 0.6 collective-permute-done.17.refs_6_
  56.9 1.1 %collective-permute-done.16.refs_5_ = bf16[1,288,128]{2,1,0:T(8,128)(2,1)S(1)} collective-permute-done((bf16[1,288,128]{2,1,0:T(8,128)(2,1)S(1)}, bf16[1,288,128]{2,1,0:T(8,128)(2,1)S(1)}, u32[]{:S(2)}, u32[]{:S(2)}) %collective-permute-start.16) | collective-permute-done | bytes 73760 | tf_op jit(solution)/shard_map/ppermute | solution.py:474
  58.1 0.1 collective-permute-start.19
  58.2 1.2 %finish.2.refs_12_ = f32[9,256,256]{2,1,0:T(8,128)} custom-call(bf16[1,288,128]{2,1,0:T(8,128)(2,1)S(1)} %get-tuple-element.94.refs_0_, bf16[1,288,128]{2,1,0:T(8,128)(2,1)S(1)} %collective-permute-done.11.refs_1_, bf16[1,288,128]{2,1,0:T(8,128)(2,1)S(1)} %collective-permute-done.12.refs_2_, bf16[1,288,128]{2,1,0:T(8,128)(2,1)S(1)} %collective-permute-done.13.refs_3_, ...), custom_call_target="tpu_custom_call" | custom-call | flops 1048576 | bytes 4194304 | tf_op jit(solution)/shard_map/finish/pallas_call | solution.py:529
  59.4 0.9 %collective-permute-done.20 = bf16[256,128]{1,0:T(8,128)(2,1)S(1)} collective-permute-done((bf16[256,128]{1,0:T(8,128)(2,1)S(1)}, bf16[256,128]{1,0:T(8,128)(2,1)S(1)}, u32[]{:S(2)}, u32[]{:S(2)}) %collective-permute-start.20) | collective-permute-done | bytes 65568 | tf_op jit(solution)/shard_map/ppermute | solution.py:340
  60.4 1.3 %finish.3 = (f32[9,256,256]{2,1,0:T(8,128)}, bf16[2,128,256]{2,1,0:T(8,128)(2,1)}) custom-call(bf16[1,288,128]{2,1,0:T(8,128)(2,1)S(1)} %get-tuple-element.105.refs_0_, bf16[1,288,128]{2,1,0:T(8,128)(2,1)S(1)} %get-tuple-element.104.refs_1_, bf16[1,288,128]{2,1,0:T(8,128)(2,1)S(1)} %get-tuple-element.103.refs_2_, ...), custom_call_target="tpu_custom_call", output_to_operand_aliasing={{0}: (12, {})} | custom-call | flops 1048576 | bytes 4194304 | tf_op jit(solution)/shard_map/finish/pallas_call | solution.py:529
  (33 shorter events, 0.3 us)
Async XLA Ops:
  0.6 7.9 %copy-start.2 = (bf16[1,32,128,256]{3,2,1,0:T(8,128)(2,1)S(1)}, bf16[1,32,128,256]{3,2,1,0:T(8,128)(2,1)}, u32[]{:S(2)}) copy-start(bf16[1,32,128,256]{3,2,1,0:T(8,128)(2,1)} %param.11) | copy-start | bytes 6291460
  0.6 7.9 %copy-start.3 = (f32[1000,256]{1,0:T(8,128)S(1)}, f32[1000,256]{1,0:T(8,128)}, u32[]{:S(2)}) copy-start(f32[1000,256]{1,0:T(8,128)} %scales.1) | copy-start | bytes 3072004
  2.2 7.4 %collective-permute-start = (bf16[96,256]{1,0:T(8,128)(2,1)S(1)}, bf16[96,256]{1,0:T(8,128)(2,1)S(1)}, u32[]{:S(2)}, u32[]{:S(2)}) collective-permute-start(bf16[96,256]{1,0:T(8,128)(2,1)S(1)} %get-tuple-element.50), channel_id=1, source_target_pairs={{0,1},{1,0},{2,3},{3,2},{4,5},{5,4},{6,7},{7,6},{8,9},{9,8},{10,11... | collective-permute-start | bytes 147464 | tf_op jit(solution)/shard_map/ppermute | solution.py:340
  5.3 6.3 %collective-permute-start.1 = (bf16[96,256]{1,0:T(8,128)(2,1)S(1)}, bf16[96,256]{1,0:T(8,128)(2,1)S(1)}, u32[]{:S(2)}, u32[]{:S(2)}) collective-permute-start(bf16[96,256]{1,0:T(8,128)(2,1)S(1)} %get-tuple-element.51), channel_id=1, source_target_pairs={{0,3},{1,2},{2,1},{3,0},{4,7},{5,6},{6,5},{7,4},{8,11},{9,10},{10,... | collective-permute-start | bytes 147464 | tf_op jit(solution)/shard_map/ppermute | solution.py:340
  7.8 5.2 %collective-permute-start.2 = (bf16[64,256]{1,0:T(8,128)(2,1)S(1)}, bf16[64,256]{1,0:T(8,128)(2,1)S(1)}, u32[]{:S(2)}, u32[]{:S(2)}) collective-permute-start(bf16[64,256]{1,0:T(8,128)(2,1)S(1)} %get-tuple-element.55), channel_id=1, source_target_pairs={{0,2},{1,3},{2,0},{3,1},{4,6},{5,7},{6,4},{7,5},{8,10},{9,11},{10,... | collective-permute-start | bytes 98312 | tf_op jit(solution)/shard_map/ppermute | solution.py:340
  11.7 1.6 %copy-start = (bf16[1,32,128,256]{3,2,1,0:T(8,128)(2,1)S(1)}, bf16[1,32,128,256]{3,2,1,0:T(8,128)(2,1)}, u32[]{:S(2)}) copy-start(bf16[1,32,128,256]{3,2,1,0:T(8,128)(2,1)} %param.6) | copy-start | bytes 6291460
  11.7 4.2 %collective-permute-start.3 = (bf16[144,256]{1,0:T(8,128)(2,1)S(1)}, bf16[144,256]{1,0:T(8,128)(2,1)S(1)}, u32[]{:S(2)}, u32[]{:S(2)}) collective-permute-start(bf16[144,256]{1,0:T(8,128)(2,1)S(1)} %get-tuple-element.57), channel_id=1, source_target_pairs={{0,4},{4,0},{8,12},{12,8},{16,20},{20,16},{24,28},{28,24},{1,5},{5... | collective-permute-start | bytes 221192 | tf_op jit(solution)/shard_map/ppermute | solution.py:384
  11.8 4.2 %collective-permute-start.4 = (bf16[144,256]{1,0:T(8,128)(2,1)S(1)}, bf16[144,256]{1,0:T(8,128)(2,1)S(1)}, u32[]{:S(2)}, u32[]{:S(2)}) collective-permute-start(bf16[144,256]{1,0:T(8,128)(2,1)S(1)} %get-tuple-element.58), channel_id=1, source_target_pairs={{4,8},{12,16},{20,24},{8,4},{16,12},{24,20},{5,9},{13,17},{21,25},... | collective-permute-start | bytes 221192 | tf_op jit(solution)/shard_map/ppermute | solution.py:383
  18.3 6.1 %collective-permute-start.5 = (bf16[4,2,288,128]{3,2,1,0:T(8,128)(2,1)S(1)}, bf16[4,2,288,128]{3,2,1,0:T(8,128)(2,1)S(1)}, u32[]{:S(2)}, u32[]{:S(2)}) collective-permute-start(bf16[4,2,288,128]{3,2,1,0:T(8,128)(2,1)S(1)} %get-tuple-element.63), channel_id=1, source_target_pairs={{0,4},{4,0},{8,12},{12,8},{16,20},{20,16},{24,28},{28,24},{1,5},{5... | collective-permute-start | bytes 1769480 | tf_op jit(solution)/shard_map/ppermute | solution.py:471
  24.4 4.0 %copy-start.1 = (bf16[3,3,256,256]{3,2,1,0:T(8,128)(2,1)S(1)}, bf16[3,3,256,256]{3,2,1,0:T(8,128)(2,1)}, u32[]{:S(2)}) copy-start(bf16[3,3,256,256]{3,2,1,0:T(8,128)(2,1)} %param.8) | copy-start | bytes 3538948
  24.6 9.3 %collective-permute-start.8 = (bf16[2,288,128]{2,1,0:T(8,128)(2,1)S(1)}, bf16[2,288,128]{2,1,0:T(8,128)(2,1)S(1)}, u32[]{:S(2)}, u32[]{:S(2)}) collective-permute-start(bf16[2,288,128]{2,1,0:T(8,128)(2,1)S(1)} %get-tuple-element.95), channel_id=1, source_target_pairs={{0,24},{4,28},{8,16},{12,20},{16,8},{20,12},{24,0},{28,4},{1,25},{... | collective-permute-start | bytes 442376 | tf_op jit(solution)/shard_map/ppermute | solution.py:474
  26.8 7.8 %collective-permute-start.7 = (bf16[2,288,128]{2,1,0:T(8,128)(2,1)S(1)}, bf16[2,288,128]{2,1,0:T(8,128)(2,1)S(1)}, u32[]{:S(2)}, u32[]{:S(2)}) collective-permute-start(bf16[2,288,128]{2,1,0:T(8,128)(2,1)S(1)} %get-tuple-element.96), channel_id=1, source_target_pairs={{0,16},{4,20},{8,24},{12,28},{16,0},{20,4},{24,8},{28,12},{1,17},{... | collective-permute-start | bytes 442376 | tf_op jit(solution)/shard_map/ppermute | solution.py:474
  28.4 7.2 %collective-permute-start.6 = (bf16[2,288,128]{2,1,0:T(8,128)(2,1)S(1)}, bf16[2,288,128]{2,1,0:T(8,128)(2,1)S(1)}, u32[]{:S(2)}, u32[]{:S(2)}) collective-permute-start(bf16[2,288,128]{2,1,0:T(8,128)(2,1)S(1)} %get-tuple-element.97), channel_id=1, source_target_pairs={{0,8},{4,12},{8,0},{12,4},{16,24},{20,28},{24,16},{28,20},{1,9},{5... | collective-permute-start | bytes 442376 | tf_op jit(solution)/shard_map/ppermute | solution.py:474
  35.7 4.4 %collective-permute-start.9 = (bf16[1,288,128]{2,1,0:T(8,128)(2,1)S(1)}, bf16[1,288,128]{2,1,0:T(8,128)(2,1)S(1)}, u32[]{:S(2)}, u32[]{:S(2)}) collective-permute-start(bf16[1,288,128]{2,1,0:T(8,128)(2,1)S(1)} %slice.105), channel_id=1, source_target_pairs={{0,1},{1,0},{2,3},{3,2},{4,5},{5,4},{6,7},{7,6},{8,9},{9,8},{10,11... | collective-permute-start | bytes 221192 | tf_op jit(solution)/shard_map/ppermute | solution.py:340
  40.1 5.5 %collective-permute-start.10 = (bf16[1,288,128]{2,1,0:T(8,128)(2,1)S(1)}, bf16[1,288,128]{2,1,0:T(8,128)(2,1)S(1)}, u32[]{:S(2)}, u32[]{:S(2)}) collective-permute-start(bf16[1,288,128]{2,1,0:T(8,128)(2,1)S(1)} %add_convert_fusion.2.after), channel_id=1, source_target_pairs={{0,2},{1,3},{2,0},{3,1},{4,6},{5,7},{6,4},{7,5},{8,10},{9,11},{10,... | collective-permute-start | bytes 221192 | tf_op jit(solution)/shard_map/ppermute | solution.py:340
  45.8 5.1 %collective-permute-start.14 = (bf16[544,128]{1,0:T(8,128)(2,1)S(1)}, bf16[544,128]{1,0:T(8,128)(2,1)S(1)}, u32[]{:S(2)}, u32[]{:S(2)}) collective-permute-start(bf16[544,128]{1,0:T(8,128)(2,1)S(1)} %constant_dynamic-update-slice_fusion), channel_id=1, source_target_pairs={{0,1},{1,0},{2,3},{3,2},{4,5},{5,4},{6,7},{7,6},{8,9},{9,8},{10,11... | collective-permute-start | bytes 417800 | tf_op jit(solution)/shard_map/ppermute | solution.py:340
  45.8 7.9 %collective-permute-start.13 = (bf16[1,288,128]{2,1,0:T(8,128)(2,1)S(1)}, bf16[1,288,128]{2,1,0:T(8,128)(2,1)S(1)}, u32[]{:S(2)}, u32[]{:S(2)}) collective-permute-start(bf16[1,288,128]{2,1,0:T(8,128)(2,1)S(1)} %get-tuple-element.94.refs_0_), channel_id=1, source_target_pairs={{0,24},{4,28},{8,16},{12,20},{16,8},{20,12},{24,0},{28,4},{1,25},{... | collective-permute-start | bytes 221192 | tf_op jit(solution)/shard_map/ppermute | solution.py:474
  47.4 7.0 %collective-permute-start.12 = (bf16[1,288,128]{2,1,0:T(8,128)(2,1)S(1)}, bf16[1,288,128]{2,1,0:T(8,128)(2,1)S(1)}, u32[]{:S(2)}, u32[]{:S(2)}) collective-permute-start(bf16[1,288,128]{2,1,0:T(8,128)(2,1)S(1)} %get-tuple-element.94.refs_0_), channel_id=1, source_target_pairs={{0,16},{4,20},{8,24},{12,28},{16,0},{20,4},{24,8},{28,12},{1,17},{... | collective-permute-start | bytes 221192 | tf_op jit(solution)/shard_map/ppermute | solution.py:474
  48.7 5.7 %collective-permute-start.11 = (bf16[1,288,128]{2,1,0:T(8,128)(2,1)S(1)}, bf16[1,288,128]{2,1,0:T(8,128)(2,1)S(1)}, u32[]{:S(2)}, u32[]{:S(2)}) collective-permute-start(bf16[1,288,128]{2,1,0:T(8,128)(2,1)S(1)} %get-tuple-element.94.refs_0_), channel_id=1, source_target_pairs={{0,8},{4,12},{8,0},{12,4},{16,24},{20,28},{24,16},{28,20},{1,9},{5... | collective-permute-start | bytes 221192 | tf_op jit(solution)/shard_map/ppermute | solution.py:474
  50.9 5.5 %collective-permute-start.18 = (bf16[1,288,128]{2,1,0:T(8,128)(2,1)S(1)}, bf16[1,288,128]{2,1,0:T(8,128)(2,1)S(1)}, u32[]{:S(2)}, u32[]{:S(2)}) collective-permute-start(bf16[1,288,128]{2,1,0:T(8,128)(2,1)S(1)} %slice_bitcast_fusion.12.refs_4_), channel_id=1, source_target_pairs={{0,24},{4,28},{8,16},{12,20},{16,8},{20,12},{24,0},{28,4},{1,25},{... | collective-permute-start | bytes 221192 | tf_op jit(solution)/shard_map/ppermute | solution.py:474
  52.4 4.6 %collective-permute-start.17 = (bf16[1,288,128]{2,1,0:T(8,128)(2,1)S(1)}, bf16[1,288,128]{2,1,0:T(8,128)(2,1)S(1)}, u32[]{:S(2)}, u32[]{:S(2)}) collective-permute-start(bf16[1,288,128]{2,1,0:T(8,128)(2,1)S(1)} %slice_bitcast_fusion.12.refs_4_), channel_id=1, source_target_pairs={{0,16},{4,20},{8,24},{12,28},{16,0},{20,4},{24,8},{28,12},{1,17},{... | collective-permute-start | bytes 221192 | tf_op jit(solution)/shard_map/ppermute | solution.py:474
  53.7 4.4 %collective-permute-start.16 = (bf16[1,288,128]{2,1,0:T(8,128)(2,1)S(1)}, bf16[1,288,128]{2,1,0:T(8,128)(2,1)S(1)}, u32[]{:S(2)}, u32[]{:S(2)}) collective-permute-start(bf16[1,288,128]{2,1,0:T(8,128)(2,1)S(1)} %slice_bitcast_fusion.12.refs_4_), channel_id=1, source_target_pairs={{0,8},{4,12},{8,0},{12,4},{16,24},{20,28},{24,16},{28,20},{1,9},{5... | collective-permute-start | bytes 221192 | tf_op jit(solution)/shard_map/ppermute | solution.py:474
  54.4 5.9 %collective-permute-start.20 = (bf16[256,128]{1,0:T(8,128)(2,1)S(1)}, bf16[256,128]{1,0:T(8,128)(2,1)S(1)}, u32[]{:S(2)}, u32[]{:S(2)}) collective-permute-start(bf16[256,128]{1,0:T(8,128)(2,1)S(1)} %pad_maximum_fusion.2), channel_id=1, source_target_pairs={{0,2},{1,3},{2,0},{3,1},{4,6},{5,7},{6,4},{7,5},{8,10},{9,11},{10,... | collective-permute-start | bytes 196616 | tf_op jit(solution)/shard_map/ppermute | solution.py:340
  56.3 4.1 %collective-permute-start.15 = (bf16[4,1,288,128]{3,2,1,0:T(8,128)(2,1)S(1)}, bf16[4,1,288,128]{3,2,1,0:T(8,128)(2,1)S(1)}, u32[]{:S(2)}, u32[]{:S(2)}) collective-permute-start(bf16[4,1,288,128]{3,2,1,0:T(8,128)(2,1)S(1)} %pad_maximum_fusion), channel_id=1, source_target_pairs={{0,4},{4,0},{8,12},{12,8},{16,20},{20,16},{24,28},{28,24},{1,5},{5... | collective-permute-start | bytes 884744 | tf_op jit(solution)/shard_map/ppermute | solution.py:471
  58.1 2.3 %collective-permute-start.19 = (bf16[4,1,288,128]{3,2,1,0:T(8,128)(2,1)S(1)}, bf16[4,1,288,128]{3,2,1,0:T(8,128)(2,1)S(1)}, u32[]{:S(2)}, u32[]{:S(2)}) collective-permute-start(bf16[4,1,288,128]{3,2,1,0:T(8,128)(2,1)S(1)} %pad_maximum_fusion.1), channel_id=1, source_target_pairs={{0,4},{4,0},{8,12},{12,8},{16,20},{20,16},{24,28},{28,24},{1,5},{5... | collective-permute-start | bytes 884744 | tf_op jit(solution)/shard_map/ppermute | solution.py:471

commit v4 on v3

--- a/solution.py
+++ b/solution.py
@@ -136,7 +136,7 @@
 
 
 def prepare_kernel(n, cr, fine, left, right, moved_in, *refs):
-    blocks, (moved, act_t, strip, sums, mid, up) = refs[:n], refs[n:]
+    blocks, (moved, act_t, strip, sums, up) = refs[:n], refs[n:]
     core, _, me = place()
     rows, width, ch = fine.shape
     cols = strip.shape[1]
@@ -153,46 +153,39 @@
         return 0
 
     lax.fori_loop(0, rows, patch, 0)
-    tall = rows // 4
-
-    def build(c):
-        for g in range(c * tall // 4, (c + 1) * tall // 4):
-            up[g] = spread_up(strip[g], width)
-            for r in range(4 * g, 4 * g + 4):
-                hidden = fine[r].astype(F32) + up[g]
-                act = (hidden * sigmoid(hidden)).astype(BF)
-                act_t[:, r * width : (r + 1) * width] = act.T
-
-    def share(c, first):
+    last = rows // 4 - 1
+
+    def build(g):
+        up[g] = spread_up(strip[g], width)
+        for r in range(4 * g, 4 * g + 4):
+            hidden = fine[r].astype(F32) + up[g]
+            act = (hidden * sigmoid(hidden)).astype(BF)
+            act_t[:, r * width : (r + 1) * width] = act.T
+
+    def share(g):
         for k in range(5):
-            out = mid if k == 4 else sums.at[k]
-            got = partial_tap(1 - core, k, c * tall, tall, act_t, moved)
-            out[...] = got if first else out[...] + got
+            got = partial_tap(1 - core, k, 4 * g, 4, act_t, moved)
+            sums[k] = got if g == 1 else sums[k] + got
 
     build(1)
-    build(2)
-    share(1, True)
-    build(0)
-    share(2, False)
-    build(3)
+    for g in range(1, last):
+        build(g + 1 if g + 1 < last else 0)
+        share(g)
+    build(last)
 
 
 def partial_tap(part, k, row, tall, act_t, moved):
     _, _, width, ch = moved.shape
-    half = ch // 2
     lhs = act_t[:, row * width : (row + tall) * width]
-    if isinstance(k, int) and k == 4:
-        lanes = pl.ds(pl.multiple_of(part * half, half), half)
-        window = moved[1, 1 + row : 1 + row + tall, :, lanes]
-    else:
-        t = part * 5 + k
-        window = moved[2 - lax.rem(t, 3), pl.ds(2 - t // 3 + row, tall)]
-    return jnp.dot(lhs, window.reshape(tall * width, -1), preferred_element_type=F32)
-
-
-def weight_taps(part, pieces, act_t, moved, out, sums=None, mid=None):
+    t = 4 if isinstance(k, int) and k == 4 else part * 5 + k
+    window = moved[2 - lax.rem(t, 3), pl.ds(2 - t // 3 + row, tall)]
+    return jnp.dot(lhs, window.reshape(tall * width, ch), preferred_element_type=F32)
+
+
+def weight_taps(part, act_t, moved, out, sums):
     _, plane, z = place()
     planes, zs, depth, half = out.shape
+    rows = moved.shape[1] - 2
     ch = 2 * half
     step = ch // (planes * zs)
     z = lax.rem(z, zs)
@@ -204,34 +197,40 @@
                 b = (p * zs + c) * step
                 out[p ^ plane, c ^ z, pl.ds(at, step), :] = acc[b : b + step].astype(BF)
 
-    def total(k, start):
-        got = [partial_tap(part, k, row, tall, act_t, moved) for row, tall in pieces]
-        return functools.reduce(jnp.add, got if start is None else [start] + got)
+    def total(k):
+        if sums is None:
+            return partial_tap(part, k, 0, rows, act_t, moved)
+        first = partial_tap(part, k, 0, 4, act_t, moved)
+        return sums[k] + first + partial_tap(part, k, rows - 4, 4, act_t, moved)
 
     def tap(k, _):
-        acc = total(k, None if sums is None else sums[k])
+        acc = total(k)
         put(k, acc[:, :half])
         put(k + 4, acc[:, half:])
         return 0
 
     lax.fori_loop(0, 4, tap, 0)
-    put(8, total(4, None if mid is None else mid[...]))
-
-
-def other_kernel(act_t, one, two, sums, mid, moved_in, out, moved):
+    return put, total
+
+
+def other_kernel(act_t, two, one, sums, moved_in, out, rest, moved):
     core, _, _ = place()
     _, rows, width, ch = moved.shape
     for slot, first in ((0, core == 1), (rows - 1, core == 0)):
         halo = jnp.where(first, one[...].astype(F32), two[...].astype(F32))
         left, right = halo[width : width + 1], halo[width + 1 : width + 2]
         spread(moved, slot, halo[:width].astype(BF), left, right)
-    tall = (rows - 2) // 4
-    weight_taps(1 - core, ((0, tall), (3 * tall, tall)), act_t, moved, out, sums, mid)
-
-
-def mine_kernel(act_t, moved, out):
+    put, total = weight_taps(1 - core, act_t, moved, out, sums)
+    middle = total(4)
+    low, high = middle[:, : ch // 2], middle[:, ch // 2 :]
+    put(8, jnp.where(core == 1, low, high))
+    rest[...] = jnp.where(core == 1, high, low)
+
+
+def mine_kernel(act_t, rest, moved, out):
     core, _, _ = place()
-    weight_taps(core, ((0, moved.shape[1] - 2),), act_t, moved, out)
+    put, _ = weight_taps(core, act_t, moved, out, None)
+    put(8, rest[...])
 
 
 def strip_order(n):
@@ -365,7 +364,7 @@
         name="load",
     )(timesteps, cot, step_scale)
 
-    shifts = [s for s in range(1, n) if is_edge(s)]
+    shifts = [s for s in range(n - 1, 0, -1) if is_edge(s)]
     for s in shifts + [s for s in range(1, n) if not is_edge(s)]:
         blocks[s] = col_swap(blocks[s], s)
 
@@ -384,17 +383,16 @@
     one = lax.ppermute(one, "row", xor_pairs(nrow, 1))
 
     groups = rows // 4
-    moved, act_t, strip, sums, mid = pl.pallas_call(
+    moved, act_t, strip, sums = pl.pallas_call(
         functools.partial(prepare_kernel, n, cr),
         out_shape=[
             shape(*moved.shape),
             shape(ch, rows * width),
             shape(groups, cols, ch),
-            shape(4, ch, ch, dtype=F32),
-            shape(ch, ch // 2, dtype=F32),
+            shape(5, ch, ch, dtype=F32),
         ],
         in_specs=[vmem()] * (4 + n),
-        out_specs=[vmem()] * 5,
+        out_specs=[vmem()] * 4,
         input_output_aliases={3: 0},
         scratch_shapes=[pltpu.VMEM((groups, width, ch), F32)],
         compiler_params=params(12),
@@ -408,25 +406,25 @@
     depth = 9 * ch // (planes * zs)
     half = ch // 2
     part = shape(planes, zs, depth, half)
-    send, moved = pl.pallas_call(
+    send, rest, moved = pl.pallas_call(
         other_kernel,
-        out_shape=[part, shape(*moved.shape)],
-        in_specs=[vmem()] * 6,
-        out_specs=[vmem()] * 2,
-        input_output_aliases={5: 1},
+        out_shape=[part, shape(ch, half, dtype=F32), shape(*moved.shape)],
+        in_specs=[vmem()] * 5,
+        out_specs=[vmem()] * 3,
+        input_output_aliases={4: 2},
         compiler_params=params(8),
-        cost_estimate=cost(9 * rows * width * ch * ch // 2, 8 << 20),
+        cost_estimate=cost(9 * rows * width * ch * ch // 4, 8 << 20),
         name="weight_other",
-    )(act_t, one, two, sums, mid, moved)
+    )(act_t, two, one, sums, moved)
     keep = pl.pallas_call(
         mine_kernel,
         out_shape=part,
-        in_specs=[vmem()] * 2,
+        in_specs=[vmem()] * 3,
         out_specs=vmem(),
         compiler_params=params(8),
-        cost_estimate=cost(9 * rows * width * ch * ch, 8 << 20),
+        cost_estimate=cost(8 * rows * width * ch * ch, 8 << 20),
         name="weight_mine",
-    )(act_t, moved)
+    )(act_t, rest, moved)
 
     done, pooled, made = [], [], 0
 

time: 61.9 us -> 60.7 us (0.981)
  Pallas kernels: 22.8 us -> 21.9 us
  starting transfers between devices: 23.9 us -> 23 us
  waiting for transfers between devices: 12.7 us -> 13.5 us
    ppermute x1, starting transfers between devices: 0.07 us -> 2.91 us  [per_device(): one = lax.ppermute(one, 'row', xor_pairs(nrow, 1))]
    ppermute x3, starting transfers between devices: 2.62 us -> 0.24 us  [core_swap(): return lax.ppermute(x, 'row', xor_pairs(nrow, 1))]
    pallas_call x2, Pallas kernels: 5.92 us -> 4.59 us  [the longest x1 2.91 us: per_device(): pl.pallas_call(mine_kernel, out_shape=part, in_specs=[vmem()] * 3, out_sp...]
    ppermute x7, starting transfers between devices: 9.53 us -> 8.49 us  [col_swap(): return lax.ppermute(x, 'col', xor_pairs(n, s))]
  transfers between devices with their start and end apart: 21 -> 21, of which waited for: 10 -> 10; matrix products, arithmetic and copies ran while one was open for 0% -> 0% of each run, Pallas kernels for 28% -> 29%
where the time goes in v4:
time: 60.7 us; the launch traced here: 60.5 us
  starting transfers between devices  23 us (38%)
  Pallas kernels  21.9 us (36%)
  waiting for transfers between devices  13.5 us (22%)
  between operations  1.57 us (3%)
    ppermute x9, starting transfers between devices, plane_swap(): return lax.ppermute(x, 'row', xor_pairs(nrow, 2 * s))  10.5 us
    ppermute x7, waiting for transfers between devices, col_swap(): return lax.ppermute(x, 'col', xor_pairs(n, s))  9.49 us
    pallas_call x3, Pallas kernels, input_piece(): pl.pallas_call(functools.partial(input_kernel, made, size, n), out_shape=...  8.93 us
    ppermute x7, starting transfers between devices, col_swap(): return lax.ppermute(x, 'col', xor_pairs(n, s))  8.49 us
    ppermute x9, waiting for transfers between devices, plane_swap(): return lax.ppermute(x, 'row', xor_pairs(nrow, 2 * s))  4 us
    pallas_call x1, Pallas kernels, per_device(): pl.pallas_call(functools.partial(prepare_kernel, n, cr), out_shape=[shape...  3.18 us
    ppermute x1, starting transfers between devices, per_device(): one = lax.ppermute(one, 'row', xor_pairs(nrow, 1))  2.91 us
    pallas_call x1, Pallas kernels, per_device(): pl.pallas_call(mine_kernel, out_shape=part, in_specs=[vmem()] * 3, out_sp...  2.91 us
  transfers between devices with their start and end apart: 21, of which 10 were waited for; matrix products, arithmetic and copies ran while one was open for 0% of the time, Pallas kernels for 29%

profile of v4, /device:TPU:0, one launch (start us, length us, event | category | flops | bytes accessed | tf_op | source)
XLA Modules:
  0.0 60.5 jit_solution(12568595776670752652)
XLA Ops:
  0.7 1.6 %start.1 = (bf16[64,256]{1,0:T(8,128)(2,1)S(1)}, bf16[96,256]{1,0:T(8,128)(2,1)S(1)}, bf16[64,256]{1,0:T(8,128)(2,1)S(1)}, bf16[96,256]{1,0:T(8,128)(2,1)S(1)}) custom-call(bf16[32,128,256]{2,1,0:T(8,128)(2,1)} %bitcast.61, bf16[2,128,256]{2,1,0:T(8,128)(2,1)} %bitcast.81), custom_call_target="tpu_custom_call" | custom-call | flops 2147483648 | bytes 4194304 | tf_op jit(solution)/shard_map/start/pallas_call | solution.py:341
  2.2 5.1 %collective-permute-start = (bf16[96,256]{1,0:T(8,128)(2,1)S(1)}, bf16[96,256]{1,0:T(8,128)(2,1)S(1)}, u32[]{:S(2)}, u32[]{:S(2)}) collective-permute-start(bf16[96,256]{1,0:T(8,128)(2,1)S(1)} %get-tuple-element.50), channel_id=1, source_target_pairs={{0,3},{1,2},{2,1},{3,0},{4,7},{5,6},{6,5},{7,4},{8,11},{9,10},{10,... | collective-permute-start | bytes 147464 | tf_op jit(solution)/shard_map/ppermute | solution.py:339
  7.3 0.0 collective-permute-start.1
  7.3 0.6 %collective-permute-start.2 = (bf16[64,256]{1,0:T(8,128)(2,1)S(1)}, bf16[64,256]{1,0:T(8,128)(2,1)S(1)}, u32[]{:S(2)}, u32[]{:S(2)}) collective-permute-start(bf16[64,256]{1,0:T(8,128)(2,1)S(1)} %get-tuple-element.55), channel_id=1, source_target_pairs={{0,2},{1,3},{2,0},{3,1},{4,6},{5,7},{6,4},{7,5},{8,10},{9,11},{10,... | collective-permute-start | bytes 98312 | tf_op jit(solution)/shard_map/ppermute | solution.py:339
  8.7 1.1 %load.1 = (bf16[3,34,128,256]{3,2,1,0:T(8,128)(2,1)S(1)}, f32[1,256]{1,0:T(1,128)S(1)}) custom-call(s32[1]{0:T(128)S(6)} %copy.23.steps, bf16[32,128,256]{2,1,0:T(8,128)(2,1)S(1)} %bitcast.62, f32[1000,256]{1,0:T(8,128)S(1)} %copy-done.3), custom_call_target="tpu_custom_call" | custom-call | flops 1048576 | bytes 4194304 | tf_op jit(solution)/shard_map/load/pallas_call | solution.py:357
  9.7 0.0 collective-permute-done.refs_0_.refs_3_
  9.7 1.7 %collective-permute-done.1.refs_1_ = bf16[96,256]{1,0:T(8,128)(2,1)S(1)} collective-permute-done((bf16[96,256]{1,0:T(8,128)(2,1)S(1)}, bf16[96,256]{1,0:T(8,128)(2,1)S(1)}, u32[]{:S(2)}, u32[]{:S(2)}) %collective-permute-start.1) | collective-permute-done | bytes 49184 | tf_op jit(solution)/shard_map/ppermute | solution.py:339
  11.4 0.1 edges.1
  11.5 0.8 %collective-permute-start.3 = (bf16[144,256]{1,0:T(8,128)(2,1)S(1)}, bf16[144,256]{1,0:T(8,128)(2,1)S(1)}, u32[]{:S(2)}, u32[]{:S(2)}) collective-permute-start(bf16[144,256]{1,0:T(8,128)(2,1)S(1)} %get-tuple-element.57), channel_id=1, source_target_pairs={{4,8},{12,16},{20,24},{8,4},{16,12},{24,20},{5,9},{13,17},{21,25},... | collective-permute-start | bytes 221192 | tf_op jit(solution)/shard_map/ppermute | solution.py:382
  12.3 2.9 %collective-permute-start.4 = (bf16[144,256]{1,0:T(8,128)(2,1)S(1)}, bf16[144,256]{1,0:T(8,128)(2,1)S(1)}, u32[]{:S(2)}, u32[]{:S(2)}) collective-permute-start(bf16[144,256]{1,0:T(8,128)(2,1)S(1)} %get-tuple-element.58), channel_id=1, source_target_pairs={{0,4},{4,0},{8,12},{12,8},{16,20},{20,16},{24,28},{28,24},{1,5},{5... | collective-permute-start | bytes 221192 | tf_op jit(solution)/shard_map/ppermute | solution.py:383
  15.2 0.0 collective-permute-done.2.refs_2_
  15.2 3.2 %prepare.1 = (bf16[3,34,128,256]{3,2,1,0:T(8,128)(2,1)S(1)}, bf16[256,4096]{1,0:T(8,128)(2,1)S(1)}, bf16[8,32,256]{2,1,0:T(8,128)(2,1)S(1)}, f32[5,256,256]{2,1,0:T(8,128)S(1)}) custom-call(bf16[32,128,256]{2,1,0:T(8,128)(2,1)S(1)} %bitcast.54, f32[32,256]{1,0:T(8,128)S(1)} %get-tuple-element.52.left, ...), custom_call_target="tpu_custom_call", output_to_operand_aliasing={{0}: (3, {})} | custom-call | flops 4294967296 | bytes 4194304 | tf_op jit(solution)/shard_map/prepare/pallas_call | solution.py:386
  18.4 1.7 %weight_other.1 = (bf16[4,2,288,128]{3,2,1,0:T(8,128)(2,1)S(1)}, f32[256,128]{1,0:T(8,128)S(1)}, bf16[3,34,128,256]{3,2,1,0:T(8,128)(2,1)S(1)}) custom-call(bf16[256,4096]{1,0:T(8,128)(2,1)S(1)} %get-tuple-element.56.act_t, bf16[144,256]{1,0:T(8,128)(2,1)S(1)} %collective-permute-done.3.two, ...), custom_call_target="tpu_custom_call", output_to_operand_aliasing={{2}: (4, {})} | custom-call | flops 603979776 | bytes 8388608 | tf_op jit(solution)/shard_map/weight_other/pallas_call | solution.py:409
  20.1 0.1 collective-permute-start.5
  20.2 2.9 %weight_mine.1 = bf16[4,2,288,128]{3,2,1,0:T(8,128)(2,1)S(1)} custom-call(bf16[256,4096]{1,0:T(8,128)(2,1)S(1)} %get-tuple-element.56.act_t, f32[256,128]{1,0:T(8,128)S(1)} %get-tuple-element.61.rest, bf16[3,34,128,256]{3,2,1,0:T(8,128)(2,1)S(1)} %get-tuple-element.62.moved), custom_call_target="tpu_custom_call" | custom-call | flops 2147483648 | bytes 8388608 | tf_op jit(solution)/shard_map/weight_mine/pallas_call | solution.py:419
  23.1 0.0 copy-start.1
  23.1 0.2 add_convert_fusion.after
  23.4 1.4 %collective-permute-start.8 = (bf16[2,288,128]{2,1,0:T(8,128)(2,1)S(1)}, bf16[2,288,128]{2,1,0:T(8,128)(2,1)S(1)}, u32[]{:S(2)}, u32[]{:S(2)}) collective-permute-start(bf16[2,288,128]{2,1,0:T(8,128)(2,1)S(1)} %get-tuple-element.95), channel_id=1, source_target_pairs={{0,24},{4,28},{8,16},{12,20},{16,8},{20,12},{24,0},{28,4},{1,25},{... | collective-permute-start | bytes 442376 | tf_op jit(solution)/shard_map/ppermute | solution.py:472
  24.7 1.6 %collective-permute-start.7 = (bf16[2,288,128]{2,1,0:T(8,128)(2,1)S(1)}, bf16[2,288,128]{2,1,0:T(8,128)(2,1)S(1)}, u32[]{:S(2)}, u32[]{:S(2)}) collective-permute-start(bf16[2,288,128]{2,1,0:T(8,128)(2,1)S(1)} %get-tuple-element.96), channel_id=1, source_target_pairs={{0,16},{4,20},{8,24},{12,28},{16,0},{20,4},{24,8},{28,12},{1,17},{... | collective-permute-start | bytes 442376 | tf_op jit(solution)/shard_map/ppermute | solution.py:472
  26.4 0.5 collective-permute-start.6
  26.9 5.5 %input_grad.3 = (bf16[32,128,256]{2,1,0:T(8,128)(2,1)}, bf16[6,2,32,128]{3,2,1,0:T(8,128)(2,1)S(1)}) custom-call(bf16[4,2,288,128]{3,2,1,0:T(8,128)(2,1)S(1)} %add_convert_fusion.after, bf16[3,34,128,256]{3,2,1,0:T(8,128)(2,1)S(1)} %get-tuple-element.62.moved, bf16[32,128,256]{2,1,0:T(8,128)(2,1)S(1)} %bitcast.55, ...), custom_call_target="tpu_custom_call" | custom-call | flops 3623878656 | bytes 4194304 | tf_op jit(solution)/shard_map/input_grad/pallas_call | solution.py:433
  32.4 1.3 %collective-permute-done.7 = bf16[2,288,128]{2,1,0:T(8,128)(2,1)S(1)} collective-permute-done((bf16[2,288,128]{2,1,0:T(8,128)(2,1)S(1)}, bf16[2,288,128]{2,1,0:T(8,128)(2,1)S(1)}, u32[]{:S(2)}, u32[]{:S(2)}) %collective-permute-start.7) | collective-permute-done | bytes 147488 | tf_op jit(solution)/shard_map/ppermute | solution.py:472
  33.7 0.1 collective-permute-done.6
  33.8 0.1 fusion.2.after
  33.9 0.9 %collective-permute-start.9 = (bf16[1,288,128]{2,1,0:T(8,128)(2,1)S(1)}, bf16[1,288,128]{2,1,0:T(8,128)(2,1)S(1)}, u32[]{:S(2)}, u32[]{:S(2)}) collective-permute-start(bf16[1,288,128]{2,1,0:T(8,128)(2,1)S(1)} %slice.105), channel_id=1, source_target_pairs={{0,1},{1,0},{2,3},{3,2},{4,5},{5,4},{6,7},{7,6},{8,9},{9,8},{10,11... | collective-permute-start | bytes 221192 | tf_op jit(solution)/shard_map/ppermute | solution.py:339
  34.7 1.7 %input_grad.4 = (bf16[32,128,256]{2,1,0:T(8,128)(2,1)}, bf16[1,2,32,128]{3,2,1,0:T(8,128)(2,1)S(1)}) custom-call(bf16[2,288,128]{2,1,0:T(8,128)(2,1)S(1)} %fusion.2.after, bf16[3,34,128,256]{3,2,1,0:T(8,128)(2,1)S(1)} %get-tuple-element.62.moved, bf16[32,128,256]{2,1,0:T(8,128)(2,1)S(1)} %bitcast.56, ...), custom_call_target="tpu_custom_call", output_to_operand_aliasing={{0}: (5, {})} | custom-call | flops 603979776 | bytes 4194304 | tf_op jit(solution)/shard_map/input_grad/pallas_call | solution.py:433
  36.5 1.8 %collective-permute-done.9 = bf16[1,288,128]{2,1,0:T(8,128)(2,1)S(1)} collective-permute-done((bf16[1,288,128]{2,1,0:T(8,128)(2,1)S(1)}, bf16[1,288,128]{2,1,0:T(8,128)(2,1)S(1)}, u32[]{:S(2)}, u32[]{:S(2)}) %collective-permute-start.9) | collective-permute-done | bytes 73760 | tf_op jit(solution)/shard_map/ppermute | solution.py:339
  38.3 0.7 %collective-permute-start.10 = (bf16[1,288,128]{2,1,0:T(8,128)(2,1)S(1)}, bf16[1,288,128]{2,1,0:T(8,128)(2,1)S(1)}, u32[]{:S(2)}, u32[]{:S(2)}) collective-permute-start(bf16[1,288,128]{2,1,0:T(8,128)(2,1)S(1)} %add_convert_fusion.2.after), channel_id=1, source_target_pairs={{0,2},{1,3},{2,0},{3,1},{4,6},{5,7},{6,4},{7,5},{8,10},{9,11},{10,... | collective-permute-start | bytes 221192 | tf_op jit(solution)/shard_map/ppermute | solution.py:339
  39.1 1.7 %input_grad.5 = (bf16[32,128,256]{2,1,0:T(8,128)(2,1)}, bf16[1,2,32,128]{3,2,1,0:T(8,128)(2,1)S(1)}) custom-call(bf16[1,288,128]{2,1,0:T(8,128)(2,1)S(1)} %add_convert_fusion.2.after, bf16[3,34,128,256]{3,2,1,0:T(8,128)(2,1)S(1)} %get-tuple-element.62.moved, bf16[32,128,256]{2,1,0:T(8,128)(2,1)S(1)} %bitcast.57, ...), custom_call_target="tpu_custom_call", output_to_operand_aliasing={{0}: (5, {})} | custom-call | flops 603979776 | bytes 4194304 | tf_op jit(solution)/shard_map/input_grad/pallas_call | solution.py:433
  40.8 3.6 %collective-permute-done.10 = bf16[1,288,128]{2,1,0:T(8,128)(2,1)S(1)} collective-permute-done((bf16[1,288,128]{2,1,0:T(8,128)(2,1)S(1)}, bf16[1,288,128]{2,1,0:T(8,128)(2,1)S(1)}, u32[]{:S(2)}, u32[]{:S(2)}) %collective-permute-start.10) | collective-permute-done | bytes 73760 | tf_op jit(solution)/shard_map/ppermute | solution.py:339
  44.5 0.2 collective-permute-start.14
  44.7 1.4 %collective-permute-start.13 = (bf16[1,288,128]{2,1,0:T(8,128)(2,1)S(1)}, bf16[1,288,128]{2,1,0:T(8,128)(2,1)S(1)}, u32[]{:S(2)}, u32[]{:S(2)}) collective-permute-start(bf16[1,288,128]{2,1,0:T(8,128)(2,1)S(1)} %get-tuple-element.94.refs_0_), channel_id=1, source_target_pairs={{0,24},{4,28},{8,16},{12,20},{16,8},{20,12},{24,0},{28,4},{1,25},{... | collective-permute-start | bytes 221192 | tf_op jit(solution)/shard_map/ppermute | solution.py:472
  46.2 1.4 %collective-permute-start.12 = (bf16[1,288,128]{2,1,0:T(8,128)(2,1)S(1)}, bf16[1,288,128]{2,1,0:T(8,128)(2,1)S(1)}, u32[]{:S(2)}, u32[]{:S(2)}) collective-permute-start(bf16[1,288,128]{2,1,0:T(8,128)(2,1)S(1)} %get-tuple-element.94.refs_0_), channel_id=1, source_target_pairs={{0,16},{4,20},{8,24},{12,28},{16,0},{20,4},{24,8},{28,12},{1,17},{... | collective-permute-start | bytes 221192 | tf_op jit(solution)/shard_map/ppermute | solution.py:472
  47.6 0.6 %collective-permute-start.11 = (bf16[1,288,128]{2,1,0:T(8,128)(2,1)S(1)}, bf16[1,288,128]{2,1,0:T(8,128)(2,1)S(1)}, u32[]{:S(2)}, u32[]{:S(2)}) collective-permute-start(bf16[1,288,128]{2,1,0:T(8,128)(2,1)S(1)} %get-tuple-element.94.refs_0_), channel_id=1, source_target_pairs={{0,8},{4,12},{8,0},{12,4},{16,24},{20,28},{24,16},{28,20},{1,9},{5... | collective-permute-start | bytes 221192 | tf_op jit(solution)/shard_map/ppermute | solution.py:472
  48.2 1.5 %collective-permute-done.14 = bf16[544,128]{1,0:T(8,128)(2,1)S(1)} collective-permute-done((bf16[544,128]{1,0:T(8,128)(2,1)S(1)}, bf16[544,128]{1,0:T(8,128)(2,1)S(1)}, u32[]{:S(2)}, u32[]{:S(2)}) %collective-permute-start.14) | collective-permute-done | bytes 139296 | tf_op jit(solution)/shard_map/ppermute | solution.py:339
  49.7 1.4 %collective-permute-start.18 = (bf16[1,288,128]{2,1,0:T(8,128)(2,1)S(1)}, bf16[1,288,128]{2,1,0:T(8,128)(2,1)S(1)}, u32[]{:S(2)}, u32[]{:S(2)}) collective-permute-start(bf16[1,288,128]{2,1,0:T(8,128)(2,1)S(1)} %slice_bitcast_fusion.12.refs_4_), channel_id=1, source_target_pairs={{0,24},{4,28},{8,16},{12,20},{16,8},{20,12},{24,0},{28,4},{1,25},{... | collective-permute-start | bytes 221192 | tf_op jit(solution)/shard_map/ppermute | solution.py:472
  51.1 1.4 %collective-permute-start.17 = (bf16[1,288,128]{2,1,0:T(8,128)(2,1)S(1)}, bf16[1,288,128]{2,1,0:T(8,128)(2,1)S(1)}, u32[]{:S(2)}, u32[]{:S(2)}) collective-permute-start(bf16[1,288,128]{2,1,0:T(8,128)(2,1)S(1)} %slice_bitcast_fusion.12.refs_4_), channel_id=1, source_target_pairs={{0,16},{4,20},{8,24},{12,28},{16,0},{20,4},{24,8},{28,12},{1,17},{... | collective-permute-start | bytes 221192 | tf_op jit(solution)/shard_map/ppermute | solution.py:472
  52.5 0.0 collective-permute-done.13.refs_3_
  52.5 0.6 %collective-permute-start.16 = (bf16[1,288,128]{2,1,0:T(8,128)(2,1)S(1)}, bf16[1,288,128]{2,1,0:T(8,128)(2,1)S(1)}, u32[]{:S(2)}, u32[]{:S(2)}) collective-permute-start(bf16[1,288,128]{2,1,0:T(8,128)(2,1)S(1)} %slice_bitcast_fusion.12.refs_4_), channel_id=1, source_target_pairs={{0,8},{4,12},{8,0},{12,4},{16,24},{20,28},{24,16},{28,20},{1,9},{5... | collective-permute-start | bytes 221192 | tf_op jit(solution)/shard_map/ppermute | solution.py:472
  53.2 1.0 %collective-permute-start.20 = (bf16[256,128]{1,0:T(8,128)(2,1)S(1)}, bf16[256,128]{1,0:T(8,128)(2,1)S(1)}, u32[]{:S(2)}, u32[]{:S(2)}) collective-permute-start(bf16[256,128]{1,0:T(8,128)(2,1)S(1)} %pad_maximum_fusion.2), channel_id=1, source_target_pairs={{0,2},{1,3},{2,0},{3,1},{4,6},{5,7},{6,4},{7,5},{8,10},{9,11},{10,... | collective-permute-start | bytes 196616 | tf_op jit(solution)/shard_map/ppermute | solution.py:339
  54.2 0.1 collective-permute-start.15
  54.3 0.7 %collective-permute-done.18.refs_7_ = bf16[1,288,128]{2,1,0:T(8,128)(2,1)S(1)} collective-permute-done((bf16[1,288,128]{2,1,0:T(8,128)(2,1)S(1)}, bf16[1,288,128]{2,1,0:T(8,128)(2,1)S(1)}, u32[]{:S(2)}, u32[]{:S(2)}) %collective-permute-start.18) | collective-permute-done | bytes 73760 | tf_op jit(solution)/shard_map/ppermute | solution.py:472
  54.9 0.8 %collective-permute-done.17.refs_6_ = bf16[1,288,128]{2,1,0:T(8,128)(2,1)S(1)} collective-permute-done((bf16[1,288,128]{2,1,0:T(8,128)(2,1)S(1)}, bf16[1,288,128]{2,1,0:T(8,128)(2,1)S(1)}, u32[]{:S(2)}, u32[]{:S(2)}) %collective-permute-start.17) | collective-permute-done | bytes 73760 | tf_op jit(solution)/shard_map/ppermute | solution.py:472
  55.7 1.2 %collective-permute-done.16.refs_5_ = bf16[1,288,128]{2,1,0:T(8,128)(2,1)S(1)} collective-permute-done((bf16[1,288,128]{2,1,0:T(8,128)(2,1)S(1)}, bf16[1,288,128]{2,1,0:T(8,128)(2,1)S(1)}, u32[]{:S(2)}, u32[]{:S(2)}) %collective-permute-start.16) | collective-permute-done | bytes 73760 | tf_op jit(solution)/shard_map/ppermute | solution.py:472
  56.9 0.1 collective-permute-start.19
  57.0 1.2 %finish.2.refs_12_ = f32[9,256,256]{2,1,0:T(8,128)} custom-call(bf16[1,288,128]{2,1,0:T(8,128)(2,1)S(1)} %get-tuple-element.94.refs_0_, bf16[1,288,128]{2,1,0:T(8,128)(2,1)S(1)} %collective-permute-done.11.refs_1_, bf16[1,288,128]{2,1,0:T(8,128)(2,1)S(1)} %collective-permute-done.12.refs_2_, bf16[1,288,128]{2,1,0:T(8,128)(2,1)S(1)} %collective-permute-done.13.refs_3_, ...), custom_call_target="tpu_custom_call" | custom-call | flops 1048576 | bytes 4194304 | tf_op jit(solution)/shard_map/finish/pallas_call | solution.py:527
  58.2 0.9 %collective-permute-done.20 = bf16[256,128]{1,0:T(8,128)(2,1)S(1)} collective-permute-done((bf16[256,128]{1,0:T(8,128)(2,1)S(1)}, bf16[256,128]{1,0:T(8,128)(2,1)S(1)}, u32[]{:S(2)}, u32[]{:S(2)}) %collective-permute-start.20) | collective-permute-done | bytes 65568 | tf_op jit(solution)/shard_map/ppermute | solution.py:339
  59.2 1.3 %finish.3 = (f32[9,256,256]{2,1,0:T(8,128)}, bf16[2,128,256]{2,1,0:T(8,128)(2,1)}) custom-call(bf16[1,288,128]{2,1,0:T(8,128)(2,1)S(1)} %get-tuple-element.105.refs_0_, bf16[1,288,128]{2,1,0:T(8,128)(2,1)S(1)} %get-tuple-element.104.refs_1_, bf16[1,288,128]{2,1,0:T(8,128)(2,1)S(1)} %get-tuple-element.103.refs_2_, ...), custom_call_target="tpu_custom_call", output_to_operand_aliasing={{0}: (12, {})} | custom-call | flops 1048576 | bytes 4194304 | tf_op jit(solution)/shard_map/finish/pallas_call | solution.py:527
  (33 shorter events, 0.3 us)
Async XLA Ops:
  0.6 8.0 %copy-start.2 = (bf16[1,32,128,256]{3,2,1,0:T(8,128)(2,1)S(1)}, bf16[1,32,128,256]{3,2,1,0:T(8,128)(2,1)}, u32[]{:S(2)}) copy-start(bf16[1,32,128,256]{3,2,1,0:T(8,128)(2,1)} %param.11) | copy-start | bytes 6291460
  0.6 8.0 %copy-start.3 = (f32[1000,256]{1,0:T(8,128)S(1)}, f32[1000,256]{1,0:T(8,128)}, u32[]{:S(2)}) copy-start(f32[1000,256]{1,0:T(8,128)} %scales.1) | copy-start | bytes 3072004
  2.2 7.5 %collective-permute-start = (bf16[96,256]{1,0:T(8,128)(2,1)S(1)}, bf16[96,256]{1,0:T(8,128)(2,1)S(1)}, u32[]{:S(2)}, u32[]{:S(2)}) collective-permute-start(bf16[96,256]{1,0:T(8,128)(2,1)S(1)} %get-tuple-element.50), channel_id=1, source_target_pairs={{0,3},{1,2},{2,1},{3,0},{4,7},{5,6},{6,5},{7,4},{8,11},{9,10},{10,... | collective-permute-start | bytes 147464 | tf_op jit(solution)/shard_map/ppermute | solution.py:339
  7.3 4.1 %collective-permute-start.1 = (bf16[96,256]{1,0:T(8,128)(2,1)S(1)}, bf16[96,256]{1,0:T(8,128)(2,1)S(1)}, u32[]{:S(2)}, u32[]{:S(2)}) collective-permute-start(bf16[96,256]{1,0:T(8,128)(2,1)S(1)} %get-tuple-element.51), channel_id=1, source_target_pairs={{0,1},{1,0},{2,3},{3,2},{4,5},{5,4},{6,7},{7,6},{8,9},{9,8},{10,11... | collective-permute-start | bytes 147464 | tf_op jit(solution)/shard_map/ppermute | solution.py:339
  7.3 7.9 %collective-permute-start.2 = (bf16[64,256]{1,0:T(8,128)(2,1)S(1)}, bf16[64,256]{1,0:T(8,128)(2,1)S(1)}, u32[]{:S(2)}, u32[]{:S(2)}) collective-permute-start(bf16[64,256]{1,0:T(8,128)(2,1)S(1)} %get-tuple-element.55), channel_id=1, source_target_pairs={{0,2},{1,3},{2,0},{3,1},{4,6},{5,7},{6,4},{7,5},{8,10},{9,11},{10,... | collective-permute-start | bytes 98312 | tf_op jit(solution)/shard_map/ppermute | solution.py:339
  11.4 3.8 %copy-start = (bf16[1,32,128,256]{3,2,1,0:T(8,128)(2,1)S(1)}, bf16[1,32,128,256]{3,2,1,0:T(8,128)(2,1)}, u32[]{:S(2)}) copy-start(bf16[1,32,128,256]{3,2,1,0:T(8,128)(2,1)} %param.6) | copy-start | bytes 6291460
  11.5 6.9 %collective-permute-start.3 = (bf16[144,256]{1,0:T(8,128)(2,1)S(1)}, bf16[144,256]{1,0:T(8,128)(2,1)S(1)}, u32[]{:S(2)}, u32[]{:S(2)}) collective-permute-start(bf16[144,256]{1,0:T(8,128)(2,1)S(1)} %get-tuple-element.57), channel_id=1, source_target_pairs={{4,8},{12,16},{20,24},{8,4},{16,12},{24,20},{5,9},{13,17},{21,25},... | collective-permute-start | bytes 221192 | tf_op jit(solution)/shard_map/ppermute | solution.py:382
  12.3 6.1 %collective-permute-start.4 = (bf16[144,256]{1,0:T(8,128)(2,1)S(1)}, bf16[144,256]{1,0:T(8,128)(2,1)S(1)}, u32[]{:S(2)}, u32[]{:S(2)}) collective-permute-start(bf16[144,256]{1,0:T(8,128)(2,1)S(1)} %get-tuple-element.58), channel_id=1, source_target_pairs={{0,4},{4,0},{8,12},{12,8},{16,20},{20,16},{24,28},{28,24},{1,5},{5... | collective-permute-start | bytes 221192 | tf_op jit(solution)/shard_map/ppermute | solution.py:383
  20.1 3.0 %collective-permute-start.5 = (bf16[4,2,288,128]{3,2,1,0:T(8,128)(2,1)S(1)}, bf16[4,2,288,128]{3,2,1,0:T(8,128)(2,1)S(1)}, u32[]{:S(2)}, u32[]{:S(2)}) collective-permute-start(bf16[4,2,288,128]{3,2,1,0:T(8,128)(2,1)S(1)} %get-tuple-element.63), channel_id=1, source_target_pairs={{0,4},{4,0},{8,12},{12,8},{16,20},{20,16},{24,28},{28,24},{1,5},{5... | collective-permute-start | bytes 1769480 | tf_op jit(solution)/shard_map/ppermute | solution.py:469
  23.1 3.8 %copy-start.1 = (bf16[3,3,256,256]{3,2,1,0:T(8,128)(2,1)S(1)}, bf16[3,3,256,256]{3,2,1,0:T(8,128)(2,1)}, u32[]{:S(2)}) copy-start(bf16[3,3,256,256]{3,2,1,0:T(8,128)(2,1)} %param.8) | copy-start | bytes 3538948
  23.4 9.0 %collective-permute-start.8 = (bf16[2,288,128]{2,1,0:T(8,128)(2,1)S(1)}, bf16[2,288,128]{2,1,0:T(8,128)(2,1)S(1)}, u32[]{:S(2)}, u32[]{:S(2)}) collective-permute-start(bf16[2,288,128]{2,1,0:T(8,128)(2,1)S(1)} %get-tuple-element.95), channel_id=1, source_target_pairs={{0,24},{4,28},{8,16},{12,20},{16,8},{20,12},{24,0},{28,4},{1,25},{... | collective-permute-start | bytes 442376 | tf_op jit(solution)/shard_map/ppermute | solution.py:472
  24.7 9.0 %collective-permute-start.7 = (bf16[2,288,128]{2,1,0:T(8,128)(2,1)S(1)}, bf16[2,288,128]{2,1,0:T(8,128)(2,1)S(1)}, u32[]{:S(2)}, u32[]{:S(2)}) collective-permute-start(bf16[2,288,128]{2,1,0:T(8,128)(2,1)S(1)} %get-tuple-element.96), channel_id=1, source_target_pairs={{0,16},{4,20},{8,24},{12,28},{16,0},{20,4},{24,8},{28,12},{1,17},{... | collective-permute-start | bytes 442376 | tf_op jit(solution)/shard_map/ppermute | solution.py:472
  26.4 7.4 %collective-permute-start.6 = (bf16[2,288,128]{2,1,0:T(8,128)(2,1)S(1)}, bf16[2,288,128]{2,1,0:T(8,128)(2,1)S(1)}, u32[]{:S(2)}, u32[]{:S(2)}) collective-permute-start(bf16[2,288,128]{2,1,0:T(8,128)(2,1)S(1)} %get-tuple-element.97), channel_id=1, source_target_pairs={{0,8},{4,12},{8,0},{12,4},{16,24},{20,28},{24,16},{28,20},{1,9},{5... | collective-permute-start | bytes 442376 | tf_op jit(solution)/shard_map/ppermute | solution.py:472
  33.9 4.4 %collective-permute-start.9 = (bf16[1,288,128]{2,1,0:T(8,128)(2,1)S(1)}, bf16[1,288,128]{2,1,0:T(8,128)(2,1)S(1)}, u32[]{:S(2)}, u32[]{:S(2)}) collective-permute-start(bf16[1,288,128]{2,1,0:T(8,128)(2,1)S(1)} %slice.105), channel_id=1, source_target_pairs={{0,1},{1,0},{2,3},{3,2},{4,5},{5,4},{6,7},{7,6},{8,9},{9,8},{10,11... | collective-permute-start | bytes 221192 | tf_op jit(solution)/shard_map/ppermute | solution.py:339
  38.3 6.1 %collective-permute-start.10 = (bf16[1,288,128]{2,1,0:T(8,128)(2,1)S(1)}, bf16[1,288,128]{2,1,0:T(8,128)(2,1)S(1)}, u32[]{:S(2)}, u32[]{:S(2)}) collective-permute-start(bf16[1,288,128]{2,1,0:T(8,128)(2,1)S(1)} %add_convert_fusion.2.after), channel_id=1, source_target_pairs={{0,2},{1,3},{2,0},{3,1},{4,6},{5,7},{6,4},{7,5},{8,10},{9,11},{10,... | collective-permute-start | bytes 221192 | tf_op jit(solution)/shard_map/ppermute | solution.py:339
  44.5 5.1 %collective-permute-start.14 = (bf16[544,128]{1,0:T(8,128)(2,1)S(1)}, bf16[544,128]{1,0:T(8,128)(2,1)S(1)}, u32[]{:S(2)}, u32[]{:S(2)}) collective-permute-start(bf16[544,128]{1,0:T(8,128)(2,1)S(1)} %constant_dynamic-update-slice_fusion), channel_id=1, source_target_pairs={{0,1},{1,0},{2,3},{3,2},{4,5},{5,4},{6,7},{7,6},{8,9},{9,8},{10,11... | collective-permute-start | bytes 417800 | tf_op jit(solution)/shard_map/ppermute | solution.py:339
  44.7 7.8 %collective-permute-start.13 = (bf16[1,288,128]{2,1,0:T(8,128)(2,1)S(1)}, bf16[1,288,128]{2,1,0:T(8,128)(2,1)S(1)}, u32[]{:S(2)}, u32[]{:S(2)}) collective-permute-start(bf16[1,288,128]{2,1,0:T(8,128)(2,1)S(1)} %get-tuple-element.94.refs_0_), channel_id=1, source_target_pairs={{0,24},{4,28},{8,16},{12,20},{16,8},{20,12},{24,0},{28,4},{1,25},{... | collective-permute-start | bytes 221192 | tf_op jit(solution)/shard_map/ppermute | solution.py:472
  46.2 7.0 %collective-permute-start.12 = (bf16[1,288,128]{2,1,0:T(8,128)(2,1)S(1)}, bf16[1,288,128]{2,1,0:T(8,128)(2,1)S(1)}, u32[]{:S(2)}, u32[]{:S(2)}) collective-permute-start(bf16[1,288,128]{2,1,0:T(8,128)(2,1)S(1)} %get-tuple-element.94.refs_0_), channel_id=1, source_target_pairs={{0,16},{4,20},{8,24},{12,28},{16,0},{20,4},{24,8},{28,12},{1,17},{... | collective-permute-start | bytes 221192 | tf_op jit(solution)/shard_map/ppermute | solution.py:472
  47.6 5.6 %collective-permute-start.11 = (bf16[1,288,128]{2,1,0:T(8,128)(2,1)S(1)}, bf16[1,288,128]{2,1,0:T(8,128)(2,1)S(1)}, u32[]{:S(2)}, u32[]{:S(2)}) collective-permute-start(bf16[1,288,128]{2,1,0:T(8,128)(2,1)S(1)} %get-tuple-element.94.refs_0_), channel_id=1, source_target_pairs={{0,8},{4,12},{8,0},{12,4},{16,24},{20,28},{24,16},{28,20},{1,9},{5... | collective-permute-start | bytes 221192 | tf_op jit(solution)/shard_map/ppermute | solution.py:472
  49.7 5.3 %collective-permute-start.18 = (bf16[1,288,128]{2,1,0:T(8,128)(2,1)S(1)}, bf16[1,288,128]{2,1,0:T(8,128)(2,1)S(1)}, u32[]{:S(2)}, u32[]{:S(2)}) collective-permute-start(bf16[1,288,128]{2,1,0:T(8,128)(2,1)S(1)} %slice_bitcast_fusion.12.refs_4_), channel_id=1, source_target_pairs={{0,24},{4,28},{8,16},{12,20},{16,8},{20,12},{24,0},{28,4},{1,25},{... | collective-permute-start | bytes 221192 | tf_op jit(solution)/shard_map/ppermute | solution.py:472
  51.1 4.6 %collective-permute-start.17 = (bf16[1,288,128]{2,1,0:T(8,128)(2,1)S(1)}, bf16[1,288,128]{2,1,0:T(8,128)(2,1)S(1)}, u32[]{:S(2)}, u32[]{:S(2)}) collective-permute-start(bf16[1,288,128]{2,1,0:T(8,128)(2,1)S(1)} %slice_bitcast_fusion.12.refs_4_), channel_id=1, source_target_pairs={{0,16},{4,20},{8,24},{12,28},{16,0},{20,4},{24,8},{28,12},{1,17},{... | collective-permute-start | bytes 221192 | tf_op jit(solution)/shard_map/ppermute | solution.py:472
  52.5 4.4 %collective-permute-start.16 = (bf16[1,288,128]{2,1,0:T(8,128)(2,1)S(1)}, bf16[1,288,128]{2,1,0:T(8,128)(2,1)S(1)}, u32[]{:S(2)}, u32[]{:S(2)}) collective-permute-start(bf16[1,288,128]{2,1,0:T(8,128)(2,1)S(1)} %slice_bitcast_fusion.12.refs_4_), channel_id=1, source_target_pairs={{0,8},{4,12},{8,0},{12,4},{16,24},{20,28},{24,16},{28,20},{1,9},{5... | collective-permute-start | bytes 221192 | tf_op jit(solution)/shard_map/ppermute | solution.py:472
  53.2 5.9 %collective-permute-start.20 = (bf16[256,128]{1,0:T(8,128)(2,1)S(1)}, bf16[256,128]{1,0:T(8,128)(2,1)S(1)}, u32[]{:S(2)}, u32[]{:S(2)}) collective-permute-start(bf16[256,128]{1,0:T(8,128)(2,1)S(1)} %pad_maximum_fusion.2), channel_id=1, source_target_pairs={{0,2},{1,3},{2,0},{3,1},{4,6},{5,7},{6,4},{7,5},{8,10},{9,11},{10,... | collective-permute-start | bytes 196616 | tf_op jit(solution)/shard_map/ppermute | solution.py:339
  54.2 4.9 %collective-permute-start.15 = (bf16[4,1,288,128]{3,2,1,0:T(8,128)(2,1)S(1)}, bf16[4,1,288,128]{3,2,1,0:T(8,128)(2,1)S(1)}, u32[]{:S(2)}, u32[]{:S(2)}) collective-permute-start(bf16[4,1,288,128]{3,2,1,0:T(8,128)(2,1)S(1)} %pad_maximum_fusion), channel_id=1, source_target_pairs={{0,4},{4,0},{8,12},{12,8},{16,20},{20,16},{24,28},{28,24},{1,5},{5... | collective-permute-start | bytes 884744 | tf_op jit(solution)/shard_map/ppermute | solution.py:469
  56.9 2.2 %collective-permute-start.19 = (bf16[4,1,288,128]{3,2,1,0:T(8,128)(2,1)S(1)}, bf16[4,1,288,128]{3,2,1,0:T(8,128)(2,1)S(1)}, u32[]{:S(2)}, u32[]{:S(2)}) collective-permute-start(bf16[4,1,288,128]{3,2,1,0:T(8,128)(2,1)S(1)} %pad_maximum_fusion.1), channel_id=1, source_target_pairs={{0,4},{4,0},{8,12},{12,8},{16,20},{20,16},{24,28},{28,24},{1,5},{5... | collective-permute-start | bytes 884744 | tf_op jit(solution)/shard_map/ppermute | solution.py:469

commit v5 on v4

--- a/solution.py
+++ b/solution.py
@@ -216,8 +216,11 @@
 def other_kernel(act_t, two, one, sums, moved_in, out, rest, moved):
     core, _, _ = place()
     _, rows, width, ch = moved.shape
+    row = lax.axis_index("row")
+    outer = (row == 0) | (row == lax.axis_size("row") - 1)
+    next_chip = jnp.where(outer, 0.0, two[...].astype(F32))
     for slot, first in ((0, core == 1), (rows - 1, core == 0)):
-        halo = jnp.where(first, one[...].astype(F32), two[...].astype(F32))
+        halo = jnp.where(first, one[...].astype(F32), next_chip)
         left, right = halo[width : width + 1], halo[width + 1 : width + 2]
         spread(moved, slot, halo[:width].astype(BF), left, right)
     put, total = weight_taps(1 - core, act_t, moved, out, sums)
@@ -378,8 +381,10 @@
         cost_estimate=cost(1 << 18, 1 << 19),
         name="edges",
     )(scale, moved, *[blocks[s] for s in shifts])
-    odd = range(1, nrow - 1, 2)
-    two = lax.ppermute(two, "row", [(i, i + 1) for i in odd] + [(i + 1, i) for i in odd])
+    odd = range(1, nrow, 2)
+    two = lax.ppermute(
+        two, "row", [(i, (i + 1) % nrow) for i in odd] + [((i + 1) % nrow, i) for i in odd]
+    )
     one = lax.ppermute(one, "row", xor_pairs(nrow, 1))
 
     groups = rows // 4
@@ -540,17 +545,19 @@
             name="finish",
         )(*pieces, *parts, *out)
 
-    spots = [(s, k * wave[0].shape[0]) for k, wave in enumerate(waves) for s in [0] + ways]
-    mine = [x for wave in waves for x in wave]
-    other = []
-    for wave in waves:
+    out, others, spots = [], [], ()
+    for k, wave in enumerate(waves):
+        if k:
+            wave[1:], out = lax.optimization_barrier((wave[1:], out))
         swapped = core_swap(jnp.stack(wave))
-        other += [swapped[i] for i in range(len(wave))]
-    out = finish([], mine, tuple((0, *spot) for spot in spots))
+        here = [(s, k * wave[0].shape[0]) for s in [0] + ways]
+        places = [(0, *spot) for spot in here] + [(1, *spot) for spot in spots]
+        out = finish(out, wave + others, tuple(places))
+        others, spots = [swapped[i] for i in range(len(wave))], here
     last, out = lax.optimization_barrier((hopped, out))
     land(bit * 2, sent, last, 0)
     parts = [x for _, x in sorted(strips[0], key=lambda pair: pair[0])]
-    grad_weight, grad_coarse = finish(out, other, tuple((1, *spot) for spot in spots), parts)
+    grad_weight, grad_coarse = finish(out, others, tuple((1, *spot) for spot in spots), parts)
     return (done[0][None], grad_coarse[None], grad_weight.reshape(3, 3, ch, ch))
 
 

time: 60.7 us -> 59.7 us (0.984)
  starting transfers between devices: 23 us -> 21.1 us
    ppermute x1, starting transfers between devices: 2.91 us -> 1.01 us  [per_device(): one = lax.ppermute(one, 'row', xor_pairs(nrow, 1))]
    ppermute x9, waiting for transfers between devices: 4 us -> 2.47 us  [plane_swap(): return lax.ppermute(x, 'row', xor_pairs(nrow, 2 * s))]
    ppermute x7, waiting for transfers between devices: 9.49 us -> 10.8 us  [col_swap(): return lax.ppermute(x, 'col', xor_pairs(n, s))]
    pallas_call x2 -> x3, Pallas kernels: 2.52 us -> 3.14 us  [finish(): pl.pallas_call(functools.partial(finish_kernel, float(pixels) ** (-0.5),...]
  transfers between devices with their start and end apart: 21 -> 21, of which waited for: 10 -> 9; matrix products, arithmetic and copies ran while one was open for 0% -> 0% of each run, Pallas kernels for 29% -> 31%
where the time goes in v5:
time: 59.7 us; the launch traced here: 59.6 us
  Pallas kernels  22.5 us (38%)
  starting transfers between devices  21.1 us (35%)
  waiting for transfers between devices  13.9 us (23%)
  between operations  1.58 us (3%)
    ppermute x7, waiting for transfers between devices, col_swap(): return lax.ppermute(x, 'col', xor_pairs(n, s))  10.8 us
    ppermute x9, starting transfers between devices, plane_swap(): return lax.ppermute(x, 'row', xor_pairs(nrow, 2 * s))  10.5 us
    pallas_call x3, Pallas kernels, input_piece(): pl.pallas_call(functools.partial(input_kernel, made, size, n), out_shape=...  8.92 us
    ppermute x7, starting transfers between devices, col_swap(): return lax.ppermute(x, 'col', xor_pairs(n, s))  8.64 us
    pallas_call x1, Pallas kernels, per_device(): pl.pallas_call(functools.partial(prepare_kernel, n, cr), out_shape=[shape...  3.18 us
    pallas_call x3, Pallas kernels, finish(): pl.pallas_call(functools.partial(finish_kernel, float(pixels) ** (-0.5),...  3.14 us
    pallas_call x1, Pallas kernels, per_device(): pl.pallas_call(mine_kernel, out_shape=part, in_specs=[vmem()] * 3, out_sp...  2.93 us
    ppermute x9, waiting for transfers between devices, plane_swap(): return lax.ppermute(x, 'row', xor_pairs(nrow, 2 * s))  2.47 us
  transfers between devices with their start and end apart: 21, of which 9 were waited for; matrix products, arithmetic and copies ran while one was open for 0% of the time, Pallas kernels for 31%

profile of v5, /device:TPU:0, one launch (start us, length us, event | category | flops | bytes accessed | tf_op | source)
XLA Modules:
  0.0 59.6 jit_solution(16619311905061913553)
XLA Ops:
  0.7 1.6 %start.1 = (bf16[64,256]{1,0:T(8,128)(2,1)S(1)}, bf16[96,256]{1,0:T(8,128)(2,1)S(1)}, bf16[64,256]{1,0:T(8,128)(2,1)S(1)}, bf16[96,256]{1,0:T(8,128)(2,1)S(1)}) custom-call(bf16[32,128,256]{2,1,0:T(8,128)(2,1)} %bitcast.61, bf16[2,128,256]{2,1,0:T(8,128)(2,1)} %bitcast.81), custom_call_target="tpu_custom_call" | custom-call | flops 2147483648 | bytes 4194304 | tf_op jit(solution)/shard_map/start/pallas_call | solution.py:344
  2.2 5.1 %collective-permute-start = (bf16[96,256]{1,0:T(8,128)(2,1)S(1)}, bf16[96,256]{1,0:T(8,128)(2,1)S(1)}, u32[]{:S(2)}, u32[]{:S(2)}) collective-permute-start(bf16[96,256]{1,0:T(8,128)(2,1)S(1)} %get-tuple-element.54), channel_id=1, source_target_pairs={{0,3},{1,2},{2,1},{3,0},{4,7},{5,6},{6,5},{7,4},{8,11},{9,10},{10,... | collective-permute-start | bytes 147464 | tf_op jit(solution)/shard_map/ppermute | solution.py:342
  7.3 0.0 collective-permute-start.1
  7.3 0.6 %collective-permute-start.2 = (bf16[64,256]{1,0:T(8,128)(2,1)S(1)}, bf16[64,256]{1,0:T(8,128)(2,1)S(1)}, u32[]{:S(2)}, u32[]{:S(2)}) collective-permute-start(bf16[64,256]{1,0:T(8,128)(2,1)S(1)} %get-tuple-element.59), channel_id=1, source_target_pairs={{0,2},{1,3},{2,0},{3,1},{4,6},{5,7},{6,4},{7,5},{8,10},{9,11},{10,... | collective-permute-start | bytes 98312 | tf_op jit(solution)/shard_map/ppermute | solution.py:342
  8.7 1.1 %load.1 = (bf16[3,34,128,256]{3,2,1,0:T(8,128)(2,1)S(1)}, f32[1,256]{1,0:T(1,128)S(1)}) custom-call(s32[1]{0:T(128)S(6)} %copy.25.steps, bf16[32,128,256]{2,1,0:T(8,128)(2,1)S(1)} %bitcast.62, f32[1000,256]{1,0:T(8,128)S(1)} %copy-done.3), custom_call_target="tpu_custom_call" | custom-call | flops 1048576 | bytes 4194304 | tf_op jit(solution)/shard_map/load/pallas_call | solution.py:360
  9.7 1.7 %collective-permute-done.1.refs_1_ = bf16[96,256]{1,0:T(8,128)(2,1)S(1)} collective-permute-done((bf16[96,256]{1,0:T(8,128)(2,1)S(1)}, bf16[96,256]{1,0:T(8,128)(2,1)S(1)}, u32[]{:S(2)}, u32[]{:S(2)}) %collective-permute-start.1) | collective-permute-done | bytes 49184 | tf_op jit(solution)/shard_map/ppermute | solution.py:342
  11.4 0.1 edges.1
  11.5 0.7 %collective-permute-start.3 = (bf16[144,256]{1,0:T(8,128)(2,1)S(1)}, bf16[144,256]{1,0:T(8,128)(2,1)S(1)}, u32[]{:S(2)}, u32[]{:S(2)}) collective-permute-start(bf16[144,256]{1,0:T(8,128)(2,1)S(1)} %get-tuple-element.61), channel_id=1, source_target_pairs={{4,8},{12,16},{20,24},{28,0},{8,4},{16,12},{24,20},{0,28},{5,9},{1... | collective-permute-start | bytes 221192 | tf_op jit(solution)/shard_map/ppermute | solution.py:385
  12.2 1.0 %collective-permute-start.4 = (bf16[144,256]{1,0:T(8,128)(2,1)S(1)}, bf16[144,256]{1,0:T(8,128)(2,1)S(1)}, u32[]{:S(2)}, u32[]{:S(2)}) collective-permute-start(bf16[144,256]{1,0:T(8,128)(2,1)S(1)} %get-tuple-element.62), channel_id=1, source_target_pairs={{0,4},{4,0},{8,12},{12,8},{16,20},{20,16},{24,28},{28,24},{1,5},{5... | collective-permute-start | bytes 221192 | tf_op jit(solution)/shard_map/ppermute | solution.py:388
  13.2 3.2 %prepare.1 = (bf16[3,34,128,256]{3,2,1,0:T(8,128)(2,1)S(1)}, bf16[256,4096]{1,0:T(8,128)(2,1)S(1)}, bf16[8,32,256]{2,1,0:T(8,128)(2,1)S(1)}, f32[5,256,256]{2,1,0:T(8,128)S(1)}) custom-call(bf16[32,128,256]{2,1,0:T(8,128)(2,1)S(1)} %bitcast.54, f32[32,256]{1,0:T(8,128)S(1)} %get-tuple-element.56.left, ...), custom_call_target="tpu_custom_call", output_to_operand_aliasing={{0}: (3, {})} | custom-call | flops 4294967296 | bytes 4194304 | tf_op jit(solution)/shard_map/prepare/pallas_call | solution.py:391
  16.4 0.6 collective-permute-done.3.two
  16.9 0.0 collective-permute-done.4.one
  16.9 1.7 %weight_other.1 = (bf16[4,2,288,128]{3,2,1,0:T(8,128)(2,1)S(1)}, f32[256,128]{1,0:T(8,128)S(1)}, bf16[3,34,128,256]{3,2,1,0:T(8,128)(2,1)S(1)}) custom-call(bf16[256,4096]{1,0:T(8,128)(2,1)S(1)} %get-tuple-element.60.act_t, bf16[144,256]{1,0:T(8,128)(2,1)S(1)} %collective-permute-done.3.two, ...), custom_call_target="tpu_custom_call", output_to_operand_aliasing={{2}: (4, {})} | custom-call | flops 603979776 | bytes 8388608 | tf_op jit(solution)/shard_map/weight_other/pallas_call | solution.py:414
  18.6 0.1 collective-permute-start.5
  18.7 2.9 %weight_mine.1 = bf16[4,2,288,128]{3,2,1,0:T(8,128)(2,1)S(1)} custom-call(bf16[256,4096]{1,0:T(8,128)(2,1)S(1)} %get-tuple-element.60.act_t, f32[256,128]{1,0:T(8,128)S(1)} %get-tuple-element.65.rest, bf16[3,34,128,256]{3,2,1,0:T(8,128)(2,1)S(1)} %get-tuple-element.66.moved), custom_call_target="tpu_custom_call" | custom-call | flops 2147483648 | bytes 8388608 | tf_op jit(solution)/shard_map/weight_mine/pallas_call | solution.py:424
  21.6 0.0 copy-start.1
  21.7 0.2 add_convert_fusion.after
  21.9 1.8 %collective-permute-start.8 = (bf16[2,288,128]{2,1,0:T(8,128)(2,1)S(1)}, bf16[2,288,128]{2,1,0:T(8,128)(2,1)S(1)}, u32[]{:S(2)}, u32[]{:S(2)}) collective-permute-start(bf16[2,288,128]{2,1,0:T(8,128)(2,1)S(1)} %get-tuple-element.103), channel_id=1, source_target_pairs={{0,24},{4,28},{8,16},{12,20},{16,8},{20,12},{24,0},{28,4},{1,25},{... | collective-permute-start | bytes 442376 | tf_op jit(solution)/shard_map/ppermute | solution.py:477
  23.7 0.7 %collective-permute-start.7 = (bf16[2,288,128]{2,1,0:T(8,128)(2,1)S(1)}, bf16[2,288,128]{2,1,0:T(8,128)(2,1)S(1)}, u32[]{:S(2)}, u32[]{:S(2)}) collective-permute-start(bf16[2,288,128]{2,1,0:T(8,128)(2,1)S(1)} %get-tuple-element.104), channel_id=1, source_target_pairs={{0,16},{4,20},{8,24},{12,28},{16,0},{20,4},{24,8},{28,12},{1,17},{... | collective-permute-start | bytes 442376 | tf_op jit(solution)/shard_map/ppermute | solution.py:477
  24.3 1.1 %collective-permute-start.6 = (bf16[2,288,128]{2,1,0:T(8,128)(2,1)S(1)}, bf16[2,288,128]{2,1,0:T(8,128)(2,1)S(1)}, u32[]{:S(2)}, u32[]{:S(2)}) collective-permute-start(bf16[2,288,128]{2,1,0:T(8,128)(2,1)S(1)} %get-tuple-element.105), channel_id=1, source_target_pairs={{0,8},{4,12},{8,0},{12,4},{16,24},{20,28},{24,16},{28,20},{1,9},{5... | collective-permute-start | bytes 442376 | tf_op jit(solution)/shard_map/ppermute | solution.py:477
  25.4 5.5 %input_grad.3 = (bf16[32,128,256]{2,1,0:T(8,128)(2,1)}, bf16[6,2,32,128]{3,2,1,0:T(8,128)(2,1)S(1)}) custom-call(bf16[4,2,288,128]{3,2,1,0:T(8,128)(2,1)S(1)} %add_convert_fusion.after, bf16[3,34,128,256]{3,2,1,0:T(8,128)(2,1)S(1)} %get-tuple-element.66.moved, bf16[32,128,256]{2,1,0:T(8,128)(2,1)S(1)} %bitcast.55, ...), custom_call_target="tpu_custom_call" | custom-call | flops 3623878656 | bytes 4194304 | tf_op jit(solution)/shard_map/input_grad/pallas_call | solution.py:438
  30.9 0.0 collective-permute-done.8
  30.9 1.3 %collective-permute-done.7 = bf16[2,288,128]{2,1,0:T(8,128)(2,1)S(1)} collective-permute-done((bf16[2,288,128]{2,1,0:T(8,128)(2,1)S(1)}, bf16[2,288,128]{2,1,0:T(8,128)(2,1)S(1)}, u32[]{:S(2)}, u32[]{:S(2)}) %collective-permute-start.7) | collective-permute-done | bytes 147488 | tf_op jit(solution)/shard_map/ppermute | solution.py:477
  32.2 0.1 fusion.2.after
  32.3 0.9 %collective-permute-start.9 = (bf16[1,288,128]{2,1,0:T(8,128)(2,1)S(1)}, bf16[1,288,128]{2,1,0:T(8,128)(2,1)S(1)}, u32[]{:S(2)}, u32[]{:S(2)}) collective-permute-start(bf16[1,288,128]{2,1,0:T(8,128)(2,1)S(1)} %slice.105), channel_id=1, source_target_pairs={{0,1},{1,0},{2,3},{3,2},{4,5},{5,4},{6,7},{7,6},{8,9},{9,8},{10,11... | collective-permute-start | bytes 221192 | tf_op jit(solution)/shard_map/ppermute | solution.py:342
  33.2 1.7 %input_grad.4 = (bf16[32,128,256]{2,1,0:T(8,128)(2,1)}, bf16[1,2,32,128]{3,2,1,0:T(8,128)(2,1)S(1)}) custom-call(bf16[2,288,128]{2,1,0:T(8,128)(2,1)S(1)} %fusion.2.after, bf16[3,34,128,256]{3,2,1,0:T(8,128)(2,1)S(1)} %get-tuple-element.66.moved, bf16[32,128,256]{2,1,0:T(8,128)(2,1)S(1)} %bitcast.56, ...), custom_call_target="tpu_custom_call", output_to_operand_aliasing={{0}: (5, {})} | custom-call | flops 603979776 | bytes 4194304 | tf_op jit(solution)/shard_map/input_grad/pallas_call | solution.py:438
  34.9 1.8 %collective-permute-done.9 = bf16[1,288,128]{2,1,0:T(8,128)(2,1)S(1)} collective-permute-done((bf16[1,288,128]{2,1,0:T(8,128)(2,1)S(1)}, bf16[1,288,128]{2,1,0:T(8,128)(2,1)S(1)}, u32[]{:S(2)}, u32[]{:S(2)}) %collective-permute-start.9) | collective-permute-done | bytes 73760 | tf_op jit(solution)/shard_map/ppermute | solution.py:342
  36.7 0.8 %collective-permute-start.10 = (bf16[1,288,128]{2,1,0:T(8,128)(2,1)S(1)}, bf16[1,288,128]{2,1,0:T(8,128)(2,1)S(1)}, u32[]{:S(2)}, u32[]{:S(2)}) collective-permute-start(bf16[1,288,128]{2,1,0:T(8,128)(2,1)S(1)} %add_convert_fusion.2.after), channel_id=1, source_target_pairs={{0,2},{1,3},{2,0},{3,1},{4,6},{5,7},{6,4},{7,5},{8,10},{9,11},{10,... | collective-permute-start | bytes 221192 | tf_op jit(solution)/shard_map/ppermute | solution.py:342
  37.6 1.7 %input_grad.5 = (bf16[32,128,256]{2,1,0:T(8,128)(2,1)}, bf16[1,2,32,128]{3,2,1,0:T(8,128)(2,1)S(1)}) custom-call(bf16[1,288,128]{2,1,0:T(8,128)(2,1)S(1)} %add_convert_fusion.2.after, bf16[3,34,128,256]{3,2,1,0:T(8,128)(2,1)S(1)} %get-tuple-element.66.moved, bf16[32,128,256]{2,1,0:T(8,128)(2,1)S(1)} %bitcast.57, ...), custom_call_target="tpu_custom_call", output_to_operand_aliasing={{0}: (5, {})} | custom-call | flops 603979776 | bytes 4194304 | tf_op jit(solution)/shard_map/input_grad/pallas_call | solution.py:438
  39.3 3.5 %collective-permute-done.10 = bf16[1,288,128]{2,1,0:T(8,128)(2,1)S(1)} collective-permute-done((bf16[1,288,128]{2,1,0:T(8,128)(2,1)S(1)}, bf16[1,288,128]{2,1,0:T(8,128)(2,1)S(1)}, u32[]{:S(2)}, u32[]{:S(2)}) %collective-permute-start.10) | collective-permute-done | bytes 73760 | tf_op jit(solution)/shard_map/ppermute | solution.py:342
  42.9 0.2 collective-permute-start.14
  43.1 1.7 %collective-permute-start.13 = (bf16[1,288,128]{2,1,0:T(8,128)(2,1)S(1)}, bf16[1,288,128]{2,1,0:T(8,128)(2,1)S(1)}, u32[]{:S(2)}, u32[]{:S(2)}) collective-permute-start(bf16[1,288,128]{2,1,0:T(8,128)(2,1)S(1)} %get-tuple-element.102.refs_0_), channel_id=1, source_target_pairs={{0,24},{4,28},{8,16},{12,20},{16,8},{20,12},{24,0},{28,4},{1,25},{... | collective-permute-start | bytes 221192 | tf_op jit(solution)/shard_map/ppermute | solution.py:477
  44.9 1.0 %collective-permute-start.12 = (bf16[1,288,128]{2,1,0:T(8,128)(2,1)S(1)}, bf16[1,288,128]{2,1,0:T(8,128)(2,1)S(1)}, u32[]{:S(2)}, u32[]{:S(2)}) collective-permute-start(bf16[1,288,128]{2,1,0:T(8,128)(2,1)S(1)} %get-tuple-element.102.refs_0_), channel_id=1, source_target_pairs={{0,16},{4,20},{8,24},{12,28},{16,0},{20,4},{24,8},{28,12},{1,17},{... | collective-permute-start | bytes 221192 | tf_op jit(solution)/shard_map/ppermute | solution.py:477
  45.8 0.8 %collective-permute-start.11 = (bf16[1,288,128]{2,1,0:T(8,128)(2,1)S(1)}, bf16[1,288,128]{2,1,0:T(8,128)(2,1)S(1)}, u32[]{:S(2)}, u32[]{:S(2)}) collective-permute-start(bf16[1,288,128]{2,1,0:T(8,128)(2,1)S(1)} %get-tuple-element.102.refs_0_), channel_id=1, source_target_pairs={{0,8},{4,12},{8,0},{12,4},{16,24},{20,28},{24,16},{28,20},{1,9},{5... | collective-permute-start | bytes 221192 | tf_op jit(solution)/shard_map/ppermute | solution.py:477
  46.6 1.5 %collective-permute-done.14 = bf16[544,128]{1,0:T(8,128)(2,1)S(1)} collective-permute-done((bf16[544,128]{1,0:T(8,128)(2,1)S(1)}, bf16[544,128]{1,0:T(8,128)(2,1)S(1)}, u32[]{:S(2)}, u32[]{:S(2)}) %collective-permute-start.14) | collective-permute-done | bytes 139296 | tf_op jit(solution)/shard_map/ppermute | solution.py:342
  48.1 1.7 %collective-permute-start.17 = (bf16[1,288,128]{2,1,0:T(8,128)(2,1)S(1)}, bf16[1,288,128]{2,1,0:T(8,128)(2,1)S(1)}, u32[]{:S(2)}, u32[]{:S(2)}) collective-permute-start(bf16[1,288,128]{2,1,0:T(8,128)(2,1)S(1)} %slice_bitcast_fusion.12.refs_0_), channel_id=1, source_target_pairs={{0,24},{4,28},{8,16},{12,20},{16,8},{20,12},{24,0},{28,4},{1,25},{... | collective-permute-start | bytes 221192 | tf_op jit(solution)/shard_map/ppermute | solution.py:477
  49.8 0.7 %collective-permute-start.16 = (bf16[1,288,128]{2,1,0:T(8,128)(2,1)S(1)}, bf16[1,288,128]{2,1,0:T(8,128)(2,1)S(1)}, u32[]{:S(2)}, u32[]{:S(2)}) collective-permute-start(bf16[1,288,128]{2,1,0:T(8,128)(2,1)S(1)} %slice_bitcast_fusion.12.refs_0_), channel_id=1, source_target_pairs={{0,16},{4,20},{8,24},{12,28},{16,0},{20,4},{24,8},{28,12},{1,17},{... | collective-permute-start | bytes 221192 | tf_op jit(solution)/shard_map/ppermute | solution.py:477
  50.5 0.0 collective-permute-done.13.refs_3_
  50.5 1.1 %collective-permute-start.15 = (bf16[1,288,128]{2,1,0:T(8,128)(2,1)S(1)}, bf16[1,288,128]{2,1,0:T(8,128)(2,1)S(1)}, u32[]{:S(2)}, u32[]{:S(2)}) collective-permute-start(bf16[1,288,128]{2,1,0:T(8,128)(2,1)S(1)} %slice_bitcast_fusion.12.refs_0_), channel_id=1, source_target_pairs={{0,8},{4,12},{8,0},{12,4},{16,24},{20,28},{24,16},{28,20},{1,9},{5... | collective-permute-start | bytes 221192 | tf_op jit(solution)/shard_map/ppermute | solution.py:477
  51.6 0.1 collective-permute-start.20
  51.7 1.0 %collective-permute-start.19 = (bf16[256,128]{1,0:T(8,128)(2,1)S(1)}, bf16[256,128]{1,0:T(8,128)(2,1)S(1)}, u32[]{:S(2)}, u32[]{:S(2)}) collective-permute-start(bf16[256,128]{1,0:T(8,128)(2,1)S(1)} %pad_maximum_fusion.2), channel_id=1, source_target_pairs={{0,2},{1,3},{2,0},{3,1},{4,6},{5,7},{6,4},{7,5},{8,10},{9,11},{10,... | collective-permute-start | bytes 196616 | tf_op jit(solution)/shard_map/ppermute | solution.py:342
  52.7 0.9 %finish.3.refs_8_ = f32[9,256,256]{2,1,0:T(8,128)} custom-call(bf16[1,288,128]{2,1,0:T(8,128)(2,1)S(1)} %get-tuple-element.102.refs_0_, bf16[1,288,128]{2,1,0:T(8,128)(2,1)S(1)} %collective-permute-done.11.refs_1_, bf16[1,288,128]{2,1,0:T(8,128)(2,1)S(1)} %collective-permute-done.12.refs_2_, bf16[1,288,128]{2,1,0:T(8,128)(2,1)S(1)} %collective-permute-done.13.refs_3_), custom_call_target="tpu_custom_call" | custom-call | flops 1048576 | bytes 4194304 | tf_op jit(solution)/shard_map/finish/pallas_call | solution.py:532
  53.7 0.5 collective-permute-done.16.refs_2_
  54.2 0.7 %collective-permute-done.15.refs_1_ = bf16[1,288,128]{2,1,0:T(8,128)(2,1)S(1)} collective-permute-done((bf16[1,288,128]{2,1,0:T(8,128)(2,1)S(1)}, bf16[1,288,128]{2,1,0:T(8,128)(2,1)S(1)}, u32[]{:S(2)}, u32[]{:S(2)}) %collective-permute-start.15) | collective-permute-done | bytes 73760 | tf_op jit(solution)/shard_map/ppermute | solution.py:477
  54.9 0.1 collective-permute-start.18
  55.0 1.2 %finish.4.refs_8_ = f32[9,256,256]{2,1,0:T(8,128)} custom-call(bf16[1,288,128]{2,1,0:T(8,128)(2,1)S(1)} %slice_bitcast_fusion.12.refs_0_, bf16[1,288,128]{2,1,0:T(8,128)(2,1)S(1)} %collective-permute-done.15.refs_1_, bf16[1,288,128]{2,1,0:T(8,128)(2,1)S(1)} %collective-permute-done.16.refs_2_, ...), custom_call_target="tpu_custom_call", output_to_operand_aliasing={{}: (8, {})} | custom-call | flops 1048576 | bytes 4194304 | tf_op jit(solution)/shard_map/finish/pallas_call | solution.py:532
  56.2 2.3 %collective-permute-done.19 = bf16[256,128]{1,0:T(8,128)(2,1)S(1)} collective-permute-done((bf16[256,128]{1,0:T(8,128)(2,1)S(1)}, bf16[256,128]{1,0:T(8,128)(2,1)S(1)}, u32[]{:S(2)}, u32[]{:S(2)}) %collective-permute-start.19) | collective-permute-done | bytes 65568 | tf_op jit(solution)/shard_map/ppermute | solution.py:342
  58.6 1.0 %finish.5 = (f32[9,256,256]{2,1,0:T(8,128)}, bf16[2,128,256]{2,1,0:T(8,128)(2,1)}) custom-call(bf16[1,288,128]{2,1,0:T(8,128)(2,1)S(1)} %get-tuple-element.113.refs_0_, bf16[1,288,128]{2,1,0:T(8,128)(2,1)S(1)} %get-tuple-element.112.refs_1_, bf16[1,288,128]{2,1,0:T(8,128)(2,1)S(1)} %get-tuple-element.111.refs_2_, ...), custom_call_target="tpu_custom_call", output_to_operand_aliasing={{0}: (8, {})} | custom-call | flops 1048576 | bytes 4194304 | tf_op jit(solution)/shard_map/finish/pallas_call | solution.py:532
  (34 shorter events, 0.3 us)
Async XLA Ops:
  0.6 8.0 %copy-start.2 = (bf16[1,32,128,256]{3,2,1,0:T(8,128)(2,1)S(1)}, bf16[1,32,128,256]{3,2,1,0:T(8,128)(2,1)}, u32[]{:S(2)}) copy-start(bf16[1,32,128,256]{3,2,1,0:T(8,128)(2,1)} %param.11) | copy-start | bytes 6291460
  0.6 8.0 %copy-start.3 = (f32[1000,256]{1,0:T(8,128)S(1)}, f32[1000,256]{1,0:T(8,128)}, u32[]{:S(2)}) copy-start(f32[1000,256]{1,0:T(8,128)} %scales.1) | copy-start | bytes 3072004
  2.2 7.5 %collective-permute-start = (bf16[96,256]{1,0:T(8,128)(2,1)S(1)}, bf16[96,256]{1,0:T(8,128)(2,1)S(1)}, u32[]{:S(2)}, u32[]{:S(2)}) collective-permute-start(bf16[96,256]{1,0:T(8,128)(2,1)S(1)} %get-tuple-element.54), channel_id=1, source_target_pairs={{0,3},{1,2},{2,1},{3,0},{4,7},{5,6},{6,5},{7,4},{8,11},{9,10},{10,... | collective-permute-start | bytes 147464 | tf_op jit(solution)/shard_map/ppermute | solution.py:342
  7.3 4.1 %collective-permute-start.1 = (bf16[96,256]{1,0:T(8,128)(2,1)S(1)}, bf16[96,256]{1,0:T(8,128)(2,1)S(1)}, u32[]{:S(2)}, u32[]{:S(2)}) collective-permute-start(bf16[96,256]{1,0:T(8,128)(2,1)S(1)} %get-tuple-element.55), channel_id=1, source_target_pairs={{0,1},{1,0},{2,3},{3,2},{4,5},{5,4},{6,7},{7,6},{8,9},{9,8},{10,11... | collective-permute-start | bytes 147464 | tf_op jit(solution)/shard_map/ppermute | solution.py:342
  7.3 5.8 %collective-permute-start.2 = (bf16[64,256]{1,0:T(8,128)(2,1)S(1)}, bf16[64,256]{1,0:T(8,128)(2,1)S(1)}, u32[]{:S(2)}, u32[]{:S(2)}) collective-permute-start(bf16[64,256]{1,0:T(8,128)(2,1)S(1)} %get-tuple-element.59), channel_id=1, source_target_pairs={{0,2},{1,3},{2,0},{3,1},{4,6},{5,7},{6,4},{7,5},{8,10},{9,11},{10,... | collective-permute-start | bytes 98312 | tf_op jit(solution)/shard_map/ppermute | solution.py:342
  11.4 1.7 %copy-start = (bf16[1,32,128,256]{3,2,1,0:T(8,128)(2,1)S(1)}, bf16[1,32,128,256]{3,2,1,0:T(8,128)(2,1)}, u32[]{:S(2)}) copy-start(bf16[1,32,128,256]{3,2,1,0:T(8,128)(2,1)} %param.6) | copy-start | bytes 6291460
  11.5 5.4 %collective-permute-start.3 = (bf16[144,256]{1,0:T(8,128)(2,1)S(1)}, bf16[144,256]{1,0:T(8,128)(2,1)S(1)}, u32[]{:S(2)}, u32[]{:S(2)}) collective-permute-start(bf16[144,256]{1,0:T(8,128)(2,1)S(1)} %get-tuple-element.61), channel_id=1, source_target_pairs={{4,8},{12,16},{20,24},{28,0},{8,4},{16,12},{24,20},{0,28},{5,9},{1... | collective-permute-start | bytes 221192 | tf_op jit(solution)/shard_map/ppermute | solution.py:385
  12.2 4.8 %collective-permute-start.4 = (bf16[144,256]{1,0:T(8,128)(2,1)S(1)}, bf16[144,256]{1,0:T(8,128)(2,1)S(1)}, u32[]{:S(2)}, u32[]{:S(2)}) collective-permute-start(bf16[144,256]{1,0:T(8,128)(2,1)S(1)} %get-tuple-element.62), channel_id=1, source_target_pairs={{0,4},{4,0},{8,12},{12,8},{16,20},{20,16},{24,28},{28,24},{1,5},{5... | collective-permute-start | bytes 221192 | tf_op jit(solution)/shard_map/ppermute | solution.py:388
  18.6 3.0 %collective-permute-start.5 = (bf16[4,2,288,128]{3,2,1,0:T(8,128)(2,1)S(1)}, bf16[4,2,288,128]{3,2,1,0:T(8,128)(2,1)S(1)}, u32[]{:S(2)}, u32[]{:S(2)}) collective-permute-start(bf16[4,2,288,128]{3,2,1,0:T(8,128)(2,1)S(1)} %get-tuple-element.67), channel_id=1, source_target_pairs={{0,4},{4,0},{8,12},{12,8},{16,20},{20,16},{24,28},{28,24},{1,5},{5... | collective-permute-start | bytes 1769480 | tf_op jit(solution)/shard_map/ppermute | solution.py:474
  21.6 3.8 %copy-start.1 = (bf16[3,3,256,256]{3,2,1,0:T(8,128)(2,1)S(1)}, bf16[3,3,256,256]{3,2,1,0:T(8,128)(2,1)}, u32[]{:S(2)}) copy-start(bf16[3,3,256,256]{3,2,1,0:T(8,128)(2,1)} %param.8) | copy-start | bytes 3538948
  21.9 9.0 %collective-permute-start.8 = (bf16[2,288,128]{2,1,0:T(8,128)(2,1)S(1)}, bf16[2,288,128]{2,1,0:T(8,128)(2,1)S(1)}, u32[]{:S(2)}, u32[]{:S(2)}) collective-permute-start(bf16[2,288,128]{2,1,0:T(8,128)(2,1)S(1)} %get-tuple-element.103), channel_id=1, source_target_pairs={{0,24},{4,28},{8,16},{12,20},{16,8},{20,12},{24,0},{28,4},{1,25},{... | collective-permute-start | bytes 442376 | tf_op jit(solution)/shard_map/ppermute | solution.py:477
  23.7 8.5 %collective-permute-start.7 = (bf16[2,288,128]{2,1,0:T(8,128)(2,1)S(1)}, bf16[2,288,128]{2,1,0:T(8,128)(2,1)S(1)}, u32[]{:S(2)}, u32[]{:S(2)}) collective-permute-start(bf16[2,288,128]{2,1,0:T(8,128)(2,1)S(1)} %get-tuple-element.104), channel_id=1, source_target_pairs={{0,16},{4,20},{8,24},{12,28},{16,0},{20,4},{24,8},{28,12},{1,17},{... | collective-permute-start | bytes 442376 | tf_op jit(solution)/shard_map/ppermute | solution.py:477
  24.3 7.9 %collective-permute-start.6 = (bf16[2,288,128]{2,1,0:T(8,128)(2,1)S(1)}, bf16[2,288,128]{2,1,0:T(8,128)(2,1)S(1)}, u32[]{:S(2)}, u32[]{:S(2)}) collective-permute-start(bf16[2,288,128]{2,1,0:T(8,128)(2,1)S(1)} %get-tuple-element.105), channel_id=1, source_target_pairs={{0,8},{4,12},{8,0},{12,4},{16,24},{20,28},{24,16},{28,20},{1,9},{5... | collective-permute-start | bytes 442376 | tf_op jit(solution)/shard_map/ppermute | solution.py:477
  32.3 4.4 %collective-permute-start.9 = (bf16[1,288,128]{2,1,0:T(8,128)(2,1)S(1)}, bf16[1,288,128]{2,1,0:T(8,128)(2,1)S(1)}, u32[]{:S(2)}, u32[]{:S(2)}) collective-permute-start(bf16[1,288,128]{2,1,0:T(8,128)(2,1)S(1)} %slice.105), channel_id=1, source_target_pairs={{0,1},{1,0},{2,3},{3,2},{4,5},{5,4},{6,7},{7,6},{8,9},{9,8},{10,11... | collective-permute-start | bytes 221192 | tf_op jit(solution)/shard_map/ppermute | solution.py:342
  36.7 6.1 %collective-permute-start.10 = (bf16[1,288,128]{2,1,0:T(8,128)(2,1)S(1)}, bf16[1,288,128]{2,1,0:T(8,128)(2,1)S(1)}, u32[]{:S(2)}, u32[]{:S(2)}) collective-permute-start(bf16[1,288,128]{2,1,0:T(8,128)(2,1)S(1)} %add_convert_fusion.2.after), channel_id=1, source_target_pairs={{0,2},{1,3},{2,0},{3,1},{4,6},{5,7},{6,4},{7,5},{8,10},{9,11},{10,... | collective-permute-start | bytes 221192 | tf_op jit(solution)/shard_map/ppermute | solution.py:342
  42.9 5.1 %collective-permute-start.14 = (bf16[544,128]{1,0:T(8,128)(2,1)S(1)}, bf16[544,128]{1,0:T(8,128)(2,1)S(1)}, u32[]{:S(2)}, u32[]{:S(2)}) collective-permute-start(bf16[544,128]{1,0:T(8,128)(2,1)S(1)} %constant_dynamic-update-slice_fusion), channel_id=1, source_target_pairs={{0,1},{1,0},{2,3},{3,2},{4,5},{5,4},{6,7},{7,6},{8,9},{9,8},{10,11... | collective-permute-start | bytes 417800 | tf_op jit(solution)/shard_map/ppermute | solution.py:342
  43.1 7.4 %collective-permute-start.13 = (bf16[1,288,128]{2,1,0:T(8,128)(2,1)S(1)}, bf16[1,288,128]{2,1,0:T(8,128)(2,1)S(1)}, u32[]{:S(2)}, u32[]{:S(2)}) collective-permute-start(bf16[1,288,128]{2,1,0:T(8,128)(2,1)S(1)} %get-tuple-element.102.refs_0_), channel_id=1, source_target_pairs={{0,24},{4,28},{8,16},{12,20},{16,8},{20,12},{24,0},{28,4},{1,25},{... | collective-permute-start | bytes 221192 | tf_op jit(solution)/shard_map/ppermute | solution.py:477
  44.9 6.7 %collective-permute-start.12 = (bf16[1,288,128]{2,1,0:T(8,128)(2,1)S(1)}, bf16[1,288,128]{2,1,0:T(8,128)(2,1)S(1)}, u32[]{:S(2)}, u32[]{:S(2)}) collective-permute-start(bf16[1,288,128]{2,1,0:T(8,128)(2,1)S(1)} %get-tuple-element.102.refs_0_), channel_id=1, source_target_pairs={{0,16},{4,20},{8,24},{12,28},{16,0},{20,4},{24,8},{28,12},{1,17},{... | collective-permute-start | bytes 221192 | tf_op jit(solution)/shard_map/ppermute | solution.py:477
  45.8 5.7 %collective-permute-start.11 = (bf16[1,288,128]{2,1,0:T(8,128)(2,1)S(1)}, bf16[1,288,128]{2,1,0:T(8,128)(2,1)S(1)}, u32[]{:S(2)}, u32[]{:S(2)}) collective-permute-start(bf16[1,288,128]{2,1,0:T(8,128)(2,1)S(1)} %get-tuple-element.102.refs_0_), channel_id=1, source_target_pairs={{0,8},{4,12},{8,0},{12,4},{16,24},{20,28},{24,16},{28,20},{1,9},{5... | collective-permute-start | bytes 221192 | tf_op jit(solution)/shard_map/ppermute | solution.py:477
  48.1 5.6 %collective-permute-start.17 = (bf16[1,288,128]{2,1,0:T(8,128)(2,1)S(1)}, bf16[1,288,128]{2,1,0:T(8,128)(2,1)S(1)}, u32[]{:S(2)}, u32[]{:S(2)}) collective-permute-start(bf16[1,288,128]{2,1,0:T(8,128)(2,1)S(1)} %slice_bitcast_fusion.12.refs_0_), channel_id=1, source_target_pairs={{0,24},{4,28},{8,16},{12,20},{16,8},{20,12},{24,0},{28,4},{1,25},{... | collective-permute-start | bytes 221192 | tf_op jit(solution)/shard_map/ppermute | solution.py:477
  49.8 4.4 %collective-permute-start.16 = (bf16[1,288,128]{2,1,0:T(8,128)(2,1)S(1)}, bf16[1,288,128]{2,1,0:T(8,128)(2,1)S(1)}, u32[]{:S(2)}, u32[]{:S(2)}) collective-permute-start(bf16[1,288,128]{2,1,0:T(8,128)(2,1)S(1)} %slice_bitcast_fusion.12.refs_0_), channel_id=1, source_target_pairs={{0,16},{4,20},{8,24},{12,28},{16,0},{20,4},{24,8},{28,12},{1,17},{... | collective-permute-start | bytes 221192 | tf_op jit(solution)/shard_map/ppermute | solution.py:477
  50.5 4.4 %collective-permute-start.15 = (bf16[1,288,128]{2,1,0:T(8,128)(2,1)S(1)}, bf16[1,288,128]{2,1,0:T(8,128)(2,1)S(1)}, u32[]{:S(2)}, u32[]{:S(2)}) collective-permute-start(bf16[1,288,128]{2,1,0:T(8,128)(2,1)S(1)} %slice_bitcast_fusion.12.refs_0_), channel_id=1, source_target_pairs={{0,8},{4,12},{8,0},{12,4},{16,24},{20,28},{24,16},{28,20},{1,9},{5... | collective-permute-start | bytes 221192 | tf_op jit(solution)/shard_map/ppermute | solution.py:477
  51.6 3.3 %collective-permute-start.20 = (bf16[4,1,288,128]{3,2,1,0:T(8,128)(2,1)S(1)}, bf16[4,1,288,128]{3,2,1,0:T(8,128)(2,1)S(1)}, u32[]{:S(2)}, u32[]{:S(2)}) collective-permute-start(bf16[4,1,288,128]{3,2,1,0:T(8,128)(2,1)S(1)} %pad_maximum_fusion.1), channel_id=1, source_target_pairs={{0,4},{4,0},{8,12},{12,8},{16,20},{20,16},{24,28},{28,24},{1,5},{5... | collective-permute-start | bytes 884744 | tf_op jit(solution)/shard_map/ppermute | solution.py:474
  51.7 6.8 %collective-permute-start.19 = (bf16[256,128]{1,0:T(8,128)(2,1)S(1)}, bf16[256,128]{1,0:T(8,128)(2,1)S(1)}, u32[]{:S(2)}, u32[]{:S(2)}) collective-permute-start(bf16[256,128]{1,0:T(8,128)(2,1)S(1)} %pad_maximum_fusion.2), channel_id=1, source_target_pairs={{0,2},{1,3},{2,0},{3,1},{4,6},{5,7},{6,4},{7,5},{8,10},{9,11},{10,... | collective-permute-start | bytes 196616 | tf_op jit(solution)/shard_map/ppermute | solution.py:342
  54.9 3.7 %collective-permute-start.18 = (bf16[4,1,288,128]{3,2,1,0:T(8,128)(2,1)S(1)}, bf16[4,1,288,128]{3,2,1,0:T(8,128)(2,1)S(1)}, u32[]{:S(2)}, u32[]{:S(2)}) collective-permute-start(bf16[4,1,288,128]{3,2,1,0:T(8,128)(2,1)S(1)} %pad_maximum_fusion), channel_id=1, source_target_pairs={{0,4},{4,0},{8,12},{12,8},{16,20},{20,16},{24,28},{28,24},{1,5},{5... | collective-permute-start | bytes 884744 | tf_op jit(solution)/shard_map/ppermute | solution.py:474

commit v6 on v5

--- a/solution.py
+++ b/solution.py
@@ -237,7 +237,7 @@
 
 
 def strip_order(n):
-    return list(range(n - 1, 0, -2)) + list(range(n - 2, -1, -2))
+    return list(range(n - 1, -1, -1))
 
 
 def input_kernel(first, size, n, after, moved, fine, strip, weight, *refs):
@@ -476,6 +476,25 @@
     def plane_swap(x, s):
         return lax.ppermute(x, "row", xor_pairs(nrow, 2 * s))
 
+    held = {s: [] for s in range(n)}
+
+    def hop(bit, extra):
+        sent = []
+        for s in [s for s in held if s & bit]:
+            sent += [(s, src, x) for src, x in held.pop(s) + [(0, pooled_strip(s))]]
+        return sent, col_swap(jnp.concatenate(extra + [x for _, _, x in sent]), bit)
+
+    def land(bit, sent, got, at):
+        for s, src, x in sent:
+            held[s ^ bit].append((src ^ bit, got[at : at + x.shape[0]]))
+            at += x.shape[0]
+
+    def ride(bit, total):
+        sent, got = hop(bit, [total.reshape(-1, half)])
+        at = total.size // half
+        land(bit, sent, got, at)
+        return got[:at].reshape(total.shape)
+
     sizes = piece_sizes(rows // 4)
     total = add(keep, core_swap(send))
     got = [plane_swap(total[s], s) for s in range(1, planes)]
@@ -486,27 +505,13 @@
     bit = halves // 2
     while bit:
         got = [col_swap(total[bit:], bit)]
+        if bit == halves // 2:
+            sent, far = hop(halves, [])
         total = add(total[:bit], *beside(got, sizes[1] if bit == 1 else 0, total))
         bit //= 2
-    total = add(total, *beside([col_swap(total, halves)], sizes[2], total))
-
-    strips = {s: [(0, pooled_strip(s))] for s in range(n)}
-
-    def hop(bit, extra):
-        sent = [(s, src, x) for s in strips if s & bit for src, x in strips[s]]
-        return sent, col_swap(jnp.concatenate(extra + [x for _, _, x in sent]), bit)
-
-    def land(bit, sent, got, at):
-        for s, src, x in sent:
-            strips.pop(s, None)
-            strips[s ^ bit].append((src ^ bit, got[at : at + x.shape[0]]))
-            at += x.shape[0]
-
-    def ride(bit, total):
-        sent, got = hop(bit, [total.reshape(-1, half)])
-        at = total.size // half
-        land(bit, sent, got, at)
-        return got[:at].reshape(total.shape)
+    got = beside([col_swap(total, halves)], sizes[2], total)
+    total = add(total, *got)
+    land(halves, sent, far, 0)
 
     bit = 1
     while bit < halves // 2:
@@ -523,7 +528,8 @@
     if aligned:
         waves[0][1:], waves[1][0] = lax.optimization_barrier((waves[0][1:], waves[1][0]))
 
-    sent, hopped = hop(bit * 2, [])
+    parts = held[0] + [(0, pooled_strip(0))]
+    parts = [x for _, x in sorted(parts, key=lambda pair: pair[0])]
     pixels = rows * nrow * width * n
 
     def finish(out, pieces, spots, parts=()):
@@ -554,9 +560,6 @@
         places = [(0, *spot) for spot in here] + [(1, *spot) for spot in spots]
         out = finish(out, wave + others, tuple(places))
         others, spots = [swapped[i] for i in range(len(wave))], here
-    last, out = lax.optimization_barrier((hopped, out))
-    land(bit * 2, sent, last, 0)
-    parts = [x for _, x in sorted(strips[0], key=lambda pair: pair[0])]
     grad_weight, grad_coarse = finish(out, others, tuple((1, *spot) for spot in spots), parts)
     return (done[0][None], grad_coarse[None], grad_weight.reshape(3, 3, ch, ch))
 

time: 59.7 us -> 57.5 us (0.963)
  waiting for transfers between devices: 13.9 us -> 11.1 us
    ppermute x7, waiting for transfers between devices: 10.8 us -> 7.35 us  [col_swap(): return lax.ppermute(x, 'col', xor_pairs(n, s))]
  transfers between devices with their start and end apart: 21 -> 21, of which waited for: 9 -> 10; matrix products, arithmetic and copies ran while one was open for 0% -> 0% of each run, Pallas kernels for 31% -> 32%
where the time goes in v6:
time: 57.5 us; the launch traced here: 57.3 us
  Pallas kernels  22.5 us (39%)
  starting transfers between devices  21.6 us (38%)
  waiting for transfers between devices  11.1 us (19%)
  between operations  1.57 us (3%)
    ppermute x9, starting transfers between devices, plane_swap(): return lax.ppermute(x, 'row', xor_pairs(nrow, 2 * s))  10.6 us
    ppermute x7, starting transfers between devices, col_swap(): return lax.ppermute(x, 'col', xor_pairs(n, s))  9.12 us
    pallas_call x3, Pallas kernels, input_piece(): pl.pallas_call(functools.partial(input_kernel, made, size, n), out_shape=...  8.93 us
    ppermute x7, waiting for transfers between devices, col_swap(): return lax.ppermute(x, 'col', xor_pairs(n, s))  7.35 us
    pallas_call x1, Pallas kernels, per_device(): pl.pallas_call(functools.partial(prepare_kernel, n, cr), out_shape=[shape...  3.18 us
    pallas_call x3, Pallas kernels, finish(): pl.pallas_call(functools.partial(finish_kernel, float(pixels) ** (-0.5),...  3.15 us
    pallas_call x1, Pallas kernels, per_device(): pl.pallas_call(mine_kernel, out_shape=part, in_specs=[vmem()] * 3, out_sp...  2.93 us
    ppermute x9, waiting for transfers between devices, plane_swap(): return lax.ppermute(x, 'row', xor_pairs(nrow, 2 * s))  2.88 us
  transfers between devices with their start and end apart: 21, of which 10 were waited for; matrix products, arithmetic and copies ran while one was open for 0% of the time, Pallas kernels for 32%

profile of v6, /device:TPU:0, one launch (start us, length us, event | category | flops | bytes accessed | tf_op | source)
XLA Modules:
  0.0 57.3 jit_solution(9903443812058270692)
XLA Ops:
  0.7 1.6 %start.1 = (bf16[64,256]{1,0:T(8,128)(2,1)S(1)}, bf16[96,256]{1,0:T(8,128)(2,1)S(1)}, bf16[64,256]{1,0:T(8,128)(2,1)S(1)}, bf16[96,256]{1,0:T(8,128)(2,1)S(1)}) custom-call(bf16[32,128,256]{2,1,0:T(8,128)(2,1)} %bitcast.60, bf16[2,128,256]{2,1,0:T(8,128)(2,1)} %bitcast.81), custom_call_target="tpu_custom_call" | custom-call | flops 2147483648 | bytes 4194304 | tf_op jit(solution)/shard_map/start/pallas_call | solution.py:344
  2.2 5.1 %collective-permute-start = (bf16[96,256]{1,0:T(8,128)(2,1)S(1)}, bf16[96,256]{1,0:T(8,128)(2,1)S(1)}, u32[]{:S(2)}, u32[]{:S(2)}) collective-permute-start(bf16[96,256]{1,0:T(8,128)(2,1)S(1)} %get-tuple-element.52), channel_id=1, source_target_pairs={{0,3},{1,2},{2,1},{3,0},{4,7},{5,6},{6,5},{7,4},{8,11},{9,10},{10,... | collective-permute-start | bytes 147464 | tf_op jit(solution)/shard_map/ppermute | solution.py:342
  7.3 0.0 collective-permute-start.1
  7.3 0.6 %collective-permute-start.2 = (bf16[64,256]{1,0:T(8,128)(2,1)S(1)}, bf16[64,256]{1,0:T(8,128)(2,1)S(1)}, u32[]{:S(2)}, u32[]{:S(2)}) collective-permute-start(bf16[64,256]{1,0:T(8,128)(2,1)S(1)} %get-tuple-element.57), channel_id=1, source_target_pairs={{0,2},{1,3},{2,0},{3,1},{4,6},{5,7},{6,4},{7,5},{8,10},{9,11},{10,... | collective-permute-start | bytes 98312 | tf_op jit(solution)/shard_map/ppermute | solution.py:342
  8.7 1.1 %load.1 = (bf16[3,34,128,256]{3,2,1,0:T(8,128)(2,1)S(1)}, f32[1,256]{1,0:T(1,128)S(1)}) custom-call(s32[1]{0:T(128)S(6)} %copy.21.steps, bf16[32,128,256]{2,1,0:T(8,128)(2,1)S(1)} %bitcast.61, f32[1000,256]{1,0:T(8,128)S(1)} %copy-done.3), custom_call_target="tpu_custom_call" | custom-call | flops 1048576 | bytes 4194304 | tf_op jit(solution)/shard_map/load/pallas_call | solution.py:360
  9.7 0.0 collective-permute-done.refs_0_.refs_3_
  9.7 1.7 %collective-permute-done.1.refs_1_ = bf16[96,256]{1,0:T(8,128)(2,1)S(1)} collective-permute-done((bf16[96,256]{1,0:T(8,128)(2,1)S(1)}, bf16[96,256]{1,0:T(8,128)(2,1)S(1)}, u32[]{:S(2)}, u32[]{:S(2)}) %collective-permute-start.1) | collective-permute-done | bytes 49184 | tf_op jit(solution)/shard_map/ppermute | solution.py:342
  11.4 0.1 edges.1
  11.5 0.7 %collective-permute-start.3 = (bf16[144,256]{1,0:T(8,128)(2,1)S(1)}, bf16[144,256]{1,0:T(8,128)(2,1)S(1)}, u32[]{:S(2)}, u32[]{:S(2)}) collective-permute-start(bf16[144,256]{1,0:T(8,128)(2,1)S(1)} %get-tuple-element.59), channel_id=1, source_target_pairs={{4,8},{12,16},{20,24},{28,0},{8,4},{16,12},{24,20},{0,28},{5,9},{1... | collective-permute-start | bytes 221192 | tf_op jit(solution)/shard_map/ppermute | solution.py:385
  12.2 1.0 %collective-permute-start.4 = (bf16[144,256]{1,0:T(8,128)(2,1)S(1)}, bf16[144,256]{1,0:T(8,128)(2,1)S(1)}, u32[]{:S(2)}, u32[]{:S(2)}) collective-permute-start(bf16[144,256]{1,0:T(8,128)(2,1)S(1)} %get-tuple-element.60), channel_id=1, source_target_pairs={{0,4},{4,0},{8,12},{12,8},{16,20},{20,16},{24,28},{28,24},{1,5},{5... | collective-permute-start | bytes 221192 | tf_op jit(solution)/shard_map/ppermute | solution.py:388
  13.2 3.2 %prepare.1 = (bf16[3,34,128,256]{3,2,1,0:T(8,128)(2,1)S(1)}, bf16[256,4096]{1,0:T(8,128)(2,1)S(1)}, bf16[8,32,256]{2,1,0:T(8,128)(2,1)S(1)}, f32[5,256,256]{2,1,0:T(8,128)S(1)}) custom-call(bf16[32,128,256]{2,1,0:T(8,128)(2,1)S(1)} %bitcast.53, f32[32,256]{1,0:T(8,128)S(1)} %get-tuple-element.54.left, ...), custom_call_target="tpu_custom_call", output_to_operand_aliasing={{0}: (3, {})} | custom-call | flops 4294967296 | bytes 4194304 | tf_op jit(solution)/shard_map/prepare/pallas_call | solution.py:391
  16.4 0.6 collective-permute-done.3.two
  16.9 0.0 collective-permute-done.4.one
  16.9 1.7 %weight_other.1 = (bf16[4,2,288,128]{3,2,1,0:T(8,128)(2,1)S(1)}, f32[256,128]{1,0:T(8,128)S(1)}, bf16[3,34,128,256]{3,2,1,0:T(8,128)(2,1)S(1)}) custom-call(bf16[256,4096]{1,0:T(8,128)(2,1)S(1)} %get-tuple-element.58.act_t, bf16[144,256]{1,0:T(8,128)(2,1)S(1)} %collective-permute-done.3.two, ...), custom_call_target="tpu_custom_call", output_to_operand_aliasing={{2}: (4, {})} | custom-call | flops 603979776 | bytes 8388608 | tf_op jit(solution)/shard_map/weight_other/pallas_call | solution.py:414
  18.6 0.1 collective-permute-start.5
  18.7 2.9 %weight_mine.1 = bf16[4,2,288,128]{3,2,1,0:T(8,128)(2,1)S(1)} custom-call(bf16[256,4096]{1,0:T(8,128)(2,1)S(1)} %get-tuple-element.58.act_t, f32[256,128]{1,0:T(8,128)S(1)} %get-tuple-element.63.rest, bf16[3,34,128,256]{3,2,1,0:T(8,128)(2,1)S(1)} %get-tuple-element.64.moved), custom_call_target="tpu_custom_call" | custom-call | flops 2147483648 | bytes 8388608 | tf_op jit(solution)/shard_map/weight_mine/pallas_call | solution.py:424
  21.6 0.0 copy-start.1
  21.7 0.2 add_convert_fusion.after
  21.9 1.8 %collective-permute-start.8 = (bf16[2,288,128]{2,1,0:T(8,128)(2,1)S(1)}, bf16[2,288,128]{2,1,0:T(8,128)(2,1)S(1)}, u32[]{:S(2)}, u32[]{:S(2)}) collective-permute-start(bf16[2,288,128]{2,1,0:T(8,128)(2,1)S(1)} %get-tuple-element.97), channel_id=1, source_target_pairs={{0,24},{4,28},{8,16},{12,20},{16,8},{20,12},{24,0},{28,4},{1,25},{... | collective-permute-start | bytes 442376 | tf_op jit(solution)/shard_map/ppermute | solution.py:477
  23.7 0.7 %collective-permute-start.7 = (bf16[2,288,128]{2,1,0:T(8,128)(2,1)S(1)}, bf16[2,288,128]{2,1,0:T(8,128)(2,1)S(1)}, u32[]{:S(2)}, u32[]{:S(2)}) collective-permute-start(bf16[2,288,128]{2,1,0:T(8,128)(2,1)S(1)} %get-tuple-element.98), channel_id=1, source_target_pairs={{0,16},{4,20},{8,24},{12,28},{16,0},{20,4},{24,8},{28,12},{1,17},{... | collective-permute-start | bytes 442376 | tf_op jit(solution)/shard_map/ppermute | solution.py:477
  24.3 1.1 %collective-permute-start.6 = (bf16[2,288,128]{2,1,0:T(8,128)(2,1)S(1)}, bf16[2,288,128]{2,1,0:T(8,128)(2,1)S(1)}, u32[]{:S(2)}, u32[]{:S(2)}) collective-permute-start(bf16[2,288,128]{2,1,0:T(8,128)(2,1)S(1)} %get-tuple-element.99), channel_id=1, source_target_pairs={{0,8},{4,12},{8,0},{12,4},{16,24},{20,28},{24,16},{28,20},{1,9},{5... | collective-permute-start | bytes 442376 | tf_op jit(solution)/shard_map/ppermute | solution.py:477
  25.4 5.5 %input_grad.3 = (bf16[32,128,256]{2,1,0:T(8,128)(2,1)}, bf16[6,2,32,128]{3,2,1,0:T(8,128)(2,1)S(1)}) custom-call(bf16[4,2,288,128]{3,2,1,0:T(8,128)(2,1)S(1)} %add_convert_fusion.after, bf16[3,34,128,256]{3,2,1,0:T(8,128)(2,1)S(1)} %get-tuple-element.64.moved, bf16[32,128,256]{2,1,0:T(8,128)(2,1)S(1)} %bitcast.54, ...), custom_call_target="tpu_custom_call" | custom-call | flops 3623878656 | bytes 4194304 | tf_op jit(solution)/shard_map/input_grad/pallas_call | solution.py:438
  30.9 1.3 %collective-permute-done.7 = bf16[2,288,128]{2,1,0:T(8,128)(2,1)S(1)} collective-permute-done((bf16[2,288,128]{2,1,0:T(8,128)(2,1)S(1)}, bf16[2,288,128]{2,1,0:T(8,128)(2,1)S(1)}, u32[]{:S(2)}, u32[]{:S(2)}) %collective-permute-start.7) | collective-permute-done | bytes 147488 | tf_op jit(solution)/shard_map/ppermute | solution.py:477
  32.2 0.1 fusion.2.after
  32.3 0.9 %collective-permute-start.9 = (bf16[1,288,128]{2,1,0:T(8,128)(2,1)S(1)}, bf16[1,288,128]{2,1,0:T(8,128)(2,1)S(1)}, u32[]{:S(2)}, u32[]{:S(2)}) collective-permute-start(bf16[1,288,128]{2,1,0:T(8,128)(2,1)S(1)} %slice.105), channel_id=1, source_target_pairs={{0,1},{1,0},{2,3},{3,2},{4,5},{5,4},{6,7},{7,6},{8,9},{9,8},{10,11... | collective-permute-start | bytes 221192 | tf_op jit(solution)/shard_map/ppermute | solution.py:342
  33.2 1.9 %collective-permute-start.14 = (bf16[256,128]{1,0:T(8,128)(2,1)S(1)}, bf16[256,128]{1,0:T(8,128)(2,1)S(1)}, u32[]{:S(2)}, u32[]{:S(2)}) collective-permute-start(bf16[256,128]{1,0:T(8,128)(2,1)S(1)} %pad_maximum_fusion.3), channel_id=1, source_target_pairs={{0,2},{1,3},{2,0},{3,1},{4,6},{5,7},{6,4},{7,5},{8,10},{9,11},{10,... | collective-permute-start | bytes 196616 | tf_op jit(solution)/shard_map/ppermute | solution.py:342
  35.0 1.7 %input_grad.4 = (bf16[32,128,256]{2,1,0:T(8,128)(2,1)}, bf16[1,2,32,128]{3,2,1,0:T(8,128)(2,1)S(1)}) custom-call(bf16[2,288,128]{2,1,0:T(8,128)(2,1)S(1)} %fusion.2.after, bf16[3,34,128,256]{3,2,1,0:T(8,128)(2,1)S(1)} %get-tuple-element.64.moved, bf16[32,128,256]{2,1,0:T(8,128)(2,1)S(1)} %bitcast.55, ...), custom_call_target="tpu_custom_call", output_to_operand_aliasing={{0}: (5, {})} | custom-call | flops 603979776 | bytes 4194304 | tf_op jit(solution)/shard_map/input_grad/pallas_call | solution.py:438
  36.8 0.7 %collective-permute-done.9 = bf16[1,288,128]{2,1,0:T(8,128)(2,1)S(1)} collective-permute-done((bf16[1,288,128]{2,1,0:T(8,128)(2,1)S(1)}, bf16[1,288,128]{2,1,0:T(8,128)(2,1)S(1)}, u32[]{:S(2)}, u32[]{:S(2)}) %collective-permute-start.9) | collective-permute-done | bytes 73760 | tf_op jit(solution)/shard_map/ppermute | solution.py:342
  37.5 0.6 %collective-permute-start.10 = (bf16[1,288,128]{2,1,0:T(8,128)(2,1)S(1)}, bf16[1,288,128]{2,1,0:T(8,128)(2,1)S(1)}, u32[]{:S(2)}, u32[]{:S(2)}) collective-permute-start(bf16[1,288,128]{2,1,0:T(8,128)(2,1)S(1)} %add_convert_fusion.2.after), channel_id=1, source_target_pairs={{0,2},{1,3},{2,0},{3,1},{4,6},{5,7},{6,4},{7,5},{8,10},{9,11},{10,... | collective-permute-start | bytes 221192 | tf_op jit(solution)/shard_map/ppermute | solution.py:342
  38.0 1.2 %collective-permute-done.14 = bf16[256,128]{1,0:T(8,128)(2,1)S(1)} collective-permute-done((bf16[256,128]{1,0:T(8,128)(2,1)S(1)}, bf16[256,128]{1,0:T(8,128)(2,1)S(1)}, u32[]{:S(2)}, u32[]{:S(2)}) %collective-permute-start.14) | collective-permute-done | bytes 65568 | tf_op jit(solution)/shard_map/ppermute | solution.py:342
  39.2 1.7 %input_grad.5 = (bf16[32,128,256]{2,1,0:T(8,128)(2,1)}, bf16[1,2,32,128]{3,2,1,0:T(8,128)(2,1)S(1)}) custom-call(bf16[1,288,128]{2,1,0:T(8,128)(2,1)S(1)} %add_convert_fusion.2.after, bf16[3,34,128,256]{3,2,1,0:T(8,128)(2,1)S(1)} %get-tuple-element.64.moved, bf16[32,128,256]{2,1,0:T(8,128)(2,1)S(1)} %bitcast.56, ...), custom_call_target="tpu_custom_call", output_to_operand_aliasing={{0}: (5, {})} | custom-call | flops 603979776 | bytes 4194304 | tf_op jit(solution)/shard_map/input_grad/pallas_call | solution.py:438
  41.0 2.3 %collective-permute-done.10 = bf16[1,288,128]{2,1,0:T(8,128)(2,1)S(1)} collective-permute-done((bf16[1,288,128]{2,1,0:T(8,128)(2,1)S(1)}, bf16[1,288,128]{2,1,0:T(8,128)(2,1)S(1)}, u32[]{:S(2)}, u32[]{:S(2)}) %collective-permute-start.10) | collective-permute-done | bytes 73760 | tf_op jit(solution)/shard_map/ppermute | solution.py:342
  43.3 0.1 collective-permute-start.15
  43.4 1.8 %collective-permute-start.13 = (bf16[1,288,128]{2,1,0:T(8,128)(2,1)S(1)}, bf16[1,288,128]{2,1,0:T(8,128)(2,1)S(1)}, u32[]{:S(2)}, u32[]{:S(2)}) collective-permute-start(bf16[1,288,128]{2,1,0:T(8,128)(2,1)S(1)} %add_convert_fusion.1.refs_0_), channel_id=1, source_target_pairs={{0,24},{4,28},{8,16},{12,20},{16,8},{20,12},{24,0},{28,4},{1,25},{... | collective-permute-start | bytes 221192 | tf_op jit(solution)/shard_map/ppermute | solution.py:477
  45.3 1.0 %collective-permute-start.12 = (bf16[1,288,128]{2,1,0:T(8,128)(2,1)S(1)}, bf16[1,288,128]{2,1,0:T(8,128)(2,1)S(1)}, u32[]{:S(2)}, u32[]{:S(2)}) collective-permute-start(bf16[1,288,128]{2,1,0:T(8,128)(2,1)S(1)} %add_convert_fusion.1.refs_0_), channel_id=1, source_target_pairs={{0,16},{4,20},{8,24},{12,28},{16,0},{20,4},{24,8},{28,12},{1,17},{... | collective-permute-start | bytes 221192 | tf_op jit(solution)/shard_map/ppermute | solution.py:477
  46.2 0.7 %collective-permute-start.11 = (bf16[1,288,128]{2,1,0:T(8,128)(2,1)S(1)}, bf16[1,288,128]{2,1,0:T(8,128)(2,1)S(1)}, u32[]{:S(2)}, u32[]{:S(2)}) collective-permute-start(bf16[1,288,128]{2,1,0:T(8,128)(2,1)S(1)} %add_convert_fusion.1.refs_0_), channel_id=1, source_target_pairs={{0,8},{4,12},{8,0},{12,4},{16,24},{20,28},{24,16},{28,20},{1,9},{5... | collective-permute-start | bytes 221192 | tf_op jit(solution)/shard_map/ppermute | solution.py:477
  47.0 1.5 %collective-permute-done.15 = bf16[544,128]{1,0:T(8,128)(2,1)S(1)} collective-permute-done((bf16[544,128]{1,0:T(8,128)(2,1)S(1)}, bf16[544,128]{1,0:T(8,128)(2,1)S(1)}, u32[]{:S(2)}, u32[]{:S(2)}) %collective-permute-start.15) | collective-permute-done | bytes 139296 | tf_op jit(solution)/shard_map/ppermute | solution.py:342
  48.5 1.8 %collective-permute-start.18 = (bf16[1,288,128]{2,1,0:T(8,128)(2,1)S(1)}, bf16[1,288,128]{2,1,0:T(8,128)(2,1)S(1)}, u32[]{:S(2)}, u32[]{:S(2)}) collective-permute-start(bf16[1,288,128]{2,1,0:T(8,128)(2,1)S(1)} %slice_bitcast_fusion.12.refs_0_), channel_id=1, source_target_pairs={{0,24},{4,28},{8,16},{12,20},{16,8},{20,12},{24,0},{28,4},{1,25},{... | collective-permute-start | bytes 221192 | tf_op jit(solution)/shard_map/ppermute | solution.py:477
  50.3 1.7 %collective-permute-start.16 = (bf16[1,288,128]{2,1,0:T(8,128)(2,1)S(1)}, bf16[1,288,128]{2,1,0:T(8,128)(2,1)S(1)}, u32[]{:S(2)}, u32[]{:S(2)}) collective-permute-start(bf16[1,288,128]{2,1,0:T(8,128)(2,1)S(1)} %slice_bitcast_fusion.12.refs_0_), channel_id=1, source_target_pairs={{0,8},{4,12},{8,0},{12,4},{16,24},{20,28},{24,16},{28,20},{1,9},{5... | collective-permute-start | bytes 221192 | tf_op jit(solution)/shard_map/ppermute | solution.py:477
  52.0 0.1 collective-permute-start.20
  52.1 0.9 %finish.3.refs_8_ = f32[9,256,256]{2,1,0:T(8,128)} custom-call(bf16[1,288,128]{2,1,0:T(8,128)(2,1)S(1)} %add_convert_fusion.1.refs_0_, bf16[1,288,128]{2,1,0:T(8,128)(2,1)S(1)} %collective-permute-done.11.refs_1_, bf16[1,288,128]{2,1,0:T(8,128)(2,1)S(1)} %collective-permute-done.12.refs_2_, bf16[1,288,128]{2,1,0:T(8,128)(2,1)S(1)} %collective-permute-done.13.refs_3_), custom_call_target="tpu_custom_call" | custom-call | flops 1048576 | bytes 4194304 | tf_op jit(solution)/shard_map/finish/pallas_call | solution.py:538
  53.0 0.7 %collective-permute-done.18.refs_3_ = bf16[1,288,128]{2,1,0:T(8,128)(2,1)S(1)} collective-permute-done((bf16[1,288,128]{2,1,0:T(8,128)(2,1)S(1)}, bf16[1,288,128]{2,1,0:T(8,128)(2,1)S(1)}, u32[]{:S(2)}, u32[]{:S(2)}) %collective-permute-start.18) | collective-permute-done | bytes 73760 | tf_op jit(solution)/shard_map/ppermute | solution.py:477
  53.7 0.9 %collective-permute-done.17.refs_2_ = bf16[1,288,128]{2,1,0:T(8,128)(2,1)S(1)} collective-permute-done((bf16[1,288,128]{2,1,0:T(8,128)(2,1)S(1)}, bf16[1,288,128]{2,1,0:T(8,128)(2,1)S(1)}, u32[]{:S(2)}, u32[]{:S(2)}) %collective-permute-start.17) | collective-permute-done | bytes 73760 | tf_op jit(solution)/shard_map/ppermute | solution.py:477
  54.6 0.0 collective-permute-done.16.refs_1_
  54.7 0.1 collective-permute-start.19
  54.8 1.2 %finish.4.refs_8_ = f32[9,256,256]{2,1,0:T(8,128)} custom-call(bf16[1,288,128]{2,1,0:T(8,128)(2,1)S(1)} %slice_bitcast_fusion.12.refs_0_, bf16[1,288,128]{2,1,0:T(8,128)(2,1)S(1)} %collective-permute-done.16.refs_1_, bf16[1,288,128]{2,1,0:T(8,128)(2,1)S(1)} %collective-permute-done.17.refs_2_, ...), custom_call_target="tpu_custom_call", output_to_operand_aliasing={{}: (8, {})} | custom-call | flops 1048576 | bytes 4194304 | tf_op jit(solution)/shard_map/finish/pallas_call | solution.py:538
  56.0 0.3 collective-permute-done.19
  56.3 1.0 %finish.5 = (f32[9,256,256]{2,1,0:T(8,128)}, bf16[2,128,256]{2,1,0:T(8,128)(2,1)}) custom-call(bf16[1,288,128]{2,1,0:T(8,128)(2,1)S(1)} %get-tuple-element.107.refs_0_, bf16[1,288,128]{2,1,0:T(8,128)(2,1)S(1)} %get-tuple-element.106.refs_1_, bf16[1,288,128]{2,1,0:T(8,128)(2,1)S(1)} %get-tuple-element.105.refs_2_, ...), custom_call_target="tpu_custom_call", output_to_operand_aliasing={{0}: (8, {})} | custom-call | flops 1048576 | bytes 4194304 | tf_op jit(solution)/shard_map/finish/pallas_call | solution.py:538
  (32 shorter events, 0.3 us)
Async XLA Ops:
  0.6 8.0 %copy-start.2 = (bf16[1,32,128,256]{3,2,1,0:T(8,128)(2,1)S(1)}, bf16[1,32,128,256]{3,2,1,0:T(8,128)(2,1)}, u32[]{:S(2)}) copy-start(bf16[1,32,128,256]{3,2,1,0:T(8,128)(2,1)} %param.11) | copy-start | bytes 6291460
  0.6 8.0 %copy-start.3 = (f32[1000,256]{1,0:T(8,128)S(1)}, f32[1000,256]{1,0:T(8,128)}, u32[]{:S(2)}) copy-start(f32[1000,256]{1,0:T(8,128)} %scales.1) | copy-start | bytes 3072004
  2.2 7.5 %collective-permute-start = (bf16[96,256]{1,0:T(8,128)(2,1)S(1)}, bf16[96,256]{1,0:T(8,128)(2,1)S(1)}, u32[]{:S(2)}, u32[]{:S(2)}) collective-permute-start(bf16[96,256]{1,0:T(8,128)(2,1)S(1)} %get-tuple-element.52), channel_id=1, source_target_pairs={{0,3},{1,2},{2,1},{3,0},{4,7},{5,6},{6,5},{7,4},{8,11},{9,10},{10,... | collective-permute-start | bytes 147464 | tf_op jit(solution)/shard_map/ppermute | solution.py:342
  7.3 4.1 %collective-permute-start.1 = (bf16[96,256]{1,0:T(8,128)(2,1)S(1)}, bf16[96,256]{1,0:T(8,128)(2,1)S(1)}, u32[]{:S(2)}, u32[]{:S(2)}) collective-permute-start(bf16[96,256]{1,0:T(8,128)(2,1)S(1)} %get-tuple-element.53), channel_id=1, source_target_pairs={{0,1},{1,0},{2,3},{3,2},{4,5},{5,4},{6,7},{7,6},{8,9},{9,8},{10,11... | collective-permute-start | bytes 147464 | tf_op jit(solution)/shard_map/ppermute | solution.py:342
  7.3 5.8 %collective-permute-start.2 = (bf16[64,256]{1,0:T(8,128)(2,1)S(1)}, bf16[64,256]{1,0:T(8,128)(2,1)S(1)}, u32[]{:S(2)}, u32[]{:S(2)}) collective-permute-start(bf16[64,256]{1,0:T(8,128)(2,1)S(1)} %get-tuple-element.57), channel_id=1, source_target_pairs={{0,2},{1,3},{2,0},{3,1},{4,6},{5,7},{6,4},{7,5},{8,10},{9,11},{10,... | collective-permute-start | bytes 98312 | tf_op jit(solution)/shard_map/ppermute | solution.py:342
  11.4 1.7 %copy-start = (bf16[1,32,128,256]{3,2,1,0:T(8,128)(2,1)S(1)}, bf16[1,32,128,256]{3,2,1,0:T(8,128)(2,1)}, u32[]{:S(2)}) copy-start(bf16[1,32,128,256]{3,2,1,0:T(8,128)(2,1)} %param.6) | copy-start | bytes 6291460
  11.5 5.4 %collective-permute-start.3 = (bf16[144,256]{1,0:T(8,128)(2,1)S(1)}, bf16[144,256]{1,0:T(8,128)(2,1)S(1)}, u32[]{:S(2)}, u32[]{:S(2)}) collective-permute-start(bf16[144,256]{1,0:T(8,128)(2,1)S(1)} %get-tuple-element.59), channel_id=1, source_target_pairs={{4,8},{12,16},{20,24},{28,0},{8,4},{16,12},{24,20},{0,28},{5,9},{1... | collective-permute-start | bytes 221192 | tf_op jit(solution)/shard_map/ppermute | solution.py:385
  12.2 4.8 %collective-permute-start.4 = (bf16[144,256]{1,0:T(8,128)(2,1)S(1)}, bf16[144,256]{1,0:T(8,128)(2,1)S(1)}, u32[]{:S(2)}, u32[]{:S(2)}) collective-permute-start(bf16[144,256]{1,0:T(8,128)(2,1)S(1)} %get-tuple-element.60), channel_id=1, source_target_pairs={{0,4},{4,0},{8,12},{12,8},{16,20},{20,16},{24,28},{28,24},{1,5},{5... | collective-permute-start | bytes 221192 | tf_op jit(solution)/shard_map/ppermute | solution.py:388
  18.6 3.0 %collective-permute-start.5 = (bf16[4,2,288,128]{3,2,1,0:T(8,128)(2,1)S(1)}, bf16[4,2,288,128]{3,2,1,0:T(8,128)(2,1)S(1)}, u32[]{:S(2)}, u32[]{:S(2)}) collective-permute-start(bf16[4,2,288,128]{3,2,1,0:T(8,128)(2,1)S(1)} %get-tuple-element.65), channel_id=1, source_target_pairs={{0,4},{4,0},{8,12},{12,8},{16,20},{20,16},{24,28},{28,24},{1,5},{5... | collective-permute-start | bytes 1769480 | tf_op jit(solution)/shard_map/ppermute | solution.py:474
  21.6 3.8 %copy-start.1 = (bf16[3,3,256,256]{3,2,1,0:T(8,128)(2,1)S(1)}, bf16[3,3,256,256]{3,2,1,0:T(8,128)(2,1)}, u32[]{:S(2)}) copy-start(bf16[3,3,256,256]{3,2,1,0:T(8,128)(2,1)} %param.8) | copy-start | bytes 3538948
  21.9 9.0 %collective-permute-start.8 = (bf16[2,288,128]{2,1,0:T(8,128)(2,1)S(1)}, bf16[2,288,128]{2,1,0:T(8,128)(2,1)S(1)}, u32[]{:S(2)}, u32[]{:S(2)}) collective-permute-start(bf16[2,288,128]{2,1,0:T(8,128)(2,1)S(1)} %get-tuple-element.97), channel_id=1, source_target_pairs={{0,24},{4,28},{8,16},{12,20},{16,8},{20,12},{24,0},{28,4},{1,25},{... | collective-permute-start | bytes 442376 | tf_op jit(solution)/shard_map/ppermute | solution.py:477
  23.7 8.5 %collective-permute-start.7 = (bf16[2,288,128]{2,1,0:T(8,128)(2,1)S(1)}, bf16[2,288,128]{2,1,0:T(8,128)(2,1)S(1)}, u32[]{:S(2)}, u32[]{:S(2)}) collective-permute-start(bf16[2,288,128]{2,1,0:T(8,128)(2,1)S(1)} %get-tuple-element.98), channel_id=1, source_target_pairs={{0,16},{4,20},{8,24},{12,28},{16,0},{20,4},{24,8},{28,12},{1,17},{... | collective-permute-start | bytes 442376 | tf_op jit(solution)/shard_map/ppermute | solution.py:477
  24.3 7.9 %collective-permute-start.6 = (bf16[2,288,128]{2,1,0:T(8,128)(2,1)S(1)}, bf16[2,288,128]{2,1,0:T(8,128)(2,1)S(1)}, u32[]{:S(2)}, u32[]{:S(2)}) collective-permute-start(bf16[2,288,128]{2,1,0:T(8,128)(2,1)S(1)} %get-tuple-element.99), channel_id=1, source_target_pairs={{0,8},{4,12},{8,0},{12,4},{16,24},{20,28},{24,16},{28,20},{1,9},{5... | collective-permute-start | bytes 442376 | tf_op jit(solution)/shard_map/ppermute | solution.py:477
  32.3 5.1 %collective-permute-start.9 = (bf16[1,288,128]{2,1,0:T(8,128)(2,1)S(1)}, bf16[1,288,128]{2,1,0:T(8,128)(2,1)S(1)}, u32[]{:S(2)}, u32[]{:S(2)}) collective-permute-start(bf16[1,288,128]{2,1,0:T(8,128)(2,1)S(1)} %slice.105), channel_id=1, source_target_pairs={{0,1},{1,0},{2,3},{3,2},{4,5},{5,4},{6,7},{7,6},{8,9},{9,8},{10,11... | collective-permute-start | bytes 221192 | tf_op jit(solution)/shard_map/ppermute | solution.py:342
  33.2 6.1 %collective-permute-start.14 = (bf16[256,128]{1,0:T(8,128)(2,1)S(1)}, bf16[256,128]{1,0:T(8,128)(2,1)S(1)}, u32[]{:S(2)}, u32[]{:S(2)}) collective-permute-start(bf16[256,128]{1,0:T(8,128)(2,1)S(1)} %pad_maximum_fusion.3), channel_id=1, source_target_pairs={{0,2},{1,3},{2,0},{3,1},{4,6},{5,7},{6,4},{7,5},{8,10},{9,11},{10,... | collective-permute-start | bytes 196616 | tf_op jit(solution)/shard_map/ppermute | solution.py:342
  37.5 5.8 %collective-permute-start.10 = (bf16[1,288,128]{2,1,0:T(8,128)(2,1)S(1)}, bf16[1,288,128]{2,1,0:T(8,128)(2,1)S(1)}, u32[]{:S(2)}, u32[]{:S(2)}) collective-permute-start(bf16[1,288,128]{2,1,0:T(8,128)(2,1)S(1)} %add_convert_fusion.2.after), channel_id=1, source_target_pairs={{0,2},{1,3},{2,0},{3,1},{4,6},{5,7},{6,4},{7,5},{8,10},{9,11},{10,... | collective-permute-start | bytes 221192 | tf_op jit(solution)/shard_map/ppermute | solution.py:342
  43.3 5.1 %collective-permute-start.15 = (bf16[544,128]{1,0:T(8,128)(2,1)S(1)}, bf16[544,128]{1,0:T(8,128)(2,1)S(1)}, u32[]{:S(2)}, u32[]{:S(2)}) collective-permute-start(bf16[544,128]{1,0:T(8,128)(2,1)S(1)} %pad_maximum_fusion.2), channel_id=1, source_target_pairs={{0,1},{1,0},{2,3},{3,2},{4,5},{5,4},{6,7},{7,6},{8,9},{9,8},{10,11... | collective-permute-start | bytes 417800 | tf_op jit(solution)/shard_map/ppermute | solution.py:342
  43.4 6.8 %collective-permute-start.13 = (bf16[1,288,128]{2,1,0:T(8,128)(2,1)S(1)}, bf16[1,288,128]{2,1,0:T(8,128)(2,1)S(1)}, u32[]{:S(2)}, u32[]{:S(2)}) collective-permute-start(bf16[1,288,128]{2,1,0:T(8,128)(2,1)S(1)} %add_convert_fusion.1.refs_0_), channel_id=1, source_target_pairs={{0,24},{4,28},{8,16},{12,20},{16,8},{20,12},{24,0},{28,4},{1,25},{... | collective-permute-start | bytes 221192 | tf_op jit(solution)/shard_map/ppermute | solution.py:477
  45.3 6.7 %collective-permute-start.12 = (bf16[1,288,128]{2,1,0:T(8,128)(2,1)S(1)}, bf16[1,288,128]{2,1,0:T(8,128)(2,1)S(1)}, u32[]{:S(2)}, u32[]{:S(2)}) collective-permute-start(bf16[1,288,128]{2,1,0:T(8,128)(2,1)S(1)} %add_convert_fusion.1.refs_0_), channel_id=1, source_target_pairs={{0,16},{4,20},{8,24},{12,28},{16,0},{20,4},{24,8},{28,12},{1,17},{... | collective-permute-start | bytes 221192 | tf_op jit(solution)/shard_map/ppermute | solution.py:477
  46.2 5.7 %collective-permute-start.11 = (bf16[1,288,128]{2,1,0:T(8,128)(2,1)S(1)}, bf16[1,288,128]{2,1,0:T(8,128)(2,1)S(1)}, u32[]{:S(2)}, u32[]{:S(2)}) collective-permute-start(bf16[1,288,128]{2,1,0:T(8,128)(2,1)S(1)} %add_convert_fusion.1.refs_0_), channel_id=1, source_target_pairs={{0,8},{4,12},{8,0},{12,4},{16,24},{20,28},{24,16},{28,20},{1,9},{5... | collective-permute-start | bytes 221192 | tf_op jit(solution)/shard_map/ppermute | solution.py:477
  48.5 5.3 %collective-permute-start.18 = (bf16[1,288,128]{2,1,0:T(8,128)(2,1)S(1)}, bf16[1,288,128]{2,1,0:T(8,128)(2,1)S(1)}, u32[]{:S(2)}, u32[]{:S(2)}) collective-permute-start(bf16[1,288,128]{2,1,0:T(8,128)(2,1)S(1)} %slice_bitcast_fusion.12.refs_0_), channel_id=1, source_target_pairs={{0,24},{4,28},{8,16},{12,20},{16,8},{20,12},{24,0},{28,4},{1,25},{... | collective-permute-start | bytes 221192 | tf_op jit(solution)/shard_map/ppermute | solution.py:477
  50.2 4.4 %collective-permute-start.17 = (bf16[1,288,128]{2,1,0:T(8,128)(2,1)S(1)}, bf16[1,288,128]{2,1,0:T(8,128)(2,1)S(1)}, u32[]{:S(2)}, u32[]{:S(2)}) collective-permute-start(bf16[1,288,128]{2,1,0:T(8,128)(2,1)S(1)} %slice_bitcast_fusion.12.refs_0_), channel_id=1, source_target_pairs={{0,16},{4,20},{8,24},{12,28},{16,0},{20,4},{24,8},{28,12},{1,17},{... | collective-permute-start | bytes 221192 | tf_op jit(solution)/shard_map/ppermute | solution.py:477
  50.3 4.4 %collective-permute-start.16 = (bf16[1,288,128]{2,1,0:T(8,128)(2,1)S(1)}, bf16[1,288,128]{2,1,0:T(8,128)(2,1)S(1)}, u32[]{:S(2)}, u32[]{:S(2)}) collective-permute-start(bf16[1,288,128]{2,1,0:T(8,128)(2,1)S(1)} %slice_bitcast_fusion.12.refs_0_), channel_id=1, source_target_pairs={{0,8},{4,12},{8,0},{12,4},{16,24},{20,28},{24,16},{28,20},{1,9},{5... | collective-permute-start | bytes 221192 | tf_op jit(solution)/shard_map/ppermute | solution.py:477
  52.0 2.7 %collective-permute-start.20 = (bf16[4,1,288,128]{3,2,1,0:T(8,128)(2,1)S(1)}, bf16[4,1,288,128]{3,2,1,0:T(8,128)(2,1)S(1)}, u32[]{:S(2)}, u32[]{:S(2)}) collective-permute-start(bf16[4,1,288,128]{3,2,1,0:T(8,128)(2,1)S(1)} %pad_maximum_fusion.1), channel_id=1, source_target_pairs={{0,4},{4,0},{8,12},{12,8},{16,20},{20,16},{24,28},{28,24},{1,5},{5... | collective-permute-start | bytes 884744 | tf_op jit(solution)/shard_map/ppermute | solution.py:474
  54.7 1.6 %collective-permute-start.19 = (bf16[4,1,288,128]{3,2,1,0:T(8,128)(2,1)S(1)}, bf16[4,1,288,128]{3,2,1,0:T(8,128)(2,1)S(1)}, u32[]{:S(2)}, u32[]{:S(2)}) collective-permute-start(bf16[4,1,288,128]{3,2,1,0:T(8,128)(2,1)S(1)} %pad_maximum_fusion), channel_id=1, source_target_pairs={{0,4},{4,0},{8,12},{12,8},{16,20},{20,16},{24,28},{28,24},{1,5},{5... | collective-permute-start | bytes 884744 | tf_op jit(solution)/shard_map/ppermute | solution.py:474

commit v7 on v6

--- a/solution.py
+++ b/solution.py
@@ -565,8 +565,7 @@
 
 
 def piece_sizes(groups):
-    sizes = [groups * 3 // 4, groups // 8]
-    return sizes + [groups - sum(sizes)]
+    return [groups * 3 // 4, 0, groups - groups * 3 // 4]
 
 
 def solution(mesh):

time: 57.5 us -> 59.7 us (1.038)
  waiting for transfers between devices: 11.1 us -> 13.6 us
  Pallas kernels: 22.5 us -> 21.5 us
  starting transfers between devices: 21.6 us -> 22.3 us
    ppermute x7, waiting for transfers between devices: 7.35 us -> 9.29 us  [col_swap(): return lax.ppermute(x, 'col', xor_pairs(n, s))]
    pallas_call x3 -> x2, Pallas kernels: 8.93 us -> 7.87 us  [input_piece(): pl.pallas_call(functools.partial(input_kernel, made, size, n), out_shape=...]
    ppermute x7, starting transfers between devices: 9.12 us -> 9.87 us  [col_swap(): return lax.ppermute(x, 'col', xor_pairs(n, s))]
    ppermute x9, waiting for transfers between devices: 2.88 us -> 3.51 us  [plane_swap(): return lax.ppermute(x, 'row', xor_pairs(nrow, 2 * s))]
  transfers between devices with their start and end apart: 21 -> 21, of which waited for: 10 -> 10; matrix products, arithmetic and copies ran while one was open for 0% -> 0% of each run, Pallas kernels for 32% -> 29%
where the time goes in v7:
time: 59.7 us; the launch traced here: 59.5 us
  starting transfers between devices  22.3 us (37%)
  Pallas kernels  21.5 us (36%)
  waiting for transfers between devices  13.6 us (23%)
  between operations  1.55 us (3%)
    ppermute x9, starting transfers between devices, plane_swap(): return lax.ppermute(x, 'row', xor_pairs(nrow, 2 * s))  10.5 us
    ppermute x7, starting transfers between devices, col_swap(): return lax.ppermute(x, 'col', xor_pairs(n, s))  9.87 us
    ppermute x7, waiting for transfers between devices, col_swap(): return lax.ppermute(x, 'col', xor_pairs(n, s))  9.29 us
    pallas_call x2, Pallas kernels, input_piece(): pl.pallas_call(functools.partial(input_kernel, made, size, n), out_shape=...  7.87 us
    ppermute x9, waiting for transfers between devices, plane_swap(): return lax.ppermute(x, 'row', xor_pairs(nrow, 2 * s))  3.51 us
    pallas_call x1, Pallas kernels, per_device(): pl.pallas_call(functools.partial(prepare_kernel, n, cr), out_shape=[shape...  3.18 us
    pallas_call x3, Pallas kernels, finish(): pl.pallas_call(functools.partial(finish_kernel, float(pixels) ** (-0.5),...  3.15 us
    pallas_call x1, Pallas kernels, per_device(): pl.pallas_call(mine_kernel, out_shape=part, in_specs=[vmem()] * 3, out_sp...  2.93 us
  transfers between devices with their start and end apart: 21, of which 10 were waited for; matrix products, arithmetic and copies ran while one was open for 0% of the time, Pallas kernels for 29%

profile of v7, /device:TPU:0, one launch (start us, length us, event | category | flops | bytes accessed | tf_op | source)
XLA Modules:
  0.0 59.5 jit_solution(7316015365171960566)
XLA Ops:
  0.7 1.6 %start.1 = (bf16[64,256]{1,0:T(8,128)(2,1)S(1)}, bf16[96,256]{1,0:T(8,128)(2,1)S(1)}, bf16[64,256]{1,0:T(8,128)(2,1)S(1)}, bf16[96,256]{1,0:T(8,128)(2,1)S(1)}) custom-call(bf16[32,128,256]{2,1,0:T(8,128)(2,1)} %bitcast.53, bf16[2,128,256]{2,1,0:T(8,128)(2,1)} %bitcast.79), custom_call_target="tpu_custom_call" | custom-call | flops 2147483648 | bytes 4194304 | tf_op jit(solution)/shard_map/start/pallas_call | solution.py:344
  2.2 5.1 %collective-permute-start = (bf16[96,256]{1,0:T(8,128)(2,1)S(1)}, bf16[96,256]{1,0:T(8,128)(2,1)S(1)}, u32[]{:S(2)}, u32[]{:S(2)}) collective-permute-start(bf16[96,256]{1,0:T(8,128)(2,1)S(1)} %get-tuple-element.45), channel_id=1, source_target_pairs={{0,3},{1,2},{2,1},{3,0},{4,7},{5,6},{6,5},{7,4},{8,11},{9,10},{10,... | collective-permute-start | bytes 147464 | tf_op jit(solution)/shard_map/ppermute | solution.py:342
  7.3 0.6 %collective-permute-start.2 = (bf16[64,256]{1,0:T(8,128)(2,1)S(1)}, bf16[64,256]{1,0:T(8,128)(2,1)S(1)}, u32[]{:S(2)}, u32[]{:S(2)}) collective-permute-start(bf16[64,256]{1,0:T(8,128)(2,1)S(1)} %get-tuple-element.50), channel_id=1, source_target_pairs={{0,2},{1,3},{2,0},{3,1},{4,6},{5,7},{6,4},{7,5},{8,10},{9,11},{10,... | collective-permute-start | bytes 98312 | tf_op jit(solution)/shard_map/ppermute | solution.py:342
  8.7 1.1 %load.1 = (bf16[3,34,128,256]{3,2,1,0:T(8,128)(2,1)S(1)}, f32[1,256]{1,0:T(1,128)S(1)}) custom-call(s32[1]{0:T(128)S(6)} %copy.19.steps, bf16[32,128,256]{2,1,0:T(8,128)(2,1)S(1)} %bitcast.54, f32[1000,256]{1,0:T(8,128)S(1)} %copy-done.3), custom_call_target="tpu_custom_call" | custom-call | flops 1048576 | bytes 4194304 | tf_op jit(solution)/shard_map/load/pallas_call | solution.py:360
  9.7 1.7 %collective-permute-done.1.refs_1_ = bf16[96,256]{1,0:T(8,128)(2,1)S(1)} collective-permute-done((bf16[96,256]{1,0:T(8,128)(2,1)S(1)}, bf16[96,256]{1,0:T(8,128)(2,1)S(1)}, u32[]{:S(2)}, u32[]{:S(2)}) %collective-permute-start.1) | collective-permute-done | bytes 49184 | tf_op jit(solution)/shard_map/ppermute | solution.py:342
  11.4 0.1 edges.1
  11.5 0.7 %collective-permute-start.3 = (bf16[144,256]{1,0:T(8,128)(2,1)S(1)}, bf16[144,256]{1,0:T(8,128)(2,1)S(1)}, u32[]{:S(2)}, u32[]{:S(2)}) collective-permute-start(bf16[144,256]{1,0:T(8,128)(2,1)S(1)} %get-tuple-element.52), channel_id=1, source_target_pairs={{4,8},{12,16},{20,24},{28,0},{8,4},{16,12},{24,20},{0,28},{5,9},{1... | collective-permute-start | bytes 221192 | tf_op jit(solution)/shard_map/ppermute | solution.py:385
  12.2 1.0 %collective-permute-start.4 = (bf16[144,256]{1,0:T(8,128)(2,1)S(1)}, bf16[144,256]{1,0:T(8,128)(2,1)S(1)}, u32[]{:S(2)}, u32[]{:S(2)}) collective-permute-start(bf16[144,256]{1,0:T(8,128)(2,1)S(1)} %get-tuple-element.53), channel_id=1, source_target_pairs={{0,4},{4,0},{8,12},{12,8},{16,20},{20,16},{24,28},{28,24},{1,5},{5... | collective-permute-start | bytes 221192 | tf_op jit(solution)/shard_map/ppermute | solution.py:388
  13.2 3.2 %prepare.1 = (bf16[3,34,128,256]{3,2,1,0:T(8,128)(2,1)S(1)}, bf16[256,4096]{1,0:T(8,128)(2,1)S(1)}, bf16[8,32,256]{2,1,0:T(8,128)(2,1)S(1)}, f32[5,256,256]{2,1,0:T(8,128)S(1)}) custom-call(bf16[32,128,256]{2,1,0:T(8,128)(2,1)S(1)} %bitcast.55, f32[32,256]{1,0:T(8,128)S(1)} %get-tuple-element.47.left, ...), custom_call_target="tpu_custom_call", output_to_operand_aliasing={{0}: (3, {})} | custom-call | flops 4294967296 | bytes 4194304 | tf_op jit(solution)/shard_map/prepare/pallas_call | solution.py:391
  16.4 0.6 collective-permute-done.3.two
  16.9 0.0 collective-permute-done.4.one
  16.9 1.7 %weight_other.1 = (bf16[4,2,288,128]{3,2,1,0:T(8,128)(2,1)S(1)}, f32[256,128]{1,0:T(8,128)S(1)}, bf16[3,34,128,256]{3,2,1,0:T(8,128)(2,1)S(1)}) custom-call(bf16[256,4096]{1,0:T(8,128)(2,1)S(1)} %get-tuple-element.51.act_t, bf16[144,256]{1,0:T(8,128)(2,1)S(1)} %collective-permute-done.3.two, ...), custom_call_target="tpu_custom_call", output_to_operand_aliasing={{2}: (4, {})} | custom-call | flops 603979776 | bytes 8388608 | tf_op jit(solution)/shard_map/weight_other/pallas_call | solution.py:414
  18.6 0.1 collective-permute-start.5
  18.7 2.9 %weight_mine.1 = bf16[4,2,288,128]{3,2,1,0:T(8,128)(2,1)S(1)} custom-call(bf16[256,4096]{1,0:T(8,128)(2,1)S(1)} %get-tuple-element.51.act_t, f32[256,128]{1,0:T(8,128)S(1)} %get-tuple-element.56.rest, bf16[3,34,128,256]{3,2,1,0:T(8,128)(2,1)S(1)} %get-tuple-element.57.moved), custom_call_target="tpu_custom_call" | custom-call | flops 2147483648 | bytes 8388608 | tf_op jit(solution)/shard_map/weight_mine/pallas_call | solution.py:424
  21.6 0.0 copy-start.2
  21.6 0.0 collective-permute-done.5
  21.7 0.2 add_convert_fusion.after
  21.9 1.8 %collective-permute-start.8 = (bf16[2,288,128]{2,1,0:T(8,128)(2,1)S(1)}, bf16[2,288,128]{2,1,0:T(8,128)(2,1)S(1)}, u32[]{:S(2)}, u32[]{:S(2)}) collective-permute-start(bf16[2,288,128]{2,1,0:T(8,128)(2,1)S(1)} %get-tuple-element.83), channel_id=1, source_target_pairs={{0,24},{4,28},{8,16},{12,20},{16,8},{20,12},{24,0},{28,4},{1,25},{... | collective-permute-start | bytes 442376 | tf_op jit(solution)/shard_map/ppermute | solution.py:477
  23.7 0.7 %collective-permute-start.7 = (bf16[2,288,128]{2,1,0:T(8,128)(2,1)S(1)}, bf16[2,288,128]{2,1,0:T(8,128)(2,1)S(1)}, u32[]{:S(2)}, u32[]{:S(2)}) collective-permute-start(bf16[2,288,128]{2,1,0:T(8,128)(2,1)S(1)} %get-tuple-element.84), channel_id=1, source_target_pairs={{0,16},{4,20},{8,24},{12,28},{16,0},{20,4},{24,8},{28,12},{1,17},{... | collective-permute-start | bytes 442376 | tf_op jit(solution)/shard_map/ppermute | solution.py:477
  24.3 1.1 %collective-permute-start.6 = (bf16[2,288,128]{2,1,0:T(8,128)(2,1)S(1)}, bf16[2,288,128]{2,1,0:T(8,128)(2,1)S(1)}, u32[]{:S(2)}, u32[]{:S(2)}) collective-permute-start(bf16[2,288,128]{2,1,0:T(8,128)(2,1)S(1)} %get-tuple-element.85), channel_id=1, source_target_pairs={{0,8},{4,12},{8,0},{12,4},{16,24},{20,28},{24,16},{28,20},{1,9},{5... | collective-permute-start | bytes 442376 | tf_op jit(solution)/shard_map/ppermute | solution.py:477
  25.4 5.5 %input_grad.2 = (bf16[32,128,256]{2,1,0:T(8,128)(2,1)}, bf16[6,2,32,128]{3,2,1,0:T(8,128)(2,1)S(1)}) custom-call(bf16[4,2,288,128]{3,2,1,0:T(8,128)(2,1)S(1)} %add_convert_fusion.after, bf16[3,34,128,256]{3,2,1,0:T(8,128)(2,1)S(1)} %get-tuple-element.57.moved, bf16[32,128,256]{2,1,0:T(8,128)(2,1)S(1)} %bitcast.56, ...), custom_call_target="tpu_custom_call" | custom-call | flops 3623878656 | bytes 4194304 | tf_op jit(solution)/shard_map/input_grad/pallas_call | solution.py:438
  30.9 0.0 collective-permute-done.8
  30.9 1.3 %collective-permute-done.7 = bf16[2,288,128]{2,1,0:T(8,128)(2,1)S(1)} collective-permute-done((bf16[2,288,128]{2,1,0:T(8,128)(2,1)S(1)}, bf16[2,288,128]{2,1,0:T(8,128)(2,1)S(1)}, u32[]{:S(2)}, u32[]{:S(2)}) %collective-permute-start.7) | collective-permute-done | bytes 147488 | tf_op jit(solution)/shard_map/ppermute | solution.py:477
  32.2 0.7 %collective-permute-start.14 = (bf16[256,128]{1,0:T(8,128)(2,1)S(1)}, bf16[256,128]{1,0:T(8,128)(2,1)S(1)}, u32[]{:S(2)}, u32[]{:S(2)}) collective-permute-start(bf16[256,128]{1,0:T(8,128)(2,1)S(1)} %pad_maximum_fusion.3), channel_id=1, source_target_pairs={{0,2},{1,3},{2,0},{3,1},{4,6},{5,7},{6,4},{7,5},{8,10},{9,11},{10,... | collective-permute-start | bytes 196616 | tf_op jit(solution)/shard_map/ppermute | solution.py:342
  32.9 0.1 fusion.2
  33.0 2.1 %collective-permute-start.9 = (bf16[1,288,128]{2,1,0:T(8,128)(2,1)S(1)}, bf16[1,288,128]{2,1,0:T(8,128)(2,1)S(1)}, u32[]{:S(2)}, u32[]{:S(2)}) collective-permute-start(bf16[1,288,128]{2,1,0:T(8,128)(2,1)S(1)} %slice.113), channel_id=1, source_target_pairs={{0,1},{1,0},{2,3},{3,2},{4,5},{5,4},{6,7},{7,6},{8,9},{9,8},{10,11... | collective-permute-start | bytes 221192 | tf_op jit(solution)/shard_map/ppermute | solution.py:342
  35.1 3.6 %collective-permute-done.14 = bf16[256,128]{1,0:T(8,128)(2,1)S(1)} collective-permute-done((bf16[256,128]{1,0:T(8,128)(2,1)S(1)}, bf16[256,128]{1,0:T(8,128)(2,1)S(1)}, u32[]{:S(2)}, u32[]{:S(2)}) %collective-permute-start.14) | collective-permute-done | bytes 65568 | tf_op jit(solution)/shard_map/ppermute | solution.py:342
  38.7 0.0 collective-permute-done.9
  38.7 1.2 %collective-permute-start.10 = (bf16[1,288,128]{2,1,0:T(8,128)(2,1)S(1)}, bf16[1,288,128]{2,1,0:T(8,128)(2,1)S(1)}, u32[]{:S(2)}, u32[]{:S(2)}) collective-permute-start(bf16[1,288,128]{2,1,0:T(8,128)(2,1)S(1)} %add_convert_fusion.2.after), channel_id=1, source_target_pairs={{0,2},{1,3},{2,0},{3,1},{4,6},{5,7},{6,4},{7,5},{8,10},{9,11},{10,... | collective-permute-start | bytes 221192 | tf_op jit(solution)/shard_map/ppermute | solution.py:342
  39.9 2.4 %input_grad.3 = (bf16[32,128,256]{2,1,0:T(8,128)(2,1)}, bf16[2,2,32,128]{3,2,1,0:T(8,128)(2,1)S(1)}) custom-call(bf16[1,288,128]{2,1,0:T(8,128)(2,1)S(1)} %add_convert_fusion.2.after, bf16[3,34,128,256]{3,2,1,0:T(8,128)(2,1)S(1)} %get-tuple-element.57.moved, bf16[32,128,256]{2,1,0:T(8,128)(2,1)S(1)} %bitcast.57, ...), custom_call_target="tpu_custom_call", output_to_operand_aliasing={{0}: (5, {})} | custom-call | flops 1207959552 | bytes 4194304 | tf_op jit(solution)/shard_map/input_grad/pallas_call | solution.py:438
  42.3 2.5 %collective-permute-done.10 = bf16[1,288,128]{2,1,0:T(8,128)(2,1)S(1)} collective-permute-done((bf16[1,288,128]{2,1,0:T(8,128)(2,1)S(1)}, bf16[1,288,128]{2,1,0:T(8,128)(2,1)S(1)}, u32[]{:S(2)}, u32[]{:S(2)}) %collective-permute-start.10) | collective-permute-done | bytes 73760 | tf_op jit(solution)/shard_map/ppermute | solution.py:342
  44.9 0.1 collective-permute-start.15
  45.0 1.7 %collective-permute-start.13 = (bf16[1,288,128]{2,1,0:T(8,128)(2,1)S(1)}, bf16[1,288,128]{2,1,0:T(8,128)(2,1)S(1)}, u32[]{:S(2)}, u32[]{:S(2)}) collective-permute-start(bf16[1,288,128]{2,1,0:T(8,128)(2,1)S(1)} %add_convert_fusion.1.refs_0_), channel_id=1, source_target_pairs={{0,24},{4,28},{8,16},{12,20},{16,8},{20,12},{24,0},{28,4},{1,25},{... | collective-permute-start | bytes 221192 | tf_op jit(solution)/shard_map/ppermute | solution.py:477
  46.8 0.7 %collective-permute-start.12 = (bf16[1,288,128]{2,1,0:T(8,128)(2,1)S(1)}, bf16[1,288,128]{2,1,0:T(8,128)(2,1)S(1)}, u32[]{:S(2)}, u32[]{:S(2)}) collective-permute-start(bf16[1,288,128]{2,1,0:T(8,128)(2,1)S(1)} %add_convert_fusion.1.refs_0_), channel_id=1, source_target_pairs={{0,16},{4,20},{8,24},{12,28},{16,0},{20,4},{24,8},{28,12},{1,17},{... | collective-permute-start | bytes 221192 | tf_op jit(solution)/shard_map/ppermute | solution.py:477
  47.5 1.1 %collective-permute-start.11 = (bf16[1,288,128]{2,1,0:T(8,128)(2,1)S(1)}, bf16[1,288,128]{2,1,0:T(8,128)(2,1)S(1)}, u32[]{:S(2)}, u32[]{:S(2)}) collective-permute-start(bf16[1,288,128]{2,1,0:T(8,128)(2,1)S(1)} %add_convert_fusion.1.refs_0_), channel_id=1, source_target_pairs={{0,8},{4,12},{8,0},{12,4},{16,24},{20,28},{24,16},{28,20},{1,9},{5... | collective-permute-start | bytes 221192 | tf_op jit(solution)/shard_map/ppermute | solution.py:477
  48.5 1.5 %collective-permute-done.15 = bf16[544,128]{1,0:T(8,128)(2,1)S(1)} collective-permute-done((bf16[544,128]{1,0:T(8,128)(2,1)S(1)}, bf16[544,128]{1,0:T(8,128)(2,1)S(1)}, u32[]{:S(2)}, u32[]{:S(2)}) %collective-permute-start.15) | collective-permute-done | bytes 139296 | tf_op jit(solution)/shard_map/ppermute | solution.py:342
  50.0 1.7 %collective-permute-start.18 = (bf16[1,288,128]{2,1,0:T(8,128)(2,1)S(1)}, bf16[1,288,128]{2,1,0:T(8,128)(2,1)S(1)}, u32[]{:S(2)}, u32[]{:S(2)}) collective-permute-start(bf16[1,288,128]{2,1,0:T(8,128)(2,1)S(1)} %slice_bitcast_fusion.12.refs_0_), channel_id=1, source_target_pairs={{0,24},{4,28},{8,16},{12,20},{16,8},{20,12},{24,0},{28,4},{1,25},{... | collective-permute-start | bytes 221192 | tf_op jit(solution)/shard_map/ppermute | solution.py:477
  51.8 0.7 %collective-permute-start.17 = (bf16[1,288,128]{2,1,0:T(8,128)(2,1)S(1)}, bf16[1,288,128]{2,1,0:T(8,128)(2,1)S(1)}, u32[]{:S(2)}, u32[]{:S(2)}) collective-permute-start(bf16[1,288,128]{2,1,0:T(8,128)(2,1)S(1)} %slice_bitcast_fusion.12.refs_0_), channel_id=1, source_target_pairs={{0,16},{4,20},{8,24},{12,28},{16,0},{20,4},{24,8},{28,12},{1,17},{... | collective-permute-start | bytes 221192 | tf_op jit(solution)/shard_map/ppermute | solution.py:477
  52.4 1.1 %collective-permute-start.16 = (bf16[1,288,128]{2,1,0:T(8,128)(2,1)S(1)}, bf16[1,288,128]{2,1,0:T(8,128)(2,1)S(1)}, u32[]{:S(2)}, u32[]{:S(2)}) collective-permute-start(bf16[1,288,128]{2,1,0:T(8,128)(2,1)S(1)} %slice_bitcast_fusion.12.refs_0_), channel_id=1, source_target_pairs={{0,8},{4,12},{8,0},{12,4},{16,24},{20,28},{24,16},{28,20},{1,9},{5... | collective-permute-start | bytes 221192 | tf_op jit(solution)/shard_map/ppermute | solution.py:477
  53.6 0.1 collective-permute-start.20
  53.7 0.9 %finish.3.refs_8_ = f32[9,256,256]{2,1,0:T(8,128)} custom-call(bf16[1,288,128]{2,1,0:T(8,128)(2,1)S(1)} %add_convert_fusion.1.refs_0_, bf16[1,288,128]{2,1,0:T(8,128)(2,1)S(1)} %collective-permute-done.11.refs_1_, bf16[1,288,128]{2,1,0:T(8,128)(2,1)S(1)} %collective-permute-done.12.refs_2_, bf16[1,288,128]{2,1,0:T(8,128)(2,1)S(1)} %collective-permute-done.13.refs_3_), custom_call_target="tpu_custom_call" | custom-call | flops 1048576 | bytes 4194304 | tf_op jit(solution)/shard_map/finish/pallas_call | solution.py:538
  54.6 0.7 %collective-permute-done.18.refs_3_ = bf16[1,288,128]{2,1,0:T(8,128)(2,1)S(1)} collective-permute-done((bf16[1,288,128]{2,1,0:T(8,128)(2,1)S(1)}, bf16[1,288,128]{2,1,0:T(8,128)(2,1)S(1)}, u32[]{:S(2)}, u32[]{:S(2)}) %collective-permute-start.18) | collective-permute-done | bytes 73760 | tf_op jit(solution)/shard_map/ppermute | solution.py:477
  55.3 0.8 %collective-permute-done.17.refs_2_ = bf16[1,288,128]{2,1,0:T(8,128)(2,1)S(1)} collective-permute-done((bf16[1,288,128]{2,1,0:T(8,128)(2,1)S(1)}, bf16[1,288,128]{2,1,0:T(8,128)(2,1)S(1)}, u32[]{:S(2)}, u32[]{:S(2)}) %collective-permute-start.17) | collective-permute-done | bytes 73760 | tf_op jit(solution)/shard_map/ppermute | solution.py:477
  56.1 0.7 %collective-permute-done.16.refs_1_ = bf16[1,288,128]{2,1,0:T(8,128)(2,1)S(1)} collective-permute-done((bf16[1,288,128]{2,1,0:T(8,128)(2,1)S(1)}, bf16[1,288,128]{2,1,0:T(8,128)(2,1)S(1)}, u32[]{:S(2)}, u32[]{:S(2)}) %collective-permute-start.16) | collective-permute-done | bytes 73760 | tf_op jit(solution)/shard_map/ppermute | solution.py:477
  56.8 0.1 collective-permute-start.19
  57.0 1.2 %finish.4.refs_8_ = f32[9,256,256]{2,1,0:T(8,128)} custom-call(bf16[1,288,128]{2,1,0:T(8,128)(2,1)S(1)} %slice_bitcast_fusion.12.refs_0_, bf16[1,288,128]{2,1,0:T(8,128)(2,1)S(1)} %collective-permute-done.16.refs_1_, bf16[1,288,128]{2,1,0:T(8,128)(2,1)S(1)} %collective-permute-done.17.refs_2_, ...), custom_call_target="tpu_custom_call", output_to_operand_aliasing={{}: (8, {})} | custom-call | flops 1048576 | bytes 4194304 | tf_op jit(solution)/shard_map/finish/pallas_call | solution.py:538
  58.2 0.3 collective-permute-done.19
  58.5 1.0 %finish.5 = (f32[9,256,256]{2,1,0:T(8,128)}, bf16[2,128,256]{2,1,0:T(8,128)(2,1)}) custom-call(bf16[1,288,128]{2,1,0:T(8,128)(2,1)S(1)} %get-tuple-element.93.refs_0_, bf16[1,288,128]{2,1,0:T(8,128)(2,1)S(1)} %get-tuple-element.92.refs_1_, bf16[1,288,128]{2,1,0:T(8,128)(2,1)S(1)} %get-tuple-element.91.refs_2_, ...), custom_call_target="tpu_custom_call", output_to_operand_aliasing={{0}: (8, {})} | custom-call | flops 1048576 | bytes 4194304 | tf_op jit(solution)/shard_map/finish/pallas_call | solution.py:538
  (31 shorter events, 0.3 us)
Async XLA Ops:
  0.6 8.0 %copy-start = (bf16[1,32,128,256]{3,2,1,0:T(8,128)(2,1)S(1)}, bf16[1,32,128,256]{3,2,1,0:T(8,128)(2,1)}, u32[]{:S(2)}) copy-start(bf16[1,32,128,256]{3,2,1,0:T(8,128)(2,1)} %param.11) | copy-start | bytes 6291460
  0.6 8.0 %copy-start.3 = (f32[1000,256]{1,0:T(8,128)S(1)}, f32[1000,256]{1,0:T(8,128)}, u32[]{:S(2)}) copy-start(f32[1000,256]{1,0:T(8,128)} %scales.1) | copy-start | bytes 3072004
  2.2 7.5 %collective-permute-start = (bf16[96,256]{1,0:T(8,128)(2,1)S(1)}, bf16[96,256]{1,0:T(8,128)(2,1)S(1)}, u32[]{:S(2)}, u32[]{:S(2)}) collective-permute-start(bf16[96,256]{1,0:T(8,128)(2,1)S(1)} %get-tuple-element.45), channel_id=1, source_target_pairs={{0,3},{1,2},{2,1},{3,0},{4,7},{5,6},{6,5},{7,4},{8,11},{9,10},{10,... | collective-permute-start | bytes 147464 | tf_op jit(solution)/shard_map/ppermute | solution.py:342
  7.3 4.1 %collective-permute-start.1 = (bf16[96,256]{1,0:T(8,128)(2,1)S(1)}, bf16[96,256]{1,0:T(8,128)(2,1)S(1)}, u32[]{:S(2)}, u32[]{:S(2)}) collective-permute-start(bf16[96,256]{1,0:T(8,128)(2,1)S(1)} %get-tuple-element.46), channel_id=1, source_target_pairs={{0,1},{1,0},{2,3},{3,2},{4,5},{5,4},{6,7},{7,6},{8,9},{9,8},{10,11... | collective-permute-start | bytes 147464 | tf_op jit(solution)/shard_map/ppermute | solution.py:342
  7.3 5.8 %collective-permute-start.2 = (bf16[64,256]{1,0:T(8,128)(2,1)S(1)}, bf16[64,256]{1,0:T(8,128)(2,1)S(1)}, u32[]{:S(2)}, u32[]{:S(2)}) collective-permute-start(bf16[64,256]{1,0:T(8,128)(2,1)S(1)} %get-tuple-element.50), channel_id=1, source_target_pairs={{0,2},{1,3},{2,0},{3,1},{4,6},{5,7},{6,4},{7,5},{8,10},{9,11},{10,... | collective-permute-start | bytes 98312 | tf_op jit(solution)/shard_map/ppermute | solution.py:342
  11.4 1.7 %copy-start.1 = (bf16[1,32,128,256]{3,2,1,0:T(8,128)(2,1)S(1)}, bf16[1,32,128,256]{3,2,1,0:T(8,128)(2,1)}, u32[]{:S(2)}) copy-start(bf16[1,32,128,256]{3,2,1,0:T(8,128)(2,1)} %param.6) | copy-start | bytes 6291460
  11.5 5.4 %collective-permute-start.3 = (bf16[144,256]{1,0:T(8,128)(2,1)S(1)}, bf16[144,256]{1,0:T(8,128)(2,1)S(1)}, u32[]{:S(2)}, u32[]{:S(2)}) collective-permute-start(bf16[144,256]{1,0:T(8,128)(2,1)S(1)} %get-tuple-element.52), channel_id=1, source_target_pairs={{4,8},{12,16},{20,24},{28,0},{8,4},{16,12},{24,20},{0,28},{5,9},{1... | collective-permute-start | bytes 221192 | tf_op jit(solution)/shard_map/ppermute | solution.py:385
  12.2 4.8 %collective-permute-start.4 = (bf16[144,256]{1,0:T(8,128)(2,1)S(1)}, bf16[144,256]{1,0:T(8,128)(2,1)S(1)}, u32[]{:S(2)}, u32[]{:S(2)}) collective-permute-start(bf16[144,256]{1,0:T(8,128)(2,1)S(1)} %get-tuple-element.53), channel_id=1, source_target_pairs={{0,4},{4,0},{8,12},{12,8},{16,20},{20,16},{24,28},{28,24},{1,5},{5... | collective-permute-start | bytes 221192 | tf_op jit(solution)/shard_map/ppermute | solution.py:388
  18.6 3.0 %collective-permute-start.5 = (bf16[4,2,288,128]{3,2,1,0:T(8,128)(2,1)S(1)}, bf16[4,2,288,128]{3,2,1,0:T(8,128)(2,1)S(1)}, u32[]{:S(2)}, u32[]{:S(2)}) collective-permute-start(bf16[4,2,288,128]{3,2,1,0:T(8,128)(2,1)S(1)} %get-tuple-element.58), channel_id=1, source_target_pairs={{0,4},{4,0},{8,12},{12,8},{16,20},{20,16},{24,28},{28,24},{1,5},{5... | collective-permute-start | bytes 1769480 | tf_op jit(solution)/shard_map/ppermute | solution.py:474
  21.6 3.8 %copy-start.2 = (bf16[3,3,256,256]{3,2,1,0:T(8,128)(2,1)S(1)}, bf16[3,3,256,256]{3,2,1,0:T(8,128)(2,1)}, u32[]{:S(2)}) copy-start(bf16[3,3,256,256]{3,2,1,0:T(8,128)(2,1)} %param.8) | copy-start | bytes 3538948
  21.9 9.0 %collective-permute-start.8 = (bf16[2,288,128]{2,1,0:T(8,128)(2,1)S(1)}, bf16[2,288,128]{2,1,0:T(8,128)(2,1)S(1)}, u32[]{:S(2)}, u32[]{:S(2)}) collective-permute-start(bf16[2,288,128]{2,1,0:T(8,128)(2,1)S(1)} %get-tuple-element.83), channel_id=1, source_target_pairs={{0,24},{4,28},{8,16},{12,20},{16,8},{20,12},{24,0},{28,4},{1,25},{... | collective-permute-start | bytes 442376 | tf_op jit(solution)/shard_map/ppermute | solution.py:477
  23.7 8.5 %collective-permute-start.7 = (bf16[2,288,128]{2,1,0:T(8,128)(2,1)S(1)}, bf16[2,288,128]{2,1,0:T(8,128)(2,1)S(1)}, u32[]{:S(2)}, u32[]{:S(2)}) collective-permute-start(bf16[2,288,128]{2,1,0:T(8,128)(2,1)S(1)} %get-tuple-element.84), channel_id=1, source_target_pairs={{0,16},{4,20},{8,24},{12,28},{16,0},{20,4},{24,8},{28,12},{1,17},{... | collective-permute-start | bytes 442376 | tf_op jit(solution)/shard_map/ppermute | solution.py:477
  24.3 7.9 %collective-permute-start.6 = (bf16[2,288,128]{2,1,0:T(8,128)(2,1)S(1)}, bf16[2,288,128]{2,1,0:T(8,128)(2,1)S(1)}, u32[]{:S(2)}, u32[]{:S(2)}) collective-permute-start(bf16[2,288,128]{2,1,0:T(8,128)(2,1)S(1)} %get-tuple-element.85), channel_id=1, source_target_pairs={{0,8},{4,12},{8,0},{12,4},{16,24},{20,28},{24,16},{28,20},{1,9},{5... | collective-permute-start | bytes 442376 | tf_op jit(solution)/shard_map/ppermute | solution.py:477
  32.2 6.5 %collective-permute-start.14 = (bf16[256,128]{1,0:T(8,128)(2,1)S(1)}, bf16[256,128]{1,0:T(8,128)(2,1)S(1)}, u32[]{:S(2)}, u32[]{:S(2)}) collective-permute-start(bf16[256,128]{1,0:T(8,128)(2,1)S(1)} %pad_maximum_fusion.3), channel_id=1, source_target_pairs={{0,2},{1,3},{2,0},{3,1},{4,6},{5,7},{6,4},{7,5},{8,10},{9,11},{10,... | collective-permute-start | bytes 196616 | tf_op jit(solution)/shard_map/ppermute | solution.py:342
  33.0 5.7 %collective-permute-start.9 = (bf16[1,288,128]{2,1,0:T(8,128)(2,1)S(1)}, bf16[1,288,128]{2,1,0:T(8,128)(2,1)S(1)}, u32[]{:S(2)}, u32[]{:S(2)}) collective-permute-start(bf16[1,288,128]{2,1,0:T(8,128)(2,1)S(1)} %slice.113), channel_id=1, source_target_pairs={{0,1},{1,0},{2,3},{3,2},{4,5},{5,4},{6,7},{7,6},{8,9},{9,8},{10,11... | collective-permute-start | bytes 221192 | tf_op jit(solution)/shard_map/ppermute | solution.py:342
  38.7 6.1 %collective-permute-start.10 = (bf16[1,288,128]{2,1,0:T(8,128)(2,1)S(1)}, bf16[1,288,128]{2,1,0:T(8,128)(2,1)S(1)}, u32[]{:S(2)}, u32[]{:S(2)}) collective-permute-start(bf16[1,288,128]{2,1,0:T(8,128)(2,1)S(1)} %add_convert_fusion.2.after), channel_id=1, source_target_pairs={{0,2},{1,3},{2,0},{3,1},{4,6},{5,7},{6,4},{7,5},{8,10},{9,11},{10,... | collective-permute-start | bytes 221192 | tf_op jit(solution)/shard_map/ppermute | solution.py:342
  44.9 5.1 %collective-permute-start.15 = (bf16[544,128]{1,0:T(8,128)(2,1)S(1)}, bf16[544,128]{1,0:T(8,128)(2,1)S(1)}, u32[]{:S(2)}, u32[]{:S(2)}) collective-permute-start(bf16[544,128]{1,0:T(8,128)(2,1)S(1)} %pad_maximum_fusion.2), channel_id=1, source_target_pairs={{0,1},{1,0},{2,3},{3,2},{4,5},{5,4},{6,7},{7,6},{8,9},{9,8},{10,11... | collective-permute-start | bytes 417800 | tf_op jit(solution)/shard_map/ppermute | solution.py:342
  45.0 7.4 %collective-permute-start.13 = (bf16[1,288,128]{2,1,0:T(8,128)(2,1)S(1)}, bf16[1,288,128]{2,1,0:T(8,128)(2,1)S(1)}, u32[]{:S(2)}, u32[]{:S(2)}) collective-permute-start(bf16[1,288,128]{2,1,0:T(8,128)(2,1)S(1)} %add_convert_fusion.1.refs_0_), channel_id=1, source_target_pairs={{0,24},{4,28},{8,16},{12,20},{16,8},{20,12},{24,0},{28,4},{1,25},{... | collective-permute-start | bytes 221192 | tf_op jit(solution)/shard_map/ppermute | solution.py:477
  46.8 6.7 %collective-permute-start.12 = (bf16[1,288,128]{2,1,0:T(8,128)(2,1)S(1)}, bf16[1,288,128]{2,1,0:T(8,128)(2,1)S(1)}, u32[]{:S(2)}, u32[]{:S(2)}) collective-permute-start(bf16[1,288,128]{2,1,0:T(8,128)(2,1)S(1)} %add_convert_fusion.1.refs_0_), channel_id=1, source_target_pairs={{0,16},{4,20},{8,24},{12,28},{16,0},{20,4},{24,8},{28,12},{1,17},{... | collective-permute-start | bytes 221192 | tf_op jit(solution)/shard_map/ppermute | solution.py:477
  47.5 6.1 %collective-permute-start.11 = (bf16[1,288,128]{2,1,0:T(8,128)(2,1)S(1)}, bf16[1,288,128]{2,1,0:T(8,128)(2,1)S(1)}, u32[]{:S(2)}, u32[]{:S(2)}) collective-permute-start(bf16[1,288,128]{2,1,0:T(8,128)(2,1)S(1)} %add_convert_fusion.1.refs_0_), channel_id=1, source_target_pairs={{0,8},{4,12},{8,0},{12,4},{16,24},{20,28},{24,16},{28,20},{1,9},{5... | collective-permute-start | bytes 221192 | tf_op jit(solution)/shard_map/ppermute | solution.py:477
  50.0 5.3 %collective-permute-start.18 = (bf16[1,288,128]{2,1,0:T(8,128)(2,1)S(1)}, bf16[1,288,128]{2,1,0:T(8,128)(2,1)S(1)}, u32[]{:S(2)}, u32[]{:S(2)}) collective-permute-start(bf16[1,288,128]{2,1,0:T(8,128)(2,1)S(1)} %slice_bitcast_fusion.12.refs_0_), channel_id=1, source_target_pairs={{0,24},{4,28},{8,16},{12,20},{16,8},{20,12},{24,0},{28,4},{1,25},{... | collective-permute-start | bytes 221192 | tf_op jit(solution)/shard_map/ppermute | solution.py:477
  51.8 4.4 %collective-permute-start.17 = (bf16[1,288,128]{2,1,0:T(8,128)(2,1)S(1)}, bf16[1,288,128]{2,1,0:T(8,128)(2,1)S(1)}, u32[]{:S(2)}, u32[]{:S(2)}) collective-permute-start(bf16[1,288,128]{2,1,0:T(8,128)(2,1)S(1)} %slice_bitcast_fusion.12.refs_0_), channel_id=1, source_target_pairs={{0,16},{4,20},{8,24},{12,28},{16,0},{20,4},{24,8},{28,12},{1,17},{... | collective-permute-start | bytes 221192 | tf_op jit(solution)/shard_map/ppermute | solution.py:477
  52.4 4.4 %collective-permute-start.16 = (bf16[1,288,128]{2,1,0:T(8,128)(2,1)S(1)}, bf16[1,288,128]{2,1,0:T(8,128)(2,1)S(1)}, u32[]{:S(2)}, u32[]{:S(2)}) collective-permute-start(bf16[1,288,128]{2,1,0:T(8,128)(2,1)S(1)} %slice_bitcast_fusion.12.refs_0_), channel_id=1, source_target_pairs={{0,8},{4,12},{8,0},{12,4},{16,24},{20,28},{24,16},{28,20},{1,9},{5... | collective-permute-start | bytes 221192 | tf_op jit(solution)/shard_map/ppermute | solution.py:477
  53.6 3.4 %collective-permute-start.20 = (bf16[4,1,288,128]{3,2,1,0:T(8,128)(2,1)S(1)}, bf16[4,1,288,128]{3,2,1,0:T(8,128)(2,1)S(1)}, u32[]{:S(2)}, u32[]{:S(2)}) collective-permute-start(bf16[4,1,288,128]{3,2,1,0:T(8,128)(2,1)S(1)} %pad_maximum_fusion.1), channel_id=1, source_target_pairs={{0,4},{4,0},{8,12},{12,8},{16,20},{20,16},{24,28},{28,24},{1,5},{5... | collective-permute-start | bytes 884744 | tf_op jit(solution)/shard_map/ppermute | solution.py:474
  56.8 1.6 %collective-permute-start.19 = (bf16[4,1,288,128]{3,2,1,0:T(8,128)(2,1)S(1)}, bf16[4,1,288,128]{3,2,1,0:T(8,128)(2,1)S(1)}, u32[]{:S(2)}, u32[]{:S(2)}) collective-permute-start(bf16[4,1,288,128]{3,2,1,0:T(8,128)(2,1)S(1)} %pad_maximum_fusion), channel_id=1, source_target_pairs={{0,4},{4,0},{8,12},{12,8},{16,20},{20,16},{24,28},{28,24},{1,5},{5... | collective-permute-start | bytes 884744 | tf_op jit(solution)/shard_map/ppermute | solution.py:474

commit v8 on v6

--- a/solution.py
+++ b/solution.py
@@ -478,22 +478,17 @@
 
     held = {s: [] for s in range(n)}
 
-    def hop(bit, extra):
+    def hop(bit):
         sent = []
         for s in [s for s in held if s & bit]:
             sent += [(s, src, x) for src, x in held.pop(s) + [(0, pooled_strip(s))]]
-        return sent, col_swap(jnp.concatenate(extra + [x for _, _, x in sent]), bit)
-
-    def land(bit, sent, got, at):
+        return sent, col_swap(jnp.concatenate([x for _, _, x in sent]), bit)
+
+    def land(bit, sent, got):
+        at = 0
         for s, src, x in sent:
             held[s ^ bit].append((src ^ bit, got[at : at + x.shape[0]]))
             at += x.shape[0]
-
-    def ride(bit, total):
-        sent, got = hop(bit, [total.reshape(-1, half)])
-        at = total.size // half
-        land(bit, sent, got, at)
-        return got[:at].reshape(total.shape)
 
     sizes = piece_sizes(rows // 4)
     total = add(keep, core_swap(send))
@@ -506,18 +501,27 @@
     while bit:
         got = [col_swap(total[bit:], bit)]
         if bit == halves // 2:
-            sent, far = hop(halves, [])
+            sent, far = hop(halves)
         total = add(total[:bit], *beside(got, sizes[1] if bit == 1 else 0, total))
         bit //= 2
-    got = beside([col_swap(total, halves)], sizes[2], total)
+    got = [col_swap(total, halves)]
+    land(halves, sent, far)
+    bit = halves // 2
+    while bit:
+        sent, near_rows = hop(bit)
+        land(bit, sent, near_rows)
+        bit //= 2
+    got = beside(got, sizes[2], total)
+    places = [src for src, _ in held[0]]
+    got, strips = lax.optimization_barrier((got, [x for _, x in held[0]]))
+    strips = list(zip(places, strips))
     total = add(total, *got)
-    land(halves, sent, far, 0)
 
     bit = 1
     while bit < halves // 2:
-        total = jnp.concatenate([total, ride(bit, total)])
+        total = jnp.concatenate([total, col_swap(total, bit)])
         bit *= 2
-    came = ride(bit, total)
+    came = col_swap(total, bit)
     if aligned:
         waves = [total, came]
     else:
@@ -526,9 +530,9 @@
     ways = list(range(1, planes))
     waves = [[x] + [plane_swap(x, s) for s in ways] for x in waves]
     if aligned:
-        waves[0][1:], waves[1][0] = lax.optimization_barrier((waves[0][1:], waves[1][0]))
-
-    parts = held[0] + [(0, pooled_strip(0))]
+        waves[0][1:], waves[1][:2] = lax.optimization_barrier((waves[0][1:], waves[1][:2]))
+
+    parts = strips + [(0, pooled_strip(0))]
     parts = [x for _, x in sorted(parts, key=lambda pair: pair[0])]
     pixels = rows * nrow * width * n
 

time: 57.5 us -> 60.2 us (1.047)
  starting transfers between devices: 21.6 us -> 24.1 us
    ppermute x7 -> x8, starting transfers between devices: 9.12 us -> 11.7 us  [col_swap(): return lax.ppermute(x, 'col', xor_pairs(n, s))]
    ppermute x9, waiting for transfers between devices: 2.88 us -> 3.66 us  [plane_swap(): return lax.ppermute(x, 'row', xor_pairs(nrow, 2 * s))]
    ppermute x7 -> x8, waiting for transfers between devices: 7.35 us -> 6.85 us  [col_swap(): return lax.ppermute(x, 'col', xor_pairs(n, s))]
  transfers between devices with their start and end apart: 21 -> 22, of which waited for: 10 -> 12; matrix products, arithmetic and copies ran while one was open for 0% -> 0% of each run, Pallas kernels for 32% -> 30%
where the time goes in v8:
time: 60.2 us; the launch traced here: 60.1 us
  starting transfers between devices  24.1 us (40%)
  Pallas kernels  22.5 us (37%)
  waiting for transfers between devices  11.4 us (19%)
  between operations  1.55 us (3%)
    ppermute x8, starting transfers between devices, col_swap(): return lax.ppermute(x, 'col', xor_pairs(n, s))  11.7 us
    ppermute x9, starting transfers between devices, plane_swap(): return lax.ppermute(x, 'row', xor_pairs(nrow, 2 * s))  10.5 us
    pallas_call x3, Pallas kernels, input_piece(): pl.pallas_call(functools.partial(input_kernel, made, size, n), out_shape=...  8.93 us
    ppermute x8, waiting for transfers between devices, col_swap(): return lax.ppermute(x, 'col', xor_pairs(n, s))  6.85 us
    ppermute x9, waiting for transfers between devices, plane_swap(): return lax.ppermute(x, 'row', xor_pairs(nrow, 2 * s))  3.66 us
    pallas_call x1, Pallas kernels, per_device(): pl.pallas_call(functools.partial(prepare_kernel, n, cr), out_shape=[shape...  3.18 us
    pallas_call x3, Pallas kernels, finish(): pl.pallas_call(functools.partial(finish_kernel, float(pixels) ** (-0.5),...  3.15 us
    pallas_call x1, Pallas kernels, per_device(): pl.pallas_call(mine_kernel, out_shape=part, in_specs=[vmem()] * 3, out_sp...  2.93 us
  transfers between devices with their start and end apart: 22, of which 12 were waited for; matrix products, arithmetic and copies ran while one was open for 0% of the time, Pallas kernels for 30%

profile of v8, /device:TPU:0, one launch (start us, length us, event | category | flops | bytes accessed | tf_op | source)
XLA Modules:
  0.0 60.1 jit_solution(9945304913711359783)
XLA Ops:
  0.7 1.6 %start.1 = (bf16[64,256]{1,0:T(8,128)(2,1)S(1)}, bf16[96,256]{1,0:T(8,128)(2,1)S(1)}, bf16[64,256]{1,0:T(8,128)(2,1)S(1)}, bf16[96,256]{1,0:T(8,128)(2,1)S(1)}) custom-call(bf16[32,128,256]{2,1,0:T(8,128)(2,1)} %bitcast.57, bf16[2,128,256]{2,1,0:T(8,128)(2,1)} %bitcast.77), custom_call_target="tpu_custom_call" | custom-call | flops 2147483648 | bytes 4194304 | tf_op jit(solution)/shard_map/start/pallas_call | solution.py:344
  2.2 5.1 %collective-permute-start = (bf16[96,256]{1,0:T(8,128)(2,1)S(1)}, bf16[96,256]{1,0:T(8,128)(2,1)S(1)}, u32[]{:S(2)}, u32[]{:S(2)}) collective-permute-start(bf16[96,256]{1,0:T(8,128)(2,1)S(1)} %get-tuple-element.56), channel_id=1, source_target_pairs={{0,3},{1,2},{2,1},{3,0},{4,7},{5,6},{6,5},{7,4},{8,11},{9,10},{10,... | collective-permute-start | bytes 147464 | tf_op jit(solution)/shard_map/ppermute | solution.py:342
  7.3 0.6 %collective-permute-start.2 = (bf16[64,256]{1,0:T(8,128)(2,1)S(1)}, bf16[64,256]{1,0:T(8,128)(2,1)S(1)}, u32[]{:S(2)}, u32[]{:S(2)}) collective-permute-start(bf16[64,256]{1,0:T(8,128)(2,1)S(1)} %get-tuple-element.61), channel_id=1, source_target_pairs={{0,2},{1,3},{2,0},{3,1},{4,6},{5,7},{6,4},{7,5},{8,10},{9,11},{10,... | collective-permute-start | bytes 98312 | tf_op jit(solution)/shard_map/ppermute | solution.py:342
  8.7 1.1 %load.1 = (bf16[3,34,128,256]{3,2,1,0:T(8,128)(2,1)S(1)}, f32[1,256]{1,0:T(1,128)S(1)}) custom-call(s32[1]{0:T(128)S(6)} %copy.21.steps, bf16[32,128,256]{2,1,0:T(8,128)(2,1)S(1)} %bitcast.58, f32[1000,256]{1,0:T(8,128)S(1)} %copy-done.3), custom_call_target="tpu_custom_call" | custom-call | flops 1048576 | bytes 4194304 | tf_op jit(solution)/shard_map/load/pallas_call | solution.py:360
  9.7 1.7 %collective-permute-done.1.refs_1_ = bf16[96,256]{1,0:T(8,128)(2,1)S(1)} collective-permute-done((bf16[96,256]{1,0:T(8,128)(2,1)S(1)}, bf16[96,256]{1,0:T(8,128)(2,1)S(1)}, u32[]{:S(2)}, u32[]{:S(2)}) %collective-permute-start.1) | collective-permute-done | bytes 49184 | tf_op jit(solution)/shard_map/ppermute | solution.py:342
  11.4 0.1 edges.1
  11.5 0.7 %collective-permute-start.3 = (bf16[144,256]{1,0:T(8,128)(2,1)S(1)}, bf16[144,256]{1,0:T(8,128)(2,1)S(1)}, u32[]{:S(2)}, u32[]{:S(2)}) collective-permute-start(bf16[144,256]{1,0:T(8,128)(2,1)S(1)} %get-tuple-element.63), channel_id=1, source_target_pairs={{4,8},{12,16},{20,24},{28,0},{8,4},{16,12},{24,20},{0,28},{5,9},{1... | collective-permute-start | bytes 221192 | tf_op jit(solution)/shard_map/ppermute | solution.py:385
  12.2 1.0 %collective-permute-start.4 = (bf16[144,256]{1,0:T(8,128)(2,1)S(1)}, bf16[144,256]{1,0:T(8,128)(2,1)S(1)}, u32[]{:S(2)}, u32[]{:S(2)}) collective-permute-start(bf16[144,256]{1,0:T(8,128)(2,1)S(1)} %get-tuple-element.64), channel_id=1, source_target_pairs={{0,4},{4,0},{8,12},{12,8},{16,20},{20,16},{24,28},{28,24},{1,5},{5... | collective-permute-start | bytes 221192 | tf_op jit(solution)/shard_map/ppermute | solution.py:388
  13.2 3.2 %prepare.1 = (bf16[3,34,128,256]{3,2,1,0:T(8,128)(2,1)S(1)}, bf16[256,4096]{1,0:T(8,128)(2,1)S(1)}, bf16[8,32,256]{2,1,0:T(8,128)(2,1)S(1)}, f32[5,256,256]{2,1,0:T(8,128)S(1)}) custom-call(bf16[32,128,256]{2,1,0:T(8,128)(2,1)S(1)} %bitcast.50, f32[32,256]{1,0:T(8,128)S(1)} %get-tuple-element.58.left, ...), custom_call_target="tpu_custom_call", output_to_operand_aliasing={{0}: (3, {})} | custom-call | flops 4294967296 | bytes 4194304 | tf_op jit(solution)/shard_map/prepare/pallas_call | solution.py:391
  16.4 0.6 collective-permute-done.3.two
  16.9 1.7 %weight_other.1 = (bf16[4,2,288,128]{3,2,1,0:T(8,128)(2,1)S(1)}, f32[256,128]{1,0:T(8,128)S(1)}, bf16[3,34,128,256]{3,2,1,0:T(8,128)(2,1)S(1)}) custom-call(bf16[256,4096]{1,0:T(8,128)(2,1)S(1)} %get-tuple-element.62.act_t, bf16[144,256]{1,0:T(8,128)(2,1)S(1)} %collective-permute-done.3.two, ...), custom_call_target="tpu_custom_call", output_to_operand_aliasing={{2}: (4, {})} | custom-call | flops 603979776 | bytes 8388608 | tf_op jit(solution)/shard_map/weight_other/pallas_call | solution.py:414
  18.6 0.1 collective-permute-start.5
  18.7 2.9 %weight_mine.1 = bf16[4,2,288,128]{3,2,1,0:T(8,128)(2,1)S(1)} custom-call(bf16[256,4096]{1,0:T(8,128)(2,1)S(1)} %get-tuple-element.62.act_t, f32[256,128]{1,0:T(8,128)S(1)} %get-tuple-element.67.rest, bf16[3,34,128,256]{3,2,1,0:T(8,128)(2,1)S(1)} %get-tuple-element.68.moved), custom_call_target="tpu_custom_call" | custom-call | flops 2147483648 | bytes 8388608 | tf_op jit(solution)/shard_map/weight_mine/pallas_call | solution.py:424
  21.7 0.2 add_convert_fusion.after
  21.9 1.8 %collective-permute-start.8 = (bf16[2,288,128]{2,1,0:T(8,128)(2,1)S(1)}, bf16[2,288,128]{2,1,0:T(8,128)(2,1)S(1)}, u32[]{:S(2)}, u32[]{:S(2)}) collective-permute-start(bf16[2,288,128]{2,1,0:T(8,128)(2,1)S(1)} %get-tuple-element.105), channel_id=1, source_target_pairs={{0,24},{4,28},{8,16},{12,20},{16,8},{20,12},{24,0},{28,4},{1,25},{... | collective-permute-start | bytes 442376 | tf_op jit(solution)/shard_map/ppermute | solution.py:477
  23.7 0.7 %collective-permute-start.7 = (bf16[2,288,128]{2,1,0:T(8,128)(2,1)S(1)}, bf16[2,288,128]{2,1,0:T(8,128)(2,1)S(1)}, u32[]{:S(2)}, u32[]{:S(2)}) collective-permute-start(bf16[2,288,128]{2,1,0:T(8,128)(2,1)S(1)} %get-tuple-element.106), channel_id=1, source_target_pairs={{0,16},{4,20},{8,24},{12,28},{16,0},{20,4},{24,8},{28,12},{1,17},{... | collective-permute-start | bytes 442376 | tf_op jit(solution)/shard_map/ppermute | solution.py:477
  24.3 1.1 %collective-permute-start.6 = (bf16[2,288,128]{2,1,0:T(8,128)(2,1)S(1)}, bf16[2,288,128]{2,1,0:T(8,128)(2,1)S(1)}, u32[]{:S(2)}, u32[]{:S(2)}) collective-permute-start(bf16[2,288,128]{2,1,0:T(8,128)(2,1)S(1)} %get-tuple-element.107), channel_id=1, source_target_pairs={{0,8},{4,12},{8,0},{12,4},{16,24},{20,28},{24,16},{28,20},{1,9},{5... | collective-permute-start | bytes 442376 | tf_op jit(solution)/shard_map/ppermute | solution.py:477
  25.4 5.5 %input_grad.3 = (bf16[32,128,256]{2,1,0:T(8,128)(2,1)}, bf16[6,2,32,128]{3,2,1,0:T(8,128)(2,1)S(1)}) custom-call(bf16[4,2,288,128]{3,2,1,0:T(8,128)(2,1)S(1)} %add_convert_fusion.after, bf16[3,34,128,256]{3,2,1,0:T(8,128)(2,1)S(1)} %get-tuple-element.68.moved, bf16[32,128,256]{2,1,0:T(8,128)(2,1)S(1)} %bitcast.51, ...), custom_call_target="tpu_custom_call" | custom-call | flops 3623878656 | bytes 4194304 | tf_op jit(solution)/shard_map/input_grad/pallas_call | solution.py:438
  30.9 1.3 %collective-permute-done.7 = bf16[2,288,128]{2,1,0:T(8,128)(2,1)S(1)} collective-permute-done((bf16[2,288,128]{2,1,0:T(8,128)(2,1)S(1)}, bf16[2,288,128]{2,1,0:T(8,128)(2,1)S(1)}, u32[]{:S(2)}, u32[]{:S(2)}) %collective-permute-start.7) | collective-permute-done | bytes 147488 | tf_op jit(solution)/shard_map/ppermute | solution.py:477
  32.2 0.7 %collective-permute-start.11 = (bf16[256,128]{1,0:T(8,128)(2,1)S(1)}, bf16[256,128]{1,0:T(8,128)(2,1)S(1)}, u32[]{:S(2)}, u32[]{:S(2)}) collective-permute-start(bf16[256,128]{1,0:T(8,128)(2,1)S(1)} %pad_maximum_fusion.2), channel_id=1, source_target_pairs={{0,2},{1,3},{2,0},{3,1},{4,6},{5,7},{6,4},{7,5},{8,10},{9,11},{10,... | collective-permute-start | bytes 196616 | tf_op jit(solution)/shard_map/ppermute | solution.py:342
  32.9 0.1 fusion.2.after
  33.0 2.1 %collective-permute-start.9 = (bf16[1,288,128]{2,1,0:T(8,128)(2,1)S(1)}, bf16[1,288,128]{2,1,0:T(8,128)(2,1)S(1)}, u32[]{:S(2)}, u32[]{:S(2)}) collective-permute-start(bf16[1,288,128]{2,1,0:T(8,128)(2,1)S(1)} %slice.101), channel_id=1, source_target_pairs={{0,1},{1,0},{2,3},{3,2},{4,5},{5,4},{6,7},{7,6},{8,9},{9,8},{10,11... | collective-permute-start | bytes 221192 | tf_op jit(solution)/shard_map/ppermute | solution.py:342
  35.1 1.7 %input_grad.4 = (bf16[32,128,256]{2,1,0:T(8,128)(2,1)}, bf16[1,2,32,128]{3,2,1,0:T(8,128)(2,1)S(1)}) custom-call(bf16[2,288,128]{2,1,0:T(8,128)(2,1)S(1)} %fusion.2.after, bf16[3,34,128,256]{3,2,1,0:T(8,128)(2,1)S(1)} %get-tuple-element.68.moved, bf16[32,128,256]{2,1,0:T(8,128)(2,1)S(1)} %bitcast.52, ...), custom_call_target="tpu_custom_call", output_to_operand_aliasing={{0}: (5, {})} | custom-call | flops 603979776 | bytes 4194304 | tf_op jit(solution)/shard_map/input_grad/pallas_call | solution.py:438
  36.8 1.8 %collective-permute-done.11 = bf16[256,128]{1,0:T(8,128)(2,1)S(1)} collective-permute-done((bf16[256,128]{1,0:T(8,128)(2,1)S(1)}, bf16[256,128]{1,0:T(8,128)(2,1)S(1)}, u32[]{:S(2)}, u32[]{:S(2)}) %collective-permute-start.11) | collective-permute-done | bytes 65568 | tf_op jit(solution)/shard_map/ppermute | solution.py:342
  38.7 0.0 collective-permute-done.9
  38.7 0.8 %collective-permute-start.12 = (bf16[256,128]{1,0:T(8,128)(2,1)S(1)}, bf16[256,128]{1,0:T(8,128)(2,1)S(1)}, u32[]{:S(2)}, u32[]{:S(2)}) collective-permute-start(bf16[256,128]{1,0:T(8,128)(2,1)S(1)} %pad_maximum_fusion.3), channel_id=1, source_target_pairs={{0,1},{1,0},{2,3},{3,2},{4,5},{5,4},{6,7},{7,6},{8,9},{9,8},{10,11... | collective-permute-start | bytes 196616 | tf_op jit(solution)/shard_map/ppermute | solution.py:342
  39.6 2.1 %collective-permute-start.10 = (bf16[1,288,128]{2,1,0:T(8,128)(2,1)S(1)}, bf16[1,288,128]{2,1,0:T(8,128)(2,1)S(1)}, u32[]{:S(2)}, u32[]{:S(2)}) collective-permute-start(bf16[1,288,128]{2,1,0:T(8,128)(2,1)S(1)} %add_convert_fusion.2.after), channel_id=1, source_target_pairs={{0,2},{1,3},{2,0},{3,1},{4,6},{5,7},{6,4},{7,5},{8,10},{9,11},{10,... | collective-permute-start | bytes 221192 | tf_op jit(solution)/shard_map/ppermute | solution.py:342
  41.7 1.7 %input_grad.5 = (bf16[32,128,256]{2,1,0:T(8,128)(2,1)}, bf16[1,2,32,128]{3,2,1,0:T(8,128)(2,1)S(1)}) custom-call(bf16[1,288,128]{2,1,0:T(8,128)(2,1)S(1)} %add_convert_fusion.2.after, bf16[3,34,128,256]{3,2,1,0:T(8,128)(2,1)S(1)} %get-tuple-element.68.moved, bf16[32,128,256]{2,1,0:T(8,128)(2,1)S(1)} %bitcast.53, ...), custom_call_target="tpu_custom_call", output_to_operand_aliasing={{0}: (5, {})} | custom-call | flops 603979776 | bytes 4194304 | tf_op jit(solution)/shard_map/input_grad/pallas_call | solution.py:438
  43.4 0.2 collective-permute-done.12
  43.6 2.4 %collective-permute-done.10 = bf16[1,288,128]{2,1,0:T(8,128)(2,1)S(1)} collective-permute-done((bf16[1,288,128]{2,1,0:T(8,128)(2,1)S(1)}, bf16[1,288,128]{2,1,0:T(8,128)(2,1)S(1)}, u32[]{:S(2)}, u32[]{:S(2)}) %collective-permute-start.10) | collective-permute-done | bytes 73760 | tf_op jit(solution)/shard_map/ppermute | solution.py:342
  46.0 0.2 collective-permute-start.16
  46.2 1.7 %collective-permute-start.15 = (bf16[1,288,128]{2,1,0:T(8,128)(2,1)S(1)}, bf16[1,288,128]{2,1,0:T(8,128)(2,1)S(1)}, u32[]{:S(2)}, u32[]{:S(2)}) collective-permute-start(bf16[1,288,128]{2,1,0:T(8,128)(2,1)S(1)} %add_convert_fusion.1.refs_0_), channel_id=1, source_target_pairs={{0,24},{4,28},{8,16},{12,20},{16,8},{20,12},{24,0},{28,4},{1,25},{... | collective-permute-start | bytes 221192 | tf_op jit(solution)/shard_map/ppermute | solution.py:477
  48.0 0.7 %collective-permute-start.14 = (bf16[1,288,128]{2,1,0:T(8,128)(2,1)S(1)}, bf16[1,288,128]{2,1,0:T(8,128)(2,1)S(1)}, u32[]{:S(2)}, u32[]{:S(2)}) collective-permute-start(bf16[1,288,128]{2,1,0:T(8,128)(2,1)S(1)} %add_convert_fusion.1.refs_0_), channel_id=1, source_target_pairs={{0,16},{4,20},{8,24},{12,28},{16,0},{20,4},{24,8},{28,12},{1,17},{... | collective-permute-start | bytes 221192 | tf_op jit(solution)/shard_map/ppermute | solution.py:477
  48.7 1.1 %collective-permute-start.13 = (bf16[1,288,128]{2,1,0:T(8,128)(2,1)S(1)}, bf16[1,288,128]{2,1,0:T(8,128)(2,1)S(1)}, u32[]{:S(2)}, u32[]{:S(2)}) collective-permute-start(bf16[1,288,128]{2,1,0:T(8,128)(2,1)S(1)} %add_convert_fusion.1.refs_0_), channel_id=1, source_target_pairs={{0,8},{4,12},{8,0},{12,4},{16,24},{20,28},{24,16},{28,20},{1,9},{5... | collective-permute-start | bytes 221192 | tf_op jit(solution)/shard_map/ppermute | solution.py:477
  49.7 0.7 %collective-permute-done.16.refs_0_ = bf16[1,288,128]{2,1,0:T(8,128)(2,1)S(1)} collective-permute-done((bf16[1,288,128]{2,1,0:T(8,128)(2,1)S(1)}, bf16[1,288,128]{2,1,0:T(8,128)(2,1)S(1)}, u32[]{:S(2)}, u32[]{:S(2)}) %collective-permute-start.16) | collective-permute-done | bytes 73760 | tf_op jit(solution)/shard_map/ppermute | solution.py:342
  50.4 0.9 %collective-permute-start.17 = (bf16[1,288,128]{2,1,0:T(8,128)(2,1)S(1)}, bf16[1,288,128]{2,1,0:T(8,128)(2,1)S(1)}, u32[]{:S(2)}, u32[]{:S(2)}) collective-permute-start(bf16[1,288,128]{2,1,0:T(8,128)(2,1)S(1)} %collective-permute-done.16.refs_0_), channel_id=1, source_target_pairs={{0,8},{4,12},{8,0},{12,4},{16,24},{20,28},{24,16},{28,20},{1,9},{5... | collective-permute-start | bytes 221192 | tf_op jit(solution)/shard_map/ppermute | solution.py:477
  51.3 1.4 %collective-permute-start.19 = (bf16[1,288,128]{2,1,0:T(8,128)(2,1)S(1)}, bf16[1,288,128]{2,1,0:T(8,128)(2,1)S(1)}, u32[]{:S(2)}, u32[]{:S(2)}) collective-permute-start(bf16[1,288,128]{2,1,0:T(8,128)(2,1)S(1)} %collective-permute-done.16.refs_0_), channel_id=1, source_target_pairs={{0,24},{4,28},{8,16},{12,20},{16,8},{20,12},{24,0},{28,4},{1,25},{... | collective-permute-start | bytes 221192 | tf_op jit(solution)/shard_map/ppermute | solution.py:477
  52.7 1.2 %collective-permute-start.18 = (bf16[1,288,128]{2,1,0:T(8,128)(2,1)S(1)}, bf16[1,288,128]{2,1,0:T(8,128)(2,1)S(1)}, u32[]{:S(2)}, u32[]{:S(2)}) collective-permute-start(bf16[1,288,128]{2,1,0:T(8,128)(2,1)S(1)} %collective-permute-done.16.refs_0_), channel_id=1, source_target_pairs={{0,16},{4,20},{8,24},{12,28},{16,0},{20,4},{24,8},{28,12},{1,17},{... | collective-permute-start | bytes 221192 | tf_op jit(solution)/shard_map/ppermute | solution.py:477
  53.9 0.2 collective-permute-done.14.refs_2_
  54.2 0.6 %collective-permute-done.17.refs_1_ = bf16[1,288,128]{2,1,0:T(8,128)(2,1)S(1)} collective-permute-done((bf16[1,288,128]{2,1,0:T(8,128)(2,1)S(1)}, bf16[1,288,128]{2,1,0:T(8,128)(2,1)S(1)}, u32[]{:S(2)}, u32[]{:S(2)}) %collective-permute-start.17) | collective-permute-done | bytes 73760 | tf_op jit(solution)/shard_map/ppermute | solution.py:477
  54.8 0.1 collective-permute-start.21
  54.9 0.9 %finish.3.refs_8_ = f32[9,256,256]{2,1,0:T(8,128)} custom-call(bf16[1,288,128]{2,1,0:T(8,128)(2,1)S(1)} %add_convert_fusion.1.refs_0_, bf16[1,288,128]{2,1,0:T(8,128)(2,1)S(1)} %collective-permute-done.13.refs_1_, bf16[1,288,128]{2,1,0:T(8,128)(2,1)S(1)} %collective-permute-done.14.refs_2_, bf16[1,288,128]{2,1,0:T(8,128)(2,1)S(1)} %collective-permute-done.15.refs_3_), custom_call_target="tpu_custom_call" | custom-call | flops 1048576 | bytes 4194304 | tf_op jit(solution)/shard_map/finish/pallas_call | solution.py:542
  55.9 0.7 %collective-permute-done.19.refs_3_ = bf16[1,288,128]{2,1,0:T(8,128)(2,1)S(1)} collective-permute-done((bf16[1,288,128]{2,1,0:T(8,128)(2,1)S(1)}, bf16[1,288,128]{2,1,0:T(8,128)(2,1)S(1)}, u32[]{:S(2)}, u32[]{:S(2)}) %collective-permute-start.19) | collective-permute-done | bytes 73760 | tf_op jit(solution)/shard_map/ppermute | solution.py:477
  56.6 0.8 %collective-permute-done.18.refs_2_ = bf16[1,288,128]{2,1,0:T(8,128)(2,1)S(1)} collective-permute-done((bf16[1,288,128]{2,1,0:T(8,128)(2,1)S(1)}, bf16[1,288,128]{2,1,0:T(8,128)(2,1)S(1)}, u32[]{:S(2)}, u32[]{:S(2)}) %collective-permute-start.18) | collective-permute-done | bytes 73760 | tf_op jit(solution)/shard_map/ppermute | solution.py:477
  57.4 0.1 collective-permute-start.20
  57.5 1.2 %finish.4.refs_8_ = f32[9,256,256]{2,1,0:T(8,128)} custom-call(bf16[1,288,128]{2,1,0:T(8,128)(2,1)S(1)} %collective-permute-done.16.refs_0_, bf16[1,288,128]{2,1,0:T(8,128)(2,1)S(1)} %collective-permute-done.17.refs_1_, bf16[1,288,128]{2,1,0:T(8,128)(2,1)S(1)} %collective-permute-done.18.refs_2_, ...), custom_call_target="tpu_custom_call", output_to_operand_aliasing={{}: (8, {})} | custom-call | flops 1048576 | bytes 4194304 | tf_op jit(solution)/shard_map/finish/pallas_call | solution.py:542
  58.8 0.3 collective-permute-done.20
  59.1 1.0 %finish.5 = (f32[9,256,256]{2,1,0:T(8,128)}, bf16[2,128,256]{2,1,0:T(8,128)(2,1)}) custom-call(bf16[1,288,128]{2,1,0:T(8,128)(2,1)S(1)} %get-tuple-element.115.refs_0_, bf16[1,288,128]{2,1,0:T(8,128)(2,1)S(1)} %get-tuple-element.114.refs_1_, bf16[1,288,128]{2,1,0:T(8,128)(2,1)S(1)} %get-tuple-element.113.refs_2_, ...), custom_call_target="tpu_custom_call", output_to_operand_aliasing={{0}: (8, {})} | custom-call | flops 1048576 | bytes 4194304 | tf_op jit(solution)/shard_map/finish/pallas_call | solution.py:542
  (33 shorter events, 0.3 us)
Async XLA Ops:
  0.6 8.0 %copy-start.2 = (bf16[1,32,128,256]{3,2,1,0:T(8,128)(2,1)S(1)}, bf16[1,32,128,256]{3,2,1,0:T(8,128)(2,1)}, u32[]{:S(2)}) copy-start(bf16[1,32,128,256]{3,2,1,0:T(8,128)(2,1)} %param.11) | copy-start | bytes 6291460
  0.6 8.0 %copy-start.3 = (f32[1000,256]{1,0:T(8,128)S(1)}, f32[1000,256]{1,0:T(8,128)}, u32[]{:S(2)}) copy-start(f32[1000,256]{1,0:T(8,128)} %scales.1) | copy-start | bytes 3072004
  2.2 7.5 %collective-permute-start = (bf16[96,256]{1,0:T(8,128)(2,1)S(1)}, bf16[96,256]{1,0:T(8,128)(2,1)S(1)}, u32[]{:S(2)}, u32[]{:S(2)}) collective-permute-start(bf16[96,256]{1,0:T(8,128)(2,1)S(1)} %get-tuple-element.56), channel_id=1, source_target_pairs={{0,3},{1,2},{2,1},{3,0},{4,7},{5,6},{6,5},{7,4},{8,11},{9,10},{10,... | collective-permute-start | bytes 147464 | tf_op jit(solution)/shard_map/ppermute | solution.py:342
  7.3 4.1 %collective-permute-start.1 = (bf16[96,256]{1,0:T(8,128)(2,1)S(1)}, bf16[96,256]{1,0:T(8,128)(2,1)S(1)}, u32[]{:S(2)}, u32[]{:S(2)}) collective-permute-start(bf16[96,256]{1,0:T(8,128)(2,1)S(1)} %get-tuple-element.57), channel_id=1, source_target_pairs={{0,1},{1,0},{2,3},{3,2},{4,5},{5,4},{6,7},{7,6},{8,9},{9,8},{10,11... | collective-permute-start | bytes 147464 | tf_op jit(solution)/shard_map/ppermute | solution.py:342
  7.3 5.8 %collective-permute-start.2 = (bf16[64,256]{1,0:T(8,128)(2,1)S(1)}, bf16[64,256]{1,0:T(8,128)(2,1)S(1)}, u32[]{:S(2)}, u32[]{:S(2)}) collective-permute-start(bf16[64,256]{1,0:T(8,128)(2,1)S(1)} %get-tuple-element.61), channel_id=1, source_target_pairs={{0,2},{1,3},{2,0},{3,1},{4,6},{5,7},{6,4},{7,5},{8,10},{9,11},{10,... | collective-permute-start | bytes 98312 | tf_op jit(solution)/shard_map/ppermute | solution.py:342
  11.4 1.7 %copy-start = (bf16[1,32,128,256]{3,2,1,0:T(8,128)(2,1)S(1)}, bf16[1,32,128,256]{3,2,1,0:T(8,128)(2,1)}, u32[]{:S(2)}) copy-start(bf16[1,32,128,256]{3,2,1,0:T(8,128)(2,1)} %param.6) | copy-start | bytes 6291460
  11.5 5.4 %collective-permute-start.3 = (bf16[144,256]{1,0:T(8,128)(2,1)S(1)}, bf16[144,256]{1,0:T(8,128)(2,1)S(1)}, u32[]{:S(2)}, u32[]{:S(2)}) collective-permute-start(bf16[144,256]{1,0:T(8,128)(2,1)S(1)} %get-tuple-element.63), channel_id=1, source_target_pairs={{4,8},{12,16},{20,24},{28,0},{8,4},{16,12},{24,20},{0,28},{5,9},{1... | collective-permute-start | bytes 221192 | tf_op jit(solution)/shard_map/ppermute | solution.py:385
  12.2 4.8 %collective-permute-start.4 = (bf16[144,256]{1,0:T(8,128)(2,1)S(1)}, bf16[144,256]{1,0:T(8,128)(2,1)S(1)}, u32[]{:S(2)}, u32[]{:S(2)}) collective-permute-start(bf16[144,256]{1,0:T(8,128)(2,1)S(1)} %get-tuple-element.64), channel_id=1, source_target_pairs={{0,4},{4,0},{8,12},{12,8},{16,20},{20,16},{24,28},{28,24},{1,5},{5... | collective-permute-start | bytes 221192 | tf_op jit(solution)/shard_map/ppermute | solution.py:388
  18.6 3.0 %collective-permute-start.5 = (bf16[4,2,288,128]{3,2,1,0:T(8,128)(2,1)S(1)}, bf16[4,2,288,128]{3,2,1,0:T(8,128)(2,1)S(1)}, u32[]{:S(2)}, u32[]{:S(2)}) collective-permute-start(bf16[4,2,288,128]{3,2,1,0:T(8,128)(2,1)S(1)} %get-tuple-element.69), channel_id=1, source_target_pairs={{0,4},{4,0},{8,12},{12,8},{16,20},{20,16},{24,28},{28,24},{1,5},{5... | collective-permute-start | bytes 1769480 | tf_op jit(solution)/shard_map/ppermute | solution.py:474
  21.6 3.8 %copy-start.1 = (bf16[3,3,256,256]{3,2,1,0:T(8,128)(2,1)S(1)}, bf16[3,3,256,256]{3,2,1,0:T(8,128)(2,1)}, u32[]{:S(2)}) copy-start(bf16[3,3,256,256]{3,2,1,0:T(8,128)(2,1)} %param.8) | copy-start | bytes 3538948
  21.9 9.0 %collective-permute-start.8 = (bf16[2,288,128]{2,1,0:T(8,128)(2,1)S(1)}, bf16[2,288,128]{2,1,0:T(8,128)(2,1)S(1)}, u32[]{:S(2)}, u32[]{:S(2)}) collective-permute-start(bf16[2,288,128]{2,1,0:T(8,128)(2,1)S(1)} %get-tuple-element.105), channel_id=1, source_target_pairs={{0,24},{4,28},{8,16},{12,20},{16,8},{20,12},{24,0},{28,4},{1,25},{... | collective-permute-start | bytes 442376 | tf_op jit(solution)/shard_map/ppermute | solution.py:477
  23.7 8.5 %collective-permute-start.7 = (bf16[2,288,128]{2,1,0:T(8,128)(2,1)S(1)}, bf16[2,288,128]{2,1,0:T(8,128)(2,1)S(1)}, u32[]{:S(2)}, u32[]{:S(2)}) collective-permute-start(bf16[2,288,128]{2,1,0:T(8,128)(2,1)S(1)} %get-tuple-element.106), channel_id=1, source_target_pairs={{0,16},{4,20},{8,24},{12,28},{16,0},{20,4},{24,8},{28,12},{1,17},{... | collective-permute-start | bytes 442376 | tf_op jit(solution)/shard_map/ppermute | solution.py:477
  24.3 7.9 %collective-permute-start.6 = (bf16[2,288,128]{2,1,0:T(8,128)(2,1)S(1)}, bf16[2,288,128]{2,1,0:T(8,128)(2,1)S(1)}, u32[]{:S(2)}, u32[]{:S(2)}) collective-permute-start(bf16[2,288,128]{2,1,0:T(8,128)(2,1)S(1)} %get-tuple-element.107), channel_id=1, source_target_pairs={{0,8},{4,12},{8,0},{12,4},{16,24},{20,28},{24,16},{28,20},{1,9},{5... | collective-permute-start | bytes 442376 | tf_op jit(solution)/shard_map/ppermute | solution.py:477
  32.2 6.5 %collective-permute-start.11 = (bf16[256,128]{1,0:T(8,128)(2,1)S(1)}, bf16[256,128]{1,0:T(8,128)(2,1)S(1)}, u32[]{:S(2)}, u32[]{:S(2)}) collective-permute-start(bf16[256,128]{1,0:T(8,128)(2,1)S(1)} %pad_maximum_fusion.2), channel_id=1, source_target_pairs={{0,2},{1,3},{2,0},{3,1},{4,6},{5,7},{6,4},{7,5},{8,10},{9,11},{10,... | collective-permute-start | bytes 196616 | tf_op jit(solution)/shard_map/ppermute | solution.py:342
  33.0 5.7 %collective-permute-start.9 = (bf16[1,288,128]{2,1,0:T(8,128)(2,1)S(1)}, bf16[1,288,128]{2,1,0:T(8,128)(2,1)S(1)}, u32[]{:S(2)}, u32[]{:S(2)}) collective-permute-start(bf16[1,288,128]{2,1,0:T(8,128)(2,1)S(1)} %slice.101), channel_id=1, source_target_pairs={{0,1},{1,0},{2,3},{3,2},{4,5},{5,4},{6,7},{7,6},{8,9},{9,8},{10,11... | collective-permute-start | bytes 221192 | tf_op jit(solution)/shard_map/ppermute | solution.py:342
  38.7 4.9 %collective-permute-start.12 = (bf16[256,128]{1,0:T(8,128)(2,1)S(1)}, bf16[256,128]{1,0:T(8,128)(2,1)S(1)}, u32[]{:S(2)}, u32[]{:S(2)}) collective-permute-start(bf16[256,128]{1,0:T(8,128)(2,1)S(1)} %pad_maximum_fusion.3), channel_id=1, source_target_pairs={{0,1},{1,0},{2,3},{3,2},{4,5},{5,4},{6,7},{7,6},{8,9},{9,8},{10,11... | collective-permute-start | bytes 196616 | tf_op jit(solution)/shard_map/ppermute | solution.py:342
  39.6 6.4 %collective-permute-start.10 = (bf16[1,288,128]{2,1,0:T(8,128)(2,1)S(1)}, bf16[1,288,128]{2,1,0:T(8,128)(2,1)S(1)}, u32[]{:S(2)}, u32[]{:S(2)}) collective-permute-start(bf16[1,288,128]{2,1,0:T(8,128)(2,1)S(1)} %add_convert_fusion.2.after), channel_id=1, source_target_pairs={{0,2},{1,3},{2,0},{3,1},{4,6},{5,7},{6,4},{7,5},{8,10},{9,11},{10,... | collective-permute-start | bytes 221192 | tf_op jit(solution)/shard_map/ppermute | solution.py:342
  46.0 4.4 %collective-permute-start.16 = (bf16[1,288,128]{2,1,0:T(8,128)(2,1)S(1)}, bf16[1,288,128]{2,1,0:T(8,128)(2,1)S(1)}, u32[]{:S(2)}, u32[]{:S(2)}) collective-permute-start(bf16[1,288,128]{2,1,0:T(8,128)(2,1)S(1)} %add_convert_fusion.1.refs_0_), channel_id=1, source_target_pairs={{0,1},{1,0},{2,3},{3,2},{4,5},{5,4},{6,7},{7,6},{8,9},{9,8},{10,11... | collective-permute-start | bytes 221192 | tf_op jit(solution)/shard_map/ppermute | solution.py:342
  46.2 6.5 %collective-permute-start.15 = (bf16[1,288,128]{2,1,0:T(8,128)(2,1)S(1)}, bf16[1,288,128]{2,1,0:T(8,128)(2,1)S(1)}, u32[]{:S(2)}, u32[]{:S(2)}) collective-permute-start(bf16[1,288,128]{2,1,0:T(8,128)(2,1)S(1)} %add_convert_fusion.1.refs_0_), channel_id=1, source_target_pairs={{0,24},{4,28},{8,16},{12,20},{16,8},{20,12},{24,0},{28,4},{1,25},{... | collective-permute-start | bytes 221192 | tf_op jit(solution)/shard_map/ppermute | solution.py:477
  48.0 6.2 %collective-permute-start.14 = (bf16[1,288,128]{2,1,0:T(8,128)(2,1)S(1)}, bf16[1,288,128]{2,1,0:T(8,128)(2,1)S(1)}, u32[]{:S(2)}, u32[]{:S(2)}) collective-permute-start(bf16[1,288,128]{2,1,0:T(8,128)(2,1)S(1)} %add_convert_fusion.1.refs_0_), channel_id=1, source_target_pairs={{0,16},{4,20},{8,24},{12,28},{16,0},{20,4},{24,8},{28,12},{1,17},{... | collective-permute-start | bytes 221192 | tf_op jit(solution)/shard_map/ppermute | solution.py:477
  48.7 5.5 %collective-permute-start.13 = (bf16[1,288,128]{2,1,0:T(8,128)(2,1)S(1)}, bf16[1,288,128]{2,1,0:T(8,128)(2,1)S(1)}, u32[]{:S(2)}, u32[]{:S(2)}) collective-permute-start(bf16[1,288,128]{2,1,0:T(8,128)(2,1)S(1)} %add_convert_fusion.1.refs_0_), channel_id=1, source_target_pairs={{0,8},{4,12},{8,0},{12,4},{16,24},{20,28},{24,16},{28,20},{1,9},{5... | collective-permute-start | bytes 221192 | tf_op jit(solution)/shard_map/ppermute | solution.py:477
  50.4 4.4 %collective-permute-start.17 = (bf16[1,288,128]{2,1,0:T(8,128)(2,1)S(1)}, bf16[1,288,128]{2,1,0:T(8,128)(2,1)S(1)}, u32[]{:S(2)}, u32[]{:S(2)}) collective-permute-start(bf16[1,288,128]{2,1,0:T(8,128)(2,1)S(1)} %collective-permute-done.16.refs_0_), channel_id=1, source_target_pairs={{0,8},{4,12},{8,0},{12,4},{16,24},{20,28},{24,16},{28,20},{1,9},{5... | collective-permute-start | bytes 221192 | tf_op jit(solution)/shard_map/ppermute | solution.py:477
  51.3 5.3 %collective-permute-start.19 = (bf16[1,288,128]{2,1,0:T(8,128)(2,1)S(1)}, bf16[1,288,128]{2,1,0:T(8,128)(2,1)S(1)}, u32[]{:S(2)}, u32[]{:S(2)}) collective-permute-start(bf16[1,288,128]{2,1,0:T(8,128)(2,1)S(1)} %collective-permute-done.16.refs_0_), channel_id=1, source_target_pairs={{0,24},{4,28},{8,16},{12,20},{16,8},{20,12},{24,0},{28,4},{1,25},{... | collective-permute-start | bytes 221192 | tf_op jit(solution)/shard_map/ppermute | solution.py:477
  52.7 4.6 %collective-permute-start.18 = (bf16[1,288,128]{2,1,0:T(8,128)(2,1)S(1)}, bf16[1,288,128]{2,1,0:T(8,128)(2,1)S(1)}, u32[]{:S(2)}, u32[]{:S(2)}) collective-permute-start(bf16[1,288,128]{2,1,0:T(8,128)(2,1)S(1)} %collective-permute-done.16.refs_0_), channel_id=1, source_target_pairs={{0,16},{4,20},{8,24},{12,28},{16,0},{20,4},{24,8},{28,12},{1,17},{... | collective-permute-start | bytes 221192 | tf_op jit(solution)/shard_map/ppermute | solution.py:477
  54.8 2.7 %collective-permute-start.21 = (bf16[4,1,288,128]{3,2,1,0:T(8,128)(2,1)S(1)}, bf16[4,1,288,128]{3,2,1,0:T(8,128)(2,1)S(1)}, u32[]{:S(2)}, u32[]{:S(2)}) collective-permute-start(bf16[4,1,288,128]{3,2,1,0:T(8,128)(2,1)S(1)} %pad_maximum_fusion.1), channel_id=1, source_target_pairs={{0,4},{4,0},{8,12},{12,8},{16,20},{20,16},{24,28},{28,24},{1,5},{5... | collective-permute-start | bytes 884744 | tf_op jit(solution)/shard_map/ppermute | solution.py:474
  57.4 1.6 %collective-permute-start.20 = (bf16[4,1,288,128]{3,2,1,0:T(8,128)(2,1)S(1)}, bf16[4,1,288,128]{3,2,1,0:T(8,128)(2,1)S(1)}, u32[]{:S(2)}, u32[]{:S(2)}) collective-permute-start(bf16[4,1,288,128]{3,2,1,0:T(8,128)(2,1)S(1)} %pad_maximum_fusion), channel_id=1, source_target_pairs={{0,4},{4,0},{8,12},{12,8},{16,20},{20,16},{24,28},{28,24},{1,5},{5... | collective-permute-start | bytes 884744 | tf_op jit(solution)/shard_map/ppermute | solution.py:474

commit v9 on v6

--- a/solution.py
+++ b/solution.py
@@ -152,7 +152,7 @@
             moved[k, r + 1, low : low + 16, :] = tile.astype(BF)
         return 0
 
-    lax.fori_loop(0, rows, patch, 0)
+    lax.fori_loop(0, rows, patch, 0, unroll=8)
     last = rows // 4 - 1
 
     def build(g):
@@ -209,7 +209,7 @@
         put(k + 4, acc[:, half:])
         return 0
 
-    lax.fori_loop(0, 4, tap, 0)
+    lax.fori_loop(0, 4, tap, 0, unroll=True)
     return put, total
 
 

time: 57.5 us -> 56.3 us (0.979)
  Pallas kernels: 22.5 us -> 21.1 us
    pallas_call x1, Pallas kernels: 1.68 us -> 0.94 us  [per_device(): pl.pallas_call(other_kernel, out_shape=[part, shape(ch, half, dtype=F32),...]
  transfers between devices with their start and end apart: 21 -> 21, of which waited for: 10 -> 10; matrix products, arithmetic and copies ran while one was open for 0% -> 0% of each run, Pallas kernels for 32% -> 31%
where the time goes in v9:
time: 56.3 us; the launch traced here: 56.1 us
  starting transfers between devices  21.6 us (38%)
  Pallas kernels  21.1 us (37%)
  waiting for transfers between devices  11.3 us (20%)
  between operations  1.57 us (3%)
    ppermute x9, starting transfers between devices, plane_swap(): return lax.ppermute(x, 'row', xor_pairs(nrow, 2 * s))  10.6 us
    ppermute x7, starting transfers between devices, col_swap(): return lax.ppermute(x, 'col', xor_pairs(n, s))  9.12 us
    pallas_call x3, Pallas kernels, input_piece(): pl.pallas_call(functools.partial(input_kernel, made, size, n), out_shape=...  8.92 us
    ppermute x7, waiting for transfers between devices, col_swap(): return lax.ppermute(x, 'col', xor_pairs(n, s))  7.36 us
    pallas_call x3, Pallas kernels, finish(): pl.pallas_call(functools.partial(finish_kernel, float(pixels) ** (-0.5),...  3.15 us
    pallas_call x1, Pallas kernels, per_device(): pl.pallas_call(functools.partial(prepare_kernel, n, cr), out_shape=[shape...  3.06 us
    ppermute x9, waiting for transfers between devices, plane_swap(): return lax.ppermute(x, 'row', xor_pairs(nrow, 2 * s))  2.99 us
    pallas_call x1, Pallas kernels, per_device(): pl.pallas_call(mine_kernel, out_shape=part, in_specs=[vmem()] * 3, out_sp...  2.36 us
  transfers between devices with their start and end apart: 21, of which 10 were waited for; matrix products, arithmetic and copies ran while one was open for 0% of the time, Pallas kernels for 31%

profile of v9, /device:TPU:0, one launch (start us, length us, event | category | flops | bytes accessed | tf_op | source)
XLA Modules:
  0.0 56.1 jit_solution(1927016993622750911)
XLA Ops:
  0.7 1.6 %start.1 = (bf16[64,256]{1,0:T(8,128)(2,1)S(1)}, bf16[96,256]{1,0:T(8,128)(2,1)S(1)}, bf16[64,256]{1,0:T(8,128)(2,1)S(1)}, bf16[96,256]{1,0:T(8,128)(2,1)S(1)}) custom-call(bf16[32,128,256]{2,1,0:T(8,128)(2,1)} %bitcast.60, bf16[2,128,256]{2,1,0:T(8,128)(2,1)} %bitcast.81), custom_call_target="tpu_custom_call" | custom-call | flops 2147483648 | bytes 4194304 | tf_op jit(solution)/shard_map/start/pallas_call | solution.py:344
  2.2 5.1 %collective-permute-start = (bf16[96,256]{1,0:T(8,128)(2,1)S(1)}, bf16[96,256]{1,0:T(8,128)(2,1)S(1)}, u32[]{:S(2)}, u32[]{:S(2)}) collective-permute-start(bf16[96,256]{1,0:T(8,128)(2,1)S(1)} %get-tuple-element.52), channel_id=1, source_target_pairs={{0,3},{1,2},{2,1},{3,0},{4,7},{5,6},{6,5},{7,4},{8,11},{9,10},{10,... | collective-permute-start | bytes 147464 | tf_op jit(solution)/shard_map/ppermute | solution.py:342
  7.3 0.0 collective-permute-start.1
  7.3 0.6 %collective-permute-start.2 = (bf16[64,256]{1,0:T(8,128)(2,1)S(1)}, bf16[64,256]{1,0:T(8,128)(2,1)S(1)}, u32[]{:S(2)}, u32[]{:S(2)}) collective-permute-start(bf16[64,256]{1,0:T(8,128)(2,1)S(1)} %get-tuple-element.57), channel_id=1, source_target_pairs={{0,2},{1,3},{2,0},{3,1},{4,6},{5,7},{6,4},{7,5},{8,10},{9,11},{10,... | collective-permute-start | bytes 98312 | tf_op jit(solution)/shard_map/ppermute | solution.py:342
  8.7 1.1 %load.1 = (bf16[3,34,128,256]{3,2,1,0:T(8,128)(2,1)S(1)}, f32[1,256]{1,0:T(1,128)S(1)}) custom-call(s32[1]{0:T(128)S(6)} %copy.21.steps, bf16[32,128,256]{2,1,0:T(8,128)(2,1)S(1)} %bitcast.61, f32[1000,256]{1,0:T(8,128)S(1)} %copy-done.3), custom_call_target="tpu_custom_call" | custom-call | flops 1048576 | bytes 4194304 | tf_op jit(solution)/shard_map/load/pallas_call | solution.py:360
  9.7 0.0 collective-permute-done.refs_0_.refs_3_
  9.7 1.7 %collective-permute-done.1.refs_1_ = bf16[96,256]{1,0:T(8,128)(2,1)S(1)} collective-permute-done((bf16[96,256]{1,0:T(8,128)(2,1)S(1)}, bf16[96,256]{1,0:T(8,128)(2,1)S(1)}, u32[]{:S(2)}, u32[]{:S(2)}) %collective-permute-start.1) | collective-permute-done | bytes 49184 | tf_op jit(solution)/shard_map/ppermute | solution.py:342
  11.4 0.1 edges.1
  11.5 0.7 %collective-permute-start.3 = (bf16[144,256]{1,0:T(8,128)(2,1)S(1)}, bf16[144,256]{1,0:T(8,128)(2,1)S(1)}, u32[]{:S(2)}, u32[]{:S(2)}) collective-permute-start(bf16[144,256]{1,0:T(8,128)(2,1)S(1)} %get-tuple-element.59), channel_id=1, source_target_pairs={{4,8},{12,16},{20,24},{28,0},{8,4},{16,12},{24,20},{0,28},{5,9},{1... | collective-permute-start | bytes 221192 | tf_op jit(solution)/shard_map/ppermute | solution.py:385
  12.2 1.0 %collective-permute-start.4 = (bf16[144,256]{1,0:T(8,128)(2,1)S(1)}, bf16[144,256]{1,0:T(8,128)(2,1)S(1)}, u32[]{:S(2)}, u32[]{:S(2)}) collective-permute-start(bf16[144,256]{1,0:T(8,128)(2,1)S(1)} %get-tuple-element.60), channel_id=1, source_target_pairs={{0,4},{4,0},{8,12},{12,8},{16,20},{20,16},{24,28},{28,24},{1,5},{5... | collective-permute-start | bytes 221192 | tf_op jit(solution)/shard_map/ppermute | solution.py:388
  13.2 3.1 %prepare.1 = (bf16[3,34,128,256]{3,2,1,0:T(8,128)(2,1)S(1)}, bf16[256,4096]{1,0:T(8,128)(2,1)S(1)}, bf16[8,32,256]{2,1,0:T(8,128)(2,1)S(1)}, f32[5,256,256]{2,1,0:T(8,128)S(1)}) custom-call(bf16[32,128,256]{2,1,0:T(8,128)(2,1)S(1)} %bitcast.53, f32[32,256]{1,0:T(8,128)S(1)} %get-tuple-element.54.left, ...), custom_call_target="tpu_custom_call", output_to_operand_aliasing={{0}: (3, {})} | custom-call | flops 4294967296 | bytes 4194304 | tf_op jit(solution)/shard_map/prepare/pallas_call | solution.py:391
  16.2 0.7 %collective-permute-done.3.two = bf16[144,256]{1,0:T(8,128)(2,1)S(1)} collective-permute-done((bf16[144,256]{1,0:T(8,128)(2,1)S(1)}, bf16[144,256]{1,0:T(8,128)(2,1)S(1)}, u32[]{:S(2)}, u32[]{:S(2)}) %collective-permute-start.3) | collective-permute-done | bytes 73760 | tf_op jit(solution)/shard_map/ppermute | solution.py:385
  16.9 0.0 collective-permute-done.4.one
  16.9 0.9 %weight_other.1 = (bf16[4,2,288,128]{3,2,1,0:T(8,128)(2,1)S(1)}, f32[256,128]{1,0:T(8,128)S(1)}, bf16[3,34,128,256]{3,2,1,0:T(8,128)(2,1)S(1)}) custom-call(bf16[256,4096]{1,0:T(8,128)(2,1)S(1)} %get-tuple-element.58.act_t, bf16[144,256]{1,0:T(8,128)(2,1)S(1)} %collective-permute-done.3.two, ...), custom_call_target="tpu_custom_call", output_to_operand_aliasing={{2}: (4, {})} | custom-call | flops 603979776 | bytes 8388608 | tf_op jit(solution)/shard_map/weight_other/pallas_call | solution.py:414
  17.9 0.1 collective-permute-start.5
  18.0 2.4 %weight_mine.1 = bf16[4,2,288,128]{3,2,1,0:T(8,128)(2,1)S(1)} custom-call(bf16[256,4096]{1,0:T(8,128)(2,1)S(1)} %get-tuple-element.58.act_t, f32[256,128]{1,0:T(8,128)S(1)} %get-tuple-element.63.rest, bf16[3,34,128,256]{3,2,1,0:T(8,128)(2,1)S(1)} %get-tuple-element.64.moved), custom_call_target="tpu_custom_call" | custom-call | flops 2147483648 | bytes 8388608 | tf_op jit(solution)/shard_map/weight_mine/pallas_call | solution.py:424
  20.3 0.0 copy-start.1
  20.3 0.2 add_convert_fusion.after
  20.6 1.7 %collective-permute-start.8 = (bf16[2,288,128]{2,1,0:T(8,128)(2,1)S(1)}, bf16[2,288,128]{2,1,0:T(8,128)(2,1)S(1)}, u32[]{:S(2)}, u32[]{:S(2)}) collective-permute-start(bf16[2,288,128]{2,1,0:T(8,128)(2,1)S(1)} %get-tuple-element.97), channel_id=1, source_target_pairs={{0,24},{4,28},{8,16},{12,20},{16,8},{20,12},{24,0},{28,4},{1,25},{... | collective-permute-start | bytes 442376 | tf_op jit(solution)/shard_map/ppermute | solution.py:477
  22.3 0.7 %collective-permute-start.7 = (bf16[2,288,128]{2,1,0:T(8,128)(2,1)S(1)}, bf16[2,288,128]{2,1,0:T(8,128)(2,1)S(1)}, u32[]{:S(2)}, u32[]{:S(2)}) collective-permute-start(bf16[2,288,128]{2,1,0:T(8,128)(2,1)S(1)} %get-tuple-element.98), channel_id=1, source_target_pairs={{0,16},{4,20},{8,24},{12,28},{16,0},{20,4},{24,8},{28,12},{1,17},{... | collective-permute-start | bytes 442376 | tf_op jit(solution)/shard_map/ppermute | solution.py:477
  22.9 1.2 %collective-permute-start.6 = (bf16[2,288,128]{2,1,0:T(8,128)(2,1)S(1)}, bf16[2,288,128]{2,1,0:T(8,128)(2,1)S(1)}, u32[]{:S(2)}, u32[]{:S(2)}) collective-permute-start(bf16[2,288,128]{2,1,0:T(8,128)(2,1)S(1)} %get-tuple-element.99), channel_id=1, source_target_pairs={{0,8},{4,12},{8,0},{12,4},{16,24},{20,28},{24,16},{28,20},{1,9},{5... | collective-permute-start | bytes 442376 | tf_op jit(solution)/shard_map/ppermute | solution.py:477
  24.1 5.5 %input_grad.3 = (bf16[32,128,256]{2,1,0:T(8,128)(2,1)}, bf16[6,2,32,128]{3,2,1,0:T(8,128)(2,1)S(1)}) custom-call(bf16[4,2,288,128]{3,2,1,0:T(8,128)(2,1)S(1)} %add_convert_fusion.after, bf16[3,34,128,256]{3,2,1,0:T(8,128)(2,1)S(1)} %get-tuple-element.64.moved, bf16[32,128,256]{2,1,0:T(8,128)(2,1)S(1)} %bitcast.54, ...), custom_call_target="tpu_custom_call" | custom-call | flops 3623878656 | bytes 4194304 | tf_op jit(solution)/shard_map/input_grad/pallas_call | solution.py:438
  29.6 1.3 %collective-permute-done.7 = bf16[2,288,128]{2,1,0:T(8,128)(2,1)S(1)} collective-permute-done((bf16[2,288,128]{2,1,0:T(8,128)(2,1)S(1)}, bf16[2,288,128]{2,1,0:T(8,128)(2,1)S(1)}, u32[]{:S(2)}, u32[]{:S(2)}) %collective-permute-start.7) | collective-permute-done | bytes 147488 | tf_op jit(solution)/shard_map/ppermute | solution.py:477
  30.9 0.1 fusion.2.after
  31.0 0.9 %collective-permute-start.9 = (bf16[1,288,128]{2,1,0:T(8,128)(2,1)S(1)}, bf16[1,288,128]{2,1,0:T(8,128)(2,1)S(1)}, u32[]{:S(2)}, u32[]{:S(2)}) collective-permute-start(bf16[1,288,128]{2,1,0:T(8,128)(2,1)S(1)} %slice.105), channel_id=1, source_target_pairs={{0,1},{1,0},{2,3},{3,2},{4,5},{5,4},{6,7},{7,6},{8,9},{9,8},{10,11... | collective-permute-start | bytes 221192 | tf_op jit(solution)/shard_map/ppermute | solution.py:342
  31.9 1.9 %collective-permute-start.14 = (bf16[256,128]{1,0:T(8,128)(2,1)S(1)}, bf16[256,128]{1,0:T(8,128)(2,1)S(1)}, u32[]{:S(2)}, u32[]{:S(2)}) collective-permute-start(bf16[256,128]{1,0:T(8,128)(2,1)S(1)} %pad_maximum_fusion.3), channel_id=1, source_target_pairs={{0,2},{1,3},{2,0},{3,1},{4,6},{5,7},{6,4},{7,5},{8,10},{9,11},{10,... | collective-permute-start | bytes 196616 | tf_op jit(solution)/shard_map/ppermute | solution.py:342
  33.7 1.7 %input_grad.4 = (bf16[32,128,256]{2,1,0:T(8,128)(2,1)}, bf16[1,2,32,128]{3,2,1,0:T(8,128)(2,1)S(1)}) custom-call(bf16[2,288,128]{2,1,0:T(8,128)(2,1)S(1)} %fusion.2.after, bf16[3,34,128,256]{3,2,1,0:T(8,128)(2,1)S(1)} %get-tuple-element.64.moved, bf16[32,128,256]{2,1,0:T(8,128)(2,1)S(1)} %bitcast.55, ...), custom_call_target="tpu_custom_call", output_to_operand_aliasing={{0}: (5, {})} | custom-call | flops 603979776 | bytes 4194304 | tf_op jit(solution)/shard_map/input_grad/pallas_call | solution.py:438
  35.5 0.7 %collective-permute-done.9 = bf16[1,288,128]{2,1,0:T(8,128)(2,1)S(1)} collective-permute-done((bf16[1,288,128]{2,1,0:T(8,128)(2,1)S(1)}, bf16[1,288,128]{2,1,0:T(8,128)(2,1)S(1)}, u32[]{:S(2)}, u32[]{:S(2)}) %collective-permute-start.9) | collective-permute-done | bytes 73760 | tf_op jit(solution)/shard_map/ppermute | solution.py:342
  36.2 0.6 %collective-permute-start.10 = (bf16[1,288,128]{2,1,0:T(8,128)(2,1)S(1)}, bf16[1,288,128]{2,1,0:T(8,128)(2,1)S(1)}, u32[]{:S(2)}, u32[]{:S(2)}) collective-permute-start(bf16[1,288,128]{2,1,0:T(8,128)(2,1)S(1)} %add_convert_fusion.2.after), channel_id=1, source_target_pairs={{0,2},{1,3},{2,0},{3,1},{4,6},{5,7},{6,4},{7,5},{8,10},{9,11},{10,... | collective-permute-start | bytes 221192 | tf_op jit(solution)/shard_map/ppermute | solution.py:342
  36.7 1.2 %collective-permute-done.14 = bf16[256,128]{1,0:T(8,128)(2,1)S(1)} collective-permute-done((bf16[256,128]{1,0:T(8,128)(2,1)S(1)}, bf16[256,128]{1,0:T(8,128)(2,1)S(1)}, u32[]{:S(2)}, u32[]{:S(2)}) %collective-permute-start.14) | collective-permute-done | bytes 65568 | tf_op jit(solution)/shard_map/ppermute | solution.py:342
  38.0 1.7 %input_grad.5 = (bf16[32,128,256]{2,1,0:T(8,128)(2,1)}, bf16[1,2,32,128]{3,2,1,0:T(8,128)(2,1)S(1)}) custom-call(bf16[1,288,128]{2,1,0:T(8,128)(2,1)S(1)} %add_convert_fusion.2.after, bf16[3,34,128,256]{3,2,1,0:T(8,128)(2,1)S(1)} %get-tuple-element.64.moved, bf16[32,128,256]{2,1,0:T(8,128)(2,1)S(1)} %bitcast.56, ...), custom_call_target="tpu_custom_call", output_to_operand_aliasing={{0}: (5, {})} | custom-call | flops 603979776 | bytes 4194304 | tf_op jit(solution)/shard_map/input_grad/pallas_call | solution.py:438
  39.7 2.3 %collective-permute-done.10 = bf16[1,288,128]{2,1,0:T(8,128)(2,1)S(1)} collective-permute-done((bf16[1,288,128]{2,1,0:T(8,128)(2,1)S(1)}, bf16[1,288,128]{2,1,0:T(8,128)(2,1)S(1)}, u32[]{:S(2)}, u32[]{:S(2)}) %collective-permute-start.10) | collective-permute-done | bytes 73760 | tf_op jit(solution)/shard_map/ppermute | solution.py:342
  42.1 0.1 collective-permute-start.15
  42.1 1.9 %collective-permute-start.13 = (bf16[1,288,128]{2,1,0:T(8,128)(2,1)S(1)}, bf16[1,288,128]{2,1,0:T(8,128)(2,1)S(1)}, u32[]{:S(2)}, u32[]{:S(2)}) collective-permute-start(bf16[1,288,128]{2,1,0:T(8,128)(2,1)S(1)} %add_convert_fusion.1.refs_0_), channel_id=1, source_target_pairs={{0,24},{4,28},{8,16},{12,20},{16,8},{20,12},{24,0},{28,4},{1,25},{... | collective-permute-start | bytes 221192 | tf_op jit(solution)/shard_map/ppermute | solution.py:477
  44.1 0.8 %collective-permute-start.12 = (bf16[1,288,128]{2,1,0:T(8,128)(2,1)S(1)}, bf16[1,288,128]{2,1,0:T(8,128)(2,1)S(1)}, u32[]{:S(2)}, u32[]{:S(2)}) collective-permute-start(bf16[1,288,128]{2,1,0:T(8,128)(2,1)S(1)} %add_convert_fusion.1.refs_0_), channel_id=1, source_target_pairs={{0,16},{4,20},{8,24},{12,28},{16,0},{20,4},{24,8},{28,12},{1,17},{... | collective-permute-start | bytes 221192 | tf_op jit(solution)/shard_map/ppermute | solution.py:477
  44.8 0.9 %collective-permute-start.11 = (bf16[1,288,128]{2,1,0:T(8,128)(2,1)S(1)}, bf16[1,288,128]{2,1,0:T(8,128)(2,1)S(1)}, u32[]{:S(2)}, u32[]{:S(2)}) collective-permute-start(bf16[1,288,128]{2,1,0:T(8,128)(2,1)S(1)} %add_convert_fusion.1.refs_0_), channel_id=1, source_target_pairs={{0,8},{4,12},{8,0},{12,4},{16,24},{20,28},{24,16},{28,20},{1,9},{5... | collective-permute-start | bytes 221192 | tf_op jit(solution)/shard_map/ppermute | solution.py:477
  45.7 1.5 %collective-permute-done.15 = bf16[544,128]{1,0:T(8,128)(2,1)S(1)} collective-permute-done((bf16[544,128]{1,0:T(8,128)(2,1)S(1)}, bf16[544,128]{1,0:T(8,128)(2,1)S(1)}, u32[]{:S(2)}, u32[]{:S(2)}) %collective-permute-start.15) | collective-permute-done | bytes 139296 | tf_op jit(solution)/shard_map/ppermute | solution.py:342
  47.2 1.9 %collective-permute-start.18 = (bf16[1,288,128]{2,1,0:T(8,128)(2,1)S(1)}, bf16[1,288,128]{2,1,0:T(8,128)(2,1)S(1)}, u32[]{:S(2)}, u32[]{:S(2)}) collective-permute-start(bf16[1,288,128]{2,1,0:T(8,128)(2,1)S(1)} %slice_bitcast_fusion.12.refs_0_), channel_id=1, source_target_pairs={{0,24},{4,28},{8,16},{12,20},{16,8},{20,12},{24,0},{28,4},{1,25},{... | collective-permute-start | bytes 221192 | tf_op jit(solution)/shard_map/ppermute | solution.py:477
  49.1 1.6 %collective-permute-start.16 = (bf16[1,288,128]{2,1,0:T(8,128)(2,1)S(1)}, bf16[1,288,128]{2,1,0:T(8,128)(2,1)S(1)}, u32[]{:S(2)}, u32[]{:S(2)}) collective-permute-start(bf16[1,288,128]{2,1,0:T(8,128)(2,1)S(1)} %slice_bitcast_fusion.12.refs_0_), channel_id=1, source_target_pairs={{0,8},{4,12},{8,0},{12,4},{16,24},{20,28},{24,16},{28,20},{1,9},{5... | collective-permute-start | bytes 221192 | tf_op jit(solution)/shard_map/ppermute | solution.py:477
  50.7 0.1 collective-permute-start.20
  50.8 0.9 %finish.3.refs_8_ = f32[9,256,256]{2,1,0:T(8,128)} custom-call(bf16[1,288,128]{2,1,0:T(8,128)(2,1)S(1)} %add_convert_fusion.1.refs_0_, bf16[1,288,128]{2,1,0:T(8,128)(2,1)S(1)} %collective-permute-done.11.refs_1_, bf16[1,288,128]{2,1,0:T(8,128)(2,1)S(1)} %collective-permute-done.12.refs_2_, bf16[1,288,128]{2,1,0:T(8,128)(2,1)S(1)} %collective-permute-done.13.refs_3_), custom_call_target="tpu_custom_call" | custom-call | flops 1048576 | bytes 4194304 | tf_op jit(solution)/shard_map/finish/pallas_call | solution.py:538
  51.7 0.7 %collective-permute-done.18.refs_3_ = bf16[1,288,128]{2,1,0:T(8,128)(2,1)S(1)} collective-permute-done((bf16[1,288,128]{2,1,0:T(8,128)(2,1)S(1)}, bf16[1,288,128]{2,1,0:T(8,128)(2,1)S(1)}, u32[]{:S(2)}, u32[]{:S(2)}) %collective-permute-start.18) | collective-permute-done | bytes 73760 | tf_op jit(solution)/shard_map/ppermute | solution.py:477
  52.4 1.0 %collective-permute-done.17.refs_2_ = bf16[1,288,128]{2,1,0:T(8,128)(2,1)S(1)} collective-permute-done((bf16[1,288,128]{2,1,0:T(8,128)(2,1)S(1)}, bf16[1,288,128]{2,1,0:T(8,128)(2,1)S(1)}, u32[]{:S(2)}, u32[]{:S(2)}) %collective-permute-start.17) | collective-permute-done | bytes 73760 | tf_op jit(solution)/shard_map/ppermute | solution.py:477
  53.4 0.0 collective-permute-done.16.refs_1_
  53.5 0.1 collective-permute-start.19
  53.6 1.2 %finish.4.refs_8_ = f32[9,256,256]{2,1,0:T(8,128)} custom-call(bf16[1,288,128]{2,1,0:T(8,128)(2,1)S(1)} %slice_bitcast_fusion.12.refs_0_, bf16[1,288,128]{2,1,0:T(8,128)(2,1)S(1)} %collective-permute-done.16.refs_1_, bf16[1,288,128]{2,1,0:T(8,128)(2,1)S(1)} %collective-permute-done.17.refs_2_, ...), custom_call_target="tpu_custom_call", output_to_operand_aliasing={{}: (8, {})} | custom-call | flops 1048576 | bytes 4194304 | tf_op jit(solution)/shard_map/finish/pallas_call | solution.py:538
  54.8 0.3 collective-permute-done.19
  55.1 1.0 %finish.5 = (f32[9,256,256]{2,1,0:T(8,128)}, bf16[2,128,256]{2,1,0:T(8,128)(2,1)}) custom-call(bf16[1,288,128]{2,1,0:T(8,128)(2,1)S(1)} %get-tuple-element.107.refs_0_, bf16[1,288,128]{2,1,0:T(8,128)(2,1)S(1)} %get-tuple-element.106.refs_1_, bf16[1,288,128]{2,1,0:T(8,128)(2,1)S(1)} %get-tuple-element.105.refs_2_, ...), custom_call_target="tpu_custom_call", output_to_operand_aliasing={{0}: (8, {})} | custom-call | flops 1048576 | bytes 4194304 | tf_op jit(solution)/shard_map/finish/pallas_call | solution.py:538
  (32 shorter events, 0.3 us)
Async XLA Ops:
  0.6 8.0 %copy-start.2 = (bf16[1,32,128,256]{3,2,1,0:T(8,128)(2,1)S(1)}, bf16[1,32,128,256]{3,2,1,0:T(8,128)(2,1)}, u32[]{:S(2)}) copy-start(bf16[1,32,128,256]{3,2,1,0:T(8,128)(2,1)} %param.11) | copy-start | bytes 6291460
  0.6 8.0 %copy-start.3 = (f32[1000,256]{1,0:T(8,128)S(1)}, f32[1000,256]{1,0:T(8,128)}, u32[]{:S(2)}) copy-start(f32[1000,256]{1,0:T(8,128)} %scales.1) | copy-start | bytes 3072004
  2.2 7.5 %collective-permute-start = (bf16[96,256]{1,0:T(8,128)(2,1)S(1)}, bf16[96,256]{1,0:T(8,128)(2,1)S(1)}, u32[]{:S(2)}, u32[]{:S(2)}) collective-permute-start(bf16[96,256]{1,0:T(8,128)(2,1)S(1)} %get-tuple-element.52), channel_id=1, source_target_pairs={{0,3},{1,2},{2,1},{3,0},{4,7},{5,6},{6,5},{7,4},{8,11},{9,10},{10,... | collective-permute-start | bytes 147464 | tf_op jit(solution)/shard_map/ppermute | solution.py:342
  7.3 4.1 %collective-permute-start.1 = (bf16[96,256]{1,0:T(8,128)(2,1)S(1)}, bf16[96,256]{1,0:T(8,128)(2,1)S(1)}, u32[]{:S(2)}, u32[]{:S(2)}) collective-permute-start(bf16[96,256]{1,0:T(8,128)(2,1)S(1)} %get-tuple-element.53), channel_id=1, source_target_pairs={{0,1},{1,0},{2,3},{3,2},{4,5},{5,4},{6,7},{7,6},{8,9},{9,8},{10,11... | collective-permute-start | bytes 147464 | tf_op jit(solution)/shard_map/ppermute | solution.py:342
  7.3 5.8 %collective-permute-start.2 = (bf16[64,256]{1,0:T(8,128)(2,1)S(1)}, bf16[64,256]{1,0:T(8,128)(2,1)S(1)}, u32[]{:S(2)}, u32[]{:S(2)}) collective-permute-start(bf16[64,256]{1,0:T(8,128)(2,1)S(1)} %get-tuple-element.57), channel_id=1, source_target_pairs={{0,2},{1,3},{2,0},{3,1},{4,6},{5,7},{6,4},{7,5},{8,10},{9,11},{10,... | collective-permute-start | bytes 98312 | tf_op jit(solution)/shard_map/ppermute | solution.py:342
  11.4 1.7 %copy-start = (bf16[1,32,128,256]{3,2,1,0:T(8,128)(2,1)S(1)}, bf16[1,32,128,256]{3,2,1,0:T(8,128)(2,1)}, u32[]{:S(2)}) copy-start(bf16[1,32,128,256]{3,2,1,0:T(8,128)(2,1)} %param.6) | copy-start | bytes 6291460
  11.5 5.4 %collective-permute-start.3 = (bf16[144,256]{1,0:T(8,128)(2,1)S(1)}, bf16[144,256]{1,0:T(8,128)(2,1)S(1)}, u32[]{:S(2)}, u32[]{:S(2)}) collective-permute-start(bf16[144,256]{1,0:T(8,128)(2,1)S(1)} %get-tuple-element.59), channel_id=1, source_target_pairs={{4,8},{12,16},{20,24},{28,0},{8,4},{16,12},{24,20},{0,28},{5,9},{1... | collective-permute-start | bytes 221192 | tf_op jit(solution)/shard_map/ppermute | solution.py:385
  12.2 4.8 %collective-permute-start.4 = (bf16[144,256]{1,0:T(8,128)(2,1)S(1)}, bf16[144,256]{1,0:T(8,128)(2,1)S(1)}, u32[]{:S(2)}, u32[]{:S(2)}) collective-permute-start(bf16[144,256]{1,0:T(8,128)(2,1)S(1)} %get-tuple-element.60), channel_id=1, source_target_pairs={{0,4},{4,0},{8,12},{12,8},{16,20},{20,16},{24,28},{28,24},{1,5},{5... | collective-permute-start | bytes 221192 | tf_op jit(solution)/shard_map/ppermute | solution.py:388
  17.9 2.5 %collective-permute-start.5 = (bf16[4,2,288,128]{3,2,1,0:T(8,128)(2,1)S(1)}, bf16[4,2,288,128]{3,2,1,0:T(8,128)(2,1)S(1)}, u32[]{:S(2)}, u32[]{:S(2)}) collective-permute-start(bf16[4,2,288,128]{3,2,1,0:T(8,128)(2,1)S(1)} %get-tuple-element.65), channel_id=1, source_target_pairs={{0,4},{4,0},{8,12},{12,8},{16,20},{20,16},{24,28},{28,24},{1,5},{5... | collective-permute-start | bytes 1769480 | tf_op jit(solution)/shard_map/ppermute | solution.py:474
  20.3 3.8 %copy-start.1 = (bf16[3,3,256,256]{3,2,1,0:T(8,128)(2,1)S(1)}, bf16[3,3,256,256]{3,2,1,0:T(8,128)(2,1)}, u32[]{:S(2)}) copy-start(bf16[3,3,256,256]{3,2,1,0:T(8,128)(2,1)} %param.8) | copy-start | bytes 3538948
  20.6 9.0 %collective-permute-start.8 = (bf16[2,288,128]{2,1,0:T(8,128)(2,1)S(1)}, bf16[2,288,128]{2,1,0:T(8,128)(2,1)S(1)}, u32[]{:S(2)}, u32[]{:S(2)}) collective-permute-start(bf16[2,288,128]{2,1,0:T(8,128)(2,1)S(1)} %get-tuple-element.97), channel_id=1, source_target_pairs={{0,24},{4,28},{8,16},{12,20},{16,8},{20,12},{24,0},{28,4},{1,25},{... | collective-permute-start | bytes 442376 | tf_op jit(solution)/shard_map/ppermute | solution.py:477
  22.3 8.6 %collective-permute-start.7 = (bf16[2,288,128]{2,1,0:T(8,128)(2,1)S(1)}, bf16[2,288,128]{2,1,0:T(8,128)(2,1)S(1)}, u32[]{:S(2)}, u32[]{:S(2)}) collective-permute-start(bf16[2,288,128]{2,1,0:T(8,128)(2,1)S(1)} %get-tuple-element.98), channel_id=1, source_target_pairs={{0,16},{4,20},{8,24},{12,28},{16,0},{20,4},{24,8},{28,12},{1,17},{... | collective-permute-start | bytes 442376 | tf_op jit(solution)/shard_map/ppermute | solution.py:477
  22.9 8.0 %collective-permute-start.6 = (bf16[2,288,128]{2,1,0:T(8,128)(2,1)S(1)}, bf16[2,288,128]{2,1,0:T(8,128)(2,1)S(1)}, u32[]{:S(2)}, u32[]{:S(2)}) collective-permute-start(bf16[2,288,128]{2,1,0:T(8,128)(2,1)S(1)} %get-tuple-element.99), channel_id=1, source_target_pairs={{0,8},{4,12},{8,0},{12,4},{16,24},{20,28},{24,16},{28,20},{1,9},{5... | collective-permute-start | bytes 442376 | tf_op jit(solution)/shard_map/ppermute | solution.py:477
  31.0 5.1 %collective-permute-start.9 = (bf16[1,288,128]{2,1,0:T(8,128)(2,1)S(1)}, bf16[1,288,128]{2,1,0:T(8,128)(2,1)S(1)}, u32[]{:S(2)}, u32[]{:S(2)}) collective-permute-start(bf16[1,288,128]{2,1,0:T(8,128)(2,1)S(1)} %slice.105), channel_id=1, source_target_pairs={{0,1},{1,0},{2,3},{3,2},{4,5},{5,4},{6,7},{7,6},{8,9},{9,8},{10,11... | collective-permute-start | bytes 221192 | tf_op jit(solution)/shard_map/ppermute | solution.py:342
  31.9 6.1 %collective-permute-start.14 = (bf16[256,128]{1,0:T(8,128)(2,1)S(1)}, bf16[256,128]{1,0:T(8,128)(2,1)S(1)}, u32[]{:S(2)}, u32[]{:S(2)}) collective-permute-start(bf16[256,128]{1,0:T(8,128)(2,1)S(1)} %pad_maximum_fusion.3), channel_id=1, source_target_pairs={{0,2},{1,3},{2,0},{3,1},{4,6},{5,7},{6,4},{7,5},{8,10},{9,11},{10,... | collective-permute-start | bytes 196616 | tf_op jit(solution)/shard_map/ppermute | solution.py:342
  36.2 5.8 %collective-permute-start.10 = (bf16[1,288,128]{2,1,0:T(8,128)(2,1)S(1)}, bf16[1,288,128]{2,1,0:T(8,128)(2,1)S(1)}, u32[]{:S(2)}, u32[]{:S(2)}) collective-permute-start(bf16[1,288,128]{2,1,0:T(8,128)(2,1)S(1)} %add_convert_fusion.2.after), channel_id=1, source_target_pairs={{0,2},{1,3},{2,0},{3,1},{4,6},{5,7},{6,4},{7,5},{8,10},{9,11},{10,... | collective-permute-start | bytes 221192 | tf_op jit(solution)/shard_map/ppermute | solution.py:342
  42.1 5.1 %collective-permute-start.15 = (bf16[544,128]{1,0:T(8,128)(2,1)S(1)}, bf16[544,128]{1,0:T(8,128)(2,1)S(1)}, u32[]{:S(2)}, u32[]{:S(2)}) collective-permute-start(bf16[544,128]{1,0:T(8,128)(2,1)S(1)} %pad_maximum_fusion.2), channel_id=1, source_target_pairs={{0,1},{1,0},{2,3},{3,2},{4,5},{5,4},{6,7},{7,6},{8,9},{9,8},{10,11... | collective-permute-start | bytes 417800 | tf_op jit(solution)/shard_map/ppermute | solution.py:342
  42.1 6.9 %collective-permute-start.13 = (bf16[1,288,128]{2,1,0:T(8,128)(2,1)S(1)}, bf16[1,288,128]{2,1,0:T(8,128)(2,1)S(1)}, u32[]{:S(2)}, u32[]{:S(2)}) collective-permute-start(bf16[1,288,128]{2,1,0:T(8,128)(2,1)S(1)} %add_convert_fusion.1.refs_0_), channel_id=1, source_target_pairs={{0,24},{4,28},{8,16},{12,20},{16,8},{20,12},{24,0},{28,4},{1,25},{... | collective-permute-start | bytes 221192 | tf_op jit(solution)/shard_map/ppermute | solution.py:477
  44.1 6.6 %collective-permute-start.12 = (bf16[1,288,128]{2,1,0:T(8,128)(2,1)S(1)}, bf16[1,288,128]{2,1,0:T(8,128)(2,1)S(1)}, u32[]{:S(2)}, u32[]{:S(2)}) collective-permute-start(bf16[1,288,128]{2,1,0:T(8,128)(2,1)S(1)} %add_convert_fusion.1.refs_0_), channel_id=1, source_target_pairs={{0,16},{4,20},{8,24},{12,28},{16,0},{20,4},{24,8},{28,12},{1,17},{... | collective-permute-start | bytes 221192 | tf_op jit(solution)/shard_map/ppermute | solution.py:477
  44.8 5.9 %collective-permute-start.11 = (bf16[1,288,128]{2,1,0:T(8,128)(2,1)S(1)}, bf16[1,288,128]{2,1,0:T(8,128)(2,1)S(1)}, u32[]{:S(2)}, u32[]{:S(2)}) collective-permute-start(bf16[1,288,128]{2,1,0:T(8,128)(2,1)S(1)} %add_convert_fusion.1.refs_0_), channel_id=1, source_target_pairs={{0,8},{4,12},{8,0},{12,4},{16,24},{20,28},{24,16},{28,20},{1,9},{5... | collective-permute-start | bytes 221192 | tf_op jit(solution)/shard_map/ppermute | solution.py:477
  47.2 5.3 %collective-permute-start.18 = (bf16[1,288,128]{2,1,0:T(8,128)(2,1)S(1)}, bf16[1,288,128]{2,1,0:T(8,128)(2,1)S(1)}, u32[]{:S(2)}, u32[]{:S(2)}) collective-permute-start(bf16[1,288,128]{2,1,0:T(8,128)(2,1)S(1)} %slice_bitcast_fusion.12.refs_0_), channel_id=1, source_target_pairs={{0,24},{4,28},{8,16},{12,20},{16,8},{20,12},{24,0},{28,4},{1,25},{... | collective-permute-start | bytes 221192 | tf_op jit(solution)/shard_map/ppermute | solution.py:477
  49.1 4.4 %collective-permute-start.17 = (bf16[1,288,128]{2,1,0:T(8,128)(2,1)S(1)}, bf16[1,288,128]{2,1,0:T(8,128)(2,1)S(1)}, u32[]{:S(2)}, u32[]{:S(2)}) collective-permute-start(bf16[1,288,128]{2,1,0:T(8,128)(2,1)S(1)} %slice_bitcast_fusion.12.refs_0_), channel_id=1, source_target_pairs={{0,16},{4,20},{8,24},{12,28},{16,0},{20,4},{24,8},{28,12},{1,17},{... | collective-permute-start | bytes 221192 | tf_op jit(solution)/shard_map/ppermute | solution.py:477
  49.1 4.4 %collective-permute-start.16 = (bf16[1,288,128]{2,1,0:T(8,128)(2,1)S(1)}, bf16[1,288,128]{2,1,0:T(8,128)(2,1)S(1)}, u32[]{:S(2)}, u32[]{:S(2)}) collective-permute-start(bf16[1,288,128]{2,1,0:T(8,128)(2,1)S(1)} %slice_bitcast_fusion.12.refs_0_), channel_id=1, source_target_pairs={{0,8},{4,12},{8,0},{12,4},{16,24},{20,28},{24,16},{28,20},{1,9},{5... | collective-permute-start | bytes 221192 | tf_op jit(solution)/shard_map/ppermute | solution.py:477
  50.7 2.8 %collective-permute-start.20 = (bf16[4,1,288,128]{3,2,1,0:T(8,128)(2,1)S(1)}, bf16[4,1,288,128]{3,2,1,0:T(8,128)(2,1)S(1)}, u32[]{:S(2)}, u32[]{:S(2)}) collective-permute-start(bf16[4,1,288,128]{3,2,1,0:T(8,128)(2,1)S(1)} %pad_maximum_fusion.1), channel_id=1, source_target_pairs={{0,4},{4,0},{8,12},{12,8},{16,20},{20,16},{24,28},{28,24},{1,5},{5... | collective-permute-start | bytes 884744 | tf_op jit(solution)/shard_map/ppermute | solution.py:474
  53.5 1.6 %collective-permute-start.19 = (bf16[4,1,288,128]{3,2,1,0:T(8,128)(2,1)S(1)}, bf16[4,1,288,128]{3,2,1,0:T(8,128)(2,1)S(1)}, u32[]{:S(2)}, u32[]{:S(2)}) collective-permute-start(bf16[4,1,288,128]{3,2,1,0:T(8,128)(2,1)S(1)} %pad_maximum_fusion), channel_id=1, source_target_pairs={{0,4},{4,0},{8,12},{12,8},{16,20},{20,16},{24,28},{28,24},{1,5},{5... | collective-permute-start | bytes 884744 | tf_op jit(solution)/shard_map/ppermute | solution.py:474

commit v10 on v9

--- a/solution.py
+++ b/solution.py
@@ -82,7 +82,7 @@
             spread(moved, r + 1, (cot[r].astype(F32) * by).astype(BF), zero, zero)
         return 0
 
-    lax.fori_loop(0, rows // 4, group, 0)
+    lax.fori_loop(0, rows // 4, group, 0, unroll=True)
 
 
 def edge_kernel(offset, shifts, scale, moved, *refs):
@@ -152,7 +152,7 @@
             moved[k, r + 1, low : low + 16, :] = tile.astype(BF)
         return 0
 
-    lax.fori_loop(0, rows, patch, 0, unroll=8)
+    lax.fori_loop(0, rows, patch, 0, unroll=True)
     last = rows // 4 - 1
 
     def build(g):

time: 56.3 us -> 56.5 us (level)
  transfers between devices with their start and end apart: 21 -> 21, of which waited for: 10 -> 10; matrix products, arithmetic and copies ran while one was open for 0% -> 0% of each run, Pallas kernels for 31% -> 32%
where the time goes in v10:
time: 56.5 us; the launch traced here: 56.3 us
  starting transfers between devices  21.7 us (38%)
  Pallas kernels  21.2 us (38%)
  waiting for transfers between devices  11.1 us (20%)
  between operations  1.73 us (3%)
    ppermute x9, starting transfers between devices, plane_swap(): return lax.ppermute(x, 'row', xor_pairs(nrow, 2 * s))  10.6 us
    ppermute x7, starting transfers between devices, col_swap(): return lax.ppermute(x, 'col', xor_pairs(n, s))  9.2 us
    pallas_call x3, Pallas kernels, input_piece(): pl.pallas_call(functools.partial(input_kernel, made, size, n), out_shape=...  9.1 us
    ppermute x7, waiting for transfers between devices, col_swap(): return lax.ppermute(x, 'col', xor_pairs(n, s))  7.12 us
    pallas_call x3, Pallas kernels, finish(): pl.pallas_call(functools.partial(finish_kernel, float(pixels) ** (-0.5),...  3.15 us
    pallas_call x1, Pallas kernels, per_device(): pl.pallas_call(functools.partial(prepare_kernel, n, cr), out_shape=[shape...  3.03 us
    ppermute x9, waiting for transfers between devices, plane_swap(): return lax.ppermute(x, 'row', xor_pairs(nrow, 2 * s))  3.03 us
    pallas_call x1, Pallas kernels, per_device(): pl.pallas_call(mine_kernel, out_shape=part, in_specs=[vmem()] * 3, out_sp...  2.36 us
  transfers between devices with their start and end apart: 21, of which 10 were waited for; matrix products, arithmetic and copies ran while one was open for 0% of the time, Pallas kernels for 32%

profile of v10, /device:TPU:0, one launch (start us, length us, event | category | flops | bytes accessed | tf_op | source)
XLA Modules:
  0.0 56.3 jit_solution(3538255331058602786)
XLA Ops:
  0.7 1.6 %start.1 = (bf16[64,256]{1,0:T(8,128)(2,1)S(1)}, bf16[96,256]{1,0:T(8,128)(2,1)S(1)}, bf16[64,256]{1,0:T(8,128)(2,1)S(1)}, bf16[96,256]{1,0:T(8,128)(2,1)S(1)}) custom-call(bf16[32,128,256]{2,1,0:T(8,128)(2,1)} %bitcast.60, bf16[2,128,256]{2,1,0:T(8,128)(2,1)} %bitcast.81), custom_call_target="tpu_custom_call" | custom-call | flops 2147483648 | bytes 4194304 | tf_op jit(solution)/shard_map/start/pallas_call | solution.py:344
  2.2 5.1 %collective-permute-start = (bf16[96,256]{1,0:T(8,128)(2,1)S(1)}, bf16[96,256]{1,0:T(8,128)(2,1)S(1)}, u32[]{:S(2)}, u32[]{:S(2)}) collective-permute-start(bf16[96,256]{1,0:T(8,128)(2,1)S(1)} %get-tuple-element.52), channel_id=1, source_target_pairs={{0,3},{1,2},{2,1},{3,0},{4,7},{5,6},{6,5},{7,4},{8,11},{9,10},{10,... | collective-permute-start | bytes 147464 | tf_op jit(solution)/shard_map/ppermute | solution.py:342
  7.3 0.0 collective-permute-start.1
  7.3 0.6 %collective-permute-start.2 = (bf16[64,256]{1,0:T(8,128)(2,1)S(1)}, bf16[64,256]{1,0:T(8,128)(2,1)S(1)}, u32[]{:S(2)}, u32[]{:S(2)}) collective-permute-start(bf16[64,256]{1,0:T(8,128)(2,1)S(1)} %get-tuple-element.57), channel_id=1, source_target_pairs={{0,2},{1,3},{2,0},{3,1},{4,6},{5,7},{6,4},{7,5},{8,10},{9,11},{10,... | collective-permute-start | bytes 98312 | tf_op jit(solution)/shard_map/ppermute | solution.py:342
  8.7 1.0 %load.1 = (bf16[3,34,128,256]{3,2,1,0:T(8,128)(2,1)S(1)}, f32[1,256]{1,0:T(1,128)S(1)}) custom-call(s32[1]{0:T(128)S(6)} %copy.21.steps, bf16[32,128,256]{2,1,0:T(8,128)(2,1)S(1)} %bitcast.61, f32[1000,256]{1,0:T(8,128)S(1)} %copy-done.3), custom_call_target="tpu_custom_call" | custom-call | flops 1048576 | bytes 4194304 | tf_op jit(solution)/shard_map/load/pallas_call | solution.py:360
  9.7 1.7 %collective-permute-done.1.refs_1_ = bf16[96,256]{1,0:T(8,128)(2,1)S(1)} collective-permute-done((bf16[96,256]{1,0:T(8,128)(2,1)S(1)}, bf16[96,256]{1,0:T(8,128)(2,1)S(1)}, u32[]{:S(2)}, u32[]{:S(2)}) %collective-permute-start.1) | collective-permute-done | bytes 49184 | tf_op jit(solution)/shard_map/ppermute | solution.py:342
  11.4 0.1 edges.1
  11.5 0.7 %collective-permute-start.3 = (bf16[144,256]{1,0:T(8,128)(2,1)S(1)}, bf16[144,256]{1,0:T(8,128)(2,1)S(1)}, u32[]{:S(2)}, u32[]{:S(2)}) collective-permute-start(bf16[144,256]{1,0:T(8,128)(2,1)S(1)} %get-tuple-element.59), channel_id=1, source_target_pairs={{4,8},{12,16},{20,24},{28,0},{8,4},{16,12},{24,20},{0,28},{5,9},{1... | collective-permute-start | bytes 221192 | tf_op jit(solution)/shard_map/ppermute | solution.py:385
  12.2 1.0 %collective-permute-start.4 = (bf16[144,256]{1,0:T(8,128)(2,1)S(1)}, bf16[144,256]{1,0:T(8,128)(2,1)S(1)}, u32[]{:S(2)}, u32[]{:S(2)}) collective-permute-start(bf16[144,256]{1,0:T(8,128)(2,1)S(1)} %get-tuple-element.60), channel_id=1, source_target_pairs={{0,4},{4,0},{8,12},{12,8},{16,20},{20,16},{24,28},{28,24},{1,5},{5... | collective-permute-start | bytes 221192 | tf_op jit(solution)/shard_map/ppermute | solution.py:388
  13.2 3.0 %prepare.1 = (bf16[3,34,128,256]{3,2,1,0:T(8,128)(2,1)S(1)}, bf16[256,4096]{1,0:T(8,128)(2,1)S(1)}, bf16[8,32,256]{2,1,0:T(8,128)(2,1)S(1)}, f32[5,256,256]{2,1,0:T(8,128)S(1)}) custom-call(bf16[32,128,256]{2,1,0:T(8,128)(2,1)S(1)} %bitcast.53, f32[32,256]{1,0:T(8,128)S(1)} %get-tuple-element.54.left, ...), custom_call_target="tpu_custom_call", output_to_operand_aliasing={{0}: (3, {})} | custom-call | flops 4294967296 | bytes 4194304 | tf_op jit(solution)/shard_map/prepare/pallas_call | solution.py:391
  16.2 0.7 %collective-permute-done.3.two = bf16[144,256]{1,0:T(8,128)(2,1)S(1)} collective-permute-done((bf16[144,256]{1,0:T(8,128)(2,1)S(1)}, bf16[144,256]{1,0:T(8,128)(2,1)S(1)}, u32[]{:S(2)}, u32[]{:S(2)}) %collective-permute-start.3) | collective-permute-done | bytes 73760 | tf_op jit(solution)/shard_map/ppermute | solution.py:385
  16.9 0.0 collective-permute-done.4.one
  16.9 0.9 %weight_other.1 = (bf16[4,2,288,128]{3,2,1,0:T(8,128)(2,1)S(1)}, f32[256,128]{1,0:T(8,128)S(1)}, bf16[3,34,128,256]{3,2,1,0:T(8,128)(2,1)S(1)}) custom-call(bf16[256,4096]{1,0:T(8,128)(2,1)S(1)} %get-tuple-element.58.act_t, bf16[144,256]{1,0:T(8,128)(2,1)S(1)} %collective-permute-done.3.two, ...), custom_call_target="tpu_custom_call", output_to_operand_aliasing={{2}: (4, {})} | custom-call | flops 603979776 | bytes 8388608 | tf_op jit(solution)/shard_map/weight_other/pallas_call | solution.py:414
  17.9 0.1 collective-permute-start.5
  18.0 2.4 %weight_mine.1 = bf16[4,2,288,128]{3,2,1,0:T(8,128)(2,1)S(1)} custom-call(bf16[256,4096]{1,0:T(8,128)(2,1)S(1)} %get-tuple-element.58.act_t, f32[256,128]{1,0:T(8,128)S(1)} %get-tuple-element.63.rest, bf16[3,34,128,256]{3,2,1,0:T(8,128)(2,1)S(1)} %get-tuple-element.64.moved), custom_call_target="tpu_custom_call" | custom-call | flops 2147483648 | bytes 8388608 | tf_op jit(solution)/shard_map/weight_mine/pallas_call | solution.py:424
  20.3 0.0 copy-start.1
  20.3 0.0 collective-permute-done.5
  20.3 0.2 add_convert_fusion.after
  20.6 1.7 %collective-permute-start.8 = (bf16[2,288,128]{2,1,0:T(8,128)(2,1)S(1)}, bf16[2,288,128]{2,1,0:T(8,128)(2,1)S(1)}, u32[]{:S(2)}, u32[]{:S(2)}) collective-permute-start(bf16[2,288,128]{2,1,0:T(8,128)(2,1)S(1)} %get-tuple-element.97), channel_id=1, source_target_pairs={{0,24},{4,28},{8,16},{12,20},{16,8},{20,12},{24,0},{28,4},{1,25},{... | collective-permute-start | bytes 442376 | tf_op jit(solution)/shard_map/ppermute | solution.py:477
  22.2 0.7 %collective-permute-start.7 = (bf16[2,288,128]{2,1,0:T(8,128)(2,1)S(1)}, bf16[2,288,128]{2,1,0:T(8,128)(2,1)S(1)}, u32[]{:S(2)}, u32[]{:S(2)}) collective-permute-start(bf16[2,288,128]{2,1,0:T(8,128)(2,1)S(1)} %get-tuple-element.98), channel_id=1, source_target_pairs={{0,16},{4,20},{8,24},{12,28},{16,0},{20,4},{24,8},{28,12},{1,17},{... | collective-permute-start | bytes 442376 | tf_op jit(solution)/shard_map/ppermute | solution.py:477
  22.9 1.2 %collective-permute-start.6 = (bf16[2,288,128]{2,1,0:T(8,128)(2,1)S(1)}, bf16[2,288,128]{2,1,0:T(8,128)(2,1)S(1)}, u32[]{:S(2)}, u32[]{:S(2)}) collective-permute-start(bf16[2,288,128]{2,1,0:T(8,128)(2,1)S(1)} %get-tuple-element.99), channel_id=1, source_target_pairs={{0,8},{4,12},{8,0},{12,4},{16,24},{20,28},{24,16},{28,20},{1,9},{5... | collective-permute-start | bytes 442376 | tf_op jit(solution)/shard_map/ppermute | solution.py:477
  24.1 5.5 %input_grad.3 = (bf16[32,128,256]{2,1,0:T(8,128)(2,1)}, bf16[6,2,32,128]{3,2,1,0:T(8,128)(2,1)S(1)}) custom-call(bf16[4,2,288,128]{3,2,1,0:T(8,128)(2,1)S(1)} %add_convert_fusion.after, bf16[3,34,128,256]{3,2,1,0:T(8,128)(2,1)S(1)} %get-tuple-element.64.moved, bf16[32,128,256]{2,1,0:T(8,128)(2,1)S(1)} %bitcast.54, ...), custom_call_target="tpu_custom_call" | custom-call | flops 3623878656 | bytes 4194304 | tf_op jit(solution)/shard_map/input_grad/pallas_call | solution.py:438
  29.6 1.3 %collective-permute-done.7 = bf16[2,288,128]{2,1,0:T(8,128)(2,1)S(1)} collective-permute-done((bf16[2,288,128]{2,1,0:T(8,128)(2,1)S(1)}, bf16[2,288,128]{2,1,0:T(8,128)(2,1)S(1)}, u32[]{:S(2)}, u32[]{:S(2)}) %collective-permute-start.7) | collective-permute-done | bytes 147488 | tf_op jit(solution)/shard_map/ppermute | solution.py:477
  30.9 0.1 fusion.2.after
  31.0 0.9 %collective-permute-start.9 = (bf16[1,288,128]{2,1,0:T(8,128)(2,1)S(1)}, bf16[1,288,128]{2,1,0:T(8,128)(2,1)S(1)}, u32[]{:S(2)}, u32[]{:S(2)}) collective-permute-start(bf16[1,288,128]{2,1,0:T(8,128)(2,1)S(1)} %slice.105), channel_id=1, source_target_pairs={{0,1},{1,0},{2,3},{3,2},{4,5},{5,4},{6,7},{7,6},{8,9},{9,8},{10,11... | collective-permute-start | bytes 221192 | tf_op jit(solution)/shard_map/ppermute | solution.py:342
  31.9 1.9 %collective-permute-start.14 = (bf16[256,128]{1,0:T(8,128)(2,1)S(1)}, bf16[256,128]{1,0:T(8,128)(2,1)S(1)}, u32[]{:S(2)}, u32[]{:S(2)}) collective-permute-start(bf16[256,128]{1,0:T(8,128)(2,1)S(1)} %pad_maximum_fusion.3), channel_id=1, source_target_pairs={{0,2},{1,3},{2,0},{3,1},{4,6},{5,7},{6,4},{7,5},{8,10},{9,11},{10,... | collective-permute-start | bytes 196616 | tf_op jit(solution)/shard_map/ppermute | solution.py:342
  33.7 1.9 %input_grad.4 = (bf16[32,128,256]{2,1,0:T(8,128)(2,1)}, bf16[1,2,32,128]{3,2,1,0:T(8,128)(2,1)S(1)}) custom-call(bf16[2,288,128]{2,1,0:T(8,128)(2,1)S(1)} %fusion.2.after, bf16[3,34,128,256]{3,2,1,0:T(8,128)(2,1)S(1)} %get-tuple-element.64.moved, bf16[32,128,256]{2,1,0:T(8,128)(2,1)S(1)} %bitcast.55, ...), custom_call_target="tpu_custom_call", output_to_operand_aliasing={{0}: (5, {})} | custom-call | flops 603979776 | bytes 4194304 | tf_op jit(solution)/shard_map/input_grad/pallas_call | solution.py:438
  35.7 0.5 collective-permute-done.9
  36.2 0.7 %collective-permute-start.10 = (bf16[1,288,128]{2,1,0:T(8,128)(2,1)S(1)}, bf16[1,288,128]{2,1,0:T(8,128)(2,1)S(1)}, u32[]{:S(2)}, u32[]{:S(2)}) collective-permute-start(bf16[1,288,128]{2,1,0:T(8,128)(2,1)S(1)} %add_convert_fusion.2.after), channel_id=1, source_target_pairs={{0,2},{1,3},{2,0},{3,1},{4,6},{5,7},{6,4},{7,5},{8,10},{9,11},{10,... | collective-permute-start | bytes 221192 | tf_op jit(solution)/shard_map/ppermute | solution.py:342
  36.8 1.1 %collective-permute-done.14 = bf16[256,128]{1,0:T(8,128)(2,1)S(1)} collective-permute-done((bf16[256,128]{1,0:T(8,128)(2,1)S(1)}, bf16[256,128]{1,0:T(8,128)(2,1)S(1)}, u32[]{:S(2)}, u32[]{:S(2)}) %collective-permute-start.14) | collective-permute-done | bytes 65568 | tf_op jit(solution)/shard_map/ppermute | solution.py:342
  37.9 1.7 %input_grad.5 = (bf16[32,128,256]{2,1,0:T(8,128)(2,1)}, bf16[1,2,32,128]{3,2,1,0:T(8,128)(2,1)S(1)}) custom-call(bf16[1,288,128]{2,1,0:T(8,128)(2,1)S(1)} %add_convert_fusion.2.after, bf16[3,34,128,256]{3,2,1,0:T(8,128)(2,1)S(1)} %get-tuple-element.64.moved, bf16[32,128,256]{2,1,0:T(8,128)(2,1)S(1)} %bitcast.56, ...), custom_call_target="tpu_custom_call", output_to_operand_aliasing={{0}: (5, {})} | custom-call | flops 603979776 | bytes 4194304 | tf_op jit(solution)/shard_map/input_grad/pallas_call | solution.py:438
  39.7 2.3 %collective-permute-done.10 = bf16[1,288,128]{2,1,0:T(8,128)(2,1)S(1)} collective-permute-done((bf16[1,288,128]{2,1,0:T(8,128)(2,1)S(1)}, bf16[1,288,128]{2,1,0:T(8,128)(2,1)S(1)}, u32[]{:S(2)}, u32[]{:S(2)}) %collective-permute-start.10) | collective-permute-done | bytes 73760 | tf_op jit(solution)/shard_map/ppermute | solution.py:342
  42.0 0.1 collective-permute-start.15
  42.1 2.0 %collective-permute-start.13 = (bf16[1,288,128]{2,1,0:T(8,128)(2,1)S(1)}, bf16[1,288,128]{2,1,0:T(8,128)(2,1)S(1)}, u32[]{:S(2)}, u32[]{:S(2)}) collective-permute-start(bf16[1,288,128]{2,1,0:T(8,128)(2,1)S(1)} %add_convert_fusion.1.refs_0_), channel_id=1, source_target_pairs={{0,24},{4,28},{8,16},{12,20},{16,8},{20,12},{24,0},{28,4},{1,25},{... | collective-permute-start | bytes 221192 | tf_op jit(solution)/shard_map/ppermute | solution.py:477
  44.1 0.7 %collective-permute-start.12 = (bf16[1,288,128]{2,1,0:T(8,128)(2,1)S(1)}, bf16[1,288,128]{2,1,0:T(8,128)(2,1)S(1)}, u32[]{:S(2)}, u32[]{:S(2)}) collective-permute-start(bf16[1,288,128]{2,1,0:T(8,128)(2,1)S(1)} %add_convert_fusion.1.refs_0_), channel_id=1, source_target_pairs={{0,16},{4,20},{8,24},{12,28},{16,0},{20,4},{24,8},{28,12},{1,17},{... | collective-permute-start | bytes 221192 | tf_op jit(solution)/shard_map/ppermute | solution.py:477
  44.8 0.9 %collective-permute-start.11 = (bf16[1,288,128]{2,1,0:T(8,128)(2,1)S(1)}, bf16[1,288,128]{2,1,0:T(8,128)(2,1)S(1)}, u32[]{:S(2)}, u32[]{:S(2)}) collective-permute-start(bf16[1,288,128]{2,1,0:T(8,128)(2,1)S(1)} %add_convert_fusion.1.refs_0_), channel_id=1, source_target_pairs={{0,8},{4,12},{8,0},{12,4},{16,24},{20,28},{24,16},{28,20},{1,9},{5... | collective-permute-start | bytes 221192 | tf_op jit(solution)/shard_map/ppermute | solution.py:477
  45.7 1.5 %collective-permute-done.15 = bf16[544,128]{1,0:T(8,128)(2,1)S(1)} collective-permute-done((bf16[544,128]{1,0:T(8,128)(2,1)S(1)}, bf16[544,128]{1,0:T(8,128)(2,1)S(1)}, u32[]{:S(2)}, u32[]{:S(2)}) %collective-permute-start.15) | collective-permute-done | bytes 139296 | tf_op jit(solution)/shard_map/ppermute | solution.py:342
  47.2 1.9 %collective-permute-start.18 = (bf16[1,288,128]{2,1,0:T(8,128)(2,1)S(1)}, bf16[1,288,128]{2,1,0:T(8,128)(2,1)S(1)}, u32[]{:S(2)}, u32[]{:S(2)}) collective-permute-start(bf16[1,288,128]{2,1,0:T(8,128)(2,1)S(1)} %slice_bitcast_fusion.12.refs_0_), channel_id=1, source_target_pairs={{0,24},{4,28},{8,16},{12,20},{16,8},{20,12},{24,0},{28,4},{1,25},{... | collective-permute-start | bytes 221192 | tf_op jit(solution)/shard_map/ppermute | solution.py:477
  49.1 1.6 %collective-permute-start.16 = (bf16[1,288,128]{2,1,0:T(8,128)(2,1)S(1)}, bf16[1,288,128]{2,1,0:T(8,128)(2,1)S(1)}, u32[]{:S(2)}, u32[]{:S(2)}) collective-permute-start(bf16[1,288,128]{2,1,0:T(8,128)(2,1)S(1)} %slice_bitcast_fusion.12.refs_0_), channel_id=1, source_target_pairs={{0,8},{4,12},{8,0},{12,4},{16,24},{20,28},{24,16},{28,20},{1,9},{5... | collective-permute-start | bytes 221192 | tf_op jit(solution)/shard_map/ppermute | solution.py:477
  50.7 0.1 collective-permute-start.20
  50.8 0.9 %finish.3.refs_8_ = f32[9,256,256]{2,1,0:T(8,128)} custom-call(bf16[1,288,128]{2,1,0:T(8,128)(2,1)S(1)} %add_convert_fusion.1.refs_0_, bf16[1,288,128]{2,1,0:T(8,128)(2,1)S(1)} %collective-permute-done.11.refs_1_, bf16[1,288,128]{2,1,0:T(8,128)(2,1)S(1)} %collective-permute-done.12.refs_2_, bf16[1,288,128]{2,1,0:T(8,128)(2,1)S(1)} %collective-permute-done.13.refs_3_), custom_call_target="tpu_custom_call" | custom-call | flops 1048576 | bytes 4194304 | tf_op jit(solution)/shard_map/finish/pallas_call | solution.py:538
  51.7 0.7 %collective-permute-done.18.refs_3_ = bf16[1,288,128]{2,1,0:T(8,128)(2,1)S(1)} collective-permute-done((bf16[1,288,128]{2,1,0:T(8,128)(2,1)S(1)}, bf16[1,288,128]{2,1,0:T(8,128)(2,1)S(1)}, u32[]{:S(2)}, u32[]{:S(2)}) %collective-permute-start.18) | collective-permute-done | bytes 73760 | tf_op jit(solution)/shard_map/ppermute | solution.py:477
  52.4 1.0 %collective-permute-done.17.refs_2_ = bf16[1,288,128]{2,1,0:T(8,128)(2,1)S(1)} collective-permute-done((bf16[1,288,128]{2,1,0:T(8,128)(2,1)S(1)}, bf16[1,288,128]{2,1,0:T(8,128)(2,1)S(1)}, u32[]{:S(2)}, u32[]{:S(2)}) %collective-permute-start.17) | collective-permute-done | bytes 73760 | tf_op jit(solution)/shard_map/ppermute | solution.py:477
  53.4 0.0 collective-permute-done.16.refs_1_
  53.5 0.1 collective-permute-start.19
  53.6 1.2 %finish.4.refs_8_ = f32[9,256,256]{2,1,0:T(8,128)} custom-call(bf16[1,288,128]{2,1,0:T(8,128)(2,1)S(1)} %slice_bitcast_fusion.12.refs_0_, bf16[1,288,128]{2,1,0:T(8,128)(2,1)S(1)} %collective-permute-done.16.refs_1_, bf16[1,288,128]{2,1,0:T(8,128)(2,1)S(1)} %collective-permute-done.17.refs_2_, ...), custom_call_target="tpu_custom_call", output_to_operand_aliasing={{}: (8, {})} | custom-call | flops 1048576 | bytes 4194304 | tf_op jit(solution)/shard_map/finish/pallas_call | solution.py:538
  54.8 0.3 collective-permute-done.19
  55.1 1.0 %finish.5 = (f32[9,256,256]{2,1,0:T(8,128)}, bf16[2,128,256]{2,1,0:T(8,128)(2,1)}) custom-call(bf16[1,288,128]{2,1,0:T(8,128)(2,1)S(1)} %get-tuple-element.107.refs_0_, bf16[1,288,128]{2,1,0:T(8,128)(2,1)S(1)} %get-tuple-element.106.refs_1_, bf16[1,288,128]{2,1,0:T(8,128)(2,1)S(1)} %get-tuple-element.105.refs_2_, ...), custom_call_target="tpu_custom_call", output_to_operand_aliasing={{0}: (8, {})} | custom-call | flops 1048576 | bytes 4194304 | tf_op jit(solution)/shard_map/finish/pallas_call | solution.py:538
  (32 shorter events, 0.3 us)
Async XLA Ops:
  0.6 8.0 %copy-start.2 = (bf16[1,32,128,256]{3,2,1,0:T(8,128)(2,1)S(1)}, bf16[1,32,128,256]{3,2,1,0:T(8,128)(2,1)}, u32[]{:S(2)}) copy-start(bf16[1,32,128,256]{3,2,1,0:T(8,128)(2,1)} %param.11) | copy-start | bytes 6291460
  0.6 8.0 %copy-start.3 = (f32[1000,256]{1,0:T(8,128)S(1)}, f32[1000,256]{1,0:T(8,128)}, u32[]{:S(2)}) copy-start(f32[1000,256]{1,0:T(8,128)} %scales.1) | copy-start | bytes 3072004
  2.2 7.5 %collective-permute-start = (bf16[96,256]{1,0:T(8,128)(2,1)S(1)}, bf16[96,256]{1,0:T(8,128)(2,1)S(1)}, u32[]{:S(2)}, u32[]{:S(2)}) collective-permute-start(bf16[96,256]{1,0:T(8,128)(2,1)S(1)} %get-tuple-element.52), channel_id=1, source_target_pairs={{0,3},{1,2},{2,1},{3,0},{4,7},{5,6},{6,5},{7,4},{8,11},{9,10},{10,... | collective-permute-start | bytes 147464 | tf_op jit(solution)/shard_map/ppermute | solution.py:342
  7.3 4.1 %collective-permute-start.1 = (bf16[96,256]{1,0:T(8,128)(2,1)S(1)}, bf16[96,256]{1,0:T(8,128)(2,1)S(1)}, u32[]{:S(2)}, u32[]{:S(2)}) collective-permute-start(bf16[96,256]{1,0:T(8,128)(2,1)S(1)} %get-tuple-element.53), channel_id=1, source_target_pairs={{0,1},{1,0},{2,3},{3,2},{4,5},{5,4},{6,7},{7,6},{8,9},{9,8},{10,11... | collective-permute-start | bytes 147464 | tf_op jit(solution)/shard_map/ppermute | solution.py:342
  7.3 5.8 %collective-permute-start.2 = (bf16[64,256]{1,0:T(8,128)(2,1)S(1)}, bf16[64,256]{1,0:T(8,128)(2,1)S(1)}, u32[]{:S(2)}, u32[]{:S(2)}) collective-permute-start(bf16[64,256]{1,0:T(8,128)(2,1)S(1)} %get-tuple-element.57), channel_id=1, source_target_pairs={{0,2},{1,3},{2,0},{3,1},{4,6},{5,7},{6,4},{7,5},{8,10},{9,11},{10,... | collective-permute-start | bytes 98312 | tf_op jit(solution)/shard_map/ppermute | solution.py:342
  11.4 1.7 %copy-start = (bf16[1,32,128,256]{3,2,1,0:T(8,128)(2,1)S(1)}, bf16[1,32,128,256]{3,2,1,0:T(8,128)(2,1)}, u32[]{:S(2)}) copy-start(bf16[1,32,128,256]{3,2,1,0:T(8,128)(2,1)} %param.6) | copy-start | bytes 6291460
  11.5 5.4 %collective-permute-start.3 = (bf16[144,256]{1,0:T(8,128)(2,1)S(1)}, bf16[144,256]{1,0:T(8,128)(2,1)S(1)}, u32[]{:S(2)}, u32[]{:S(2)}) collective-permute-start(bf16[144,256]{1,0:T(8,128)(2,1)S(1)} %get-tuple-element.59), channel_id=1, source_target_pairs={{4,8},{12,16},{20,24},{28,0},{8,4},{16,12},{24,20},{0,28},{5,9},{1... | collective-permute-start | bytes 221192 | tf_op jit(solution)/shard_map/ppermute | solution.py:385
  12.2 4.8 %collective-permute-start.4 = (bf16[144,256]{1,0:T(8,128)(2,1)S(1)}, bf16[144,256]{1,0:T(8,128)(2,1)S(1)}, u32[]{:S(2)}, u32[]{:S(2)}) collective-permute-start(bf16[144,256]{1,0:T(8,128)(2,1)S(1)} %get-tuple-element.60), channel_id=1, source_target_pairs={{0,4},{4,0},{8,12},{12,8},{16,20},{20,16},{24,28},{28,24},{1,5},{5... | collective-permute-start | bytes 221192 | tf_op jit(solution)/shard_map/ppermute | solution.py:388
  17.9 2.5 %collective-permute-start.5 = (bf16[4,2,288,128]{3,2,1,0:T(8,128)(2,1)S(1)}, bf16[4,2,288,128]{3,2,1,0:T(8,128)(2,1)S(1)}, u32[]{:S(2)}, u32[]{:S(2)}) collective-permute-start(bf16[4,2,288,128]{3,2,1,0:T(8,128)(2,1)S(1)} %get-tuple-element.65), channel_id=1, source_target_pairs={{0,4},{4,0},{8,12},{12,8},{16,20},{20,16},{24,28},{28,24},{1,5},{5... | collective-permute-start | bytes 1769480 | tf_op jit(solution)/shard_map/ppermute | solution.py:474
  20.3 3.8 %copy-start.1 = (bf16[3,3,256,256]{3,2,1,0:T(8,128)(2,1)S(1)}, bf16[3,3,256,256]{3,2,1,0:T(8,128)(2,1)}, u32[]{:S(2)}) copy-start(bf16[3,3,256,256]{3,2,1,0:T(8,128)(2,1)} %param.8) | copy-start | bytes 3538948
  20.6 9.0 %collective-permute-start.8 = (bf16[2,288,128]{2,1,0:T(8,128)(2,1)S(1)}, bf16[2,288,128]{2,1,0:T(8,128)(2,1)S(1)}, u32[]{:S(2)}, u32[]{:S(2)}) collective-permute-start(bf16[2,288,128]{2,1,0:T(8,128)(2,1)S(1)} %get-tuple-element.97), channel_id=1, source_target_pairs={{0,24},{4,28},{8,16},{12,20},{16,8},{20,12},{24,0},{28,4},{1,25},{... | collective-permute-start | bytes 442376 | tf_op jit(solution)/shard_map/ppermute | solution.py:477
  22.2 8.7 %collective-permute-start.7 = (bf16[2,288,128]{2,1,0:T(8,128)(2,1)S(1)}, bf16[2,288,128]{2,1,0:T(8,128)(2,1)S(1)}, u32[]{:S(2)}, u32[]{:S(2)}) collective-permute-start(bf16[2,288,128]{2,1,0:T(8,128)(2,1)S(1)} %get-tuple-element.98), channel_id=1, source_target_pairs={{0,16},{4,20},{8,24},{12,28},{16,0},{20,4},{24,8},{28,12},{1,17},{... | collective-permute-start | bytes 442376 | tf_op jit(solution)/shard_map/ppermute | solution.py:477
  22.9 8.0 %collective-permute-start.6 = (bf16[2,288,128]{2,1,0:T(8,128)(2,1)S(1)}, bf16[2,288,128]{2,1,0:T(8,128)(2,1)S(1)}, u32[]{:S(2)}, u32[]{:S(2)}) collective-permute-start(bf16[2,288,128]{2,1,0:T(8,128)(2,1)S(1)} %get-tuple-element.99), channel_id=1, source_target_pairs={{0,8},{4,12},{8,0},{12,4},{16,24},{20,28},{24,16},{28,20},{1,9},{5... | collective-permute-start | bytes 442376 | tf_op jit(solution)/shard_map/ppermute | solution.py:477
  31.0 5.1 %collective-permute-start.9 = (bf16[1,288,128]{2,1,0:T(8,128)(2,1)S(1)}, bf16[1,288,128]{2,1,0:T(8,128)(2,1)S(1)}, u32[]{:S(2)}, u32[]{:S(2)}) collective-permute-start(bf16[1,288,128]{2,1,0:T(8,128)(2,1)S(1)} %slice.105), channel_id=1, source_target_pairs={{0,1},{1,0},{2,3},{3,2},{4,5},{5,4},{6,7},{7,6},{8,9},{9,8},{10,11... | collective-permute-start | bytes 221192 | tf_op jit(solution)/shard_map/ppermute | solution.py:342
  31.9 6.1 %collective-permute-start.14 = (bf16[256,128]{1,0:T(8,128)(2,1)S(1)}, bf16[256,128]{1,0:T(8,128)(2,1)S(1)}, u32[]{:S(2)}, u32[]{:S(2)}) collective-permute-start(bf16[256,128]{1,0:T(8,128)(2,1)S(1)} %pad_maximum_fusion.3), channel_id=1, source_target_pairs={{0,2},{1,3},{2,0},{3,1},{4,6},{5,7},{6,4},{7,5},{8,10},{9,11},{10,... | collective-permute-start | bytes 196616 | tf_op jit(solution)/shard_map/ppermute | solution.py:342
  36.2 5.8 %collective-permute-start.10 = (bf16[1,288,128]{2,1,0:T(8,128)(2,1)S(1)}, bf16[1,288,128]{2,1,0:T(8,128)(2,1)S(1)}, u32[]{:S(2)}, u32[]{:S(2)}) collective-permute-start(bf16[1,288,128]{2,1,0:T(8,128)(2,1)S(1)} %add_convert_fusion.2.after), channel_id=1, source_target_pairs={{0,2},{1,3},{2,0},{3,1},{4,6},{5,7},{6,4},{7,5},{8,10},{9,11},{10,... | collective-permute-start | bytes 221192 | tf_op jit(solution)/shard_map/ppermute | solution.py:342
  42.0 5.1 %collective-permute-start.15 = (bf16[544,128]{1,0:T(8,128)(2,1)S(1)}, bf16[544,128]{1,0:T(8,128)(2,1)S(1)}, u32[]{:S(2)}, u32[]{:S(2)}) collective-permute-start(bf16[544,128]{1,0:T(8,128)(2,1)S(1)} %pad_maximum_fusion.2), channel_id=1, source_target_pairs={{0,1},{1,0},{2,3},{3,2},{4,5},{5,4},{6,7},{7,6},{8,9},{9,8},{10,11... | collective-permute-start | bytes 417800 | tf_op jit(solution)/shard_map/ppermute | solution.py:342
  42.1 7.0 %collective-permute-start.13 = (bf16[1,288,128]{2,1,0:T(8,128)(2,1)S(1)}, bf16[1,288,128]{2,1,0:T(8,128)(2,1)S(1)}, u32[]{:S(2)}, u32[]{:S(2)}) collective-permute-start(bf16[1,288,128]{2,1,0:T(8,128)(2,1)S(1)} %add_convert_fusion.1.refs_0_), channel_id=1, source_target_pairs={{0,24},{4,28},{8,16},{12,20},{16,8},{20,12},{24,0},{28,4},{1,25},{... | collective-permute-start | bytes 221192 | tf_op jit(solution)/shard_map/ppermute | solution.py:477
  44.1 6.6 %collective-permute-start.12 = (bf16[1,288,128]{2,1,0:T(8,128)(2,1)S(1)}, bf16[1,288,128]{2,1,0:T(8,128)(2,1)S(1)}, u32[]{:S(2)}, u32[]{:S(2)}) collective-permute-start(bf16[1,288,128]{2,1,0:T(8,128)(2,1)S(1)} %add_convert_fusion.1.refs_0_), channel_id=1, source_target_pairs={{0,16},{4,20},{8,24},{12,28},{16,0},{20,4},{24,8},{28,12},{1,17},{... | collective-permute-start | bytes 221192 | tf_op jit(solution)/shard_map/ppermute | solution.py:477
  44.8 5.9 %collective-permute-start.11 = (bf16[1,288,128]{2,1,0:T(8,128)(2,1)S(1)}, bf16[1,288,128]{2,1,0:T(8,128)(2,1)S(1)}, u32[]{:S(2)}, u32[]{:S(2)}) collective-permute-start(bf16[1,288,128]{2,1,0:T(8,128)(2,1)S(1)} %add_convert_fusion.1.refs_0_), channel_id=1, source_target_pairs={{0,8},{4,12},{8,0},{12,4},{16,24},{20,28},{24,16},{28,20},{1,9},{5... | collective-permute-start | bytes 221192 | tf_op jit(solution)/shard_map/ppermute | solution.py:477
  47.2 5.3 %collective-permute-start.18 = (bf16[1,288,128]{2,1,0:T(8,128)(2,1)S(1)}, bf16[1,288,128]{2,1,0:T(8,128)(2,1)S(1)}, u32[]{:S(2)}, u32[]{:S(2)}) collective-permute-start(bf16[1,288,128]{2,1,0:T(8,128)(2,1)S(1)} %slice_bitcast_fusion.12.refs_0_), channel_id=1, source_target_pairs={{0,24},{4,28},{8,16},{12,20},{16,8},{20,12},{24,0},{28,4},{1,25},{... | collective-permute-start | bytes 221192 | tf_op jit(solution)/shard_map/ppermute | solution.py:477
  49.1 4.4 %collective-permute-start.17 = (bf16[1,288,128]{2,1,0:T(8,128)(2,1)S(1)}, bf16[1,288,128]{2,1,0:T(8,128)(2,1)S(1)}, u32[]{:S(2)}, u32[]{:S(2)}) collective-permute-start(bf16[1,288,128]{2,1,0:T(8,128)(2,1)S(1)} %slice_bitcast_fusion.12.refs_0_), channel_id=1, source_target_pairs={{0,16},{4,20},{8,24},{12,28},{16,0},{20,4},{24,8},{28,12},{1,17},{... | collective-permute-start | bytes 221192 | tf_op jit(solution)/shard_map/ppermute | solution.py:477
  49.1 4.4 %collective-permute-start.16 = (bf16[1,288,128]{2,1,0:T(8,128)(2,1)S(1)}, bf16[1,288,128]{2,1,0:T(8,128)(2,1)S(1)}, u32[]{:S(2)}, u32[]{:S(2)}) collective-permute-start(bf16[1,288,128]{2,1,0:T(8,128)(2,1)S(1)} %slice_bitcast_fusion.12.refs_0_), channel_id=1, source_target_pairs={{0,8},{4,12},{8,0},{12,4},{16,24},{20,28},{24,16},{28,20},{1,9},{5... | collective-permute-start | bytes 221192 | tf_op jit(solution)/shard_map/ppermute | solution.py:477
  50.7 2.9 %collective-permute-start.20 = (bf16[4,1,288,128]{3,2,1,0:T(8,128)(2,1)S(1)}, bf16[4,1,288,128]{3,2,1,0:T(8,128)(2,1)S(1)}, u32[]{:S(2)}, u32[]{:S(2)}) collective-permute-start(bf16[4,1,288,128]{3,2,1,0:T(8,128)(2,1)S(1)} %pad_maximum_fusion.1), channel_id=1, source_target_pairs={{0,4},{4,0},{8,12},{12,8},{16,20},{20,16},{24,28},{28,24},{1,5},{5... | collective-permute-start | bytes 884744 | tf_op jit(solution)/shard_map/ppermute | solution.py:474
  53.5 1.6 %collective-permute-start.19 = (bf16[4,1,288,128]{3,2,1,0:T(8,128)(2,1)S(1)}, bf16[4,1,288,128]{3,2,1,0:T(8,128)(2,1)S(1)}, u32[]{:S(2)}, u32[]{:S(2)}) collective-permute-start(bf16[4,1,288,128]{3,2,1,0:T(8,128)(2,1)S(1)} %pad_maximum_fusion), channel_id=1, source_target_pairs={{0,4},{4,0},{8,12},{12,8},{16,20},{20,16},{24,28},{28,24},{1,5},{5... | collective-permute-start | bytes 884744 | tf_op jit(solution)/shard_map/ppermute | solution.py:474
